TPU v7x, 32 devices: a whole 2x2x4 slice. The times are simulated.
32 devices in a mesh: blk: 8 (over z, y), head: 4 (over x, core).
Axes of the slice: x: 2, y: 2, z: 4, core: 2. Of those that a mesh axis runs over, the one named last changes fastest.
Arguments:
- tokens: bfloat16 [8192, 768], P('blk'), may hold values from -6 to 6
- seg_ids: int32 [8192], replicated, may hold values from 0 to 6, as said below
- gain_attn: float32 [768], replicated, may hold values from 0.25 to 1.75
- w_query: bfloat16 [768, 768], P('blk', 'head'), may hold values from -0.21875 to 0.21875
- w_key: bfloat16 [768, 768], P('blk', 'head'), may hold values from -0.21875 to 0.21875
- w_value: bfloat16 [768, 768], P('blk', 'head'), may hold values from -0.21875 to 0.21875
- conv_kernels: float32 [3, 3, 768], P(None, None, 'head'), may hold values from -4 to 4
- w_out: bfloat16 [768, 768], P('head', 'blk'), may hold values from -0.875 to 0.875
- gain_ffn: float32 [768], replicated, may hold values from 0.25 to 1.75
- w_up: bfloat16 [768, 3072], P('blk', 'head'), may hold values from -0.21875 to 0.21875
- w_down: bfloat16 [3072, 768], P('head', 'blk'), may hold values from -0.109375 to 0.109375
- cotangent: bfloat16 [8192, 768], P('blk'), may hold values from -6 to 6
Outputs:
- output: bfloat16 [8192, 768], P('blk')
- grad_tokens: float32 [8192, 768], P('blk')
- grad_gain_attn: float32 [768], replicated
- grad_w_query: float32 [768, 768], P('blk', 'head')
- grad_w_key: float32 [768, 768], P('blk', 'head')
- grad_w_value: float32 [768, 768], P('blk', 'head')
- grad_conv_kernels: float32 [3, 3, 768], P(None, None, 'head')
- grad_w_out: float32 [768, 768], P('head', 'blk')
- grad_gain_ffn: float32 [768], replicated
- grad_w_up: float32 [768, 3072], P('blk', 'head')
- grad_w_down: float32 [3072, 768], P('head', 'blk')
Inputs may be any that keep to these rules, and one draw needn't show every extreme that they name: `seg_ids`: document numbers of the packed stream: 0 at the first token, rising by one at each new document and never falling. The first document has 1 to 1023 tokens, the last is cut short, every other has 1024 or 2048 tokens, and at least one document of 2048 tokens lies whole in the stream.
All inputs are finite; a program needn't handle non-finite values.
Results may differ from a plain program's by a relative error of at most 0.019.
The roundings to bfloat16 on the way count: a program that leaves them out, or rounds other values in their place, can miss the bound.
Values may be sent and summed in bfloat16 or wider, within the bound.
No kernel may reach another device: no remote copies, remote signals or barrier semaphores. Data moves between devices by JAX's collectives and lax.ppermute only.
A program may use at most 192 MiB of HBM per device.

v0:
```python
import jax
import jax.numpy as jnp
from jax import lax
from jax.sharding import PartitionSpec as P

DH = 64
REACH = 2


EPS = 1e-06
MASKED = -1e30


def shifted(block, axis, distance):
    devices = range(lax.axis_size(axis))
    route = [(i - distance, i) for i in devices if i - distance in devices]
    return lax.ppermute(block, axis, route)


def split_up(x, dim, peers):
    before, after = (x.shape[:dim], x.shape[dim + 1 :])
    return jnp.moveaxis(x.reshape(*before, peers, -1, *after), dim, 0)


def sum_at_owner(x, axis, dim):
    blocks = split_up(x, dim, lax.axis_size(axis))
    arrived = lax.all_to_all(blocks, axis, split_axis=0, concat_axis=0, tiled=True)
    return arrived.astype(jnp.float32).sum(axis=0)


def sent_together(arrays, axis, dim, along):
    ends, at = ([], 0)
    for a in arrays[:-1]:
        at += a.shape[along]
        ends.append(at)
    both = jnp.concatenate(arrays, axis=along)
    return tuple(jnp.split(sum_at_owner(both, axis, dim), ends, axis=along))


def norm_parts(values, gain_vec):
    factor = lax.rsqrt(jnp.mean(values * values, axis=-1, keepdims=True) + EPS)
    unit_rows = values * factor
    return (unit_rows * gain_vec, unit_rows, factor)


def norm_back(grad_in, unit_rows, factor, gain_vec):
    scaled_grad = grad_in * gain_vec
    inner_mean = jnp.mean(scaled_grad * unit_rows, axis=-1, keepdims=True)
    return (factor * (scaled_grad - unit_rows * inner_mean), jnp.sum(grad_in * unit_rows, axis=0))


def contract(first_mat, second_mat, first_dim, second_dim):
    return lax.dot_general(
        first_mat,
        second_mat,
        (((first_dim,), (second_dim,)), ((), ())),
        preferred_element_type=jnp.float32,
    )


def shifted_taps(joined, own_ids, before_ids, tok_rows):
    tap_terms = []
    for tap_shift in (1, 2):
        same_doc = (before_ids[2 - tap_shift : 2 - tap_shift + tok_rows] == own_ids)[:, None]
        tap_terms.append(jnp.where(same_doc, joined[2 - tap_shift : 2 - tap_shift + tok_rows], 0.0))
    return tap_terms


def conv_back(grad_in, next_rows, tap_table, own_ids, next_ids, tok_rows):
    joined = jnp.concatenate([grad_in, next_rows], axis=0)
    later_ids = jnp.concatenate([own_ids, next_ids])
    result = tap_table[0] * grad_in
    for tap_shift in (1, 2):
        same_doc = (later_ids[tap_shift : tap_shift + tok_rows] == own_ids)[:, None]
        result = result + tap_table[tap_shift] * jnp.where(
            same_doc, joined[tap_shift : tap_shift + tok_rows], 0.0
        )
    return result


def block_scores(queries, key_blk, query_pos, key_pos, query_ids, key_ids, score_scale):
    scores = (
        jnp.einsum("qhd,khd->hqk", queries, key_blk, preferred_element_type=jnp.float32)
        * score_scale
    )
    allowed = (query_ids[:, None] == key_ids[None, :]) & (key_pos[None, :] <= query_pos[:, None])
    return jnp.where(allowed[None], scores, MASKED)


def attend_block(
    queries, key_list, value_list, id_list, pos_list, query_pos, query_ids, score_scale
):
    scores = [
        block_scores(
            queries,
            key_list[slot],
            query_pos,
            pos_list[slot],
            query_ids,
            id_list[slot],
            score_scale,
        )
        for slot in range(len(key_list))
    ]
    top_score = jnp.max(scores[0], axis=-1)
    for score_blk in scores[1:]:
        top_score = jnp.maximum(top_score, jnp.max(score_blk, axis=-1))
    exp_total = jnp.zeros_like(top_score)
    for score_blk in scores:
        exp_total = exp_total + jnp.sum(jnp.exp(score_blk - top_score[..., None]), axis=-1)
    log_total = top_score + jnp.log(exp_total)
    block_out = jnp.zeros((queries.shape[0], queries.shape[1], queries.shape[2]), jnp.float32)
    for slot in range(len(key_list)):
        prob_blk = jnp.exp(scores[slot] - log_total[..., None]).astype(jnp.bfloat16)
        block_out = block_out + jnp.einsum(
            "hqk,khd->qhd", prob_blk, value_list[slot], preferred_element_type=jnp.float32
        )
    return (block_out, log_total)


def attend_back(
    queries,
    d_out,
    key_list,
    value_list,
    id_list,
    pos_list,
    query_pos,
    query_ids,
    log_total,
    score_scale,
):
    prob_list, dprob_list = ([], [])
    delta_rows = jnp.zeros_like(log_total)
    for slot in range(len(key_list)):
        score_blk = block_scores(
            queries,
            key_list[slot],
            query_pos,
            pos_list[slot],
            query_ids,
            id_list[slot],
            score_scale,
        )
        prob_blk = jnp.exp(score_blk - log_total[..., None])
        dprob_blk = jnp.einsum(
            "qhd,khd->hqk", d_out, value_list[slot], preferred_element_type=jnp.float32
        )
        delta_rows = delta_rows + jnp.sum(prob_blk * dprob_blk, axis=-1)
        prob_list.append(prob_blk)
        dprob_list.append(dprob_blk)
    d_queries = jnp.zeros(queries.shape, jnp.float32)
    d_key_list, d_value_list = ([], [])
    for slot in range(len(key_list)):
        d_score = (prob_list[slot] * (dprob_list[slot] - delta_rows[..., None])).astype(
            jnp.bfloat16
        )
        d_queries = (
            d_queries
            + jnp.einsum(
                "hqk,khd->qhd", d_score, key_list[slot], preferred_element_type=jnp.float32
            )
            * score_scale
        )
        d_key_list.append(
            jnp.einsum("hqk,qhd->khd", d_score, queries, preferred_element_type=jnp.float32)
            * score_scale
        )
        d_value_list.append(
            jnp.einsum(
                "hqk,qhd->khd",
                prob_list[slot].astype(jnp.bfloat16),
                d_out,
                preferred_element_type=jnp.float32,
            )
        )
    return (d_queries, d_key_list, d_value_list)


def body(
    tokens,
    seg_ids,
    gain_attn,
    w_query,
    w_key,
    w_value,
    conv_kernels,
    w_out,
    gain_ffn,
    w_up,
    w_down,
    cotangent,
):
    tok_rows = tokens.shape[0]
    head_cols = conv_kernels.shape[2]
    heads_here = head_cols // DH
    score_scale = DH ** (-0.5)
    query_rows = min(512, tok_rows)
    blk_place = lax.axis_index("blk")
    padded_ids = jnp.pad(seg_ids, (REACH * tok_rows, 2), constant_values=-1)
    window = lax.dynamic_slice_in_dim(padded_ids, blk_place * tok_rows, (REACH + 1) * tok_rows + 2)
    own_ids = window[REACH * tok_rows : (REACH + 1) * tok_rows]
    before_ids = window[REACH * tok_rows - 2 : (REACH + 1) * tok_rows]
    next_ids = window[(REACH + 1) * tok_rows :]
    full_query, full_key, full_value, full_out, full_up, full_down = (
        lax.all_gather(w_query, "blk", axis=0, tiled=True),
        lax.all_gather(w_key, "blk", axis=0, tiled=True),
        lax.all_gather(w_value, "blk", axis=0, tiled=True),
        lax.all_gather(w_out, "blk", axis=1, tiled=True),
        lax.all_gather(w_up, "blk", axis=0, tiled=True),
        lax.all_gather(w_down, "blk", axis=1, tiled=True),
    )
    w_mix = jnp.concatenate([full_query, full_key, full_value], axis=1)
    tap_table = jnp.transpose(conv_kernels, (1, 0, 2)).reshape(3, 3 * head_cols)
    inputs = tokens.astype(jnp.float32)
    normed, unit_one, factor_one = norm_parts(inputs, gain_attn)
    normed_low = normed.astype(jnp.bfloat16)
    raw_low = jnp.dot(normed_low, w_mix, preferred_element_type=jnp.float32).astype(jnp.bfloat16)
    before = shifted(raw_low[tok_rows - 2 :], "blk", 1)
    joined = jnp.concatenate([before, raw_low], axis=0).astype(jnp.float32)
    raw_here = joined[2:]
    tap_terms = shifted_taps(joined, own_ids, before_ids, tok_rows)
    mixed = tap_table[0] * raw_here + tap_table[1] * tap_terms[0] + tap_table[2] * tap_terms[1]
    mixed_low = mixed.astype(jnp.bfloat16)
    queries = mixed_low[:, :head_cols].reshape(tok_rows, heads_here, DH)
    keys_flat = mixed_low[:, head_cols : 2 * head_cols]
    values_flat = mixed_low[:, 2 * head_cols :]
    own_pos = jnp.arange(tok_rows, dtype=jnp.int32)
    id_list = [
        window[(REACH - hop_count) * tok_rows : (REACH - hop_count + 1) * tok_rows]
        for hop_count in range(REACH + 1)
    ]
    pos_list = [own_pos - hop_count * tok_rows for hop_count in range(REACH + 1)]
    key_list = [keys_flat.reshape(tok_rows, heads_here, DH)]
    value_list = [values_flat.reshape(tok_rows, heads_here, DH)]
    for hop_count in range(1, REACH + 1):
        moved_keys, moved_values = shifted((keys_flat, values_flat), "blk", hop_count)
        key_list.append(moved_keys.reshape(tok_rows, heads_here, DH))
        value_list.append(moved_values.reshape(tok_rows, heads_here, DH))
    out_parts, total_parts = ([], [])
    for row_start in range(0, tok_rows, query_rows):
        block_out, log_total = attend_block(
            queries[row_start : row_start + query_rows],
            key_list,
            value_list,
            id_list,
            pos_list,
            own_pos[row_start : row_start + query_rows],
            own_ids[row_start : row_start + query_rows],
            score_scale,
        )
        out_parts.append(block_out)
        total_parts.append(log_total)
    attended = jnp.concatenate(out_parts, axis=0).reshape(tok_rows, head_cols).astype(jnp.bfloat16)
    branch = lax.psum(jnp.dot(attended, full_out, preferred_element_type=jnp.float32), "head")
    hidden = inputs + branch
    normed_ffn, unit_two, factor_two = norm_parts(hidden, gain_ffn)
    normed_ffn_low = normed_ffn.astype(jnp.bfloat16)
    up_rows = jnp.dot(normed_ffn_low, full_up, preferred_element_type=jnp.float32)
    act_rows = jnp.square(jnp.maximum(up_rows, 0.0)).astype(jnp.bfloat16)
    ffn_sum = lax.psum(
        jnp.dot(act_rows, full_down, preferred_element_type=jnp.float32).astype(jnp.bfloat16),
        "head",
    ).astype(jnp.float32)
    output = (hidden + ffn_sum).astype(jnp.bfloat16)
    d_act = contract(cotangent, full_down, 1, 1)
    grad_down = contract(act_rows, cotangent, 0, 0)
    d_up = (d_act * 2.0 * jnp.maximum(up_rows, 0.0)).astype(jnp.bfloat16)
    grad_up = contract(normed_ffn_low, d_up, 0, 0)
    d_normed_ffn = lax.psum(contract(d_up, full_up, 1, 1).astype(jnp.bfloat16), "head").astype(
        jnp.float32
    )
    d_hidden_norm, gain_ffn_part = norm_back(d_normed_ffn, unit_two, factor_two, gain_ffn)
    d_hidden = cotangent.astype(jnp.float32) + d_hidden_norm
    d_branch = d_hidden.astype(jnp.bfloat16)
    grad_out = contract(attended, d_branch, 0, 0)
    d_attended = (
        contract(d_branch, full_out, 1, 1).astype(jnp.bfloat16).reshape(tok_rows, heads_here, DH)
    )
    back_keys, back_values = ([key_list[0]], [value_list[0]])
    for hop_count in range(1, REACH + 1):
        again_keys, again_values = shifted((keys_flat, values_flat), "blk", hop_count)
        back_keys.append(again_keys.reshape(tok_rows, heads_here, DH))
        back_values.append(again_values.reshape(tok_rows, heads_here, DH))
    d_query_parts = []
    key_accum = [
        jnp.zeros((tok_rows, heads_here, DH), jnp.float32) for hop_count in range(REACH + 1)
    ]
    value_accum = [
        jnp.zeros((tok_rows, heads_here, DH), jnp.float32) for hop_count in range(REACH + 1)
    ]
    for part_index, row_start in enumerate(range(0, tok_rows, query_rows)):
        d_queries, d_key_list, d_value_list = attend_back(
            queries[row_start : row_start + query_rows],
            d_attended[row_start : row_start + query_rows],
            back_keys,
            back_values,
            id_list,
            pos_list,
            own_pos[row_start : row_start + query_rows],
            own_ids[row_start : row_start + query_rows],
            total_parts[part_index],
            score_scale,
        )
        d_query_parts.append(d_queries)
        key_accum = [key_accum[slot] + d_key_list[slot] for slot in range(REACH + 1)]
        value_accum = [value_accum[slot] + d_value_list[slot] for slot in range(REACH + 1)]
    d_query_flat = jnp.concatenate(d_query_parts, axis=0).reshape(tok_rows, head_cols)
    d_key_flat = key_accum[0].reshape(tok_rows, head_cols)
    d_value_flat = value_accum[0].reshape(tok_rows, head_cols)
    for hop_count in range(1, REACH + 1):
        back_key, back_value = (
            shifted(
                key_accum[hop_count].reshape(tok_rows, head_cols).astype(jnp.bfloat16),
                "blk",
                -hop_count,
            ).astype(jnp.float32),
            shifted(
                value_accum[hop_count].reshape(tok_rows, head_cols).astype(jnp.bfloat16),
                "blk",
                -hop_count,
            ).astype(jnp.float32),
        )
        d_key_flat = d_key_flat + back_key
        d_value_flat = d_value_flat + back_value
    d_mixed = jnp.concatenate([d_query_flat, d_key_flat, d_value_flat], axis=1)
    next_rows = shifted(d_mixed[:2], "blk", -1)
    d_raw = conv_back(d_mixed, next_rows, tap_table, own_ids, next_ids, tok_rows).astype(
        jnp.bfloat16
    )
    d_taps = jnp.stack(
        [
            jnp.sum(d_mixed * raw_here, axis=0),
            jnp.sum(d_mixed * tap_terms[0], axis=0),
            jnp.sum(d_mixed * tap_terms[1], axis=0),
        ]
    )
    d_kernels = jnp.transpose(d_taps.reshape(3, 3, head_cols), (1, 0, 2))
    grad_mix = contract(normed_low, d_raw, 0, 0)
    grad_query = grad_mix[:, :head_cols]
    grad_key = grad_mix[:, head_cols : 2 * head_cols]
    grad_value = grad_mix[:, 2 * head_cols :]
    d_normed = lax.psum(contract(d_raw, w_mix, 1, 1).astype(jnp.bfloat16), "head").astype(
        jnp.float32
    )
    d_input_norm, gain_attn_part = norm_back(d_normed, unit_one, factor_one, gain_attn)
    grad_tokens = d_hidden + d_input_norm
    (
        grad_query_shard,
        grad_key_shard,
        grad_value_shard,
        grad_out_shard,
        grad_up_shard,
        grad_down_shard,
    ) = (
        *sent_together(
            (
                grad_query.astype(jnp.bfloat16),
                grad_key.astype(jnp.bfloat16),
                grad_value.astype(jnp.bfloat16),
            ),
            "blk",
            0,
            1,
        ),
        sum_at_owner(grad_out.astype(jnp.bfloat16), "blk", 1),
        sum_at_owner(grad_up.astype(jnp.bfloat16), "blk", 0),
        sum_at_owner(grad_down.astype(jnp.bfloat16), "blk", 1),
    )
    grad_kernels, grad_gain_attn, grad_gain_ffn = lax.psum(
        (d_kernels, gain_attn_part, gain_ffn_part), "blk"
    )
    return (
        output,
        grad_tokens,
        grad_gain_attn,
        grad_query_shard,
        grad_key_shard,
        grad_value_shard,
        grad_kernels,
        grad_out_shard,
        grad_gain_ffn,
        grad_up_shard,
        grad_down_shard,
    )


def solution(mesh):
    return jax.shard_map(
        body,
        mesh=mesh,
        in_specs=(
            P("blk", None),
            P(),
            P(),
            P("blk", "head"),
            P("blk", "head"),
            P("blk", "head"),
            P(None, None, "head"),
            P("head", "blk"),
            P(),
            P("blk", "head"),
            P("head", "blk"),
            P("blk", None),
        ),
        out_specs=(
            P("blk", None),
            P("blk", None),
            P(),
            P("blk", "head"),
            P("blk", "head"),
            P("blk", "head"),
            P(None, None, "head"),
            P("head", "blk"),
            P(),
            P("blk", "head"),
            P("head", "blk"),
        ),
        check_vma=False,
    )
```

profile of v0, /device:TPU:0, one launch (start us, length us, event | category | flops | bytes accessed | tf_op | source)
XLA Modules:
  0.0 706.7 jit_solution(17160485848710682333)
XLA Ops:
  9.9 33.0 %all_gather.20 = bf16[768,192]{1,0:T(8,128)(2,1)S(1)} all-gather(bf16[96,192]{1,0:T(8,128)(2,1)} %param.17), channel_id=1, replica_groups=mesh['blk'=8,'head'=4] {'blk'}, dimensions={0}, use_global_device_ids=true | all-gather | bytes 331776 | tf_op jit(solution)/shard_map/all_gather | solution.py:208
  42.8 31.4 %all_gather.19 = bf16[768,192]{1,0:T(8,128)(2,1)S(1)} all-gather(bf16[96,192]{1,0:T(8,128)(2,1)} %param.16), channel_id=1, replica_groups=mesh['blk'=8,'head'=4] {'blk'}, dimensions={0}, use_global_device_ids=true | all-gather | bytes 331776 | tf_op jit(solution)/shard_map/all_gather | solution.py:207
  74.2 31.3 %all_gather.18 = bf16[768,192]{1,0:T(8,128)(2,1)S(1)} all-gather(bf16[96,192]{1,0:T(8,128)(2,1)} %param.15), channel_id=1, replica_groups=mesh['blk'=8,'head'=4] {'blk'}, dimensions={0}, use_global_device_ids=true | all-gather | bytes 331776 | tf_op jit(solution)/shard_map/all_gather | solution.py:206
  105.5 3.0 convolution_convert_fusion.5
  109.7 3.5 collective-permute-start
  114.2 33.4 %all_gather.21 = bf16[192,768]{0,1:T(8,128)(2,1)} all-gather(bf16[192,96]{0,1:T(8,128)(2,1)S(1)} %copy.24), channel_id=1, replica_groups=mesh['blk'=8,'head'=4] {'blk'}, dimensions={1}, use_global_device_ids=true | all-gather | bytes 331776 | tf_op jit(solution)/shard_map/all_gather | solution.py:209
  148.2 3.0 compare_and_fusion.2
  151.6 2.6 maximum_convert_fusion
  157.4 3.7 collective-permute-start.1
  161.1 4.8 collective-permute-start.4
  166.0 2.2 collective-permute-start.3
  171.0 4.6 fusion.5
  177.0 4.4 fusion.4
  182.9 14.1 %exponential_reduce_fusion.1 = (f32[3,512]{1,0:T(4,128)S(1)}, f32[3,512]{1,0:T(4,128)S(1)}, f32[3,512]{1,0:T(4,128)S(1)}, f32[3,512]{1,0:T(4,128)S(1)}, f32[3,512]{1,0:T(4,128)S(1)}, /*index=5*/f32[3,512]{1,0:T(4,128)S(1)}) fusion(f32[3,512,1024]{2,1,0:T(8,128)} %get-tuple-element.78, f32[3,512]{1,0:T(4,128)S(1)} %maximum_maximum_fusion, ...), kind=kLoop, calls=%fused_computation.16 | loop fusion | flops 37739520 | bytes 40943616 | tf_op jit(solution)/shard_map/reduce_sum | solution.py:110
  207.8 2.0 fusion.50
  210.6 2.3 fusion.89
  214.3 65.9 %all-reduce.7.cloned.1.call-done = f32[1024,768]{1,0:T(8,128)} async-done(((f32[1024,768]{1,0:T(8,128)}), f32[1024,768]{1,0:T(8,128)}) %all-reduce.7.cloned.1.call-update) | async-done | bytes 3145744 | tf_op jit(solution)/shard_map/psum | solution.py:255
  280.2 3.0 multiply_reduce_fusion.6
  283.8 4.9 fusion.84
  288.7 8.9 %all-gather.5.cloned.1.call-done = bf16[768,768]{0,1:T(8,128)(2,1)} async-done(((bf16[768,96]{0,1:T(8,128)(2,1)}), bf16[768,768]{0,1:T(8,128)(2,1)}) %all-gather.5.cloned.1.call-update) | async-done | bytes 1179664 | tf_op jit(solution)/shard_map/all_gather | solution.py:211
  297.6 4.2 multiply_convert_fusion.6
  303.0 2.6 convolution_convert_fusion.1
  305.7 4.9 convolution_convert_fusion.3
  310.6 2.6 convolution_convert_fusion.4
  313.3 33.9 %all-reduce.9.cloned.1.call-done = bf16[1024,768]{1,0:T(8,128)(2,1)} async-done(((bf16[1024,768]{1,0:T(8,128)(2,1)}), bf16[1024,768]{1,0:T(8,128)(2,1)}) %all-reduce.9.cloned.1.call-update) | async-done | bytes 1572880 | tf_op jit(solution)/shard_map/psum | solution.py:270
  347.1 3.2 fusion.24
  350.4 2.9 fusion.23
  354.7 2.8 fusion.67
  357.9 3.3 fusion.76
  361.2 3.6 fusion.94
  364.8 3.7 fusion.95
  368.5 3.6 fusion.90
  372.2 3.7 fusion.91
  375.9 13.0 %multiply_reduce_fusion.1 = (f32[3,512]{1,0:T(4,128)S(1)}, f32[3,512]{1,0:T(4,128)S(1)}, f32[3,512]{1,0:T(4,128)S(1)}, f32[3,512,1024]{2,1,0:T(8,128)}) fusion(f32[3,512,1024]{2,1,0:T(8,128)} %get-tuple-element.78, f32[3,512]{1,0:T(4,128)S(1)} %log_add_fusion, pred[512,1024]{1,0:T(8,128)(4,1)S(1)} %copy-done.34, f32[3,512,1024]{2,1,0:T(8,128)} %fusion.94, ...), kind=kOutput, calls=%fused_computation.4 | convolution fusion | flops 224914944 | bytes 39936000 | tf_op jit(solution)/shard_map/qhd,khd->hqk/dot_general | solution.py:146
  389.6 17.8 %multiply_convert_fusion.1 = (bf16[3,512,1024]{2,1,0:T(8,128)(2,1)}, bf16[3,512,1024]{2,1,0:T(8,128)(2,1)S(1)}, bf16[3,512,1024]{2,1,0:T(8,128)(2,1)}) fusion(f32[3,512,1024]{2,1,0:T(8,128)} %get-tuple-element.85, f32[3,512,1024]{2,1,0:T(8,128)} %get-tuple-element.78, f32[3,512]{1,0:T(4,128)} %add_add_fusion, f32[3,512]{1,0:T(4,128)S(1)} %log_add_fusion, ...), kind=kLoop, calls=%fused_computation.1 | loop fusion | flops 28311552 | bytes 48771072 | tf_op jit(solution)/shard_map/convert_element_type | solution.py:155
  407.4 4.6 fusion.98
  418.7 2.7 fusion.42
  423.2 2.7 fusion.41
  428.9 13.2 %multiply_reduce_fusion.4 = (f32[3,512]{1,0:T(4,128)S(1)}, f32[3,512]{1,0:T(4,128)S(1)}, f32[3,512]{1,0:T(4,128)S(1)}, f32[3,512,1024]{2,1,0:T(8,128)}) fusion(f32[3,512,1024]{2,1,0:T(8,128)} %copy-done.5, f32[3,512]{1,0:T(4,128)S(1)} %log_add_fusion.1, pred[512,1024]{1,0:T(8,128)(4,1)S(1)} %copy-done.32, f32[3,512,1024]{2,1,0:T(8,128)} %fusion.90, ...), kind=kOutput, calls=%fused_computation.10 | convolution fusion | flops 224914944 | bytes 39936000 | tf_op jit(solution)/shard_map/qhd,khd->hqk/dot_general | solution.py:146
  442.1 18.0 %multiply_convert_fusion.4 = (bf16[3,512,1024]{2,1,0:T(8,128)(2,1)}, bf16[3,512,1024]{2,1,0:T(8,128)(2,1)S(1)}, bf16[3,512,1024]{2,1,0:T(8,128)(2,1)}) fusion(f32[3,512,1024]{2,1,0:T(8,128)} %get-tuple-element.86, f32[3,512,1024]{2,1,0:T(8,128)} %copy-done.5, f32[3,512]{1,0:T(4,128)S(1)} %add_add_fusion.1, f32[3,512]{1,0:T(4,128)S(1)} %log_add_fusion.1, ...), kind=kLoop, calls=%fused_computation.7 | loop fusion | flops 28311552 | bytes 48771072 | tf_op jit(solution)/shard_map/convert_element_type | solution.py:155
  460.1 3.3 fusion.40
  469.8 12.6 %all-to-all-start.1 = ((bf16[8,192,96]{2,1,0:T(8,128)(2,1)}), bf16[8,192,96]{2,1,0:T(8,128)(2,1)}, u32[]{:S(2)}, u32[]{:S(2)}) async-start(bf16[8,192,96]{2,1,0:T(8,128)(2,1)} %bitcast.128), calls=%async_computation.1 | async-start | bytes 786432 | tf_op jit(solution)/shard_map/all_to_all | solution.py:27
  482.4 3.8 fusion.93
  486.2 4.1 fusion.44
  490.3 7.2 %all-to-all-done.1 = bf16[8,192,96]{2,1,0:T(8,128)(2,1)} async-done(((bf16[8,192,96]{2,1,0:T(8,128)(2,1)}), bf16[8,192,96]{2,1,0:T(8,128)(2,1)}, u32[]{:S(2)}, u32[]{:S(2)}) %all-to-all-start.1) | async-done | bytes 294944 | tf_op jit(solution)/shard_map/all_to_all | solution.py:27
  497.5 4.5 all-to-all-start.2
  502.0 3.1 fusion.92
  508.9 2.8 convolution_add_fusion.2
  512.9 13.8 %all-to-all-done.2 = bf16[8,96,768]{2,1,0:T(8,128)(2,1)} async-done(((bf16[8,96,768]{2,1,0:T(8,128)(2,1)}), bf16[8,96,768]{2,1,0:T(8,128)(2,1)}, u32[]{:S(2)}, u32[]{:S(2)}) %all-to-all-start.2) | async-done | bytes 1179680 | tf_op jit(solution)/shard_map/all_to_all | solution.py:27
  526.6 3.6 all-to-all-start.3
  534.7 14.0 %collective-permute-done.9 = f32[2,576]{0,1:T(8,128)S(1)} collective-permute-done((f32[2,576]{0,1:T(8,128)S(1)}, f32[2,576]{0,1:T(8,128)S(1)}, u32[]{:S(2)}, u32[]{:S(2)}) %collective-permute-start.9) | collective-permute-done | bytes 4640 | tf_op jit(solution)/shard_map/ppermute | solution.py:17
  549.0 4.8 multiply_reduce_fusion.9
  553.8 2.2 convolution_convert_fusion.6
  555.9 2.3 copy.25
  560.0 16.1 %all-to-all-start = ((bf16[8,96,576]{2,1,0:T(8,128)(2,1)}), bf16[8,96,576]{2,1,0:T(8,128)(2,1)}, u32[]{:S(2)}, u32[]{:S(2)}) async-start(bf16[8,96,576]{2,1,0:T(8,128)(2,1)} %bitcast.29), calls=%async_computation | async-start | bytes 1966080 | tf_op jit(solution)/shard_map/all_to_all | solution.py:27
  576.4 4.8 convolution_convert_fusion.2
  581.2 2.8 convolution_convert_fusion
  586.7 2.2 convert_reduce_fusion.1
  588.8 2.2 convert_reduce_fusion
  591.0 7.4 %all-to-all-done = bf16[8,96,576]{2,1,0:T(8,128)(2,1)} async-done(((bf16[8,96,576]{2,1,0:T(8,128)(2,1)}), bf16[8,96,576]{2,1,0:T(8,128)(2,1)}, u32[]{:S(2)}, u32[]{:S(2)}) %all-to-all-start) | async-done | bytes 884768 | tf_op jit(solution)/shard_map/all_to_all | solution.py:27
  600.6 53.4 %all-reduce.11.cloned.1.call-done = (bf16[1024,768]{1,0:T(8,128)(2,1)}, bf16[1024,768]{1,0:T(8,128)(2,1)}) async-done(((bf16[1024,768]{1,0:T(8,128)(2,1)}, bf16[1024,768]{1,0:T(8,128)(2,1)}), (bf16[1024,768]{1,0:T(8,128)(2,1)}, bf16[1024,768]{1,0:T(8,128)(2,1)})) %all-reduce.11.cloned.1.call-update) | async-done | bytes 3145744 | tf_op jit(solution)/shard_map/psum | solution.py:261
  654.0 3.0 add_convert_fusion
  658.9 2.5 fusion.20
  661.5 37.7 %all-reduce.1 = (f32[768]{0:T(1024)}, f32[3,3,192]{2,1,0:T(4,128)}, f32[768]{0:T(1024)}) all-reduce(f32[768]{0:T(1024)S(1)} %get-tuple-element.16, f32[3,3,192]{2,1,0:T(4,128)S(1)} %maximum_bitcast_fusion, f32[768]{0:T(1024)S(1)} %copy-done.91), channel_id=1, replica_groups=mesh['blk'=8,'head'=4] {'blk'}, use_global_device_ids=true, to_apply=%region_27.28 | all-reduce | flops 3264 | bytes 26112 | tf_op jit(solution)/shard_map/psum | solution.py:370
  (349 shorter events, 66.6 us)
Async XLA Ops:
  8.0 272.2 %all-reduce.7.cloned.1.call-start = ((), (), s32[]{:S(2)}) async-start(), calls=%async_computation.4 | async-start | bytes 6291456 | tf_op jit(solution)/shard_map/psum | solution.py:255
  9.9 98.7 %copy-start.78 = (f32[1024]{0:T(1024)}, f32[1024]{0:T(1024)S(1)}, u32[]{:S(2)}) copy-start(f32[1024]{0:T(1024)S(1)} %add_rsqrt_fusion.1) | copy-start | bytes 12292
  42.8 65.7 %copy-start.71 = (bf16[768,192]{1,0:T(8,128)(2,1)}, bf16[768,192]{1,0:T(8,128)(2,1)S(1)}, u32[]{:S(2)}) copy-start(bf16[768,192]{1,0:T(8,128)(2,1)S(1)} %all_gather.20) | copy-start | bytes 884740
  74.2 34.4 %copy-start.73 = (bf16[768,192]{1,0:T(8,128)(2,1)}, bf16[768,192]{1,0:T(8,128)(2,1)S(1)}, u32[]{:S(2)}) copy-start(bf16[768,192]{1,0:T(8,128)(2,1)S(1)} %all_gather.19) | copy-start | bytes 884740
  105.5 7.8 %copy-start.70 = (s32[8192]{0:T(1024)S(1)}, s32[8192]{0:T(1024)}, u32[]{:S(2)}) copy-start(s32[8192]{0:T(1024)} %param.13) | copy-start | bytes 98308
  105.5 8.6 %copy-start.77 = (bf16[192,96]{1,0:T(8,128)(2,1)S(1)}, bf16[192,96]{1,0:T(8,128)(2,1)}, u32[]{:S(2)}) copy-start(bf16[192,96]{1,0:T(8,128)(2,1)} %param.19) | copy-start | bytes 110596
  109.6 41.7 %copy-start.97 = (f32[3,3,192]{2,1,0:T(4,128)S(1)}, f32[3,3,192]{2,1,0:T(4,128)}, u32[]{:S(2)}) copy-start(f32[3,3,192]{2,1,0:T(4,128)} %param.18) | copy-start | bytes 20740
  109.7 41.8 %collective-permute-start = (bf16[2,576]{0,1:T(8,128)(2,1)S(1)}, bf16[2,576]{0,1:T(8,128)(2,1)S(1)}, u32[]{:S(2)}, u32[]{:S(2)}) collective-permute-start(bf16[2,576]{0,1:T(8,128)(2,1)S(1)} %slice.174), channel_id=1, source_target_pairs={{0,4},{4,8},{8,12},{12,16},{16,20},{20,24},{24,28},{1,5},{5,9},{9,... | collective-permute-start | bytes 6920 | tf_op jit(solution)/shard_map/ppermute | solution.py:17
  148.2 6.0 copy-start.95
  151.2 45.7 %copy-start.21 = (pred[512,1024]{1,0:T(8,128)(4,1)}, pred[512,1024]{1,0:T(8,128)(4,1)S(1)}, u32[]{:S(2)}) copy-start(pred[512,1024]{1,0:T(8,128)(4,1)S(1)} %get-tuple-element.71) | copy-start | bytes 1572868
  151.2 47.8 %copy-start.33 = (pred[512,1024]{1,0:T(8,128)(4,1)}, pred[512,1024]{1,0:T(8,128)(4,1)S(1)}, u32[]{:S(2)}) copy-start(pred[512,1024]{1,0:T(8,128)(4,1)S(1)} %get-tuple-element.69) | copy-start | bytes 1572868
  151.2 50.4 %copy-start.24 = (pred[512,1024]{1,0:T(8,128)(4,1)}, pred[512,1024]{1,0:T(8,128)(4,1)S(1)}, u32[]{:S(2)}) copy-start(pred[512,1024]{1,0:T(8,128)(4,1)S(1)} %get-tuple-element.72) | copy-start | bytes 1572868
  151.2 52.4 %copy-start.30 = (pred[512,1024]{1,0:T(8,128)(4,1)}, pred[512,1024]{1,0:T(8,128)(4,1)S(1)}, u32[]{:S(2)}) copy-start(pred[512,1024]{1,0:T(8,128)(4,1)S(1)} %get-tuple-element.70) | copy-start | bytes 1572868
  151.3 54.5 %copy-start.36 = (pred[512,1024]{1,0:T(8,128)(4,1)}, pred[512,1024]{1,0:T(8,128)(4,1)S(1)}, u32[]{:S(2)}) copy-start(pred[512,1024]{1,0:T(8,128)(4,1)S(1)} %get-tuple-element.68) | copy-start | bytes 1572868
  151.3 56.5 %copy-start.27 = (pred[512,1024]{1,0:T(8,128)(4,1)}, pred[512,1024]{1,0:T(8,128)(4,1)S(1)}, u32[]{:S(2)}) copy-start(pred[512,1024]{1,0:T(8,128)(4,1)S(1)} %get-tuple-element.67) | copy-start | bytes 1572868
  156.1 13.5 %copy-start.39 = (bf16[1024,192]{0,1:T(8,128)(2,1)}, bf16[1024,192]{0,1:T(8,128)(2,1)S(1)}, u32[]{:S(2)}) copy-start(bf16[1024,192]{0,1:T(8,128)(2,1)S(1)} %get-tuple-element.45) | copy-start | bytes 1179652
  156.1 45.6 %copy-start.55 = (bf16[1024,192]{0,1:T(8,128)(2,1)}, bf16[1024,192]{0,1:T(8,128)(2,1)S(1)}, u32[]{:S(2)}) copy-start(bf16[1024,192]{0,1:T(8,128)(2,1)S(1)} %get-tuple-element.46) | copy-start | bytes 1179652
  156.1 14.8 %collective-permute-start.2 = (bf16[1024,192]{0,1:T(8,128)(2,1)S(1)}, bf16[1024,192]{0,1:T(8,128)(2,1)S(1)}, u32[]{:S(2)}, u32[]{:S(2)}) collective-permute-start(bf16[1024,192]{0,1:T(8,128)(2,1)S(1)} %get-tuple-element.45), channel_id=1, source_target_pairs={{0,8},{4,12},{8,16},{12,20},{16,24},{20,28},{1,9},{5,13},{9,17},{1... | collective-permute-start | bytes 1179656 | tf_op jit(solution)/shard_map/ppermute | solution.py:17
  157.4 19.6 %collective-permute-start.1 = (bf16[1024,192]{0,1:T(8,128)(2,1)S(1)}, bf16[1024,192]{0,1:T(8,128)(2,1)S(1)}, u32[]{:S(2)}, u32[]{:S(2)}) collective-permute-start(bf16[1024,192]{0,1:T(8,128)(2,1)S(1)} %get-tuple-element.45), channel_id=1, source_target_pairs={{0,4},{4,8},{8,12},{12,16},{16,20},{20,24},{24,28},{1,5},{5,9},{9,... | collective-permute-start | bytes 1179656 | tf_op jit(solution)/shard_map/ppermute | solution.py:17
  161.1 44.5 %collective-permute-start.4 = (bf16[1024,192]{0,1:T(8,128)(2,1)S(1)}, bf16[1024,192]{0,1:T(8,128)(2,1)S(1)}, u32[]{:S(2)}, u32[]{:S(2)}) collective-permute-start(bf16[1024,192]{0,1:T(8,128)(2,1)S(1)} %get-tuple-element.46), channel_id=1, source_target_pairs={{0,8},{4,12},{8,16},{12,20},{16,24},{20,28},{1,9},{5,13},{9,17},{1... | collective-permute-start | bytes 1179656 | tf_op jit(solution)/shard_map/ppermute | solution.py:17
  166.0 33.0 %collective-permute-start.3 = (bf16[1024,192]{0,1:T(8,128)(2,1)S(1)}, bf16[1024,192]{0,1:T(8,128)(2,1)S(1)}, u32[]{:S(2)}, u32[]{:S(2)}) collective-permute-start(bf16[1024,192]{0,1:T(8,128)(2,1)S(1)} %get-tuple-element.46), channel_id=1, source_target_pairs={{0,4},{4,8},{8,12},{12,16},{16,20},{20,24},{24,28},{1,5},{5,9},{9,... | collective-permute-start | bytes 1179656 | tf_op jit(solution)/shard_map/ppermute | solution.py:17
  169.5 27.4 %copy-start.2 = (f32[3,512,1024]{2,1,0:T(8,128)}, f32[3,512,1024]{2,1,0:T(8,128)S(1)}, u32[]{:S(2)}) copy-start(f32[3,512,1024]{2,1,0:T(8,128)S(1)} %get-tuple-element.76) | copy-start | bytes 18874372
  170.9 30.7 %copy-start.3 = (f32[3,512,1024]{2,1,0:T(8,128)}, f32[3,512,1024]{2,1,0:T(8,128)S(1)}, u32[]{:S(2)}) copy-start(f32[3,512,1024]{2,1,0:T(8,128)S(1)} %get-tuple-element.82) | copy-start | bytes 18874372
  177.0 30.8 %copy-start.4 = (f32[3,512,1024]{2,1,0:T(8,128)}, f32[3,512,1024]{2,1,0:T(8,128)S(1)}, u32[]{:S(2)}) copy-start(f32[3,512,1024]{2,1,0:T(8,128)S(1)} %get-tuple-element.80) | copy-start | bytes 18874372
  182.8 20.9 %copy-start.5 = (f32[3,512,1024]{2,1,0:T(8,128)}, f32[3,512,1024]{2,1,0:T(8,128)S(1)}, u32[]{:S(2)}) copy-start(f32[3,512,1024]{2,1,0:T(8,128)S(1)} %get-tuple-element.84) | copy-start | bytes 18874372
  212.9 70.9 %all-gather.3.cloned.1.call-start = ((), (), s32[]{:S(2)}) async-start(), calls=%async_computation.5 | async-start | bytes 1327104 | tf_op jit(solution)/shard_map/all_gather | solution.py:210
  213.5 84.1 %all-gather.5.cloned.1.call-start = ((), (), s32[]{:S(2)}) async-start(), calls=%async_computation.6 | async-start | bytes 1327104 | tf_op jit(solution)/shard_map/all_gather | solution.py:211
  214.1 133.1 %all-reduce.9.cloned.1.call-start = ((), (), s32[]{:S(2)}) async-start(), calls=%async_computation.7 | async-start | bytes 3145728 | tf_op jit(solution)/shard_map/psum | solution.py:270
  283.2 67.2 %copy-start.7 = (f32[1024,768]{1,0:T(8,128)}, f32[1024,768]{1,0:T(8,128)S(1)}, u32[]{:S(2)}) copy-start(f32[1024,768]{1,0:T(8,128)S(1)} %get-tuple-element.41) | copy-start | bytes 9437188
  347.1 6.9 slice-start.8
  354.0 18.1 %copy-start.60 = (bf16[512,192]{0,1:T(8,128)(2,1)}, bf16[512,192]{0,1:T(8,128)(2,1)S(1)}, u32[]{:S(2)}) copy-start(bf16[512,192]{0,1:T(8,128)(2,1)S(1)} %get-tuple-element.48) | copy-start | bytes 589828
  354.0 21.8 %copy-start.57 = (bf16[512,192]{0,1:T(8,128)(2,1)}, bf16[512,192]{0,1:T(8,128)(2,1)S(1)}, u32[]{:S(2)}) copy-start(bf16[512,192]{0,1:T(8,128)(2,1)S(1)} %get-tuple-element.47) | copy-start | bytes 589828
  364.8 11.1 %slice-start = ((s8[6291456]{0:T(1024)(128)(4,1)}), s8[4194304]{0:T(1024)(128)(4,1)S(1)}, s32[]{:S(2)}) async-start(s8[6291456]{0:T(1024)(128)(4,1)} %bitcast.129), calls=%async_computation.9 | async-start | bytes 8388608
  368.5 7.4 %slice-start.1 = ((s8[6291456]{0:T(1024)(128)(4,1)}), s8[2097152]{0:T(1024)(128)(4,1)S(1)}, s32[]{:S(2)}) async-start(s8[6291456]{0:T(1024)(128)(4,1)} %bitcast.129), calls=%async_computation.10 | async-start | bytes 4194304
  407.4 20.0 %copy-start.16 = (bf16[3,512,1024]{2,1,0:T(8,128)(2,1)}, bf16[3,512,1024]{2,1,0:T(8,128)(2,1)S(1)}, u32[]{:S(2)}) copy-start(bf16[3,512,1024]{2,1,0:T(8,128)(2,1)S(1)} %get-tuple-element.63) | copy-start | bytes 9437188
  407.4 6.5 copy-start.17
  421.4 7.5 %slice-start.4 = ((s8[6291456]{0:T(1024)(128)(4,1)}), s8[4194304]{0:T(1024)(128)(4,1)S(1)}, s32[]{:S(2)}) async-start(s8[6291456]{0:T(1024)(128)(4,1)} %bitcast.133), calls=%async_computation.13 | async-start | bytes 8388608
  421.4 7.5 %slice-start.5 = ((s8[6291456]{0:T(1024)(128)(4,1)}), s8[2097152]{0:T(1024)(128)(4,1)S(1)}, s32[]{:S(2)}) async-start(s8[6291456]{0:T(1024)(128)(4,1)} %bitcast.133), calls=%async_computation.14 | async-start | bytes 4194304
  421.4 108.8 %collective-permute-start.8 = (bf16[1024,192]{0,1:T(8,128)(2,1)}, bf16[1024,192]{0,1:T(8,128)(2,1)}, u32[]{:S(2)}, u32[]{:S(2)}) collective-permute-start(bf16[1024,192]{0,1:T(8,128)(2,1)} %bitcast.28), channel_id=1, source_target_pairs={{8,0},{12,4},{16,8},{20,12},{24,16},{28,20},{9,1},{13,5},{17,9},{2... | collective-permute-start | bytes 1179656 | tf_op jit(solution)/shard_map/ppermute | solution.py:17
  425.9 104.3 %collective-permute-start.7 = (bf16[1024,192]{0,1:T(8,128)(2,1)}, bf16[1024,192]{0,1:T(8,128)(2,1)}, u32[]{:S(2)}, u32[]{:S(2)}) collective-permute-start(bf16[1024,192]{0,1:T(8,128)(2,1)} %bitcast.26), channel_id=1, source_target_pairs={{4,0},{8,4},{12,8},{16,12},{20,16},{24,20},{28,24},{5,1},{9,5},{13... | collective-permute-start | bytes 1179656 | tf_op jit(solution)/shard_map/ppermute | solution.py:17
  460.1 6.0 copy-start.12
  463.4 68.1 %collective-permute-start.6 = (bf16[1024,192]{0,1:T(8,128)(2,1)}, bf16[1024,192]{0,1:T(8,128)(2,1)}, u32[]{:S(2)}, u32[]{:S(2)}) collective-permute-start(bf16[1024,192]{0,1:T(8,128)(2,1)} %bitcast.22), channel_id=1, source_target_pairs={{8,0},{12,4},{16,8},{20,12},{24,16},{28,20},{9,1},{13,5},{17,9},{2... | collective-permute-start | bytes 1179656 | tf_op jit(solution)/shard_map/ppermute | solution.py:17
  466.1 20.1 %copy-start.43 = (bf16[1024,192]{0,1:T(8,128)(2,1)S(1)}, bf16[1024,192]{0,1:T(8,128)(2,1)}, u32[]{:S(2)}) copy-start(bf16[1024,192]{0,1:T(8,128)(2,1)} %copy-done.42) | copy-start | bytes 1179652
  466.1 65.4 %collective-permute-start.5 = (bf16[1024,192]{0,1:T(8,128)(2,1)}, bf16[1024,192]{0,1:T(8,128)(2,1)}, u32[]{:S(2)}, u32[]{:S(2)}) collective-permute-start(bf16[1024,192]{0,1:T(8,128)(2,1)} %bitcast.20), channel_id=1, source_target_pairs={{4,0},{8,4},{12,8},{16,12},{20,16},{24,20},{28,24},{5,1},{9,5},{13... | collective-permute-start | bytes 1179656 | tf_op jit(solution)/shard_map/ppermute | solution.py:17
  469.8 27.7 %all-to-all-start.1 = ((bf16[8,192,96]{2,1,0:T(8,128)(2,1)}), bf16[8,192,96]{2,1,0:T(8,128)(2,1)}, u32[]{:S(2)}, u32[]{:S(2)}) async-start(bf16[8,192,96]{2,1,0:T(8,128)(2,1)} %bitcast.128), calls=%async_computation.1 | async-start | bytes 786432 | tf_op jit(solution)/shard_map/all_to_all | solution.py:27
  486.2 15.7 %copy-start.41 = (bf16[1024,192]{0,1:T(8,128)(2,1)S(1)}, bf16[1024,192]{0,1:T(8,128)(2,1)}, u32[]{:S(2)}) copy-start(bf16[1024,192]{0,1:T(8,128)(2,1)} %copy-done.39) | copy-start | bytes 1179652
  486.2 20.5 %slice-start.6 = ((s8[6291456]{0:T(1024)(128)(4,1)}), s8[2097152]{0:T(1024)(128)(4,1)S(1)}, s32[]{:S(2)}) async-start(s8[6291456]{0:T(1024)(128)(4,1)} %bitcast.135), calls=%async_computation.15 | async-start | bytes 4194304
  497.5 29.1 %all-to-all-start.2 = ((bf16[8,96,768]{2,1,0:T(8,128)(2,1)}), bf16[8,96,768]{2,1,0:T(8,128)(2,1)}, u32[]{:S(2)}, u32[]{:S(2)}) async-start(bf16[8,96,768]{2,1,0:T(8,128)(2,1)} %bitcast.201), calls=%async_computation.2 | async-start | bytes 2359296 | tf_op jit(solution)/shard_map/all_to_all | solution.py:27
  512.8 17.4 %copy-start.69 = (f32[3,64,1024]{2,1,0:T(8,128)S(1)}, f32[3,64,1024]{2,1,0:T(8,128)}, u32[]{:S(2)}) copy-start(f32[3,64,1024]{2,1,0:T(8,128)} %convolution_add_fusion.2) | copy-start | bytes 2359300
  512.8 18.8 %copy-start.48 = (f32[3,64,1024]{2,1,0:T(8,128)S(1)}, f32[3,64,1024]{2,1,0:T(8,128)}, u32[]{:S(2)}) copy-start(f32[3,64,1024]{2,1,0:T(8,128)} %fusion.38) | copy-start | bytes 2359300
  526.6 33.4 %all-to-all-start.3 = ((bf16[8,768,96]{1,2,0:T(8,128)(2,1)}), bf16[8,768,96]{1,2,0:T(8,128)(2,1)S(1)}, u32[]{:S(2)}, u32[]{:S(2)}) async-start(bf16[8,768,96]{1,2,0:T(8,128)(2,1)} %bitcast.200), calls=%async_computation.3 | async-start | bytes 2359296 | tf_op jit(solution)/shard_map/all_to_all | solution.py:27
  533.1 15.7 %copy-start.1 = (f32[1026,576]{0,1:T(8,128)S(1)}, f32[1026,576]{0,1:T(8,128)}, u32[]{:S(2)}) copy-start(f32[1026,576]{0,1:T(8,128)} %copy-done) | copy-start | bytes 7091716
  533.1 15.7 %copy-start.81 = (f32[576]{0:T(1024)S(1)}, f32[576]{0:T(1024)}, u32[]{:S(2)}) copy-start(f32[576]{0:T(1024)} %copy-done.80) | copy-start | bytes 6916
  533.2 15.7 %copy-start.83 = (f32[576]{0:T(1024)S(1)}, f32[576]{0:T(1024)}, u32[]{:S(2)}) copy-start(f32[576]{0:T(1024)} %copy-done.82) | copy-start | bytes 6916
  533.2 15.7 %copy-start.85 = (f32[576]{0:T(1024)S(1)}, f32[576]{0:T(1024)}, u32[]{:S(2)}) copy-start(f32[576]{0:T(1024)} %copy-done.84) | copy-start | bytes 6916
  533.2 15.7 %copy-start.94 = (pred[1024]{0:T(1024)(128)(4,1)S(1)}, pred[1024]{0:T(1024)(128)(4,1)}, u32[]{:S(2)}) copy-start(pred[1024]{0:T(1024)(128)(4,1)} %copy-done.93) | copy-start | bytes 3076
  533.2 15.7 %copy-start.96 = (pred[1024]{0:T(1024)(128)(4,1)S(1)}, pred[1024]{0:T(1024)(128)(4,1)}, u32[]{:S(2)}) copy-start(pred[1024]{0:T(1024)(128)(4,1)} %copy-done.95) | copy-start | bytes 3076
  533.2 15.7 %copy-start.98 = (pred[1024]{0:T(1024)(128)(4,1)S(1)}, pred[1024]{0:T(1024)(128)(4,1)}, u32[]{:S(2)}) copy-start(pred[1024]{0:T(1024)(128)(4,1)} %get-tuple-element.38) | copy-start | bytes 3076
  533.2 15.7 %copy-start.99 = (pred[1024]{0:T(1024)(128)(4,1)S(1)}, pred[1024]{0:T(1024)(128)(4,1)}, u32[]{:S(2)}) copy-start(pred[1024]{0:T(1024)(128)(4,1)} %get-tuple-element.52) | copy-start | bytes 3076
  533.3 15.4 %collective-permute-start.9 = (f32[2,576]{0,1:T(8,128)S(1)}, f32[2,576]{0,1:T(8,128)S(1)}, u32[]{:S(2)}, u32[]{:S(2)}) collective-permute-start(f32[2,576]{0,1:T(8,128)S(1)} %slice.186), channel_id=1, source_target_pairs={{4,0},{8,4},{12,8},{16,12},{20,16},{24,20},{28,24},{5,1},{9,5},{13... | collective-permute-start | bytes 13832 | tf_op jit(solution)/shard_map/ppermute | solution.py:17
  560.0 21.2 %copy-start.47 = (bf16[8,768,96]{1,2,0:T(8,128)(2,1)}, bf16[8,768,96]{1,2,0:T(8,128)(2,1)S(1)}, u32[]{:S(2)}) copy-start(bf16[8,768,96]{1,2,0:T(8,128)(2,1)S(1)} %all-to-all-done.3) | copy-start | bytes 3538948
  560.0 38.5 %all-to-all-start = ((bf16[8,96,576]{2,1,0:T(8,128)(2,1)}), bf16[8,96,576]{2,1,0:T(8,128)(2,1)}, u32[]{:S(2)}, u32[]{:S(2)}) async-start(bf16[8,96,576]{2,1,0:T(8,128)(2,1)} %bitcast.29), calls=%async_computation | async-start | bytes 1966080 | tf_op jit(solution)/shard_map/all_to_all | solution.py:27
  576.0 77.9 %all-reduce.11.cloned.1.call-start = ((), (), s32[]{:S(2)}) async-start(), calls=%async_computation.8 | async-start | bytes 6291456 | tf_op jit(solution)/shard_map/psum | solution.py:261
  584.0 70.0 %copy-start.8 = (f32[1024,768]{1,0:T(8,128)S(1)}, f32[1024,768]{1,0:T(8,128)}, u32[]{:S(2)}) copy-start(f32[1024,768]{1,0:T(8,128)} %copy-done.7) | copy-start | bytes 9437188
  (78 other events, 278.0 us)
Sparse Core Ops, SparseCore 0:
  213.0 67.1 all-reduce.6
  305.7 41.3 all-reduce.8
  584.1 69.8 all-reduce.10
Sparse Core Ops, SparseCore 1:
  215.6 40.1 all-gather.2
  257.7 39.8 all-gather.4
where the time goes:
time: 714 us; the launch traced here: 707 us
  waiting for transfers between devices  207 us (29%)
  blocking collectives  167 us (23%)
  matrix products  149 us (21%)
  other arithmetic  92.9 us (13%)
  starting transfers between devices  60.1 us (8%)
  between operations  17.3 us (2%)
  local copies, waits for them, and re-layouts  13.3 us (2%)
    psum x1, waiting for transfers between devices, body(): lax.psum(jnp.dot(attended, full_out, preferred_element_type=jnp.float32),...  65.9 us
    psum x1, waiting for transfers between devices, body(): lax.psum(jnp.dot(act_rows, full_down, preferred_element_type=jnp.float32)...  53.4 us
    dot_general x6, matrix products, attend_back(): jnp.einsum('qhd,khd->hqk', d_out, value_list[slot], preferred_element_typ...  40.9 us
    psum x1, blocking collectives, body(): lax.psum((d_kernels, gain_attn_part, gain_ffn_part), 'blk')  37.7 us
    all_to_all x4, starting transfers between devices, sum_at_owner(): lax.all_to_all(blocks, axis, split_axis=0, concat_axis=0, tiled=True)  36.7 us
    convert_element_type x2, other arithmetic, attend_back(): (prob_list[slot] * (dprob_list[slot] - delta_rows[..., None])).astype(jnp...  35.8 us
    psum x1, waiting for transfers between devices, body(): lax.psum(contract(d_up, full_up, 1, 1).astype(jnp.bfloat16), 'head')  33.9 us
    all_gather x1, blocking collectives, body(): lax.all_gather(w_out, 'blk', axis=1, tiled=True)  33.4 us
  transfers between devices with their start and end apart: 19, of which 9 were waited for; matrix products, arithmetic and copies ran while one was open for 21% of the time, Pallas kernels for 0%

commit v1 on v0

v1 whole, which is shorter than its diff:
```python
import functools

import jax
import jax.numpy as jnp
from jax import lax
from jax.experimental import pallas as pl
from jax.experimental.pallas import tpu as pltpu
from jax.sharding import PartitionSpec as P

DH = 64
REACH = 2
EPS = 1e-06
MASKED = -1e30
TILE = 256
HALO = 16
F32 = jnp.float32
BF16 = jnp.bfloat16
VMEM_LIMIT = 56 * 1024 * 1024
COST = pl.CostEstimate(flops=1, bytes_accessed=1, transcendentals=0)


def params(**kw):
    return pltpu.CompilerParams(vmem_limit_bytes=VMEM_LIMIT, **kw)


def whole():
    return pl.BlockSpec(memory_space=pltpu.VMEM)


def mm(a, b, ca=1, cb=0):
    return lax.dot_general(a, b, (((ca,), (cb,)), ((), ())), preferred_element_type=F32)


def swap(x, axis, mask):
    return lax.ppermute(x, axis, [(i, i ^ mask) for i in range(lax.axis_size(axis))])


def moved(x, axis, distance):
    size = lax.axis_size(axis)
    return lax.ppermute(x, axis, [(i, i + distance) for i in range(size) if 0 <= i + distance < size])


def bit_groups(axis):
    bits = list(range(lax.axis_size(axis).bit_length() - 2, -1, -1))
    upper, groups = bits[:-1], []
    while upper:
        groups.append(tuple(upper[:2]))
        upper = upper[2:]
    return groups + [(0,)]


def bit_of(axis, bit):
    return ((lax.axis_index(axis) >> bit) & 1) == 1


def in_order(pieces, axis, group):
    both = jnp.stack(pieces)
    if len(group) == 1:
        return jnp.where(bit_of(axis, group[0]), both[::-1], both)
    both = both.reshape(2, 2, *both.shape[1:])
    both = jnp.where(bit_of(axis, group[0]), both[::-1], both)
    both = jnp.where(bit_of(axis, group[1]), both[:, ::-1], both)
    return both.reshape(4, *both.shape[2:])


def masks_of(group):
    if len(group) == 1:
        return [0, 1 << group[0]]
    hi, lo = 1 << group[0], 1 << group[1]
    return [0, lo, hi, hi | lo]


def gather_all(shard, axis, after=None):
    lead = 1
    out = shard[None]
    for group in bit_groups(axis):
        pieces = [out] + [swap(out, axis, m) for m in masks_of(group)[1:]]
        if after is not None:
            *pieces, after = lax.optimization_barrier((*pieces, after))
        out = in_order(pieces, axis, group)
        out = jnp.moveaxis(out, 0, 1)
        lead *= out.shape[1]
        out = out.reshape(lead, *shard.shape)
    return out


def chosen(full, axis, group):
    r = 1 << len(group)
    out = full.reshape(-1, r, *full.shape[1:])
    mine = (lax.axis_index(axis) >> group[-1]) & (r - 1)
    return [lax.dynamic_index_in_dim(out, mine ^ (m >> group[-1]), 1, keepdims=False) for m in masks_of(group)]


def sum_scatter(full, axis, groups):
    out = full
    for group in reversed(groups):
        keep, *send = chosen(out, axis, group)
        total = keep.astype(F32)
        for m, part in zip(masks_of(group)[1:], send):
            total = total + swap(part, axis, m).astype(F32)
        out = total.astype(BF16)
    return total.reshape(full.shape[1:])


def sum_everywhere(x, axis):
    mask = 1
    while mask < lax.axis_size(axis):
        x = x + swap(x, axis, mask)
        mask *= 2
    return x


def quarters(own):
    far = swap(own, "head", 2)
    return own, far, swap(own, "head", 1), swap(far, "head", 1)


PAIR = 2 * DH
KV = 3 * PAIR
KEY_LANES = ((0, PAIR), (0, PAIR), (2 * PAIR, KV))
VALUE_LANES = ((PAIR, 2 * PAIR), (PAIR, 2 * PAIR), (2 * PAIR, KV))
KEY_ROWS = (0, DH, 2 * PAIR)
VALUE_ROWS = (PAIR, PAIR + DH, 2 * PAIR + DH)


def arranged(q, k, v):
    return jnp.concatenate([k[..., :PAIR], v[..., :PAIR], k[..., PAIR:], v[..., PAIR:], q], axis=-1)


def separated(x):
    k = jnp.concatenate([x[..., :PAIR], x[..., 2 * PAIR : 2 * PAIR + DH]], axis=-1)
    v = jnp.concatenate([x[..., PAIR : 2 * PAIR], x[..., 2 * PAIR + DH : KV]], axis=-1)
    return x[..., KV:], k, v


def unit_times_gain(x, gain):
    return x * lax.rsqrt(jnp.mean(x * x, axis=-1, keepdims=True) + EPS) * gain


def mix_rows(buf_ref, mix_ref, taps, starts, base, rows):
    mix_ref[...] = (
        taps[0:1] * buf_ref[8 : 8 + rows, :]
        + taps[1:2] * buf_ref[7 : 7 + rows, :]
        + taps[2:3] * buf_ref[6 : 6 + rows, :]
    )
    for start in starts:
        r = start - base

        @pl.when((r >= 0) & (r < rows))
        def _(r=r):
            mix_ref[pl.ds(r, 1), :] = taps[0:1] * buf_ref[pl.ds(8 + r, 1), :]

        @pl.when((r + 1 >= 0) & (r + 1 < rows))
        def _(r=r):
            mix_ref[pl.ds(r + 1, 1), :] = (
                taps[0:1] * buf_ref[pl.ds(9 + r, 1), :] + taps[1:2] * buf_ref[pl.ds(8 + r, 1), :]
            )


def project_own_kernel(
    meta_ref, x_ref, halo_ref, gain_ref, w_ref, taps_ref,
    raw_halo_ref, raw_ref, normed_ref, q_ref, kv_ref, kvt_ref, buf_ref, mix_ref, *, base,
):
    i = pl.program_id(0)
    rows = x_ref.shape[0]
    gain = gain_ref[...]
    w = w_ref[...]

    @pl.when(i == 0)
    def _():
        halo = jnp.where(meta_ref[HAS_ONE] == 1, halo_ref[...].astype(F32), 0.0)
        normed = unit_times_gain(halo, gain).astype(BF16)
        raw_low = mm(normed, w).astype(BF16)
        raw_halo_ref[...] = raw_low[:, KV:]
        buf_ref[0:8, :] = raw_low.astype(F32)[HALO - 8 :, :]

    normed = unit_times_gain(x_ref[...].astype(F32), gain).astype(BF16)
    raw_low = mm(normed, w).astype(BF16)
    normed_ref[...] = normed
    raw_ref[...] = raw_low
    raw = raw_low.astype(F32)
    buf_ref[8 : 8 + rows, :] = raw
    mix_rows(buf_ref, mix_ref, taps_ref[...], [meta_ref[STARTS + n] for n in range(8)], base + i * rows, rows)
    buf_ref[0:8, :] = raw[rows - 8 :, :]
    q_ref[...] = mix_ref[:, KV:].astype(BF16)
    kv = mix_ref[:, :KV]
    kv_ref[...] = kv.astype(BF16)
    kvt_ref[...] = kv.T.astype(BF16)


def project_own(meta, tokens, halo, gain, w, taps):
    rows, dim = tokens.shape
    width = w.shape[1]
    step = 2 * TILE
    tile = lambda n: pl.BlockSpec((step, n), lambda i, *_: (i, 0))
    return pl.pallas_call(
        functools.partial(project_own_kernel, base=REACH * rows),
        out_shape=(
            jax.ShapeDtypeStruct((HALO, width - KV), BF16),
            jax.ShapeDtypeStruct((rows, width), BF16),
            jax.ShapeDtypeStruct((rows, dim), BF16),
            jax.ShapeDtypeStruct((rows, width - KV), BF16),
            jax.ShapeDtypeStruct((rows, KV), BF16),
            jax.ShapeDtypeStruct((KV, rows), BF16),
        ),
        grid_spec=pltpu.PrefetchScalarGridSpec(
            num_scalar_prefetch=1,
            grid=(rows // step,),
            in_specs=[tile(dim), whole(), whole(), whole(), whole()],
            out_specs=(
                whole(),
                tile(width),
                tile(dim),
                tile(width - KV),
                tile(KV),
                pl.BlockSpec((KV, step), lambda i, *_: (0, i)),
            ),
            scratch_shapes=[pltpu.VMEM((8 + step, width), F32), pltpu.VMEM((step, width), F32)],
        ),
        compiler_params=params(),
        cost_estimate=COST,
        name="project_own",
    )(meta, tokens, halo, gain, w, taps)


def project_earlier_kernel(meta_ref, *refs):
    pieces = refs[:8]
    gain_ref, w_ref, taps_ref, raw_ref, normed_ref, kv_ref, kvt_ref, x_ref, buf_ref, mix_ref = refs[8:]
    i = pl.program_id(0)
    rows = x_ref.shape[0]
    quarter = pieces[0].shape[0]

    @pl.when(i == 0)
    def _():
        buf_ref[0:8, :] = jnp.zeros((8, KV), F32)

    for hop in range(REACH):
        for slot, d in enumerate((0, 2, 1, 3)):
            place = 4 * hop + (meta_ref[0] ^ d)

            @pl.when(i == place >> 1)
            def _(piece=pieces[4 * hop + slot], place=place):
                x_ref[pl.ds(pl.multiple_of((place & 1) * quarter, quarter), quarter), :] = piece[...]

    exists = jnp.where(i < pl.num_programs(0) // REACH, meta_ref[HAS_TWO], meta_ref[HAS_ONE])
    x = jnp.where(exists == 1, x_ref[...].astype(F32), 0.0)
    normed = unit_times_gain(x, gain_ref[...]).astype(BF16)
    normed_ref[...] = normed
    raw_low = mm(normed, w_ref[:, :KV]).astype(BF16)
    raw_ref[...] = raw_low
    raw = raw_low.astype(F32)
    buf_ref[8 : 8 + rows, :] = raw
    mix_rows(buf_ref, mix_ref, taps_ref[:, :KV], [meta_ref[STARTS + n] for n in range(8)], i * rows, rows)
    buf_ref[0:8, :] = raw[rows - 8 :, :]
    kv = mix_ref[...]
    kv_ref[...] = kv.astype(BF16)
    kvt_ref[...] = kv.T.astype(BF16)


def project_earlier(meta, pieces, gain, w, taps):
    quarter, dim = pieces[0].shape
    step = 2 * quarter
    span = len(pieces) * quarter
    tile = lambda n: pl.BlockSpec((step, n), lambda i, *_: (i, 0))
    return pl.pallas_call(
        project_earlier_kernel,
        out_shape=(
            jax.ShapeDtypeStruct((span, KV), BF16),
            jax.ShapeDtypeStruct((span, dim), BF16),
            jax.ShapeDtypeStruct((span, KV), BF16),
            jax.ShapeDtypeStruct((KV, span), BF16),
        ),
        grid_spec=pltpu.PrefetchScalarGridSpec(
            num_scalar_prefetch=1,
            grid=(span // step,),
            in_specs=[whole()] * 11,
            out_specs=(tile(KV), tile(dim), tile(KV), pl.BlockSpec((KV, step), lambda i, *_: (0, i))),
            scratch_shapes=[
                pltpu.VMEM((step, dim), BF16),
                pltpu.VMEM((8 + step, KV), F32),
                pltpu.VMEM((step, KV), F32),
            ],
        ),
        compiler_params=params(),
        cost_estimate=COST,
        name="project_earlier",
    )(meta, *pieces, gain, w, taps)


LOW, FULL, STARTS = 1, 5, 9
HAS_ONE, HAS_TWO, NEXT_ONE, NEXT_TWO = 17, 18, 19, 20


def key_loops(meta_ref, qt, begin, end, step):
    low = jnp.maximum(meta_ref[LOW + qt], begin)
    middle = jnp.clip(meta_ref[FULL + qt], low, jnp.maximum(end, low))

    def run(masked):
        def one(kt, carry):
            step(kt, masked)
            return carry

        return one

    lax.fori_loop(low, middle, run(True), 0)
    lax.fori_loop(middle, end, run(False), 0)


def masked_scores(scores, kt, first_ref, diagonal, ahead=0):
    keys = lax.broadcasted_iota(jnp.int32, scores.shape, 0)
    allowed = keys >= first_ref[...] - kt * TILE
    if diagonal:
        allowed = allowed & (keys <= lax.broadcasted_iota(jnp.int32, scores.shape, 1) + ahead)
    return jnp.where(allowed, scores, MASKED)


def query_operands(across):
    zero = jnp.zeros((DH, across.shape[1]), across.dtype)
    return (
        jnp.concatenate([across[:DH], zero], axis=0),
        jnp.concatenate([zero, across[DH:PAIR]], axis=0),
        jnp.concatenate([across[PAIR:], zero], axis=0),
    )


def value_operands(across):
    zero = jnp.zeros((DH, across.shape[1]), across.dtype)
    return (
        jnp.concatenate([across[:DH], zero], axis=0),
        jnp.concatenate([zero, across[DH:PAIR]], axis=0),
        jnp.concatenate([zero, across[PAIR:]], axis=0),
    )


def eights(x, how):
    return how(x.reshape(x.shape[0] // 8, 8, x.shape[1]), axis=0)


def attend_tiles(meta_ref, q_ref, kv_ref, kvt_ref, first_ref, acc_ref, top_ref, sum_ref, *, begin, diagonal):
    qt = pl.program_id(0)
    queries = query_operands((q_ref[...].astype(F32) * (DH**-0.5)).T.astype(BF16))
    end = begin + kv_ref.shape[0] // TILE
    own = begin + qt
    acc_ref[...] = jnp.zeros_like(acc_ref)
    top_ref[...] = jnp.full(top_ref.shape, MASKED, F32)
    sum_ref[...] = jnp.zeros_like(sum_ref)

    def scores_of(kt, h, masked, diag):
        at = pl.ds(pl.multiple_of((kt - begin) * TILE, TILE), TILE)
        scores = mm(kv_ref[at, KEY_LANES[h][0] : KEY_LANES[h][1]], queries[h])
        return masked_scores(scores, kt, first_ref, diag) if masked else scores

    def top(kt, masked, diag=False):
        for h in range(3):
            rows = slice(8 * h, 8 * h + 8)
            top_ref[rows, :] = jnp.maximum(top_ref[rows, :], eights(scores_of(kt, h, masked, diag), jnp.max))

    def add(kt, masked, diag=False):
        at = pl.ds(pl.multiple_of((kt - begin) * TILE, TILE), TILE)
        for h in range(3):
            weights = jnp.exp(scores_of(kt, h, masked, diag) - top_ref[8 * h : 8 * h + 1, :])
            rows = slice(8 * h, 8 * h + 8)
            sum_ref[rows, :] += eights(weights, jnp.sum)
            values = kvt_ref[VALUE_ROWS[h] : VALUE_ROWS[h] + DH, at]
            acc_ref[h * DH : (h + 1) * DH, :] += mm(values, weights.astype(BF16))

    for step in (top, add):
        if diagonal:
            key_loops(meta_ref, qt, begin, own, step)
            step(own, True, True)
        else:
            key_loops(meta_ref, qt, begin, end, step)
        if step is top:
            for h in range(3):
                rows = slice(8 * h, 8 * h + 8)
                top_ref[rows, :] = jnp.broadcast_to(jnp.max(top_ref[rows, :], axis=0, keepdims=True), (8, TILE))
    for h in range(3):
        rows = slice(8 * h, 8 * h + 8)
        sum_ref[rows, :] = jnp.broadcast_to(jnp.sum(sum_ref[rows, :], axis=0, keepdims=True), (8, TILE))


def attend_own_kernel(meta_ref, q_ref, kv_ref, kvt_ref, first_ref, acc_ref, stat_ref, top_ref, sum_ref, *, begin):
    attend_tiles(
        meta_ref, q_ref, kv_ref, kvt_ref, first_ref, acc_ref, top_ref, sum_ref, begin=begin, diagonal=True
    )
    stat_ref[0, 0:24, :] = top_ref[...]
    stat_ref[0, 24:48, :] = sum_ref[...]


def attend_earlier_kernel(
    meta_ref, q_ref, kv_ref, kvt_ref, first_ref, acc_own_ref, stat_own_ref,
    att_ref, ot_ref, lse_ref, acc_ref, top_ref, sum_ref,
):
    attend_tiles(meta_ref, q_ref, kv_ref, kvt_ref, first_ref, acc_ref, top_ref, sum_ref, begin=0, diagonal=False)
    for h in range(3):
        rows = slice(h * DH, (h + 1) * DH)
        top_here, top_own = top_ref[8 * h : 8 * h + 1, :], stat_own_ref[0, 8 * h : 8 * h + 1, :]
        top = jnp.maximum(top_here, top_own)
        here, own = jnp.exp(top_here - top), jnp.exp(top_own - top)
        total = here * sum_ref[8 * h : 8 * h + 1, :] + own * stat_own_ref[0, 24 + 8 * h : 25 + 8 * h, :]
        out = (acc_ref[rows, :] * here + acc_own_ref[rows, :] * own) / total
        ot_ref[rows, :] = out
        att_ref[0, rows, :] = out.astype(BF16)
        lse_ref[0, h : h + 1, :] = top + jnp.log(total)


def slot_of(i, meta):
    d = i ^ meta[0]
    return (d >> 1) | ((d & 1) << 1)


def attend_own(meta, q, kv, kvt, first_row):
    rows, part = q.shape
    tiles = rows // TILE
    across = pl.BlockSpec((part, TILE), lambda i, *_: (0, i))
    return pl.pallas_call(
        functools.partial(attend_own_kernel, begin=REACH * tiles),
        out_shape=(
            jax.ShapeDtypeStruct((part, rows), F32),
            jax.ShapeDtypeStruct((tiles, 48, TILE), F32),
        ),
        grid_spec=pltpu.PrefetchScalarGridSpec(
            num_scalar_prefetch=1,
            grid=(tiles,),
            in_specs=[
                pl.BlockSpec((TILE, part), lambda i, *_: (i, 0)),
                whole(),
                whole(),
                pl.BlockSpec((1, TILE), lambda i, *_: (0, i)),
            ],
            out_specs=(across, pl.BlockSpec((1, 48, TILE), lambda i, *_: (i, 0, 0))),
            scratch_shapes=[pltpu.VMEM((24, TILE), F32), pltpu.VMEM((24, TILE), F32)],
        ),
        compiler_params=params(),
        cost_estimate=COST,
        name="attend_own",
    )(meta, q, kv, kvt, first_row)


def attend_earlier(meta, q, kv, kvt, first_row, acc_own, stat_own):
    rows, part = q.shape
    tiles = rows // TILE
    across = pl.BlockSpec((part, TILE), lambda i, *_: (0, i))
    return pl.pallas_call(
        attend_earlier_kernel,
        out_shape=(
            jax.ShapeDtypeStruct((tiles, part, TILE), BF16),
            jax.ShapeDtypeStruct((part, rows), F32),
            jax.ShapeDtypeStruct((tiles, 8, TILE), F32),
        ),
        grid_spec=pltpu.PrefetchScalarGridSpec(
            num_scalar_prefetch=1,
            grid=(tiles,),
            in_specs=[
                pl.BlockSpec((TILE, part), lambda i, *_: (i, 0)),
                whole(),
                whole(),
                pl.BlockSpec((1, TILE), lambda i, *_: (0, i)),
                across,
                pl.BlockSpec((1, 48, TILE), lambda i, *_: (i, 0, 0)),
            ],
            out_specs=(
                pl.BlockSpec((1, part, TILE), lambda i, meta: (slot_of(i, meta), 0, 0)),
                across,
                pl.BlockSpec((1, 8, TILE), lambda i, *_: (i, 0, 0)),
            ),
            scratch_shapes=[
                pltpu.VMEM((part, TILE), F32),
                pltpu.VMEM((24, TILE), F32),
                pltpu.VMEM((24, TILE), F32),
            ],
        ),
        compiler_params=params(),
        cost_estimate=COST,
        name="attend_earlier",
    )(meta, q, kv, kvt, first_row, acc_own, stat_own)


def back_operands(q_ref, dt_ref, ot_ref, lse_ref):
    scaled = q_ref[...].astype(F32) * (DH**-0.5)
    d_out_t = dt_ref[0]
    d_wide = d_out_t.astype(F32)
    delta = [
        jnp.sum(d_wide[h * DH : (h + 1) * DH] * ot_ref[h * DH : (h + 1) * DH, :], axis=0, keepdims=True)
        for h in range(3)
    ]
    queries, d_out = scaled.astype(BF16), d_wide.T.astype(BF16)
    zero = jnp.zeros((TILE, DH), BF16)
    lane = lax.broadcasted_iota(jnp.int32, (TILE, PAIR), 1)

    def two(x):
        pair = x[:, :PAIR]
        none = jnp.zeros_like(pair)
        return jnp.concatenate([jnp.where(lane < DH, pair, none), jnp.where(lane < DH, none, pair)], axis=0)

    single = jnp.concatenate(
        [
            jnp.concatenate([queries[:, PAIR:], zero], axis=1),
            jnp.concatenate([zero, d_out[:, PAIR:]], axis=1),
        ],
        axis=0,
    )
    return (
        query_operands(scaled.T.astype(BF16)),
        value_operands(d_out_t),
        (two(queries), two(d_out), single),
        [lse_ref[0, h : h + 1, :] for h in range(3)],
        delta,
    )


def back_step(kt, masked, diag, operands, refs, begin, lead, ahead=0):
    queries_t, d_out_t, stacked, lse, delta = operands
    kv_ref, kvt_ref, first_ref, grad_ref, dq_ref = refs
    at = pl.ds(pl.multiple_of((kt - begin) * TILE, TILE), TILE)
    weights, grads = [], []
    for h in range(3):
        scores = mm(kv_ref[at, KEY_LANES[h][0] : KEY_LANES[h][1]], queries_t[h])
        if masked:
            scores = masked_scores(scores, kt, first_ref, diag, ahead)
        probs = jnp.exp(scores - lse[h])
        d_probs = mm(kv_ref[at, VALUE_LANES[h][0] : VALUE_LANES[h][1]], d_out_t[h])
        d_scores = (probs * (d_probs - delta[h])).astype(BF16)
        weights.append(probs.astype(BF16))
        grads.append(d_scores)
        dq_ref[h * DH : (h + 1) * DH, :] += mm(kvt_ref[KEY_ROWS[h] : KEY_ROWS[h] + DH, at], d_scores)
    to = pl.ds(pl.multiple_of(lead + (kt - begin) * TILE, 8), TILE)
    grad_ref[to, :PAIR] += mm(jnp.concatenate(grads[:2], axis=1), stacked[0])
    grad_ref[to, PAIR : 2 * PAIR] += mm(jnp.concatenate(weights[:2], axis=1), stacked[1])
    grad_ref[to, 2 * PAIR : KV] += mm(jnp.concatenate([grads[2], weights[2]], axis=1), stacked[2])


def unmix_rows(grad_ref, raw_ref, fix_ref, taps, starts, rows, sums_ref):
    width = grad_ref.shape[1]

    def raw_row(r):
        group = raw_ref[pl.ds(pl.multiple_of((r // HALO) * HALO, HALO), HALO), :].astype(F32)
        row = lax.broadcasted_iota(jnp.int32, group.shape, 0)
        return jnp.sum(jnp.where(row == r % HALO, group, 0.0), axis=0, keepdims=True)

    sums_ref[...] = jnp.zeros_like(sums_ref)
    inside = [(s >= 1) & (s <= rows + 1) for s in starts]
    for n, s in enumerate(starts):

        @pl.when(inside[n])
        def _(n=n, s=s):
            one_before = grad_ref[pl.ds(7 + s, 1), :]
            fix_ref[2 * n : 2 * n + 1, :] = taps[0:1] * one_before
            fix_ref[2 * n + 1 : 2 * n + 2, :] = taps[0:1] * grad_ref[pl.ds(6 + s, 1), :] + taps[1:2] * one_before
            here = grad_ref[pl.ds(8 + s, 1), :]

            @pl.when(s >= 2)
            def _():
                sums_ref[2:3, :] -= raw_row(jnp.maximum(s - 2, 0)) * here

            @pl.when(s <= rows)
            def _():
                raw_one = raw_row(s - 1)
                sums_ref[1:2, :] -= raw_one * here
                following = starts[n + 1] if n + 1 < len(starts) else s + 2

                @pl.when(following != s + 1)
                def _():
                    sums_ref[2:3, :] -= raw_one * grad_ref[pl.ds(9 + s, 1), :]

    sizes = [HALO] * (1 if rows % TILE else 0) + [TILE] * (rows // TILE)
    lo = 0
    totals = [jnp.zeros((8, width), F32) for _ in range(3)]
    for size in sizes:
        now = grad_ref[8 + lo : 8 + lo + size, :]
        one = grad_ref[9 + lo : 9 + lo + size, :]
        two = grad_ref[10 + lo : 10 + lo + size, :]
        raw = raw_ref[lo : lo + size, :].astype(F32)
        for j, shifted in enumerate((now, one, two)):
            totals[j] = totals[j] + eights(raw * shifted, jnp.sum)
        grad_ref[8 + lo : 8 + lo + size, :] = taps[0:1] * now + taps[1:2] * one + taps[2:3] * two
        lo += size
    for j in range(3):
        sums_ref[j : j + 1, :] += jnp.sum(totals[j], axis=0, keepdims=True)
    for n in reversed(range(len(starts))):

        @pl.when(inside[n])
        def _(n=n, s=starts[n]):
            grad_ref[pl.ds(7 + s, 1), :] = fix_ref[2 * n : 2 * n + 1, :]
            grad_ref[pl.ds(6 + s, 1), :] = fix_ref[2 * n + 1 : 2 * n + 2, :]


def earlier_back_kernel(
    meta_ref, q_ref, dt_ref, ot_ref, lse_ref, first_ref, kv_ref, kvt_ref, kv_own_ref, kvt_own_ref, raw_ref,
    raw_halo_ref, taps_ref, dq_ref, two_ref, one_ref, next_ref, sums_ref, sums_q_ref,
    grad_ref, grad_q_ref, fix_ref, fix_q_ref,
):
    qt = pl.program_id(0)
    before = kv_ref.shape[0]
    tiles = before // TILE

    @pl.when(qt == 0)
    def _():
        grad_ref[...] = jnp.zeros_like(grad_ref)
        grad_q_ref[...] = jnp.zeros_like(grad_q_ref)

    dq_ref[...] = jnp.zeros_like(dq_ref)

    @pl.when(meta_ref[LOW + qt] <= tiles)
    def _():
        operands = back_operands(q_ref, dt_ref, ot_ref, lse_ref)
        refs = (kv_ref, kvt_ref, first_ref, grad_ref, dq_ref)
        own = (kv_own_ref, kvt_own_ref, first_ref, grad_ref, dq_ref)
        key_loops(meta_ref, qt, 0, tiles, lambda kt, masked: back_step(kt, masked, False, operands, refs, 0, 8))
        back_step(tiles, True, True, operands, own, tiles, 8 + before, qt * TILE)

    @pl.when(qt == 0)
    def _():
        grad_q_ref[8 + HALO : 16 + HALO, :] = dq_ref[:, :PAIR].T[:8] * (DH**-0.5)

    @pl.when(qt == pl.num_programs(0) - 1)
    def _():
        starts = [meta_ref[STARTS + n] for n in range(8)]
        next_ref[...] = grad_ref[8 + before : 8 + before + TILE, :]
        unmix_rows(grad_ref, raw_ref, fix_ref, taps_ref[:, :KV], starts, before, sums_ref)
        starts = [s - (before - HALO) for s in starts]
        unmix_rows(grad_q_ref, raw_halo_ref, fix_q_ref, taps_ref[:, KV:], starts, HALO, sums_q_ref)
        half = before // 2
        two_ref[...] = grad_ref[8 : 8 + half, :].astype(BF16)
        one_ref[0:half, :] = grad_ref[8 + half : 8 + before, :].astype(BF16)
        queries = grad_q_ref[8 : 8 + HALO, :]
        one_ref[half : half + HALO, :] = jnp.concatenate([queries, jnp.zeros_like(queries)], axis=1).astype(BF16)


def tile_specs(part):
    return [
        pl.BlockSpec((TILE, part), lambda i, *_: (i, 0)),
        pl.BlockSpec((1, part, TILE), lambda i, meta: (slot_of(i, meta), 0, 0)),
        pl.BlockSpec((part, TILE), lambda i, *_: (0, i)),
        pl.BlockSpec((1, 8, TILE), lambda i, *_: (i, 0, 0)),
        pl.BlockSpec((1, TILE), lambda i, *_: (0, i)),
    ]


def earlier_back(meta, q, d_out_t, out_t, lse, first_row, kv, kvt, kv_own, kvt_own, raw, raw_halo, taps):
    rows, part = q.shape
    before = kv.shape[0]
    return pl.pallas_call(
        earlier_back_kernel,
        out_shape=(
            jax.ShapeDtypeStruct((part, rows), F32),
            jax.ShapeDtypeStruct((rows, KV), BF16),
            jax.ShapeDtypeStruct((rows + HALO, KV), BF16),
            jax.ShapeDtypeStruct((TILE, KV), F32),
            jax.ShapeDtypeStruct((8, KV), F32),
            jax.ShapeDtypeStruct((8, part), F32),
        ),
        grid_spec=pltpu.PrefetchScalarGridSpec(
            num_scalar_prefetch=1,
            grid=(rows // TILE,),
            in_specs=tile_specs(part)
            + [
                whole(),
                whole(),
                pl.BlockSpec((TILE, KV), lambda i, *_: (0, 0)),
                pl.BlockSpec((KV, TILE), lambda i, *_: (0, 0)),
                whole(),
                whole(),
                whole(),
            ],
            out_specs=(pl.BlockSpec((part, TILE), lambda i, *_: (0, i)), *[whole()] * 5),
            scratch_shapes=[
                pltpu.VMEM((8 + before + TILE + 8, KV), F32),
                pltpu.VMEM((8 + HALO + 8, part), F32),
                pltpu.VMEM((16, KV), F32),
                pltpu.VMEM((16, part), F32),
            ],
        ),
        compiler_params=params(),
        cost_estimate=COST,
        name="earlier_back",
    )(meta, q, d_out_t, out_t, lse, first_row, kv, kvt, kv_own, kvt_own, raw, raw_halo, taps)


def own_back_kernel(
    meta_ref, q_ref, dt_ref, ot_ref, lse_ref, first_ref, dq_in_ref, kv_ref, kvt_ref, raw_ref, taps_ref, next_ref,
    d_raw_ref, sums_ref, dq_ref, grad_ref, fix_ref, *, begin,
):
    qt = pl.program_id(0)
    rows = kv_ref.shape[0]

    @pl.when(qt == 0)
    def _():
        grad_ref[...] = jnp.zeros_like(grad_ref)
        grad_ref[8 : 8 + TILE, :KV] = next_ref[...]

    dq_ref[...] = dq_in_ref[...]

    @pl.when(qt > 0)
    def _():
        operands = back_operands(q_ref, dt_ref, ot_ref, lse_ref)
        refs = (kv_ref, kvt_ref, first_ref, grad_ref, dq_ref)
        step = lambda kt, masked: back_step(kt, masked, False, operands, refs, begin, 8)
        key_loops(meta_ref, qt, begin + 1, begin + qt, step)
        back_step(begin + qt, True, True, operands, refs, begin, 8)

    to = pl.ds(pl.multiple_of(8 + qt * TILE, 8), TILE)
    grad_ref[to, KV:] = dq_ref[...].T * (DH**-0.5)

    @pl.when(qt == pl.num_programs(0) - 1)
    def _():
        starts = [meta_ref[STARTS + n] - begin * TILE for n in range(8)]
        unmix_rows(grad_ref, raw_ref, fix_ref, taps_ref[...], starts, rows, sums_ref)
        d_raw_ref[...] = grad_ref[8 : 8 + rows, :].astype(BF16)


def own_back(meta, q, d_out_t, out_t, lse, first_row, dq_t, kv, kvt, raw, taps, grad_next):
    rows, part = q.shape
    width = raw.shape[1]
    return pl.pallas_call(
        functools.partial(own_back_kernel, begin=REACH * rows // TILE),
        out_shape=(
            jax.ShapeDtypeStruct((rows, width), BF16),
            jax.ShapeDtypeStruct((8, width), F32),
        ),
        grid_spec=pltpu.PrefetchScalarGridSpec(
            num_scalar_prefetch=1,
            grid=(rows // TILE,),
            in_specs=tile_specs(part) + [pl.BlockSpec((part, TILE), lambda i, *_: (0, i))] + [whole()] * 5,
            out_specs=(whole(), whole()),
            scratch_shapes=[
                pltpu.VMEM((part, TILE), F32),
                pltpu.VMEM((8 + rows + 8, width), F32),
                pltpu.VMEM((16, width), F32),
            ],
        ),
        compiler_params=params(),
        cost_estimate=COST,
        name="own_back",
    )(meta, q, d_out_t, out_t, lse, first_row, dq_t, kv, kvt, raw, taps, grad_next)


def after_attend_kernel(a0, a1, a2, a3, w0, w1, w2, w3, x_ref, gain_ref, hidden_ref, normed_ref):
    branch = mm(a0[...], w0[...], 0, 0)
    for a, w in ((a1, w1), (a2, w2), (a3, w3)):
        branch = branch + mm(a[...], w[...], 0, 0)
    hidden = x_ref[...].astype(F32) + branch
    hidden_ref[...] = hidden
    factor = lax.rsqrt(jnp.mean(hidden * hidden, axis=-1, keepdims=True) + EPS)
    normed_ref[...] = (hidden * factor * gain_ref[...]).astype(BF16)


def after_attend(attended, w_out, x, gain):
    rows, dim = x.shape
    return pl.pallas_call(
        after_attend_kernel,
        out_shape=(jax.ShapeDtypeStruct((rows, dim), F32), jax.ShapeDtypeStruct((rows, dim), BF16)),
        in_specs=[whole()] * 10,
        out_specs=(whole(), whole()),
        compiler_params=params(),
        cost_estimate=COST,
        name="after_attend",
    )(*attended, *w_out, x, gain)


def feed_kernel(x_ref, cot_ref, up_ref, down_ref, act_ref, d_up_ref, keep_ref, send_ref):
    up = mm(x_ref[...], up_ref[...])
    pos = jnp.maximum(up, 0.0)
    act_ref[...] = (pos * pos).astype(BF16)
    d_act = mm(cot_ref[...], down_ref[...])
    d_up = (d_act * 2.0 * pos).astype(BF16)
    d_up_ref[...] = d_up
    back = mm(d_up, up_ref[...], 1, 1).astype(BF16)

    @pl.when(pl.program_id(0) == 0)
    def _():
        keep_ref[...] = back

    @pl.when(pl.program_id(0) == 1)
    def _():
        send_ref[...] = back


def feed(x, cot, w_up, w_down_t):
    rows, dim = x.shape
    units = w_up.shape[1]
    step = rows // 2
    tile = lambda n: pl.BlockSpec((step, n), lambda i: (i, 0))
    return pl.pallas_call(
        feed_kernel,
        out_shape=(
            jax.ShapeDtypeStruct((rows, units), BF16),
            jax.ShapeDtypeStruct((rows, units), BF16),
            jax.ShapeDtypeStruct((step, dim), BF16),
            jax.ShapeDtypeStruct((step, dim), BF16),
        ),
        grid=(2,),
        in_specs=[tile(dim), tile(dim), whole(), whole()],
        out_specs=(tile(units), tile(units), whole(), whole()),
        compiler_params=params(),
        cost_estimate=COST,
        name="feed",
    )(x, cot, w_up, w_down_t)


def feed_out_kernel(act_ref, down_ref, keep_ref, send_ref):
    out = mm(act_ref[...], down_ref[...], 1, 1).astype(BF16)

    @pl.when(pl.program_id(0) == 0)
    def _():
        keep_ref[...] = out

    @pl.when(pl.program_id(0) == 1)
    def _():
        send_ref[...] = out


def feed_out(act, w_down_t):
    rows, units = act.shape
    dim = w_down_t.shape[0]
    half = jax.ShapeDtypeStruct((rows // 2, dim), BF16)
    return pl.pallas_call(
        feed_out_kernel,
        out_shape=(half, half),
        grid=(2,),
        in_specs=[pl.BlockSpec((rows // 2, units), lambda i: (i, 0)), whole()],
        out_specs=(whole(), whole()),
        compiler_params=params(),
        cost_estimate=COST,
        name="feed_out",
    )(act, w_down_t)


def feed_grads_kernel(x_ref, d_up_ref, cot_ref, act_ref, up_ref, down_ref):
    up_ref[...] = mm(x_ref[...], d_up_ref[...], 0, 0).astype(BF16)
    down_ref[...] = mm(cot_ref[...], act_ref[...], 0, 0).astype(BF16)


def feed_grads(x, d_up, cot, act):
    rows, dim = x.shape
    units = act.shape[1]
    block = pl.BlockSpec((rows, TILE), lambda i: (0, i))
    out = pl.BlockSpec((TILE, units), lambda i: (i, 0))
    shape = jax.ShapeDtypeStruct((dim, units), BF16)
    return pl.pallas_call(
        feed_grads_kernel,
        out_shape=(shape, shape),
        grid=(dim // TILE,),
        in_specs=[block, whole(), block, whole()],
        out_specs=(out, out),
        compiler_params=params(),
        cost_estimate=COST,
        name="feed_grads",
    )(x, d_up, cot, act)


def mix_grads_kernel(e_ref, two_ref, one_ref, o_ref, d_raw_ref, out_t_ref, grad_ref):
    rows = two_ref.shape[0]
    part = out_t_ref.shape[1]
    grad = mm(o_ref[...], d_raw_ref[...], 0, 0)
    kv = mm(e_ref[:rows, :], two_ref[...], 0, 0) + mm(e_ref[rows:, :], one_ref[:rows, :], 0, 0)
    q = mm(e_ref[2 * rows - HALO :, :], one_ref[rows:, :], 0, 0)[:, :part]
    grad_ref[:, :KV] = (grad[:, :KV] + kv).astype(BF16)
    grad_ref[:, KV:] = jnp.concatenate([grad[:, KV:] + q, out_t_ref[...].astype(F32)], axis=1).astype(BF16)


def mix_grads(normed_e, d_two, d_one, normed, d_raw, out_t):
    dim = normed.shape[1]
    width = d_raw.shape[1] + out_t.shape[1]
    block = lambda x: pl.BlockSpec((x.shape[0], TILE), lambda i: (0, i))
    out = lambda n: pl.BlockSpec((TILE, n), lambda i: (i, 0))
    return pl.pallas_call(
        mix_grads_kernel,
        out_shape=jax.ShapeDtypeStruct((dim, width), BF16),
        grid=(dim // TILE,),
        in_specs=[block(normed_e), whole(), whole(), block(normed), whole(), out(out_t.shape[1])],
        out_specs=out(width),
        compiler_params=params(),
        cost_estimate=COST,
        name="mix_grads",
    )(normed_e, d_two, d_one, normed, d_raw, out_t)


def before_back_kernel(
    s_ref, r_ref, hidden_ref, gain_ref, cot_ref, w0, w1, w2, w3, a0, a1, a2, a3,
    d_hidden_ref, d0, d1, d2, d3, keep_ref, send_ref, sum_ref,
):
    d_normed = s_ref[...].astype(F32) + r_ref[...].astype(F32)
    hidden = hidden_ref[...]
    factor = lax.rsqrt(jnp.mean(hidden * hidden, axis=-1, keepdims=True) + EPS)
    unit = hidden * factor
    sum_ref[...] = jnp.sum(d_normed * unit, axis=0, keepdims=True)
    scaled = d_normed * gain_ref[...]
    inner = jnp.mean(scaled * unit, axis=-1, keepdims=True)
    d_hidden = cot_ref[...].astype(F32) + factor * (scaled - unit * inner)
    d_hidden_ref[...] = d_hidden
    d_branch = d_hidden.astype(BF16)
    for w, d in ((w0, d0), (w1, d1), (w2, d2), (w3, d3)):
        d[...] = mm(w[...], d_branch, 1, 1).astype(BF16)
    for a, to in ((a0, keep_ref.at[0]), (a1, keep_ref.at[1]), (a2, send_ref.at[0]), (a3, send_ref.at[1])):
        to[...] = mm(a[...], d_branch).astype(BF16)


def before_back(chip_sum, far_sum, hidden, gain, cot, w_out, attended):
    rows, dim = hidden.shape
    part = w_out[0].shape[0]
    return pl.pallas_call(
        before_back_kernel,
        out_shape=(
            jax.ShapeDtypeStruct((rows, dim), F32),
            *[jax.ShapeDtypeStruct((part, rows), BF16)] * 4,
            *[jax.ShapeDtypeStruct((2, part, dim), BF16)] * 2,
            jax.ShapeDtypeStruct((1, dim), F32),
        ),
        in_specs=[whole()] * 13,
        out_specs=tuple([whole()] * 8),
        compiler_params=params(),
        cost_estimate=COST,
        name="before_back",
    )(chip_sum, far_sum, hidden, gain, cot, *w_out, *attended)


def d_normed_kernel(meta_ref, own_ref, one_ref, halo_ref, two_ref, x_ref, w_ref, keep_ref, send_ref, sum_ref):
    i = pl.program_id(0)
    step = own_ref.shape[0]
    later = jnp.where(meta_ref[NEXT_ONE] == 1, one_ref[...].astype(F32), 0.0)
    later = later + jnp.where(meta_ref[NEXT_TWO] == 1, two_ref[...].astype(F32), 0.0)
    own = own_ref[...].astype(F32)
    queries = own[:, KV:]
    part = queries.shape[1]
    last = (i == pl.num_programs(0) - 1) & (meta_ref[NEXT_ONE] == 1)
    halo = jnp.where(last, halo_ref[...].astype(F32)[:, :part], 0.0)
    queries = queries + jnp.concatenate([jnp.zeros((step - HALO, part), F32), halo], axis=0)
    d_raw = jnp.concatenate([own[:, :KV] + later, queries], axis=1).astype(BF16)
    d_normed = mm(d_raw, w_ref[...], 1, 1)
    for n in range(step // TILE):
        slot = slot_of(i * (step // TILE) + n, meta_ref)
        rows = d_normed[n * TILE : (n + 1) * TILE].astype(BF16)
        to = pl.ds(pl.multiple_of((slot & 1) * TILE, TILE), TILE)

        @pl.when(slot < 2)
        def _(rows=rows, to=to):
            keep_ref[to, :] = rows

        @pl.when(slot >= 2)
        def _(rows=rows, to=to):
            send_ref[to, :] = rows

    x = x_ref[...].astype(F32)
    unit = x * lax.rsqrt(jnp.mean(x * x, axis=-1, keepdims=True) + EPS)

    @pl.when(i == 0)
    def _():
        sum_ref[...] = jnp.zeros_like(sum_ref)

    sum_ref[...] += jnp.sum(d_normed * unit, axis=0, keepdims=True)


def d_normed_parts(meta, own, one, two, x, w):
    rows, dim = x.shape
    width = w.shape[1]
    step = 2 * TILE
    tile = lambda n: pl.BlockSpec((step, n), lambda i, *_: (i, 0))
    return pl.pallas_call(
        d_normed_kernel,
        out_shape=(
            jax.ShapeDtypeStruct((rows // 2, dim), BF16),
            jax.ShapeDtypeStruct((rows // 2, dim), BF16),
            jax.ShapeDtypeStruct((1, dim), F32),
        ),
        grid_spec=pltpu.PrefetchScalarGridSpec(
            num_scalar_prefetch=1,
            grid=(rows // step,),
            in_specs=[
                tile(width),
                tile(KV),
                pl.BlockSpec((HALO, KV), lambda i, *_: (rows // HALO, 0)),
                tile(KV),
                tile(dim),
                whole(),
            ],
            out_specs=(whole(), whole(), pl.BlockSpec((1, dim), lambda i, *_: (0, 0))),
        ),
        compiler_params=params(),
        cost_estimate=COST,
        name="d_normed_parts",
    )(meta, own, one, one, two, x, w)


def grad_tokens_kernel(s_ref, r_ref, x_ref, gain_ref, d_hidden_ref, out_ref):
    d_normed = s_ref[...].astype(F32) + r_ref[...].astype(F32)
    x = x_ref[...].astype(F32)
    factor = lax.rsqrt(jnp.mean(x * x, axis=-1, keepdims=True) + EPS)
    unit = x * factor
    scaled = d_normed * gain_ref[...]
    inner = jnp.mean(scaled * unit, axis=-1, keepdims=True)
    out_ref[...] = (d_hidden_ref[...] + factor * (scaled - unit * inner)).astype(BF16)


def grad_tokens_own(chip_sum, far_sum, x, gain, d_hidden):
    return pl.pallas_call(
        grad_tokens_kernel,
        out_shape=jax.ShapeDtypeStruct(x.shape, BF16),
        in_specs=[whole()] * 5,
        out_specs=whole(),
        compiler_params=params(),
        name="grad_tokens_own",
    )(chip_sum, far_sum, x, gain, d_hidden)


def by_place(pieces):
    hi, lo = bit_of("head", 1), bit_of("head", 0)
    both = jnp.stack([jnp.stack([pieces[0], pieces[2]]), jnp.stack([pieces[1], pieces[3]])])
    both = jnp.where(hi, both[::-1], both)
    both = jnp.where(lo, both[:, ::-1], both)
    return both.reshape(-1, both.shape[-1])


def sum_halves(keep, send):
    return (keep.astype(F32) + swap(send, "head", 1).astype(F32)).astype(BF16)


def body(
    tokens,
    seg_ids,
    gain_attn,
    w_query,
    w_key,
    w_value,
    conv_kernels,
    w_out,
    gain_ffn,
    w_up,
    w_down,
    cotangent,
):
    rows, dim = tokens.shape
    part = conv_kernels.shape[2]
    quarter = rows // lax.axis_size("head")
    blk = lax.axis_index("blk")
    head = lax.axis_index("head")
    own_quarter = lax.dynamic_slice_in_dim(tokens, head * quarter, quarter)
    two = moved(own_quarter, "blk", 2)
    halo = moved(tokens[rows - HALO :], "blk", 1)
    w_mix = gather_all(arranged(w_query, w_key, w_value), "blk").reshape(dim, 3 * part)
    one = swap(jnp.where(bit_of("blk", 0), two, own_quarter), "blk", 1)
    pieces = quarters(two) + quarters(one)
    span = (REACH + 1) * rows
    padded_ids = jnp.pad(seg_ids, (REACH * rows, 0), constant_values=-1)
    window = lax.dynamic_slice_in_dim(padded_ids, blk * rows, span)
    starts = jnp.sum((window[None, :] <= window[0] + jnp.arange(8)[:, None]).astype(jnp.int32), axis=1)
    place = jnp.arange(REACH * rows, span, dtype=jnp.int32)
    first_row = jnp.max(jnp.where(starts[:, None] <= place, starts[:, None], 0), axis=0)
    low = first_row[::TILE] // TILE
    full = (first_row[TILE - 1 :: TILE] + TILE - 1) // TILE
    last = lax.axis_size("blk") - 1
    exists = jnp.stack([blk >= 1, blk >= 2, blk + 1 <= last, blk + 2 <= last])
    meta = jnp.concatenate([head[None], low, full, starts, exists]).astype(jnp.int32)
    first_row = first_row[None]
    taps = arranged(*conv_kernels)
    gain_one, gain_two = gain_attn[None], gain_ffn[None]

    raw_halo, raw, normed, q, kv, kvt = project_own(meta, tokens, halo, gain_one, w_mix, taps)
    acc_own, stat_own = attend_own(meta, q, kv, kvt, first_row)
    raw_e, normed_e, kv_e, kvt_e = project_earlier(meta, pieces, gain_one, w_mix, taps)
    att, out_t, lse = attend_earlier(meta, q, kv_e, kvt_e, first_row, acc_own, stat_own)

    units = w_up.shape[1]
    shard = w_up.shape[0]
    packed = jnp.concatenate([w_up, w_out.T.reshape(-1, units)])
    packed, _ = lax.optimization_barrier((packed, one))
    wide = gather_all(packed, "blk")
    full_up = wide[:, :shard].reshape(dim, units)
    out_full = wide[:, shard:].reshape(dim, part).T
    packed_down, _ = lax.optimization_barrier((w_down.T, pieces[5]))
    down_t = gather_all(packed_down, "blk", raw_e).reshape(dim, units)
    out_pieces = quarters(out_full)

    near = swap(att[2:], "head", 1)
    across = swap(jnp.stack([att[1], near[1]]), "head", 2)
    attended = (att[0], across[0], near[0], across[1])
    hidden, normed_two = after_attend(attended, out_pieces, own_quarter, gain_two)
    hi, lo = bit_of("head", 1), bit_of("head", 0)
    cot = cotangent.reshape(2, 2, quarter, dim)
    cot = jnp.where(hi, cot[::-1], cot)
    cot = jnp.where(lo, cot[:, ::-1], cot)
    cot = jnp.swapaxes(cot, 0, 1).reshape(rows, dim)
    ffn_in = jnp.concatenate(quarters(normed_two))
    act, d_up, *back = feed(ffn_in, cot, full_up, down_t)
    chip_back = sum_halves(*back)
    grad_up, grad_down_t = feed_grads(ffn_in, d_up, cot, act)
    both = jnp.stack([grad_up.reshape(-1, shard, units), grad_down_t.reshape(-1, shard, units)], axis=1)
    group = bit_groups("blk")[-1]
    both, both_send = chosen(both, "blk", group)
    both_near = swap(both_send, "blk", 1)
    far_back = swap(chip_back[quarter:], "head", 2)
    d_hidden, *d_outs, keep_out, send_out, gain_two_part = before_back(
        chip_back[:quarter], far_back, hidden, gain_two, cot[:quarter], out_pieces, attended
    )
    across = swap(jnp.stack([d_outs[1], d_outs[3]]), "head", 2)
    near = swap(jnp.stack([d_outs[2], across[1]]), "head", 1)
    d_out_t = jnp.stack([d_outs[0], across[0], near[0], near[1]])
    d_out_t, both_near = lax.optimization_barrier((d_out_t, both_near))

    dq_t, d_two, d_one, grad_next, sums_before, sums_halo = earlier_back(
        meta, q, d_out_t, out_t, lse, first_row, kv_e, kvt_e, kv, kvt, raw_e, raw_halo, taps
    )
    from_two = moved(d_two, "blk", -2)
    from_one = moved(d_one, "blk", -1)
    d_raw, sums_own = own_back(meta, q, d_out_t, out_t, lse, first_row, dq_t, kv, kvt, raw, taps, grad_next)

    both = (both.astype(F32) + both_near.astype(F32)).astype(BF16)
    both = sum_scatter(both, "blk", bit_groups("blk")[:-1])
    grad_up_shard, grad_down_shard = both[0], both[1].T
    act_late, _ = lax.optimization_barrier((act, dq_t))
    chip_ffn = sum_halves(*feed_out(act_late, down_t))
    far_ffn = swap(chip_ffn[quarter:], "head", 2)
    output = (hidden + (chip_ffn[:quarter].astype(F32) + far_ffn.astype(F32))).astype(BF16)
    output = by_place(quarters(output))
    chip_out = keep_out.astype(F32) + swap(send_out, "head", 1).astype(F32)
    far = swap(chip_out[1].astype(BF16), "head", 2)
    grad_out = (chip_out[0] + far.astype(F32)).astype(BF16).T

    grad_mix = mix_grads(normed_e, d_two, d_one, normed, d_raw, grad_out)
    mix_shard = sum_scatter(grad_mix.reshape(-1, shard, 4 * part), "blk", bit_groups("blk"))
    grad_query_shard, grad_key_shard, grad_value_shard = separated(mix_shard[:, : 3 * part])
    grad_out_shard = mix_shard[:, 3 * part :].T

    *back, gain_one_part = d_normed_parts(meta, d_raw, from_one, from_two, tokens, w_mix)
    chip_back = sum_halves(*back)
    far_back = swap(chip_back[quarter:], "head", 2)
    grad_tokens = grad_tokens_own(chip_back[:quarter], far_back, own_quarter, gain_one, d_hidden)
    grad_tokens = by_place(quarters(grad_tokens)).astype(F32)

    taps_part = jnp.concatenate([sums_own[:3, :KV] + sums_before[:3], sums_own[:3, KV:] + sums_halo[:3]], axis=1)
    taps_part = jnp.stack(separated(taps_part)).reshape(-1)
    gains = sum_everywhere(jnp.concatenate([gain_two_part, gain_one_part]), "head")
    small = sum_everywhere(jnp.concatenate([gains.reshape(-1), taps_part]), "blk")
    grad_gain_ffn, grad_gain_attn = small[:dim], small[dim : 2 * dim]
    grad_kernels = small[2 * dim :].reshape(3, 3, part)
    return (
        output,
        grad_tokens,
        grad_gain_attn,
        grad_query_shard,
        grad_key_shard,
        grad_value_shard,
        grad_kernels,
        grad_out_shard,
        grad_gain_ffn,
        grad_up_shard,
        grad_down_shard,
    )


def solution(mesh):
    return jax.shard_map(
        body,
        mesh=mesh,
        in_specs=(
            P("blk", None),
            P(),
            P(),
            P("blk", "head"),
            P("blk", "head"),
            P("blk", "head"),
            P(None, None, "head"),
            P("head", "blk"),
            P(),
            P("blk", "head"),
            P("head", "blk"),
            P("blk", None),
        ),
        out_specs=(
            P("blk", None),
            P("blk", None),
            P(),
            P("blk", "head"),
            P("blk", "head"),
            P("blk", "head"),
            P(None, None, "head"),
            P("head", "blk"),
            P(),
            P("blk", "head"),
            P("head", "blk"),
        ),
        check_vma=False,
    )
```

time: 714 us -> 389 us (0.54); the launches traced: 707 us -> 389 us
  blocking collectives: 167 us -> 0 us
  matrix products: 149 us -> 0 us
  Pallas kernels: 0 us -> 107 us
  waiting for transfers between devices: 207 us -> 113 us
  other arithmetic: 92.9 us -> 36.7 us
  starting transfers between devices: 60.1 us -> 95.2 us
  local copies, waits for them, and re-layouts: 13.3 us -> 35.6 us
  between operations: 17.3 us -> 1.9 us
    psum x3 -> x0, waiting for transfers between devices: 153 us -> none  [the longest x1 65.9 us: body(): lax.psum(jnp.dot(attended, full_out, preferred_element_type=jnp.float32),...]
    dot_general x48 -> x0, matrix products: 149 us -> none  [the longest x6 40.9 us: attend_back(): jnp.einsum('qhd,khd->hqk', d_out, value_list[slot], preferred_element_typ...]
    all_gather x4 -> x0, blocking collectives: 129 us -> none  [the longest x1 33.4 us: body(): lax.all_gather(w_out, 'blk', axis=1, tiled=True)]
    pallas_call x0 -> x14, Pallas kernels: none -> 107 us  [the longest x1 14.5 us: own_back(): pl.pallas_call(functools.partial(own_back_kernel, begin=REACH * rows // T...]
    ppermute x10 -> x60, waiting for transfers between devices: 14 us -> 113 us  [the longest x56 80.6 us: swap(): lax.ppermute(x, axis, [(i, i ^ mask) for i in range(lax.axis_size(axis))])]
    ppermute x10 -> x60, starting transfers between devices: 22.8 us -> 95.2 us  [the longest x56 85.9 us: swap(): lax.ppermute(x, axis, [(i, i ^ mask) for i in range(lax.axis_size(axis))])]
    psum x1 -> x0, blocking collectives: 37.7 us -> none  [body(): lax.psum((d_kernels, gain_attn_part, gain_ffn_part), 'blk')]
    all_to_all x4 -> x0, starting transfers between devices: 36.7 us -> none  [sum_at_owner(): lax.all_to_all(blocks, axis, split_axis=0, concat_axis=0, tiled=True)]
  transfers between devices with their start and end apart: 19 -> 60, of which waited for: 9 -> 21; matrix products, arithmetic and copies ran while one was open for 21% -> 15% of each run, Pallas kernels for 0% -> 25%
where the time goes in v1:
time: 389 us
  waiting for transfers between devices  113 us (29%)
  Pallas kernels  107 us (28%)
  starting transfers between devices  95.2 us (24%)
  other arithmetic  36.7 us (9%)
  local copies, waits for them, and re-layouts  35.6 us (9%)
    ppermute x56, starting transfers between devices, swap(): lax.ppermute(x, axis, [(i, i ^ mask) for i in range(lax.axis_size(axis))])  85.9 us
    ppermute x56, waiting for transfers between devices, swap(): lax.ppermute(x, axis, [(i, i ^ mask) for i in range(lax.axis_size(axis))])  80.6 us
    ppermute x4, waiting for transfers between devices, moved(): lax.ppermute(x, axis, [(i, i + distance) for i in range(size) if 0 <= i +...  32 us
    pallas_call x1, Pallas kernels, own_back(): pl.pallas_call(functools.partial(own_back_kernel, begin=REACH * rows // T...  14.5 us
    pallas_call x1, Pallas kernels, attend_own(): pl.pallas_call(functools.partial(attend_own_kernel, begin=REACH * tiles),...  13.1 us
    pallas_call x1, Pallas kernels, earlier_back(): pl.pallas_call(earlier_back_kernel, out_shape=(jax.ShapeDtypeStruct((part...  13 us
    pallas_call x1, Pallas kernels, project_earlier(): pl.pallas_call(project_earlier_kernel, out_shape=(jax.ShapeDtypeStruct((s...  9.49 us
    ppermute x4, starting transfers between devices, moved(): lax.ppermute(x, axis, [(i, i + distance) for i in range(size) if 0 <= i +...  9.3 us
  transfers between devices with their start and end apart: 60, of which 21 were waited for; matrix products, arithmetic and copies ran while one was open for 15% of the time, Pallas kernels for 25%

profile of v1, /device:TPU:0, one launch (start us, length us, event | category | flops | bytes accessed | tf_op | source)
XLA Modules:
  0.0 389.0 jit_solution(11274784648365939675)
XLA Ops:
  4.5 5.1 %collective-permute-start.3 = (bf16[1,96,576]{2,1,0:T(8,128)(2,1)S(1)}, bf16[1,96,576]{2,1,0:T(8,128)(2,1)S(1)}, u32[]{:S(2)}, u32[]{:S(2)}) collective-permute-start(bf16[1,96,576]{2,1,0:T(8,128)(2,1)S(1)} %bitcast.174), channel_id=1, source_target_pairs={{0,24},{4,28},{8,16},{12,20},{16,8},{20,12},{24,0},{28,4},{1,25},{... | collective-permute-start | bytes 331784 | tf_op jit(solution)/shard_map/ppermute | solution.py:35
  11.0 3.6 collective-permute-start
  15.6 3.2 collective-permute-start.5
  22.3 1.5 collective-permute-start.4
  23.8 2.5 collective-permute-done.5.refs_0_
  27.5 1.8 collective-permute-start.9
  31.6 1.6 collective-permute-start.6
  33.2 3.4 collective-permute-done.4
  36.7 6.0 %collective-permute-done.9.refs_4_ = bf16[256,768]{1,0:T(8,128)(2,1)S(1)} collective-permute-done((bf16[256,768]{1,0:T(8,128)(2,1)S(1)}, bf16[256,768]{1,0:T(8,128)(2,1)S(1)}, u32[]{:S(2)}, u32[]{:S(2)}) %collective-permute-start.9) | collective-permute-done | bytes 393248 | tf_op jit(solution)/shard_map/ppermute | solution.py:35
  42.6 2.4 collective-permute-start.17
  47.0 1.5 collective-permute-start.10
  49.7 7.6 %project_own.1 = (bf16[16,192]{1,0:T(8,128)(2,1)}, bf16[1024,576]{1,0:T(8,128)(2,1)}, bf16[1024,768]{1,0:T(8,128)(2,1)}, bf16[1024,192]{1,0:T(8,128)(2,1)}, bf16...) custom-call(s32[21]{0:T(128)} %concatenate.34.meta_ref, bf16[1024,768]{1,0:T(8,128)(2,1)} %x_ref.3, ...), custom_call_target="tpu_custom_call" | custom-call | flops 1 | bytes 1 | tf_op jit(solution)/shard_map/project_own/pallas_call | solution.py:196
  58.0 13.1 %attend_own.1 = (f32[192,1024]{1,0:T(8,128)}, f32[4,48,256]{2,1,0:T(8,128)}) custom-call(s32[21]{0:T(128)} %concatenate.34.meta_ref, bf16[1024,192]{1,0:T(8,128)(2,1)} %get-tuple-element.66.q_ref, bf16[1024,384]{1,0:T(8,128)(2,1)} %get-tuple-element.69.kv_ref.kv_own_ref, bf16[384,1024]{1,0:T(8,128)(2,1)} %get-tuple-element.70.kvt_ref.kvt_own_ref, ...), custom_call_target="tpu_custom_call" | custom-call | flops 1 | bytes 1 | tf_op jit(solution)/shard_map/attend_own/pallas_call | solution.py:416
  73.3 1.7 collective-permute-start.26
  75.1 1.4 collective-permute-start.27
  76.6 1.4 collective-permute-start.18
  78.8 9.5 %project_earlier.1 = (bf16[2048,384]{1,0:T(8,128)(2,1)}, bf16[2048,768]{1,0:T(8,128)(2,1)}, bf16[2048,384]{1,0:T(8,128)(2,1)}, bf16[384,2048]{1,0:T(8,128)(2,1)}) custom-call(s32[21]{0:T(128)} %concatenate.34.meta_ref, bf16[256,768]{1,0:T(8,128)(2,1)} %copy-done.6, bf16[256,768]{1,0:T(8,128)(2,1)} %copy-done.13, bf16[256,768]{1,0:T(8,128)(2,1)} %copy-done.15, ...), custom_call_target="tpu_custom_call" | custom-call | flops 1 | bytes 1 | tf_op jit(solution)/shard_map/project_earlier/pallas_call | solution.py:265
  88.3 5.8 %attend_earlier.1 = (bf16[4,192,256]{2,1,0:T(8,128)(2,1)}, f32[192,1024]{1,0:T(8,128)}, f32[4,8,256]{2,1,0:T(8,128)}) custom-call(s32[21]{0:T(128)} %concatenate.34.meta_ref, bf16[1024,192]{1,0:T(8,128)(2,1)} %get-tuple-element.66.q_ref, bf16[2048,384]{1,0:T(8,128)(2,1)} %get-tuple-element.67.kv_ref, bf16[384,2048]{1,0:T(8,128)(2,1)} %get-tuple-element.68.kvt_ref, ...), custom_call_target="tpu_custom_call" | custom-call | flops 1 | bytes 1 | tf_op jit(solution)/shard_map/attend_earlier/pallas_call | solution.py:444
  96.3 3.3 collective-permute-start.28
  103.2 1.5 collective-permute-start.14
  104.7 6.6 %collective-permute-done.19.w1 = bf16[192,768]{1,0:T(8,128)(2,1)} collective-permute-done((bf16[192,768]{1,0:T(8,128)(2,1)S(1)}, bf16[192,768]{1,0:T(8,128)(2,1)}, u32[]{:S(2)}, u32[]{:S(2)}) %collective-permute-start.19) | collective-permute-done | bytes 294944 | tf_op jit(solution)/shard_map/ppermute | solution.py:35
  111.3 2.4 reverse_select_fusion.5
  115.3 3.1 after_attend.1
  119.3 1.4 copy.74
  121.8 1.4 pad_maximum_fusion.3
  123.3 6.5 %collective-permute-done.22 = bf16[256,768]{1,0:T(8,128)(2,1)S(1)} collective-permute-done((bf16[256,768]{1,0:T(8,128)(2,1)}, bf16[256,768]{1,0:T(8,128)(2,1)S(1)}, u32[]{:S(2)}, u32[]{:S(2)}) %collective-permute-start.22) | collective-permute-done | bytes 393248 | tf_op jit(solution)/shard_map/ppermute | solution.py:35
  132.7 8.5 %feed.1 = (bf16[1024,768]{1,0:T(8,128)(2,1)}, bf16[1024,768]{1,0:T(8,128)(2,1)}, bf16[512,768]{1,0:T(8,128)(2,1)}, bf16[512,768]{1,0:T(8,128)(2,1)}) custom-call(bf16[1024,768]{1,0:T(8,128)(2,1)} %copy-done, bf16[1024,768]{1,0:T(8,128)(2,1)} %bitcast.139, bf16[768,768]{1,0:T(8,128)(2,1)} %bitcast.151, bf16[768,768]{1,0:T(8,128)(2,1)} %bitcast.145), custom_call_target="tpu_custom_call" | custom-call | flops 1 | bytes 1 | tf_op jit(solution)/shard_map/feed/pallas_call | solution.py:784
  141.4 2.3 collective-permute-done.29
  146.4 6.4 %feed_grads.1 = (bf16[768,768]{1,0:T(8,128)(2,1)}, bf16[768,768]{1,0:T(8,128)(2,1)}) custom-call(bf16[1024,768]{1,0:T(8,128)(2,1)} %copy-done, bf16[1024,768]{1,0:T(8,128)(2,1)} %get-tuple-element.92.d_up_ref, bf16[1024,768]{1,0:T(8,128)(2,1)} %bitcast.140, bf16[1024,768]{1,0:T(8,128)(2,1)} %get-tuple-element.100.act_ref), custom_call_target="tpu_custom_call" | custom-call | flops 1 | bytes 1 | tf_op jit(solution)/shard_map/feed_grads/pallas_call | solution.py:840
  152.8 1.8 fusion.2
  155.7 1.8 slice.228.cot_ref
  158.2 4.3 %before_back.1 = (f32[256,768]{1,0:T(8,128)}, bf16[192,256]{1,0:T(8,128)(2,1)}, bf16[192,256]{1,0:T(8,128)(2,1)}, bf16[192,256]{1,0:T(8,128)(2,1)}, bf16[192,256...) custom-call(bf16[256,768]{1,0:T(8,128)(2,1)} %get-tuple-element.184.s_ref, ...), custom_call_target="tpu_custom_call" | custom-call | flops 1 | bytes 1 | tf_op jit(solution)/shard_map/before_back/pallas_call | solution.py:902
  163.5 1.6 collective-permute-start.31
  165.1 5.2 %collective-permute-done.31 = bf16[2,192,256]{2,1,0:T(8,128)(2,1)S(1)} collective-permute-done((bf16[2,192,256]{2,1,0:T(8,128)(2,1)S(1)}, bf16[2,192,256]{2,1,0:T(8,128)(2,1)S(1)}, u32[]{:S(2)}, u32[]{:S(2)}) %collective-permute-start.31) | collective-permute-done | bytes 196640 | tf_op jit(solution)/shard_map/ppermute | solution.py:35
  170.3 1.6 pad_maximum_fusion.11
  173.7 1.7 pad_maximum_fusion.8.dt_ref
  175.4 8.4 %collective-permute-done.33 = bf16[4,2,96,768]{3,2,1,0:T(8,128)(2,1)} collective-permute-done((bf16[4,2,96,768]{3,2,1,0:T(8,128)(2,1)}, bf16[4,2,96,768]{3,2,1,0:T(8,128)(2,1)}, u32[]{:S(2)}, u32[]{:S(2)}) %collective-permute-start.33) | collective-permute-done | bytes 1179680 | tf_op jit(solution)/shard_map/ppermute | solution.py:35
  183.7 13.0 %earlier_back.1 = (f32[192,1024]{1,0:T(8,128)}, bf16[1024,384]{1,0:T(8,128)(2,1)}, bf16[1040,384]{1,0:T(8,128)(2,1)}, f32[256,384]{1,0:T(8,128)}, f32[8,384]{1,0:T(8,128)}, /*index=5*/f32[8,192]{1,0:T(8,128)}) custom-call(s32[21]{0:T(128)} %concatenate.34.meta_ref, bf16[1024,192]{1,0:T(8,128)(2,1)} %get-tuple-element.66.q_ref, ...), custom_call_target="tpu_custom_call" | custom-call | flops 1 | bytes 1 | tf_op jit(solution)/shard_map/earlier_back/pallas_call | solution.py:643
  196.7 14.5 %own_back.1 = (bf16[1024,576]{1,0:T(8,128)(2,1)}, f32[8,576]{1,0:T(8,128)}) custom-call(s32[21]{0:T(128)} %concatenate.34.meta_ref, bf16[1024,192]{1,0:T(8,128)(2,1)} %get-tuple-element.66.q_ref, bf16[4,192,256]{2,1,0:T(8,128)(2,1)} %pad_maximum_fusion.8.dt_ref, f32[192,1024]{1,0:T(8,128)} %get-tuple-element.96.ot_ref, ...), custom_call_target="tpu_custom_call" | custom-call | flops 1 | bytes 1 | tf_op jit(solution)/shard_map/own_back/pallas_call | solution.py:715
  212.1 4.5 %feed_out.1 = (bf16[512,768]{1,0:T(8,128)(2,1)}, bf16[512,768]{1,0:T(8,128)(2,1)}) custom-call(bf16[1024,768]{1,0:T(8,128)(2,1)} %get-tuple-element.100.act_ref, bf16[768,768]{1,0:T(8,128)(2,1)} %bitcast.146), custom_call_target="tpu_custom_call" | custom-call | flops 1 | bytes 1 | tf_op jit(solution)/shard_map/feed_out/pallas_call | solution.py:817
  219.9 2.6 fusion
  223.2 2.1 constant_dynamic-slice_fusion.2
  225.3 39.0 %collective-permute-start.59 = (bf16[1,2,96,768]{3,2,1,0:T(8,128)(2,1)}, bf16[1,2,96,768]{3,2,1,0:T(8,128)(2,1)}, u32[]{:S(2)}, u32[]{:S(2)}) collective-permute-start(bf16[1,2,96,768]{3,2,1,0:T(8,128)(2,1)} %get-tuple-element.179), channel_id=1, source_target_pairs={{0,24},{4,28},{8,16},{12,20},{16,8},{20,12},{24,0},{28,4},{1,25},{... | collective-permute-start | bytes 884744 | tf_op jit(solution)/shard_map/ppermute | solution.py:35
  266.4 29.5 %collective-permute-done.40.two_ref = bf16[1024,384]{1,0:T(8,128)(2,1)} collective-permute-done((bf16[1024,384]{1,0:T(8,128)(2,1)}, bf16[1024,384]{1,0:T(8,128)(2,1)}, u32[]{:S(2)}, u32[]{:S(2)}) %collective-permute-start.40) | collective-permute-done | bytes 786464 | tf_op jit(solution)/shard_map/ppermute | solution.py:40
  295.9 1.6 collective-permute-start.52
  297.5 6.7 %d_normed_parts.1 = (bf16[512,768]{1,0:T(8,128)(2,1)}, bf16[512,768]{1,0:T(8,128)(2,1)}, f32[1,768]{1,0:T(1,128)}) custom-call(s32[21]{0:T(128)} %concatenate.34.meta_ref, bf16[1024,576]{1,0:T(8,128)(2,1)} %get-tuple-element.105.own_ref.d_raw_ref, bf16[1040,384]{1,0:T(8,128)(2,1)} %copy-done.3, bf16[1040,384]{1,0:T(8,128)(2,1)} %copy-done.3, ...), custom_call_target="tpu_custom_call" | custom-call | flops 1 | bytes 1 | tf_op jit(solution)/shard_map/d_normed_parts/pallas_call | solution.py:959
  305.2 8.4 %collective-permute-done.58 = bf16[1,2,96,768]{3,2,1,0:T(8,128)(2,1)} collective-permute-done((bf16[1,2,96,768]{3,2,1,0:T(8,128)(2,1)}, bf16[1,2,96,768]{3,2,1,0:T(8,128)(2,1)}, u32[]{:S(2)}, u32[]{:S(2)}) %collective-permute-start.58) | collective-permute-done | bytes 294944 | tf_op jit(solution)/shard_map/ppermute | solution.py:35
  313.7 1.4 convert_add_fusion.3
  315.1 1.6 collective-permute-start.47
  317.5 7.2 %mix_grads.1 = bf16[768,768]{1,0:T(8,128)(2,1)} custom-call(bf16[2048,768]{1,0:T(8,128)(2,1)} %get-tuple-element.116.e_ref, bf16[1024,384]{1,0:T(8,128)(2,1)} %get-tuple-element.107.two_ref, bf16[1040,384]{1,0:T(8,128)(2,1)} %get-tuple-element.106.one_ref, bf16[1024,768]{1,0:T(8,128)(2,1)} %get-tuple-element.117.o_ref, ...), custom_call_target="tpu_custom_call" | custom-call | flops 1 | bytes 1 | tf_op jit(solution)/shard_map/mix_grads/pallas_call | solution.py:867
  324.9 2.0 dynamic-slice_bitcast_fusion
  326.8 1.9 collective-permute-start.53
  329.7 2.9 collective-permute-done.49
  333.5 1.4 add_convert_fusion.1
  335.6 1.7 collective-permute-done.50
  338.5 2.5 collective-permute-done.53
  343.3 3.5 collective-permute-start.54
  347.5 3.3 collective-permute-done.56
  350.8 4.5 %collective-permute-done.55 = bf16[1,96,768]{2,1,0:T(8,128)(2,1)S(1)} collective-permute-done((bf16[1,96,768]{2,1,0:T(8,128)(2,1)S(1)}, bf16[1,96,768]{2,1,0:T(8,128)(2,1)S(1)}, u32[]{:S(2)}, u32[]{:S(2)}) %collective-permute-start.55) | collective-permute-done | bytes 147488 | tf_op jit(solution)/shard_map/ppermute | solution.py:35
  361.9 8.0 %collective-permute-done.42.r_ref = bf16[256,768]{1,0:T(8,128)(2,1)S(1)} collective-permute-done((bf16[256,768]{1,0:T(8,128)(2,1)S(1)}, bf16[256,768]{1,0:T(8,128)(2,1)S(1)}, u32[]{:S(2)}, u32[]{:S(2)}) %collective-permute-start.42) | collective-permute-done | bytes 393248 | tf_op jit(solution)/shard_map/ppermute | solution.py:35
  370.6 2.7 grad_tokens_own.1
  375.1 9.1 %collective-permute-done.44 = bf16[256,768]{1,0:T(8,128)(2,1)S(1)} collective-permute-done((bf16[256,768]{1,0:T(8,128)(2,1)}, bf16[256,768]{1,0:T(8,128)(2,1)S(1)}, u32[]{:S(2)}, u32[]{:S(2)}) %collective-permute-start.44) | collective-permute-done | bytes 393248 | tf_op jit(solution)/shard_map/ppermute | solution.py:35
  384.2 1.4 reverse_select_fusion.2
  386.8 2.0 bitcast_convert_fusion
  (270 shorter events, 65.6 us)
Async XLA Ops:
  4.5 17.5 %collective-permute-start.3 = (bf16[1,96,576]{2,1,0:T(8,128)(2,1)S(1)}, bf16[1,96,576]{2,1,0:T(8,128)(2,1)S(1)}, u32[]{:S(2)}, u32[]{:S(2)}) collective-permute-start(bf16[1,96,576]{2,1,0:T(8,128)(2,1)S(1)} %bitcast.174), channel_id=1, source_target_pairs={{0,24},{4,28},{8,16},{12,20},{16,8},{20,12},{24,0},{28,4},{1,25},{... | collective-permute-start | bytes 331784 | tf_op jit(solution)/shard_map/ppermute | solution.py:35
  9.6 12.4 %collective-permute-start.2 = (bf16[1,96,576]{2,1,0:T(8,128)(2,1)S(1)}, bf16[1,96,576]{2,1,0:T(8,128)(2,1)S(1)}, u32[]{:S(2)}, u32[]{:S(2)}) collective-permute-start(bf16[1,96,576]{2,1,0:T(8,128)(2,1)S(1)} %bitcast.175), channel_id=1, source_target_pairs={{0,16},{4,20},{8,24},{12,28},{16,0},{20,4},{24,8},{28,12},{1,17},{... | collective-permute-start | bytes 331784 | tf_op jit(solution)/shard_map/ppermute | solution.py:35
  9.6 12.4 %collective-permute-start.1 = (bf16[1,96,576]{2,1,0:T(8,128)(2,1)S(1)}, bf16[1,96,576]{2,1,0:T(8,128)(2,1)S(1)}, u32[]{:S(2)}, u32[]{:S(2)}) collective-permute-start(bf16[1,96,576]{2,1,0:T(8,128)(2,1)S(1)} %bitcast.176), channel_id=1, source_target_pairs={{0,8},{4,12},{8,0},{12,4},{16,24},{20,28},{24,16},{28,20},{1,9},{5... | collective-permute-start | bytes 331784 | tf_op jit(solution)/shard_map/ppermute | solution.py:35
  11.0 36.0 %collective-permute-start = (bf16[16,768]{1,0:T(8,128)(2,1)S(1)}, bf16[16,768]{1,0:T(8,128)(2,1)S(1)}, u32[]{:S(2)}, u32[]{:S(2)}) collective-permute-start(bf16[16,768]{1,0:T(8,128)(2,1)S(1)} %slice.168), channel_id=1, source_target_pairs={{0,4},{4,8},{8,12},{12,16},{16,20},{20,24},{24,28},{1,5},{5,9},{9,... | collective-permute-start | bytes 73736 | tf_op jit(solution)/shard_map/ppermute | solution.py:40
  15.6 10.7 %collective-permute-start.5 = (bf16[256,768]{1,0:T(8,128)(2,1)S(1)}, bf16[256,768]{1,0:T(8,128)(2,1)S(1)}, u32[]{:S(2)}, u32[]{:S(2)}) collective-permute-start(bf16[256,768]{1,0:T(8,128)(2,1)S(1)} %constant_dynamic-slice_fusion.6.x_ref), channel_id=1, source_target_pairs={{0,8},{4,12},{8,16},{12,20},{16,24},{20,28},{1,9},{5,13},{9,17},{1... | collective-permute-start | bytes 1179656 | tf_op jit(solution)/shard_map/ppermute | solution.py:40
  22.3 14.2 %collective-permute-start.4 = (bf16[4,96,576]{2,1,0:T(8,128)(2,1)S(1)}, bf16[4,96,576]{2,1,0:T(8,128)(2,1)S(1)}, u32[]{:S(2)}, u32[]{:S(2)}) collective-permute-start(bf16[4,96,576]{2,1,0:T(8,128)(2,1)S(1)} %bitcast.161), channel_id=1, source_target_pairs={{0,4},{4,0},{8,12},{12,8},{16,20},{20,16},{24,28},{28,24},{1,5},{5... | collective-permute-start | bytes 1327112 | tf_op jit(solution)/shard_map/ppermute | solution.py:35
  26.3 31.1 %copy-start.6 = (bf16[256,768]{1,0:T(8,128)(2,1)}, bf16[256,768]{1,0:T(8,128)(2,1)S(1)}, u32[]{:S(2)}) copy-start(bf16[256,768]{1,0:T(8,128)(2,1)S(1)} %collective-permute-done.5.refs_0_) | copy-start | bytes 1179652
  27.5 15.1 %collective-permute-start.9 = (bf16[256,768]{1,0:T(8,128)(2,1)S(1)}, bf16[256,768]{1,0:T(8,128)(2,1)S(1)}, u32[]{:S(2)}, u32[]{:S(2)}) collective-permute-start(bf16[256,768]{1,0:T(8,128)(2,1)S(1)} %broadcast_select_fusion), channel_id=1, source_target_pairs={{0,4},{4,0},{8,12},{12,8},{16,20},{20,16},{24,28},{28,24},{1,5},{5... | collective-permute-start | bytes 1179656 | tf_op jit(solution)/shard_map/ppermute | solution.py:35
  31.6 25.7 %collective-permute-start.6 = (bf16[256,768]{1,0:T(8,128)(2,1)S(1)}, bf16[256,768]{1,0:T(8,128)(2,1)S(1)}, u32[]{:S(2)}, u32[]{:S(2)}) collective-permute-start(bf16[256,768]{1,0:T(8,128)(2,1)S(1)} %collective-permute-done.5.refs_0_), channel_id=1, source_target_pairs={{0,2},{1,3},{2,0},{3,1},{4,6},{5,7},{6,4},{7,5},{8,10},{9,11},{10,... | collective-permute-start | bytes 1179656 | tf_op jit(solution)/shard_map/ppermute | solution.py:35
  42.6 28.5 %copy-start.12 = (bf16[256,768]{1,0:T(8,128)(2,1)}, bf16[256,768]{1,0:T(8,128)(2,1)S(1)}, u32[]{:S(2)}) copy-start(bf16[256,768]{1,0:T(8,128)(2,1)S(1)} %collective-permute-done.9.refs_4_) | copy-start | bytes 1179652
  42.6 14.8 %collective-permute-start.17 = (bf16[1,120,768]{2,1,0:T(8,128)(2,1)S(1)}, bf16[1,120,768]{2,1,0:T(8,128)(2,1)S(1)}, u32[]{:S(2)}, u32[]{:S(2)}) collective-permute-start(bf16[1,120,768]{2,1,0:T(8,128)(2,1)S(1)} %bitcast.170), channel_id=1, source_target_pairs={{0,24},{4,28},{8,16},{12,20},{16,8},{20,12},{24,0},{28,4},{1,25},{... | collective-permute-start | bytes 552968 | tf_op jit(solution)/shard_map/ppermute | solution.py:35
  45.1 26.0 %collective-permute-start.16 = (bf16[1,120,768]{2,1,0:T(8,128)(2,1)S(1)}, bf16[1,120,768]{2,1,0:T(8,128)(2,1)S(1)}, u32[]{:S(2)}, u32[]{:S(2)}) collective-permute-start(bf16[1,120,768]{2,1,0:T(8,128)(2,1)S(1)} %bitcast.171), channel_id=1, source_target_pairs={{0,16},{4,20},{8,24},{12,28},{16,0},{20,4},{24,8},{28,12},{1,17},{... | collective-permute-start | bytes 552968 | tf_op jit(solution)/shard_map/ppermute | solution.py:35
  46.3 25.0 %collective-permute-start.15 = (bf16[1,120,768]{2,1,0:T(8,128)(2,1)S(1)}, bf16[1,120,768]{2,1,0:T(8,128)(2,1)S(1)}, u32[]{:S(2)}, u32[]{:S(2)}) collective-permute-start(bf16[1,120,768]{2,1,0:T(8,128)(2,1)S(1)} %bitcast.172), channel_id=1, source_target_pairs={{0,8},{4,12},{8,0},{12,4},{16,24},{20,28},{24,16},{28,20},{1,9},{5... | collective-permute-start | bytes 552968 | tf_op jit(solution)/shard_map/ppermute | solution.py:35
  47.0 24.3 %collective-permute-start.10 = (bf16[256,768]{1,0:T(8,128)(2,1)S(1)}, bf16[256,768]{1,0:T(8,128)(2,1)S(1)}, u32[]{:S(2)}, u32[]{:S(2)}) collective-permute-start(bf16[256,768]{1,0:T(8,128)(2,1)S(1)} %collective-permute-done.9.refs_4_), channel_id=1, source_target_pairs={{0,2},{1,3},{2,0},{3,1},{4,6},{5,7},{6,4},{7,5},{8,10},{9,11},{10,... | collective-permute-start | bytes 1179656 | tf_op jit(solution)/shard_map/ppermute | solution.py:35
  57.4 14.0 %copy-start.13 = (bf16[256,768]{1,0:T(8,128)(2,1)}, bf16[256,768]{1,0:T(8,128)(2,1)S(1)}, u32[]{:S(2)}) copy-start(bf16[256,768]{1,0:T(8,128)(2,1)S(1)} %collective-permute-done.6.refs_1_) | copy-start | bytes 1179652
  57.4 16.0 %collective-permute-start.7 = (bf16[256,768]{1,0:T(8,128)(2,1)S(1)}, bf16[256,768]{1,0:T(8,128)(2,1)S(1)}, u32[]{:S(2)}, u32[]{:S(2)}) collective-permute-start(bf16[256,768]{1,0:T(8,128)(2,1)S(1)} %collective-permute-done.5.refs_0_), channel_id=1, source_target_pairs={{0,1},{1,0},{2,3},{3,2},{4,5},{5,4},{6,7},{7,6},{8,9},{9,8},{10,11... | collective-permute-start | bytes 1179656 | tf_op jit(solution)/shard_map/ppermute | solution.py:35
  57.5 17.6 %collective-permute-start.8 = (bf16[256,768]{1,0:T(8,128)(2,1)S(1)}, bf16[256,768]{1,0:T(8,128)(2,1)S(1)}, u32[]{:S(2)}, u32[]{:S(2)}) collective-permute-start(bf16[256,768]{1,0:T(8,128)(2,1)S(1)} %collective-permute-done.6.refs_1_), channel_id=1, source_target_pairs={{0,1},{1,0},{2,3},{3,2},{4,5},{5,4},{6,7},{7,6},{8,9},{9,8},{10,11... | collective-permute-start | bytes 1179656 | tf_op jit(solution)/shard_map/ppermute | solution.py:35
  71.1 5.5 %collective-permute-start.11 = (bf16[256,768]{1,0:T(8,128)(2,1)S(1)}, bf16[256,768]{1,0:T(8,128)(2,1)S(1)}, u32[]{:S(2)}, u32[]{:S(2)}) collective-permute-start(bf16[256,768]{1,0:T(8,128)(2,1)S(1)} %collective-permute-done.9.refs_4_), channel_id=1, source_target_pairs={{0,1},{1,0},{2,3},{3,2},{4,5},{5,4},{6,7},{7,6},{8,9},{9,8},{10,11... | collective-permute-start | bytes 1179656 | tf_op jit(solution)/shard_map/ppermute | solution.py:35
  71.4 6.7 %collective-permute-start.12 = (bf16[256,768]{1,0:T(8,128)(2,1)S(1)}, bf16[256,768]{1,0:T(8,128)(2,1)S(1)}, u32[]{:S(2)}, u32[]{:S(2)}) collective-permute-start(bf16[256,768]{1,0:T(8,128)(2,1)S(1)} %collective-permute-done.10.refs_5_), channel_id=1, source_target_pairs={{0,1},{1,0},{2,3},{3,2},{4,5},{5,4},{6,7},{7,6},{8,9},{9,8},{10,11... | collective-permute-start | bytes 1179656 | tf_op jit(solution)/shard_map/ppermute | solution.py:35
  72.0 23.1 %collective-permute-start.25 = (bf16[1,96,768]{2,1,0:T(8,128)(2,1)S(1)}, bf16[1,96,768]{2,1,0:T(8,128)(2,1)S(1)}, u32[]{:S(2)}, u32[]{:S(2)}) collective-permute-start(bf16[1,96,768]{2,1,0:T(8,128)(2,1)S(1)} %bitcast.188), channel_id=1, source_target_pairs={{0,8},{4,12},{8,0},{12,4},{16,24},{20,28},{24,16},{28,20},{1,9},{5... | collective-permute-start | bytes 442376 | tf_op jit(solution)/shard_map/ppermute | solution.py:35
  73.3 21.8 %collective-permute-start.26 = (bf16[1,96,768]{2,1,0:T(8,128)(2,1)S(1)}, bf16[1,96,768]{2,1,0:T(8,128)(2,1)S(1)}, u32[]{:S(2)}, u32[]{:S(2)}) collective-permute-start(bf16[1,96,768]{2,1,0:T(8,128)(2,1)S(1)} %bitcast.189), channel_id=1, source_target_pairs={{0,16},{4,20},{8,24},{12,28},{16,0},{20,4},{24,8},{28,12},{1,17},{... | collective-permute-start | bytes 442376 | tf_op jit(solution)/shard_map/ppermute | solution.py:35
  75.1 20.1 %collective-permute-start.27 = (bf16[1,96,768]{2,1,0:T(8,128)(2,1)S(1)}, bf16[1,96,768]{2,1,0:T(8,128)(2,1)S(1)}, u32[]{:S(2)}, u32[]{:S(2)}) collective-permute-start(bf16[1,96,768]{2,1,0:T(8,128)(2,1)S(1)} %bitcast.190), channel_id=1, source_target_pairs={{0,24},{4,28},{8,16},{12,20},{16,8},{20,12},{24,0},{28,4},{1,25},{... | collective-permute-start | bytes 442376 | tf_op jit(solution)/shard_map/ppermute | solution.py:35
  76.6 23.6 %collective-permute-start.18 = (bf16[4,120,768]{2,1,0:T(8,128)(2,1)S(1)}, bf16[4,120,768]{2,1,0:T(8,128)(2,1)S(1)}, u32[]{:S(2)}, u32[]{:S(2)}) collective-permute-start(bf16[4,120,768]{2,1,0:T(8,128)(2,1)S(1)} %bitcast.152), channel_id=1, source_target_pairs={{0,4},{4,0},{8,12},{12,8},{16,20},{20,16},{24,28},{28,24},{1,5},{5... | collective-permute-start | bytes 2211848 | tf_op jit(solution)/shard_map/ppermute | solution.py:35
  95.0 6.8 %collective-permute-start.13 = (bf16[2,192,256]{2,1,0:T(8,128)(2,1)S(1)}, bf16[2,192,256]{2,1,0:T(8,128)(2,1)S(1)}, u32[]{:S(2)}, u32[]{:S(2)}) collective-permute-start(bf16[2,192,256]{2,1,0:T(8,128)(2,1)S(1)} %slice.179), channel_id=1, source_target_pairs={{0,1},{1,0},{2,3},{3,2},{4,5},{5,4},{6,7},{7,6},{8,9},{9,8},{10,11... | collective-permute-start | bytes 589832 | tf_op jit(solution)/shard_map/ppermute | solution.py:35
  96.3 25.5 %collective-permute-start.28 = (bf16[4,96,768]{2,1,0:T(8,128)(2,1)}, bf16[4,96,768]{2,1,0:T(8,128)(2,1)}, u32[]{:S(2)}, u32[]{:S(2)}) collective-permute-start(bf16[4,96,768]{2,1,0:T(8,128)(2,1)} %bitcast.52), channel_id=1, source_target_pairs={{0,4},{4,0},{8,12},{12,8},{16,20},{20,16},{24,28},{28,24},{1,5},{5... | collective-permute-start | bytes 1769480 | tf_op jit(solution)/shard_map/ppermute | solution.py:35
  101.2 10.0 %collective-permute-start.19 = (bf16[192,768]{1,0:T(8,128)(2,1)S(1)}, bf16[192,768]{1,0:T(8,128)(2,1)}, u32[]{:S(2)}, u32[]{:S(2)}) collective-permute-start(bf16[192,768]{1,0:T(8,128)(2,1)S(1)} %bitcast.155), channel_id=1, source_target_pairs={{0,2},{1,3},{2,0},{3,1},{4,6},{5,7},{6,4},{7,5},{8,10},{9,11},{10,... | collective-permute-start | bytes 884744 | tf_op jit(solution)/shard_map/ppermute | solution.py:35
  101.8 13.5 %collective-permute-start.20 = (bf16[192,768]{1,0:T(8,128)(2,1)S(1)}, bf16[192,768]{1,0:T(8,128)(2,1)}, u32[]{:S(2)}, u32[]{:S(2)}) collective-permute-start(bf16[192,768]{1,0:T(8,128)(2,1)S(1)} %bitcast.156), channel_id=1, source_target_pairs={{0,1},{1,0},{2,3},{3,2},{4,5},{5,4},{6,7},{7,6},{8,9},{9,8},{10,11... | collective-permute-start | bytes 884744 | tf_op jit(solution)/shard_map/ppermute | solution.py:35
  103.2 11.4 %collective-permute-start.14 = (bf16[2,192,256]{2,1,0:T(8,128)(2,1)}, bf16[2,192,256]{2,1,0:T(8,128)(2,1)S(1)}, u32[]{:S(2)}, u32[]{:S(2)}) collective-permute-start(bf16[2,192,256]{2,1,0:T(8,128)(2,1)} %pad_maximum_fusion.9), channel_id=1, source_target_pairs={{0,2},{1,3},{2,0},{3,1},{4,6},{5,7},{6,4},{7,5},{8,10},{9,11},{10,... | collective-permute-start | bytes 589832 | tf_op jit(solution)/shard_map/ppermute | solution.py:35
  111.3 4.1 %collective-permute-start.21 = (bf16[192,768]{1,0:T(8,128)(2,1)}, bf16[192,768]{1,0:T(8,128)(2,1)}, u32[]{:S(2)}, u32[]{:S(2)}) collective-permute-start(bf16[192,768]{1,0:T(8,128)(2,1)} %collective-permute-done.19.w1), channel_id=1, source_target_pairs={{0,1},{1,0},{2,3},{3,2},{4,5},{5,4},{6,7},{7,6},{8,9},{9,8},{10,11... | collective-permute-start | bytes 884744 | tf_op jit(solution)/shard_map/ppermute | solution.py:35
  118.5 11.4 %collective-permute-start.22 = (bf16[256,768]{1,0:T(8,128)(2,1)}, bf16[256,768]{1,0:T(8,128)(2,1)S(1)}, u32[]{:S(2)}, u32[]{:S(2)}) collective-permute-start(bf16[256,768]{1,0:T(8,128)(2,1)} %get-tuple-element.76), channel_id=1, source_target_pairs={{0,2},{1,3},{2,0},{3,1},{4,6},{5,7},{6,4},{7,5},{8,10},{9,11},{10,... | collective-permute-start | bytes 1179656 | tf_op jit(solution)/shard_map/ppermute | solution.py:35
  123.2 7.9 %collective-permute-start.23 = (bf16[256,768]{1,0:T(8,128)(2,1)S(1)}, bf16[256,768]{1,0:T(8,128)(2,1)S(1)}, u32[]{:S(2)}, u32[]{:S(2)}) collective-permute-start(bf16[256,768]{1,0:T(8,128)(2,1)S(1)} %copy-done.22), channel_id=1, source_target_pairs={{0,1},{1,0},{2,3},{3,2},{4,5},{5,4},{6,7},{7,6},{8,9},{9,8},{10,11... | collective-permute-start | bytes 1179656 | tf_op jit(solution)/shard_map/ppermute | solution.py:35
  129.8 1.7 collective-permute-start.24
  141.2 2.6 collective-permute-start.29
  145.9 11.6 %collective-permute-start.30 = (bf16[256,768]{1,0:T(8,128)(2,1)S(1)}, bf16[256,768]{1,0:T(8,128)(2,1)S(1)}, u32[]{:S(2)}, u32[]{:S(2)}) collective-permute-start(bf16[256,768]{1,0:T(8,128)(2,1)S(1)} %get-tuple-element.183), channel_id=1, source_target_pairs={{0,2},{1,3},{2,0},{3,1},{4,6},{5,7},{6,4},{7,5},{8,10},{9,11},{10,... | collective-permute-start | bytes 1179656 | tf_op jit(solution)/shard_map/ppermute | solution.py:35
  155.7 28.1 %collective-permute-start.33 = (bf16[4,2,96,768]{3,2,1,0:T(8,128)(2,1)}, bf16[4,2,96,768]{3,2,1,0:T(8,128)(2,1)}, u32[]{:S(2)}, u32[]{:S(2)}) collective-permute-start(bf16[4,2,96,768]{3,2,1,0:T(8,128)(2,1)} %bitcast.138), channel_id=1, source_target_pairs={{0,4},{4,0},{8,12},{12,8},{16,20},{20,16},{24,28},{28,24},{1,5},{5... | collective-permute-start | bytes 3538952 | tf_op jit(solution)/shard_map/ppermute | solution.py:35
  163.5 6.8 %collective-permute-start.31 = (bf16[2,192,256]{2,1,0:T(8,128)(2,1)S(1)}, bf16[2,192,256]{2,1,0:T(8,128)(2,1)S(1)}, u32[]{:S(2)}, u32[]{:S(2)}) collective-permute-start(bf16[2,192,256]{2,1,0:T(8,128)(2,1)S(1)} %pad_maximum_fusion.10), channel_id=1, source_target_pairs={{0,2},{1,3},{2,0},{3,1},{4,6},{5,7},{6,4},{7,5},{8,10},{9,11},{10,... | collective-permute-start | bytes 589832 | tf_op jit(solution)/shard_map/ppermute | solution.py:35
  171.9 1.8 collective-permute-start.32
  172.2 92.1 %collective-permute-start.51 = (bf16[2,192,768]{2,1,0:T(8,128)(2,1)}, bf16[2,192,768]{2,1,0:T(8,128)(2,1)}, u32[]{:S(2)}, u32[]{:S(2)}) collective-permute-start(bf16[2,192,768]{2,1,0:T(8,128)(2,1)} %get-tuple-element.119), channel_id=1, source_target_pairs={{0,1},{1,0},{2,3},{3,2},{4,5},{5,4},{6,7},{7,6},{8,9},{9,8},{10,11... | collective-permute-start | bytes 1769480 | tf_op jit(solution)/shard_map/ppermute | solution.py:35
  196.7 14.6 %copy-start.35 = (f32[8,384]{1,0:T(8,128)S(1)}, f32[8,384]{1,0:T(8,128)}, u32[]{:S(2)}) copy-start(f32[8,384]{1,0:T(8,128)} %get-tuple-element.115) | copy-start | bytes 36868
  216.6 79.3 %collective-permute-start.39 = (bf16[1040,384]{1,0:T(8,128)(2,1)}, bf16[1040,384]{1,0:T(8,128)(2,1)S(1)}, u32[]{:S(2)}, u32[]{:S(2)}) collective-permute-start(bf16[1040,384]{1,0:T(8,128)(2,1)} %get-tuple-element.106.one_ref), channel_id=1, source_target_pairs={{4,0},{8,4},{12,8},{16,12},{20,16},{24,20},{28,24},{5,1},{9,5},{13... | collective-permute-start | bytes 2396168 | tf_op jit(solution)/shard_map/ppermute | solution.py:40
  217.9 78.0 %collective-permute-start.40 = (bf16[1024,384]{1,0:T(8,128)(2,1)}, bf16[1024,384]{1,0:T(8,128)(2,1)}, u32[]{:S(2)}, u32[]{:S(2)}) collective-permute-start(bf16[1024,384]{1,0:T(8,128)(2,1)} %get-tuple-element.107.two_ref), channel_id=1, source_target_pairs={{8,0},{12,4},{16,8},{20,12},{24,16},{28,20},{9,1},{13,5},{17,9},{2... | collective-permute-start | bytes 2359304 | tf_op jit(solution)/shard_map/ppermute | solution.py:40
  225.3 79.7 %collective-permute-start.59 = (bf16[1,2,96,768]{3,2,1,0:T(8,128)(2,1)}, bf16[1,2,96,768]{3,2,1,0:T(8,128)(2,1)}, u32[]{:S(2)}, u32[]{:S(2)}) collective-permute-start(bf16[1,2,96,768]{3,2,1,0:T(8,128)(2,1)} %get-tuple-element.179), channel_id=1, source_target_pairs={{0,24},{4,28},{8,16},{12,20},{16,8},{20,12},{24,0},{28,4},{1,25},{... | collective-permute-start | bytes 884744 | tf_op jit(solution)/shard_map/ppermute | solution.py:35
  264.3 49.4 %collective-permute-start.58 = (bf16[1,2,96,768]{3,2,1,0:T(8,128)(2,1)}, bf16[1,2,96,768]{3,2,1,0:T(8,128)(2,1)}, u32[]{:S(2)}, u32[]{:S(2)}) collective-permute-start(bf16[1,2,96,768]{3,2,1,0:T(8,128)(2,1)} %get-tuple-element.180), channel_id=1, source_target_pairs={{0,16},{4,20},{8,24},{12,28},{16,0},{20,4},{24,8},{28,12},{1,17},{... | collective-permute-start | bytes 884744 | tf_op jit(solution)/shard_map/ppermute | solution.py:35
  264.3 49.4 %collective-permute-start.57 = (bf16[1,2,96,768]{3,2,1,0:T(8,128)(2,1)}, bf16[1,2,96,768]{3,2,1,0:T(8,128)(2,1)}, u32[]{:S(2)}, u32[]{:S(2)}) collective-permute-start(bf16[1,2,96,768]{3,2,1,0:T(8,128)(2,1)} %get-tuple-element.178), channel_id=1, source_target_pairs={{0,8},{4,12},{8,0},{12,4},{16,24},{20,28},{24,16},{28,20},{1,9},{5... | collective-permute-start | bytes 884744 | tf_op jit(solution)/shard_map/ppermute | solution.py:35
  295.9 36.7 %collective-permute-start.34 = (bf16[512,768]{1,0:T(8,128)(2,1)}, bf16[512,768]{1,0:T(8,128)(2,1)S(1)}, u32[]{:S(2)}, u32[]{:S(2)}) collective-permute-start(bf16[512,768]{1,0:T(8,128)(2,1)} %get-tuple-element.102), channel_id=1, source_target_pairs={{0,1},{1,0},{2,3},{3,2},{4,5},{5,4},{6,7},{7,6},{8,9},{9,8},{10,11... | collective-permute-start | bytes 2359304 | tf_op jit(solution)/shard_map/ppermute | solution.py:35
  295.9 20.7 %collective-permute-start.52 = (bf16[192,768]{0,1:T(8,128)(2,1)S(1)}, bf16[192,768]{0,1:T(8,128)(2,1)S(1)}, u32[]{:S(2)}, u32[]{:S(2)}) collective-permute-start(bf16[192,768]{0,1:T(8,128)(2,1)S(1)} %fusion.8), channel_id=1, source_target_pairs={{0,2},{1,3},{2,0},{3,1},{4,6},{5,7},{6,4},{7,5},{8,10},{9,11},{10,... | collective-permute-start | bytes 884744 | tf_op jit(solution)/shard_map/ppermute | solution.py:35
  305.0 10.0 %collective-permute-start.46 = (f32[2,768]{1,0:T(2,128)S(1)}, f32[2,768]{1,0:T(2,128)S(1)}, u32[]{:S(2)}, u32[]{:S(2)}) collective-permute-start(f32[2,768]{1,0:T(2,128)S(1)} %pad_maximum_fusion.16), channel_id=1, source_target_pairs={{0,1},{1,0},{2,3},{3,2},{4,5},{5,4},{6,7},{7,6},{8,9},{9,8},{10,11... | collective-permute-start | bytes 18440 | tf_op jit(solution)/shard_map/ppermute | solution.py:35
  315.1 9.6 %collective-permute-start.47 = (f32[2,768]{1,0:T(2,128)S(1)}, f32[2,768]{1,0:T(2,128)S(1)}, u32[]{:S(2)}, u32[]{:S(2)}) collective-permute-start(f32[2,768]{1,0:T(2,128)S(1)} %fusion.9), channel_id=1, source_target_pairs={{0,2},{1,3},{2,0},{3,1},{4,6},{5,7},{6,4},{7,5},{8,10},{9,11},{10,... | collective-permute-start | bytes 18440 | tf_op jit(solution)/shard_map/ppermute | solution.py:35
  324.8 4.0 %collective-permute-start.48 = (f32[3264]{0:T(1024)S(1)}, f32[3264]{0:T(1024)S(1)}, u32[]{:S(2)}, u32[]{:S(2)}) collective-permute-start(f32[3264]{0:T(1024)S(1)} %constant_dynamic-update-slice_fusion.5), channel_id=1, source_target_pairs={{0,4},{4,0},{8,12},{12,8},{16,20},{20,16},{24,28},{28,24},{1,5},{5... | collective-permute-start | bytes 39176 | tf_op jit(solution)/shard_map/ppermute | solution.py:35
  326.8 14.2 %collective-permute-start.53 = (bf16[4,96,768]{2,1,0:T(8,128)(2,1)}, bf16[4,96,768]{2,1,0:T(8,128)(2,1)}, u32[]{:S(2)}, u32[]{:S(2)}) collective-permute-start(bf16[4,96,768]{2,1,0:T(8,128)(2,1)} %dynamic-slice_bitcast_fusion), channel_id=1, source_target_pairs={{0,4},{4,0},{8,12},{12,8},{16,20},{20,16},{24,28},{28,24},{1,5},{5... | collective-permute-start | bytes 1769480 | tf_op jit(solution)/shard_map/ppermute | solution.py:35
  328.8 3.8 collective-permute-start.49
  332.6 4.6 %collective-permute-start.50 = (f32[3264]{0:T(1024)S(1)}, f32[3264]{0:T(1024)S(1)}, u32[]{:S(2)}, u32[]{:S(2)}) collective-permute-start(f32[3264]{0:T(1024)S(1)} %add.154), channel_id=1, source_target_pairs={{0,16},{4,20},{8,24},{12,28},{16,0},{20,4},{24,8},{28,12},{1,17},{... | collective-permute-start | bytes 39176 | tf_op jit(solution)/shard_map/ppermute | solution.py:35
  335.0 11.8 %collective-permute-start.35 = (bf16[256,768]{1,0:T(8,128)(2,1)S(1)}, bf16[256,768]{1,0:T(8,128)(2,1)S(1)}, u32[]{:S(2)}, u32[]{:S(2)}) collective-permute-start(bf16[256,768]{1,0:T(8,128)(2,1)S(1)} %slice.232), channel_id=1, source_target_pairs={{0,2},{1,3},{2,0},{3,1},{4,6},{5,7},{6,4},{7,5},{8,10},{9,11},{10,... | collective-permute-start | bytes 1179656 | tf_op jit(solution)/shard_map/ppermute | solution.py:35
  335.6 20.6 %collective-permute-start.41 = (bf16[512,768]{1,0:T(8,128)(2,1)}, bf16[512,768]{1,0:T(8,128)(2,1)}, u32[]{:S(2)}, u32[]{:S(2)}) collective-permute-start(bf16[512,768]{1,0:T(8,128)(2,1)} %get-tuple-element.109), channel_id=1, source_target_pairs={{0,1},{1,0},{2,3},{3,2},{4,5},{5,4},{6,7},{7,6},{8,9},{9,8},{10,11... | collective-permute-start | bytes 2359304 | tf_op jit(solution)/shard_map/ppermute | solution.py:35
  342.3 8.5 %collective-permute-start.56 = (bf16[1,96,768]{2,1,0:T(8,128)(2,1)S(1)}, bf16[1,96,768]{2,1,0:T(8,128)(2,1)S(1)}, u32[]{:S(2)}, u32[]{:S(2)}) collective-permute-start(bf16[1,96,768]{2,1,0:T(8,128)(2,1)S(1)} %get-tuple-element.188), channel_id=1, source_target_pairs={{0,24},{4,28},{8,16},{12,20},{16,8},{20,12},{24,0},{28,4},{1,25},{... | collective-permute-start | bytes 442376 | tf_op jit(solution)/shard_map/ppermute | solution.py:35
  342.4 13.0 %collective-permute-start.55 = (bf16[1,96,768]{2,1,0:T(8,128)(2,1)S(1)}, bf16[1,96,768]{2,1,0:T(8,128)(2,1)S(1)}, u32[]{:S(2)}, u32[]{:S(2)}) collective-permute-start(bf16[1,96,768]{2,1,0:T(8,128)(2,1)S(1)} %get-tuple-element.189), channel_id=1, source_target_pairs={{0,16},{4,20},{8,24},{12,28},{16,0},{20,4},{24,8},{28,12},{1,17},{... | collective-permute-start | bytes 442376 | tf_op jit(solution)/shard_map/ppermute | solution.py:35
  343.3 12.1 %collective-permute-start.54 = (bf16[1,96,768]{2,1,0:T(8,128)(2,1)S(1)}, bf16[1,96,768]{2,1,0:T(8,128)(2,1)S(1)}, u32[]{:S(2)}, u32[]{:S(2)}) collective-permute-start(bf16[1,96,768]{2,1,0:T(8,128)(2,1)S(1)} %get-tuple-element.187), channel_id=1, source_target_pairs={{0,8},{4,12},{8,0},{12,4},{16,24},{20,28},{24,16},{28,20},{1,9},{5... | collective-permute-start | bytes 442376 | tf_op jit(solution)/shard_map/ppermute | solution.py:35
  346.9 9.3 %collective-permute-start.37 = (bf16[256,768]{1,0:T(8,128)(2,1)S(1)}, bf16[256,768]{1,0:T(8,128)(2,1)S(1)}, u32[]{:S(2)}, u32[]{:S(2)}) collective-permute-start(bf16[256,768]{1,0:T(8,128)(2,1)S(1)} %add_convert_fusion.3), channel_id=1, source_target_pairs={{0,2},{1,3},{2,0},{3,1},{4,6},{5,7},{6,4},{7,5},{8,10},{9,11},{10,... | collective-permute-start | bytes 1179656 | tf_op jit(solution)/shard_map/ppermute | solution.py:35
  350.8 10.9 %collective-permute-start.36 = (bf16[256,768]{1,0:T(8,128)(2,1)S(1)}, bf16[256,768]{1,0:T(8,128)(2,1)S(1)}, u32[]{:S(2)}, u32[]{:S(2)}) collective-permute-start(bf16[256,768]{1,0:T(8,128)(2,1)S(1)} %add_convert_fusion.3), channel_id=1, source_target_pairs={{0,1},{1,0},{2,3},{3,2},{4,5},{5,4},{6,7},{7,6},{8,9},{9,8},{10,11... | collective-permute-start | bytes 1179656 | tf_op jit(solution)/shard_map/ppermute | solution.py:35
  356.2 5.6 %collective-permute-start.38 = (bf16[256,768]{1,0:T(8,128)(2,1)S(1)}, bf16[256,768]{1,0:T(8,128)(2,1)S(1)}, u32[]{:S(2)}, u32[]{:S(2)}) collective-permute-start(bf16[256,768]{1,0:T(8,128)(2,1)S(1)} %collective-permute-done.37), channel_id=1, source_target_pairs={{0,1},{1,0},{2,3},{3,2},{4,5},{5,4},{6,7},{7,6},{8,9},{9,8},{10,11... | collective-permute-start | bytes 1179656 | tf_op jit(solution)/shard_map/ppermute | solution.py:35
  358.3 11.5 %collective-permute-start.42 = (bf16[256,768]{1,0:T(8,128)(2,1)S(1)}, bf16[256,768]{1,0:T(8,128)(2,1)S(1)}, u32[]{:S(2)}, u32[]{:S(2)}) collective-permute-start(bf16[256,768]{1,0:T(8,128)(2,1)S(1)} %get-tuple-element.181), channel_id=1, source_target_pairs={{0,2},{1,3},{2,0},{3,1},{4,6},{5,7},{6,4},{7,5},{8,10},{9,11},{10,... | collective-permute-start | bytes 1179656 | tf_op jit(solution)/shard_map/ppermute | solution.py:35
  373.2 10.9 %collective-permute-start.44 = (bf16[256,768]{1,0:T(8,128)(2,1)}, bf16[256,768]{1,0:T(8,128)(2,1)S(1)}, u32[]{:S(2)}, u32[]{:S(2)}) collective-permute-start(bf16[256,768]{1,0:T(8,128)(2,1)} %grad_tokens_own.1), channel_id=1, source_target_pairs={{0,2},{1,3},{2,0},{3,1},{4,6},{5,7},{6,4},{7,5},{8,10},{9,11},{10,... | collective-permute-start | bytes 1179656 | tf_op jit(solution)/shard_map/ppermute | solution.py:35
  374.7 10.9 %collective-permute-start.43 = (bf16[256,768]{1,0:T(8,128)(2,1)S(1)}, bf16[256,768]{1,0:T(8,128)(2,1)S(1)}, u32[]{:S(2)}, u32[]{:S(2)}) collective-permute-start(bf16[256,768]{1,0:T(8,128)(2,1)S(1)} %copy-done.7), channel_id=1, source_target_pairs={{0,1},{1,0},{2,3},{3,2},{4,5},{5,4},{6,7},{7,6},{8,9},{9,8},{10,11... | collective-permute-start | bytes 1179656 | tf_op jit(solution)/shard_map/ppermute | solution.py:35
  384.2 1.7 collective-permute-start.45
  (33 other events, 190.5 us)

commit v2 on v1

v2 whole, which is shorter than its diff:
```python
import functools

import jax
import jax.numpy as jnp
from jax import lax
from jax.experimental import pallas as pl
from jax.experimental.pallas import tpu as pltpu
from jax.sharding import PartitionSpec as P

DH = 64
REACH = 2
EPS = 1e-06
MASKED = -1e30
TILE = 256
HALO = 16
F32 = jnp.float32
BF16 = jnp.bfloat16
MIB = 1024 * 1024
COST = pl.CostEstimate(flops=1, bytes_accessed=1, transcendentals=0)


def params(mib=20):
    return pltpu.CompilerParams(vmem_limit_bytes=mib * MIB)


def whole():
    return pl.BlockSpec(memory_space=pltpu.VMEM)


def mm(a, b, ca=1, cb=0):
    return lax.dot_general(a, b, (((ca,), (cb,)), ((), ())), preferred_element_type=F32)


def swap(x, axis, mask):
    return lax.ppermute(x, axis, [(i, i ^ mask) for i in range(lax.axis_size(axis))])


def moved(x, axis, distance):
    size = lax.axis_size(axis)
    return lax.ppermute(x, axis, [(i, i + distance) for i in range(size) if 0 <= i + distance < size])


def bit_groups(axis):
    bits = list(range(lax.axis_size(axis).bit_length() - 2, -1, -1))
    upper, groups = bits[:-1], []
    while upper:
        groups.append(tuple(upper[:2]))
        upper = upper[2:]
    return groups + [(0,)]


def bit_of(axis, bit):
    return ((lax.axis_index(axis) >> bit) & 1) == 1


def in_order(pieces, axis, group):
    both = jnp.stack(pieces)
    if len(group) == 1:
        return jnp.where(bit_of(axis, group[0]), both[::-1], both)
    both = both.reshape(2, 2, *both.shape[1:])
    both = jnp.where(bit_of(axis, group[0]), both[::-1], both)
    both = jnp.where(bit_of(axis, group[1]), both[:, ::-1], both)
    return both.reshape(4, *both.shape[2:])


def masks_of(group):
    if len(group) == 1:
        return [0, 1 << group[0]]
    hi, lo = 1 << group[0], 1 << group[1]
    return [0, lo, hi, hi | lo]


def gathered(out, axis, groups, size, after=None):
    for group in groups:
        pieces = [out] + [swap(out, axis, m) for m in masks_of(group)[1:]]
        if after is not None:
            *pieces, after = lax.optimization_barrier((*pieces, after))
        out = jnp.moveaxis(in_order(pieces, axis, group), 0, 1)
        out = out.reshape(-1, *size)
    return out


def chosen(full, axis, group):
    r = 1 << len(group)
    out = full.reshape(full.shape[0], -1, r, *full.shape[2:])
    mine = (lax.axis_index(axis) >> group[-1]) & (r - 1)
    return [lax.dynamic_index_in_dim(out, mine ^ (m >> group[-1]), 2, keepdims=False) for m in masks_of(group)]


def received(parts, axis, group):
    keep, *send = parts
    return [keep] + [swap(part, axis, m) for m, part in zip(masks_of(group)[1:], send)]


def total_of(parts):
    total = parts[0].astype(F32)
    for part in parts[1:]:
        total = total + part.astype(F32)
    return total


def sum_scatter(full, axis, groups):
    *rest, last = reversed(groups)
    out = full
    for group in rest:
        out = total_of(received(chosen(out, axis, group), axis, group)).astype(BF16)
    return received(chosen(out, axis, last), axis, last)


def sum_everywhere(x, axis, groups):
    for group in groups:
        x = total_of([x] + [swap(x, axis, m) for m in masks_of(group)[1:]])
    return x


def quarters(own):
    far = swap(own, "head", 2)
    return own, far, swap(own, "head", 1), swap(far, "head", 1)


PAIR = 2 * DH
KV = 3 * PAIR
KEY_LANES = ((0, PAIR), (0, PAIR), (2 * PAIR, KV))
VALUE_LANES = ((PAIR, 2 * PAIR), (PAIR, 2 * PAIR), (2 * PAIR, KV))
KEY_ROWS = (0, DH, 2 * PAIR)
VALUE_ROWS = (PAIR, PAIR + DH, 2 * PAIR + DH)


def arranged(q, k, v):
    return jnp.concatenate([k[..., :PAIR], v[..., :PAIR], k[..., PAIR:], v[..., PAIR:], q], axis=-1)


def separated(x):
    k = jnp.concatenate([x[..., :PAIR], x[..., 2 * PAIR : 2 * PAIR + DH]], axis=-1)
    v = jnp.concatenate([x[..., PAIR : 2 * PAIR], x[..., 2 * PAIR + DH : KV]], axis=-1)
    return x[..., KV:], k, v


def pack_kernel(up_ref, out_ref, down_ref, packed_ref, down_t_ref):
    shard, units = up_ref.shape
    out_t = out_ref[...].astype(F32).T
    few = packed_ref.shape[0] - shard
    packed_ref[0:shard, :] = up_ref[...]
    out_t = jnp.concatenate([out_t[n : n + few] for n in range(0, shard, few)], axis=1)
    packed_ref[shard:, :] = out_t.astype(BF16)
    down_t_ref[...] = down_ref[...].astype(F32).T.astype(BF16)


def pack(w_up, w_out, w_down):
    shard, units = w_up.shape
    part = w_out.shape[0]
    return pl.pallas_call(
        pack_kernel,
        out_shape=(
            jax.ShapeDtypeStruct((shard + shard * part // units, units), BF16),
            jax.ShapeDtypeStruct((shard, units), BF16),
        ),
        in_specs=[whole()] * 3,
        out_specs=(whole(), whole()),
        compiler_params=params(),
        cost_estimate=COST,
        name="pack",
    )(w_up, w_out, w_down)


def unit_times_gain(x, gain):
    return x * lax.rsqrt(jnp.mean(x * x, axis=-1, keepdims=True) + EPS) * gain


def mix_rows(buf_ref, mix_ref, taps, starts, base, rows):
    mix_ref[...] = (
        taps[0:1] * buf_ref[8 : 8 + rows, :]
        + taps[1:2] * buf_ref[7 : 7 + rows, :]
        + taps[2:3] * buf_ref[6 : 6 + rows, :]
    )
    for start in starts:
        r = start - base

        @pl.when((r >= 0) & (r < rows))
        def _(r=r):
            mix_ref[pl.ds(r, 1), :] = taps[0:1] * buf_ref[pl.ds(8 + r, 1), :]

        @pl.when((r + 1 >= 0) & (r + 1 < rows))
        def _(r=r):
            mix_ref[pl.ds(r + 1, 1), :] = (
                taps[0:1] * buf_ref[pl.ds(9 + r, 1), :] + taps[1:2] * buf_ref[pl.ds(8 + r, 1), :]
            )


def project_own_kernel(
    meta_ref, x_ref, halo_ref, gain_ref, w_in_ref, taps_ref,
    w_ref, raw_halo_ref, raw_ref, normed_ref, q_ref, kv_ref, kvt_ref, buf_ref, mix_ref, *, base,
):
    i = pl.program_id(0)
    rows = x_ref.shape[0]
    gain = gain_ref[...]

    @pl.when(i == 0)
    def _():
        w_in = w_in_ref[...]
        part = w_in.shape[1] // 3
        w_ref[...] = arranged(w_in[:, :part], w_in[:, part : 2 * part], w_in[:, 2 * part : 3 * part])

    w = w_ref[...]

    @pl.when(i == 0)
    def _():
        halo = jnp.where(meta_ref[HAS_ONE] == 1, halo_ref[...].astype(F32), 0.0)
        normed = unit_times_gain(halo, gain).astype(BF16)
        raw_low = mm(normed, w).astype(BF16)
        raw_halo_ref[...] = raw_low[:, KV:]
        buf_ref[0:8, :] = raw_low.astype(F32)[HALO - 8 :, :]

    normed = unit_times_gain(x_ref[...].astype(F32), gain).astype(BF16)
    raw_low = mm(normed, w).astype(BF16)
    normed_ref[...] = normed
    raw_ref[...] = raw_low
    raw = raw_low.astype(F32)
    buf_ref[8 : 8 + rows, :] = raw
    mix_rows(buf_ref, mix_ref, taps_ref[...], [meta_ref[STARTS + n] for n in range(8)], base + i * rows, rows)
    buf_ref[0:8, :] = raw[rows - 8 :, :]
    q_ref[...] = mix_ref[:, KV:].astype(BF16)
    kv = mix_ref[:, :KV]
    kv_ref[...] = kv.astype(BF16)
    kvt_ref[...] = kv.T.astype(BF16)


def project_own(meta, tokens, halo, gain, w, taps):
    rows, dim = tokens.shape
    width = w.shape[1]
    step = 2 * TILE
    tile = lambda n: pl.BlockSpec((step, n), lambda i, *_: (i, 0))
    return pl.pallas_call(
        functools.partial(project_own_kernel, base=REACH * rows),
        out_shape=(
            jax.ShapeDtypeStruct((dim, width), BF16),
            jax.ShapeDtypeStruct((HALO, width - KV), BF16),
            jax.ShapeDtypeStruct((rows, width), BF16),
            jax.ShapeDtypeStruct((rows, dim), BF16),
            jax.ShapeDtypeStruct((rows, width - KV), BF16),
            jax.ShapeDtypeStruct((rows, KV), BF16),
            jax.ShapeDtypeStruct((KV, rows), BF16),
        ),
        grid_spec=pltpu.PrefetchScalarGridSpec(
            num_scalar_prefetch=1,
            grid=(rows // step,),
            in_specs=[tile(dim), whole(), whole(), whole(), whole()],
            out_specs=(
                whole(),
                whole(),
                tile(width),
                tile(dim),
                tile(width - KV),
                tile(KV),
                pl.BlockSpec((KV, step), lambda i, *_: (0, i)),
            ),
            scratch_shapes=[pltpu.VMEM((8 + step, width), F32), pltpu.VMEM((step, width), F32)],
        ),
        compiler_params=params(),
        cost_estimate=COST,
        name="project_own",
    )(meta, tokens, halo, gain, w, taps)


def project_earlier_kernel(meta_ref, *refs):
    pieces = refs[:8]
    gain_ref, w_ref, taps_ref, raw_ref, normed_ref, kv_ref, kvt_ref, x_ref, buf_ref, mix_ref = refs[8:]
    i = pl.program_id(0)
    rows = x_ref.shape[0]
    quarter = pieces[0].shape[0]

    @pl.when(i == 0)
    def _():
        buf_ref[0:8, :] = jnp.zeros((8, KV), F32)

    for hop in range(REACH):
        for slot, d in enumerate((0, 2, 1, 3)):
            place = 4 * hop + (meta_ref[0] ^ d)

            @pl.when(i == place >> 1)
            def _(piece=pieces[4 * hop + slot], place=place):
                x_ref[pl.ds(pl.multiple_of((place & 1) * quarter, quarter), quarter), :] = piece[...]

    exists = jnp.where(i < pl.num_programs(0) // REACH, meta_ref[HAS_TWO], meta_ref[HAS_ONE])
    x = jnp.where(exists == 1, x_ref[...].astype(F32), 0.0)
    normed = unit_times_gain(x, gain_ref[...]).astype(BF16)
    normed_ref[...] = normed
    raw_low = mm(normed, w_ref[:, :KV]).astype(BF16)
    raw_ref[...] = raw_low
    raw = raw_low.astype(F32)
    buf_ref[8 : 8 + rows, :] = raw
    mix_rows(buf_ref, mix_ref, taps_ref[:, :KV], [meta_ref[STARTS + n] for n in range(8)], i * rows, rows)
    buf_ref[0:8, :] = raw[rows - 8 :, :]
    kv = mix_ref[...]
    kv_ref[...] = kv.astype(BF16)
    kvt_ref[...] = kv.T.astype(BF16)


def project_earlier(meta, pieces, gain, w, taps):
    quarter, dim = pieces[0].shape
    step = 2 * quarter
    span = len(pieces) * quarter
    tile = lambda n: pl.BlockSpec((step, n), lambda i, *_: (i, 0))
    return pl.pallas_call(
        project_earlier_kernel,
        out_shape=(
            jax.ShapeDtypeStruct((span, KV), BF16),
            jax.ShapeDtypeStruct((span, dim), BF16),
            jax.ShapeDtypeStruct((span, KV), BF16),
            jax.ShapeDtypeStruct((KV, span), BF16),
        ),
        grid_spec=pltpu.PrefetchScalarGridSpec(
            num_scalar_prefetch=1,
            grid=(span // step,),
            in_specs=[whole()] * 11,
            out_specs=(tile(KV), tile(dim), tile(KV), pl.BlockSpec((KV, step), lambda i, *_: (0, i))),
            scratch_shapes=[
                pltpu.VMEM((step, dim), BF16),
                pltpu.VMEM((8 + step, KV), F32),
                pltpu.VMEM((step, KV), F32),
            ],
        ),
        compiler_params=params(),
        cost_estimate=COST,
        name="project_earlier",
    )(meta, *pieces, gain, w, taps)


LOW, FULL, STARTS = 1, 5, 9
HAS_ONE, HAS_TWO, NEXT_ONE, NEXT_TWO = 17, 18, 19, 20


STEP = 2 * TILE


def masked_scores(scores, key_base, query_base, first, diagonal):
    keys = lax.broadcasted_iota(jnp.int32, scores.shape, 0)
    allowed = keys >= first - key_base
    if diagonal is not None:
        allowed = allowed & (keys <= lax.broadcasted_iota(jnp.int32, scores.shape, 1) + (query_base - diagonal))
    return jnp.where(allowed, scores, MASKED)


def place_heads(to_ref, lanes, across, halves):
    zero = jnp.zeros((DH, across.shape[1]), to_ref.dtype)
    for h, half in enumerate(halves):
        to_ref[h, half * DH : (half + 1) * DH, lanes] = across[h * DH : (h + 1) * DH].astype(to_ref.dtype)
        to_ref[h, (1 - half) * DH : (2 - half) * DH, lanes] = zero


KEY_HALVES, VALUE_HALVES = (0, 1, 0), (0, 1, 1)


def eights(x, how):
    return how(x.reshape(x.shape[0] // 8, 8, x.shape[1]), axis=0)


def query_tiles(rows):
    return [slice(n, n + TILE) for n in range(0, rows, TILE)]


def staged(items, first, second, depth=2):
    waiting = []
    for item in items:
        waiting.append((item, first(item)))
        if len(waiting) > depth:
            second(*waiting.pop(0))
    for pair in waiting:
        second(*pair)


def attend_tiles(steps, q_ref, kv_ref, kvt_ref, first_ref, acc_ref, q_across_ref, top_ref, sum_ref):
    for lanes in query_tiles(q_ref.shape[0]):
        place_heads(q_across_ref, lanes, (q_ref[lanes, :].astype(F32) * (DH**-0.5)).T, KEY_HALVES)
    acc_ref[...] = jnp.zeros_like(acc_ref)
    top_ref[...] = jnp.full(top_ref.shape, MASKED, F32)
    sum_ref[...] = jnp.zeros_like(sum_ref)

    def run(row, keys, window_row, begin, masked, diagonal):
        at = pl.ds(row, keys)
        items = [(h, lanes) for h in range(3) for lanes in query_tiles(q_ref.shape[0])[begin // TILE :]]
        key_rows = [kv_ref[at, KEY_LANES[h][0] : KEY_LANES[h][1]] for h in range(3)]
        values = [kvt_ref[VALUE_ROWS[h] : VALUE_ROWS[h] + DH, at] for h in range(3)]
        queries = [q_across_ref[h, :, lanes] for h, lanes in items]
        tops = [top_ref[h : h + 1, lanes] for h, lanes in items]
        firsts = {lanes.start: first_ref[:, lanes] for _, lanes in items}
        results = []

        def first(n):
            h, lanes = items[n]
            scores = mm(key_rows[h], queries[n])
            if masked:
                scores = masked_scores(scores, window_row, lanes.start, firsts[lanes.start], diagonal)
            return scores

        def second(n, scores):
            h, lanes = items[n]
            top = jnp.maximum(tops[n], jnp.max(eights(scores, jnp.max), axis=0, keepdims=True))
            weights = jnp.exp(scores - top)
            total = jnp.sum(eights(weights, jnp.sum), axis=0, keepdims=True)
            results.append((top, total, mm(values[h], weights.astype(BF16))))

        staged(range(len(items)), first, second)
        for n, (h, lanes) in enumerate(items):
            top, total, out = results[n]
            fade = jnp.exp(tops[n] - top)
            top_ref[h : h + 1, lanes] = top
            sum_ref[h : h + 1, lanes] = sum_ref[h : h + 1, lanes] * fade + total
            rows = slice(h * DH, (h + 1) * DH)
            acc_ref[rows, lanes] = acc_ref[rows, lanes] * fade + out

    steps(run)


def earlier_steps(meta_ref, before, rows):
    last = rows // TILE - 1
    end = before // STEP
    low = meta_ref[LOW] // (STEP // TILE)
    full = (meta_ref[FULL + last] + STEP // TILE - 1) // (STEP // TILE)
    middle = jnp.clip(full, low, jnp.maximum(end, low))

    def steps(run):
        def one(masked):
            def step(n, carry):
                row = pl.multiple_of(n * STEP, STEP)
                run(row, STEP, row, 0, masked, None)
                return carry

            return step

        lax.fori_loop(low, middle, one(True), 0)
        lax.fori_loop(middle, end, one(False), 0)

    return steps


def attend_own_kernel(q_ref, kv_ref, kvt_ref, first_ref, acc_ref, stat_ref, q_across_ref, *, base):
    rows = q_ref.shape[0]

    def steps(run):
        for row in range(0, rows, STEP):
            run(row, STEP, base + row, row, True, row)

    top_ref, sum_ref = stat_ref.at[0:8], stat_ref.at[8:16]
    attend_tiles(steps, q_ref, kv_ref, kvt_ref, first_ref, acc_ref, q_across_ref, top_ref, sum_ref)


def attend_earlier_kernel(
    meta_ref, q_ref, kv_ref, kvt_ref, first_ref, acc_own_ref, stat_own_ref,
    att_ref, ot_ref, lse_ref, q_across_ref, top_ref, sum_ref,
):
    rows = q_ref.shape[0]
    steps = earlier_steps(meta_ref, kv_ref.shape[0], rows)
    attend_tiles(steps, q_ref, kv_ref, kvt_ref, first_ref, ot_ref, q_across_ref, top_ref, sum_ref)
    for h in range(3):
        to = slice(h * DH, (h + 1) * DH)
        top_here, top_own = top_ref[h : h + 1, :], stat_own_ref[h : h + 1, :]
        top = jnp.maximum(top_here, top_own)
        here, own = jnp.exp(top_here - top), jnp.exp(top_own - top)
        total = here * sum_ref[h : h + 1, :] + own * stat_own_ref[8 + h : 9 + h, :]
        out = ot_ref[to, :] * (here / total) + acc_own_ref[to, :] * (own / total)
        ot_ref[to, :] = out
        lse_ref[h : h + 1, :] = top + jnp.log(total)
        for n, lanes in enumerate(query_tiles(rows)):
            att_ref[slot_of(n, meta_ref), to, :] = out[:, lanes].astype(BF16)


def slot_of(i, meta):
    d = i ^ meta[0]
    return (d >> 1) | ((d & 1) << 1)


def attend_own(q, kv, kvt, first_row):
    rows, part = q.shape
    return pl.pallas_call(
        functools.partial(attend_own_kernel, base=REACH * rows),
        out_shape=(jax.ShapeDtypeStruct((part, rows), F32), jax.ShapeDtypeStruct((16, rows), F32)),
        in_specs=[whole()] * 4,
        out_specs=(whole(), whole()),
        scratch_shapes=[pltpu.VMEM((3, PAIR, rows), BF16)],
        compiler_params=params(),
        cost_estimate=COST,
        name="attend_own",
    )(q, kv, kvt, first_row)


def attend_earlier(meta, q, kv, kvt, first_row, acc_own, stat_own):
    rows, part = q.shape
    return pl.pallas_call(
        attend_earlier_kernel,
        out_shape=(
            jax.ShapeDtypeStruct((rows // TILE, part, TILE), BF16),
            jax.ShapeDtypeStruct((part, rows), F32),
            jax.ShapeDtypeStruct((8, rows), F32),
        ),
        in_specs=[pl.BlockSpec(memory_space=pltpu.SMEM)] + [whole()] * 6,
        out_specs=(whole(), whole(), whole()),
        scratch_shapes=[
            pltpu.VMEM((3, PAIR, rows), BF16),
            pltpu.VMEM((8, rows), F32),
            pltpu.VMEM((8, rows), F32),
        ],
        compiler_params=params(),
        cost_estimate=COST,
        name="attend_earlier",
    )(meta, q, kv, kvt, first_row, acc_own, stat_own)


def back_scratch(rows):
    return [
        pltpu.VMEM((3, PAIR, rows), BF16),
        pltpu.VMEM((3, PAIR, rows), BF16),
        pltpu.VMEM((3, rows, PAIR), BF16),
        pltpu.VMEM((3, rows, PAIR), BF16),
        pltpu.VMEM((8, rows), F32),
        pltpu.VMEM((3, STEP, rows), BF16),
        pltpu.VMEM((3, STEP, rows), BF16),
    ]


def back_prepare(meta_ref, q_ref, dt_ref, ot_ref, scratch):
    q_across_ref, d_across_ref, q_alone_ref, d_alone_ref, delta_ref = scratch[:5]
    lane = lax.broadcasted_iota(jnp.int32, (TILE, PAIR), 1)
    none = jnp.zeros((TILE, PAIR), BF16)

    def alone(to_ref, rows, x, halves):
        last = jnp.concatenate([x[:, PAIR:]] * 2, axis=1)
        for h, half in enumerate(halves):
            to_ref[h, rows, :] = jnp.where((lane < DH) == (half == 0), x[:, :PAIR] if h < 2 else last, none)

    for n, rows in enumerate(query_tiles(q_ref.shape[0])):
        scaled = q_ref[rows, :].astype(F32) * (DH**-0.5)
        place_heads(q_across_ref, rows, scaled.T, KEY_HALVES)
        alone(q_alone_ref, rows, scaled.astype(BF16), KEY_HALVES)
        d_wide = dt_ref[slot_of(n, meta_ref)].astype(F32)
        place_heads(d_across_ref, rows, d_wide, VALUE_HALVES)
        alone(d_alone_ref, rows, d_wide.T.astype(BF16), VALUE_HALVES)
        terms = d_wide * ot_ref[:, rows]
        for h in range(3):
            delta_ref[h : h + 1, rows] = jnp.sum(terms[h * DH : (h + 1) * DH], axis=0, keepdims=True)


def back_step(row, keys, window_row, begin, masked, diagonal, kv_ref, kvt_ref, lse_ref, first_ref, grad_ref, lead, dq_ref, scratch):
    q_across_ref, d_across_ref, q_alone_ref, d_alone_ref, delta_ref, p_ref, ds_ref = scratch
    rows = dq_ref.shape[1]
    at = pl.ds(row, keys)
    items = [(h, lanes) for h in range(3) for lanes in query_tiles(rows)[begin // TILE :]]
    key_rows = [kv_ref[at, KEY_LANES[h][0] : KEY_LANES[h][1]] for h in range(3)]
    value_rows = [kv_ref[at, VALUE_LANES[h][0] : VALUE_LANES[h][1]] for h in range(3)]
    keys_t = [kvt_ref[KEY_ROWS[h] : KEY_ROWS[h] + DH, at] for h in range(3)]
    queries = [q_across_ref[h, :, lanes] for h, lanes in items]
    d_outs = [d_across_ref[h, :, lanes] for h, lanes in items]
    lses = [lse_ref[h : h + 1, lanes] for h, lanes in items]
    deltas = [delta_ref[h : h + 1, lanes] for h, lanes in items]
    firsts = {lanes.start: first_ref[:, lanes] for _, lanes in items}
    results = []

    def first(n):
        h, lanes = items[n]
        scores = mm(key_rows[h], queries[n])
        if masked:
            scores = masked_scores(scores, window_row, lanes.start, firsts[lanes.start], diagonal)
        return scores, mm(value_rows[h], d_outs[n])

    def second(n, both):
        h, lanes = items[n]
        scores, d_probs = both
        probs = jnp.exp(scores - lses[n])
        d_scores = (probs * (d_probs - deltas[n])).astype(BF16)
        p_ref[h, :keys, lanes] = probs.astype(BF16)
        ds_ref[h, :keys, lanes] = d_scores
        results.append(mm(keys_t[h], d_scores))

    staged(range(len(items)), first, second, 1)
    for n, (h, lanes) in enumerate(items):
        dq_ref[h * DH : (h + 1) * DH, lanes] += results[n]
    seen = slice(begin, rows)
    to = pl.ds(pl.multiple_of(lead + row, 8), keys)
    terms = (
        ((ds_ref, q_alone_ref, 0), (ds_ref, q_alone_ref, 1)),
        ((p_ref, d_alone_ref, 0), (p_ref, d_alone_ref, 1)),
        ((ds_ref, q_alone_ref, 2), (p_ref, d_alone_ref, 2)),
    )
    for n, ((left_a, right_a, a), (left_b, right_b, b)) in enumerate(terms):
        lanes = slice(n * PAIR, (n + 1) * PAIR)
        grad_ref[to, lanes] += mm(left_a[a, :keys, seen], right_a[a, seen, :]) + mm(
            left_b[b, :keys, seen], right_b[b, seen, :]
        )


def unmix_rows(grad_ref, raw_ref, fix_ref, taps, starts, rows, sums_ref):
    width = grad_ref.shape[1]

    def raw_row(r):
        group = raw_ref[pl.ds(pl.multiple_of((r // HALO) * HALO, HALO), HALO), :].astype(F32)
        row = lax.broadcasted_iota(jnp.int32, group.shape, 0)
        return jnp.sum(jnp.where(row == r % HALO, group, 0.0), axis=0, keepdims=True)

    sums_ref[...] = jnp.zeros_like(sums_ref)
    inside = [(s >= 1) & (s <= rows + 1) for s in starts]
    for n, s in enumerate(starts):

        @pl.when(inside[n])
        def _(n=n, s=s):
            one_before = grad_ref[pl.ds(7 + s, 1), :]
            fix_ref[2 * n : 2 * n + 1, :] = taps[0:1] * one_before
            fix_ref[2 * n + 1 : 2 * n + 2, :] = taps[0:1] * grad_ref[pl.ds(6 + s, 1), :] + taps[1:2] * one_before
            here = grad_ref[pl.ds(8 + s, 1), :]

            @pl.when(s >= 2)
            def _():
                sums_ref[2:3, :] -= raw_row(jnp.maximum(s - 2, 0)) * here

            @pl.when(s <= rows)
            def _():
                raw_one = raw_row(s - 1)
                sums_ref[1:2, :] -= raw_one * here
                following = starts[n + 1] if n + 1 < len(starts) else s + 2

                @pl.when(following != s + 1)
                def _():
                    sums_ref[2:3, :] -= raw_one * grad_ref[pl.ds(9 + s, 1), :]

    sizes = [HALO] * (1 if rows % TILE else 0) + [TILE] * (rows // TILE)
    lo = 0
    totals = [jnp.zeros((8, width), F32) for _ in range(3)]
    for size in sizes:
        now = grad_ref[8 + lo : 8 + lo + size, :]
        one = grad_ref[9 + lo : 9 + lo + size, :]
        two = grad_ref[10 + lo : 10 + lo + size, :]
        raw = raw_ref[lo : lo + size, :].astype(F32)
        for j, shifted in enumerate((now, one, two)):
            totals[j] = totals[j] + eights(raw * shifted, jnp.sum)
        grad_ref[8 + lo : 8 + lo + size, :] = taps[0:1] * now + taps[1:2] * one + taps[2:3] * two
        lo += size
    for j in range(3):
        sums_ref[j : j + 1, :] += jnp.sum(totals[j], axis=0, keepdims=True)
    for n in reversed(range(len(starts))):

        @pl.when(inside[n])
        def _(n=n, s=starts[n]):
            grad_ref[pl.ds(7 + s, 1), :] = fix_ref[2 * n : 2 * n + 1, :]
            grad_ref[pl.ds(6 + s, 1), :] = fix_ref[2 * n + 1 : 2 * n + 2, :]


def earlier_back_kernel(
    meta_ref, q_ref, dt_ref, ot_ref, lse_ref, first_ref, kv_ref, kvt_ref, kv_own_ref, kvt_own_ref, raw_ref,
    raw_halo_ref, taps_ref, dq_ref, two_ref, one_ref, next_ref, sums_ref, sums_q_ref,
    grad_ref, grad_q_ref, fix_ref, fix_q_ref, *scratch,
):
    before = kv_ref.shape[0]
    rows = q_ref.shape[0]
    grad_ref[...] = jnp.zeros_like(grad_ref)
    grad_q_ref[...] = jnp.zeros_like(grad_q_ref)
    dq_ref[...] = jnp.zeros_like(dq_ref)
    back_prepare(meta_ref, q_ref, dt_ref, ot_ref, scratch)
    run = lambda *step: back_step(*step, kv_ref, kvt_ref, lse_ref, first_ref, grad_ref, 8, dq_ref, scratch)
    earlier_steps(meta_ref, before, rows)(run)
    back_step(
        0, TILE, before, 0, True, 0, kv_own_ref, kvt_own_ref, lse_ref, first_ref, grad_ref, 8 + before, dq_ref, scratch
    )
    grad_q_ref[8 + HALO : 16 + HALO, :] = dq_ref[:, :PAIR].T[:8] * (DH**-0.5)
    starts = [meta_ref[STARTS + n] for n in range(8)]
    next_ref[...] = grad_ref[8 + before : 8 + before + TILE, :]
    unmix_rows(grad_ref, raw_ref, fix_ref, taps_ref[:, :KV], starts, before, sums_ref)
    starts = [s - (before - HALO) for s in starts]
    unmix_rows(grad_q_ref, raw_halo_ref, fix_q_ref, taps_ref[:, KV:], starts, HALO, sums_q_ref)
    half = before // 2
    two_ref[...] = grad_ref[8 : 8 + half, :].astype(BF16)
    one_ref[0:half, :] = grad_ref[8 + half : 8 + before, :].astype(BF16)
    queries = grad_q_ref[8 : 8 + HALO, :]
    one_ref[half : half + HALO, :] = jnp.concatenate([queries, jnp.zeros_like(queries)], axis=1).astype(BF16)


def earlier_back(meta, q, d_out_t, out_t, lse, first_row, kv, kvt, kv_own, kvt_own, raw, raw_halo, taps):
    rows, part = q.shape
    before = kv.shape[0]
    return pl.pallas_call(
        earlier_back_kernel,
        out_shape=(
            jax.ShapeDtypeStruct((part, rows), F32),
            jax.ShapeDtypeStruct((rows, KV), BF16),
            jax.ShapeDtypeStruct((rows + HALO, KV), BF16),
            jax.ShapeDtypeStruct((TILE, KV), F32),
            jax.ShapeDtypeStruct((8, KV), F32),
            jax.ShapeDtypeStruct((8, part), F32),
        ),
        grid=(1,),
        in_specs=[pl.BlockSpec(memory_space=pltpu.SMEM)]
        + [whole()] * 7
        + [
            pl.BlockSpec((TILE, KV), lambda i: (0, 0)),
            pl.BlockSpec((KV, TILE), lambda i: (0, 0)),
            whole(),
            whole(),
            whole(),
        ],
        out_specs=tuple([whole()] * 6),
        scratch_shapes=[
            pltpu.VMEM((8 + before + TILE + 8, KV), F32),
            pltpu.VMEM((8 + HALO + 8, part), F32),
            pltpu.VMEM((16, KV), F32),
            pltpu.VMEM((16, part), F32),
            *back_scratch(rows),
        ],
        compiler_params=params(34),
        cost_estimate=COST,
        name="earlier_back",
    )(meta, q, d_out_t, out_t, lse, first_row, kv, kvt, kv_own, kvt_own, raw, raw_halo, taps)


def own_back_kernel(
    meta_ref, q_ref, dt_ref, ot_ref, lse_ref, first_ref, dq_in_ref, kv_ref, kvt_ref, raw_ref, taps_ref, next_ref,
    normed_e_ref, two_ref, one_ref, normed_ref, out_keep_ref, out_near_ref, out_far_ref,
    d_raw_ref, sums_ref, mix_ref, dq_ref, grad_ref, fix_ref, *scratch,
):
    rows = kv_ref.shape[0]
    base = REACH * rows
    grad_ref[...] = jnp.zeros_like(grad_ref)
    grad_ref[8 : 8 + TILE, :KV] = next_ref[...]
    dq_ref[...] = dq_in_ref[...]
    back_prepare(meta_ref, q_ref, dt_ref, ot_ref, scratch)
    row = TILE
    while row < rows:
        keys = TILE if row % STEP else STEP
        back_step(
            row, keys, base + row, row, True, row, kv_ref, kvt_ref, lse_ref, first_ref, grad_ref, 8, dq_ref, scratch
        )
        row += keys
    for lanes in query_tiles(rows):
        grad_ref[8 + lanes.start : 8 + lanes.stop, KV:] = dq_ref[:, lanes].T * (DH**-0.5)
    starts = [meta_ref[STARTS + n] - base for n in range(8)]
    unmix_rows(grad_ref, raw_ref, fix_ref, taps_ref[...], starts, rows, sums_ref)
    d_raw_ref[...] = grad_ref[8 : 8 + rows, :].astype(BF16)
    part = out_keep_ref.shape[0]
    out_grad = out_keep_ref[...].astype(F32) + out_near_ref[0].astype(F32) + out_far_ref[...].astype(F32)
    for n in range(normed_ref.shape[1] // TILE):
        lanes = slice(n * TILE, (n + 1) * TILE)
        grad = mm(normed_ref[:, lanes], d_raw_ref[...], 0, 0)
        earlier = mm(normed_e_ref[:rows, lanes], two_ref[...], 0, 0)
        earlier = earlier + mm(normed_e_ref[rows:, lanes], one_ref[:rows, :], 0, 0)
        halo = mm(normed_e_ref[2 * rows - HALO :, lanes], one_ref[rows:, :], 0, 0)[:, :part]
        mix_ref[lanes, :KV] = (grad[:, :KV] + earlier).astype(BF16)
        rest = jnp.concatenate([grad[:, KV:] + halo, out_grad[:, lanes].T], axis=1)
        mix_ref[lanes, KV:] = rest.astype(BF16)


def own_back(
    meta, q, d_out_t, out_t, lse, first_row, dq_t, kv, kvt, raw, taps, grad_next, normed_e, two, one, normed, *grad_out
):
    rows, part = q.shape
    width = raw.shape[1]
    return pl.pallas_call(
        own_back_kernel,
        out_shape=(
            jax.ShapeDtypeStruct((rows, width), BF16),
            jax.ShapeDtypeStruct((8, width), F32),
            jax.ShapeDtypeStruct((normed.shape[1], width + part), BF16),
        ),
        in_specs=[pl.BlockSpec(memory_space=pltpu.SMEM)] + [whole()] * 18,
        out_specs=(whole(), whole(), whole()),
        scratch_shapes=[
            pltpu.VMEM((part, rows), F32),
            pltpu.VMEM((8 + rows + 8, width), F32),
            pltpu.VMEM((16, width), F32),
            *back_scratch(rows),
        ],
        compiler_params=params(34),
        cost_estimate=COST,
        name="own_back",
    )(
        meta, q, d_out_t, out_t, lse, first_row, dq_t, kv, kvt, raw, taps, grad_next,
        normed_e, two, one, normed, *grad_out,
    )


def after_attend_kernel(a0, a1, a2, a3, w0, w1, w2, w3, x_ref, gain_ref, hidden_ref, normed_ref):
    branch = mm(a0[...], w0[...], 0, 0)
    for a, w in ((a1, w1), (a2, w2), (a3, w3)):
        branch = branch + mm(a[...], w[...], 0, 0)
    hidden = x_ref[...].astype(F32) + branch
    hidden_ref[...] = hidden
    factor = lax.rsqrt(jnp.mean(hidden * hidden, axis=-1, keepdims=True) + EPS)
    normed_ref[...] = (hidden * factor * gain_ref[...]).astype(BF16)


def after_attend(attended, w_out, x, gain):
    rows, dim = x.shape
    return pl.pallas_call(
        after_attend_kernel,
        out_shape=(jax.ShapeDtypeStruct((rows, dim), F32), jax.ShapeDtypeStruct((rows, dim), BF16)),
        in_specs=[whole()] * 10,
        out_specs=(whole(), whole()),
        compiler_params=params(),
        cost_estimate=COST,
        name="after_attend",
    )(*attended, *w_out, x, gain)


def feed_kernel(x0, x2, x1, x3, cot_ref, up_ref, down_ref, x_ref, act_ref, d_up_ref, keep_ref, send_ref):
    def half(first, second, back_ref):
        x = jnp.concatenate([first[...], second[...]], axis=0)
        x_ref[...] = x
        up = mm(x, up_ref[...])
        pos = jnp.maximum(up, 0.0)
        act_ref[...] = (pos * pos).astype(BF16)
        d_act = mm(cot_ref[...], down_ref[...])
        d_up = (d_act * 2.0 * pos).astype(BF16)
        d_up_ref[...] = d_up
        back_ref[...] = mm(d_up, up_ref[...], 1, 1).astype(BF16)

    @pl.when(pl.program_id(0) == 0)
    def _():
        half(x0, x2, keep_ref)

    @pl.when(pl.program_id(0) == 1)
    def _():
        half(x1, x3, send_ref)


def feed(x, cot, w_up, w_down_t):
    rows, dim = cot.shape
    units = w_up.shape[1]
    step = rows // 2
    tile = lambda n: pl.BlockSpec((step, n), lambda i: (i, 0))
    return pl.pallas_call(
        feed_kernel,
        out_shape=(
            jax.ShapeDtypeStruct((rows, dim), BF16),
            jax.ShapeDtypeStruct((rows, units), BF16),
            jax.ShapeDtypeStruct((rows, units), BF16),
            jax.ShapeDtypeStruct((step, dim), BF16),
            jax.ShapeDtypeStruct((step, dim), BF16),
        ),
        grid=(2,),
        in_specs=[whole()] * 4 + [tile(dim), whole(), whole()],
        out_specs=(tile(dim), tile(units), tile(units), whole(), whole()),
        compiler_params=params(),
        cost_estimate=COST,
        name="feed",
    )(*x, cot, w_up, w_down_t)


def feed_rest_kernel(x_ref, d_up_ref, cot_ref, act_ref, down_ref, grads_ref, keep_ref, send_ref):
    grads_ref[0] = mm(x_ref[...], d_up_ref[...], 0, 0).astype(BF16)
    grads_ref[1] = mm(cot_ref[...], act_ref[...], 0, 0).astype(BF16)
    out = mm(act_ref[...], down_ref[...], 1, 1).astype(BF16)
    half = out.shape[0] // 2
    keep_ref[...] = out[:half]
    send_ref[...] = out[half:]


def feed_rest(x, d_up, cot, act, w_down_t):
    rows, dim = x.shape
    units = act.shape[1]
    block = pl.BlockSpec((rows, TILE), lambda i: (0, i))
    half = pl.BlockSpec((rows // 2, TILE), lambda i: (0, i))
    return pl.pallas_call(
        feed_rest_kernel,
        out_shape=(
            jax.ShapeDtypeStruct((2, dim, units), BF16),
            jax.ShapeDtypeStruct((rows // 2, dim), BF16),
            jax.ShapeDtypeStruct((rows // 2, dim), BF16),
        ),
        grid=(dim // TILE,),
        in_specs=[block, whole(), block, whole(), pl.BlockSpec((TILE, units), lambda i: (i, 0))],
        out_specs=(pl.BlockSpec((2, TILE, units), lambda i: (0, i, 0)), half, half),
        compiler_params=params(),
        cost_estimate=COST,
        name="feed_rest",
    )(x, d_up, cot, act, w_down_t)


def before_back_kernel(
    s_ref, r_ref, hidden_ref, gain_ref, cot_ref, w0, w1, w2, w3, a0, a1, a2, a3,
    d_hidden_ref, d0, d1, d2, d3, keep_ref, keep_far_ref, send_ref, sum_ref,
):
    d_normed = s_ref[...].astype(F32) + r_ref[...].astype(F32)
    hidden = hidden_ref[...]
    factor = lax.rsqrt(jnp.mean(hidden * hidden, axis=-1, keepdims=True) + EPS)
    unit = hidden * factor
    sum_ref[...] = jnp.sum(d_normed * unit, axis=0, keepdims=True)
    scaled = d_normed * gain_ref[...]
    inner = jnp.mean(scaled * unit, axis=-1, keepdims=True)
    d_hidden = cot_ref[...].astype(F32) + factor * (scaled - unit * inner)
    d_hidden_ref[...] = d_hidden
    d_branch = d_hidden.astype(BF16)
    for w, d in ((w0, d0), (w1, d1), (w2, d2), (w3, d3)):
        d[...] = mm(w[...], d_branch, 1, 1).astype(BF16)
    for a, to in ((a0, keep_ref), (a1, keep_far_ref), (a2, send_ref.at[0]), (a3, send_ref.at[1])):
        to[...] = mm(a[...], d_branch).astype(BF16)


def before_back(chip_sum, far_sum, hidden, gain, cot, w_out, attended):
    rows, dim = hidden.shape
    part = w_out[0].shape[0]
    return pl.pallas_call(
        before_back_kernel,
        out_shape=(
            jax.ShapeDtypeStruct((rows, dim), F32),
            *[jax.ShapeDtypeStruct((part, rows), BF16)] * 4,
            *[jax.ShapeDtypeStruct((part, dim), BF16)] * 2,
            jax.ShapeDtypeStruct((2, part, dim), BF16),
            jax.ShapeDtypeStruct((1, dim), F32),
        ),
        in_specs=[whole()] * 13,
        out_specs=tuple([whole()] * 9),
        compiler_params=params(),
        cost_estimate=COST,
        name="before_back",
    )(chip_sum, far_sum, hidden, gain, cot, *w_out, *attended)


def d_normed_kernel(meta_ref, own_ref, one_ref, halo_ref, two_ref, x_ref, w_ref, keep_ref, send_ref, sum_ref):
    i = pl.program_id(0)
    step = own_ref.shape[0]
    later = jnp.where(meta_ref[NEXT_ONE] == 1, one_ref[...].astype(F32), 0.0)
    later = later + jnp.where(meta_ref[NEXT_TWO] == 1, two_ref[...].astype(F32), 0.0)
    own = own_ref[...].astype(F32)
    queries = own[:, KV:]
    part = queries.shape[1]
    last = (i == pl.num_programs(0) - 1) & (meta_ref[NEXT_ONE] == 1)
    halo = jnp.where(last, halo_ref[...].astype(F32)[:, :part], 0.0)
    queries = queries + jnp.concatenate([jnp.zeros((step - HALO, part), F32), halo], axis=0)
    d_raw = jnp.concatenate([own[:, :KV] + later, queries], axis=1).astype(BF16)
    d_normed = mm(d_raw, w_ref[...], 1, 1)
    for n in range(step // TILE):
        slot = slot_of(i * (step // TILE) + n, meta_ref)
        rows = d_normed[n * TILE : (n + 1) * TILE].astype(BF16)
        to = pl.ds(pl.multiple_of((slot & 1) * TILE, TILE), TILE)

        @pl.when(slot < 2)
        def _(rows=rows, to=to):
            keep_ref[to, :] = rows

        @pl.when(slot >= 2)
        def _(rows=rows, to=to):
            send_ref[to, :] = rows

    x = x_ref[...].astype(F32)
    unit = x * lax.rsqrt(jnp.mean(x * x, axis=-1, keepdims=True) + EPS)

    @pl.when(i == 0)
    def _():
        sum_ref[...] = jnp.zeros_like(sum_ref)

    sum_ref[...] += jnp.sum(d_normed * unit, axis=0, keepdims=True)


def d_normed_parts(meta, own, one, two, x, w):
    rows, dim = x.shape
    width = w.shape[1]
    step = 2 * TILE
    tile = lambda n: pl.BlockSpec((step, n), lambda i, *_: (i, 0))
    return pl.pallas_call(
        d_normed_kernel,
        out_shape=(
            jax.ShapeDtypeStruct((rows // 2, dim), BF16),
            jax.ShapeDtypeStruct((rows // 2, dim), BF16),
            jax.ShapeDtypeStruct((1, dim), F32),
        ),
        grid_spec=pltpu.PrefetchScalarGridSpec(
            num_scalar_prefetch=1,
            grid=(rows // step,),
            in_specs=[
                tile(width),
                tile(KV),
                pl.BlockSpec((HALO, KV), lambda i, *_: (rows // HALO, 0)),
                tile(KV),
                tile(dim),
                whole(),
            ],
            out_specs=(whole(), whole(), pl.BlockSpec((1, dim), lambda i, *_: (0, 0))),
        ),
        compiler_params=params(),
        cost_estimate=COST,
        name="d_normed_parts",
    )(meta, own, one, one, two, x, w)


def grad_tokens_kernel(s_ref, r_ref, x_ref, gain_ref, d_hidden_ref, out_ref):
    d_normed = s_ref[...].astype(F32) + r_ref[...].astype(F32)
    x = x_ref[...].astype(F32)
    factor = lax.rsqrt(jnp.mean(x * x, axis=-1, keepdims=True) + EPS)
    unit = x * factor
    scaled = d_normed * gain_ref[...]
    inner = jnp.mean(scaled * unit, axis=-1, keepdims=True)
    out_ref[...] = (d_hidden_ref[...] + factor * (scaled - unit * inner)).astype(BF16)


def grad_tokens_own(chip_sum, far_sum, x, gain, d_hidden):
    return pl.pallas_call(
        grad_tokens_kernel,
        out_shape=jax.ShapeDtypeStruct(x.shape, BF16),
        in_specs=[whole()] * 5,
        out_specs=whole(),
        compiler_params=params(),
        name="grad_tokens_own",
    )(chip_sum, far_sum, x, gain, d_hidden)


def assemble_kernel(meta_ref, *refs):
    *pieces, out_ref = refs
    for piece, d in zip(pieces, (0, 2, 1, 3)):

        @pl.when(pl.program_id(0) == (meta_ref[0] ^ d))
        def _(piece=piece):
            out_ref[...] = piece[...].astype(out_ref.dtype)


def by_place(meta, pieces, dtype):
    rows, dim = pieces[0].shape
    return pl.pallas_call(
        assemble_kernel,
        out_shape=jax.ShapeDtypeStruct((4 * rows, dim), dtype),
        grid_spec=pltpu.PrefetchScalarGridSpec(
            num_scalar_prefetch=1,
            grid=(4,),
            in_specs=[whole()] * 4,
            out_specs=pl.BlockSpec((rows, dim), lambda i, *_: (i, 0)),
        ),
        compiler_params=params(),
        cost_estimate=COST,
        name="assemble",
    )(meta, *pieces)


def sum_halves(keep, send):
    return (keep.astype(F32) + swap(send, "head", 1).astype(F32)).astype(BF16)


def body(
    tokens,
    seg_ids,
    gain_attn,
    w_query,
    w_key,
    w_value,
    conv_kernels,
    w_out,
    gain_ffn,
    w_up,
    w_down,
    cotangent,
):
    rows, dim = tokens.shape
    part = conv_kernels.shape[2]
    quarter = rows // lax.axis_size("head")
    blk = lax.axis_index("blk")
    head = lax.axis_index("head")
    groups = bit_groups("blk")
    together = lax.optimization_barrier
    own_quarter = lax.dynamic_slice_in_dim(tokens, head * quarter, quarter)
    two = moved(own_quarter, "blk", 2)
    shard, units = w_up.shape
    w_mix = jnp.concatenate([w_query, w_key, w_value], axis=1)
    packed, down_some = pack(w_up, w_out, w_down)
    w_some = gathered(w_mix[None], "blk", groups[:-1], w_mix.shape)
    one = swap(jnp.where(bit_of("blk", 0), two, own_quarter), "blk", 1)
    pieces = [*quarters(two), *quarters(one)]
    halo = moved(tokens[rows - HALO :], "blk", 1)
    w_mix = gathered(w_some, "blk", groups[-1:], w_mix.shape).reshape(dim, 3 * part)
    packed, _, _ = together((packed, w_some, two))
    span = (REACH + 1) * rows
    padded_ids = jnp.pad(seg_ids, (REACH * rows, 0), constant_values=-1)
    window = lax.dynamic_slice_in_dim(padded_ids, blk * rows, span)
    starts = jnp.sum((window[None, :] <= window[0] + jnp.arange(8)[:, None]).astype(jnp.int32), axis=1)
    place = jnp.arange(REACH * rows, span, dtype=jnp.int32)
    first_row = jnp.max(jnp.where(starts[:, None] <= place, starts[:, None], 0), axis=0)
    low = first_row[::TILE] // TILE
    full = (first_row[TILE - 1 :: TILE] + TILE - 1) // TILE
    last = lax.axis_size("blk") - 1
    exists = jnp.stack([blk >= 1, blk >= 2, blk + 1 <= last, blk + 2 <= last])
    meta = jnp.concatenate([head[None], low, full, starts, exists]).astype(jnp.int32)
    first_row = first_row[None]
    taps = arranged(*conv_kernels)
    gain_one, gain_two = gain_attn[None], gain_ffn[None]

    w_mix, *pieces[:2], pieces[4] = together((w_mix, *pieces[:2], pieces[4]))
    w_mix, raw_halo, raw, normed, q, kv, kvt = project_own(meta, tokens, halo, gain_one, w_mix, taps)
    packed_some = gathered(packed[None], "blk", groups[:-1], packed.shape, raw)
    down_some, _ = together((down_some, raw))
    q, pieces[5] = together((q, pieces[5]))
    acc_own, stat_own = attend_own(q, kv, kvt, first_row)
    wide = gathered(packed_some, "blk", groups[-1:], packed.shape, acc_own)
    down_some = gathered(down_some[None], "blk", groups[:-1], (shard, dim), acc_own)
    full_up = wide[:, :shard].reshape(dim, units)
    out_full = wide[:, shard:].reshape(-1, packed.shape[0] - shard, units // part, part)
    out_full = jnp.swapaxes(out_full, 1, 2).reshape(dim, part).T
    out_far = swap(out_full, "head", 2)
    down_t = gathered(down_some, "blk", groups[-1:], (shard, dim)).reshape(dim, units)
    raw_e, normed_e, kv_e, kvt_e = project_earlier(meta, pieces, gain_one, w_mix, taps)
    out_far, out_full, _ = together((out_far, out_full, raw_e))
    out_pieces = [out_full, out_far, swap(out_full, "head", 1), swap(out_far, "head", 1)]
    hi, lo = bit_of("head", 1), bit_of("head", 0)
    cot = cotangent.reshape(2, 2, quarter, dim)
    cot = jnp.where(hi, cot[::-1], cot)
    cot = jnp.where(lo, cot[:, ::-1], cot)
    cot = jnp.swapaxes(cot, 0, 1).reshape(rows, dim)
    kv_late, cot, full_up, *out_pieces = together((kv_e, cot, full_up, *out_pieces))
    att, out_t, lse = attend_earlier(meta, q, kv_late, kvt_e, first_row, acc_own, stat_own)

    near = swap(att[2:], "head", 1)
    across = swap(jnp.stack([att[1], near[1]]), "head", 2)
    attended = (att[0], across[0], near[0], across[1])
    quarter_late, down_t = together((own_quarter, down_t))
    hidden, normed_two = after_attend(attended, out_pieces, quarter_late, gain_two)
    ffn_in, act, d_up, *back = feed(quarters(normed_two), cot, full_up, down_t)
    chip_back = sum_halves(*back)
    far_back = swap(chip_back[quarter:], "head", 2)
    feed_grads, *ffn = feed_rest(ffn_in, d_up, cot, act, down_t)
    near_parts = chosen(feed_grads.reshape(2, -1, shard, units), "blk", groups[-1])
    far_back, *near_parts = together((far_back, *near_parts))
    near_parts = received(near_parts, "blk", groups[-1])
    d_hidden, *d_outs, keep_out, keep_far, send_out, gain_two_part = before_back(
        chip_back[:quarter], far_back, hidden, gain_two, cot[:quarter], out_pieces, attended
    )
    across = swap(jnp.stack([d_outs[1], d_outs[3]]), "head", 2)
    near = swap(jnp.stack([d_outs[2], across[1]]), "head", 1)
    d_out_t = jnp.stack([d_outs[0], across[0], near[0], near[1]])
    chip_ffn = sum_halves(*ffn)
    near_out = swap(send_out, "head", 1)
    far_out = swap(total_of([keep_far, near_out[1]]).astype(BF16), "head", 2)
    d_out_t, chip_ffn = together((d_out_t, chip_ffn))
    far_ffn = swap(chip_ffn[quarter:], "head", 2)

    dq_t, d_two, d_one, grad_next, sums_before, sums_halo = earlier_back(
        meta, q, d_out_t, out_t, lse, first_row, kv_e, kvt_e, kv, kvt, raw_e, raw_halo, taps
    )
    from_two = moved(d_two, "blk", -2)
    from_one = moved(d_one, "blk", -1)
    dq_t, far_ffn, far_out = together((dq_t, far_ffn, far_out))
    d_raw, sums_own, grad_mix = own_back(
        meta, q, d_out_t, out_t, lse, first_row, dq_t, kv, kvt, raw, taps, grad_next,
        normed_e, d_two, d_one, normed, keep_out, near_out, far_out,
    )
    chip_ffn, far_ffn, _ = together((chip_ffn, far_ffn, d_raw))
    output = list(quarters((hidden + total_of([chip_ffn[:quarter], far_ffn])).astype(BF16)))
    gain_two_part, _ = together((gain_two_part, d_raw))
    gain_two_part = sum_everywhere(gain_two_part, "head", [(0,), (1,)])
    d_raw, gain_two_part, *more = together((d_raw, gain_two_part, *output, *near_parts))
    output, near_parts = more[:4], more[4:]
    mix_parts = chosen(grad_mix.reshape(1, -1, shard, 4 * part), "blk", groups[-1])
    mix_parts = received(mix_parts, "blk", groups[-1])
    *back, gain_one_part = d_normed_parts(meta, d_raw, from_one, from_two, tokens, w_mix)
    chip_back = sum_halves(*back)
    far_back = swap(chip_back[quarter:], "head", 2)
    _, *near_parts = together((back[0], *near_parts))
    feed_grads = sum_scatter(total_of(near_parts).astype(BF16), "blk", groups[:-1])
    _, gain_one_part = together((chip_back, gain_one_part))
    gain_one_part = sum_everywhere(gain_one_part, "head", [(0,), (1,)])
    grad_tokens = grad_tokens_own(chip_back[:quarter], far_back, own_quarter, gain_one, d_hidden)
    grad_tokens = list(quarters(grad_tokens))
    grad_tokens[2], gain_one_part, output[0], *mix_parts = together(
        (grad_tokens[2], gain_one_part, output[0], *mix_parts)
    )
    grad_tokens = by_place(meta, grad_tokens, F32)
    mix_parts = sum_scatter(total_of(mix_parts).astype(BF16), "blk", groups[:-1])

    output = by_place(meta, output, BF16)
    feed_grads = total_of(feed_grads).reshape(2, shard, units)
    grad_up_shard, grad_down_shard = feed_grads[0], feed_grads[1].T
    mix_shard = total_of(mix_parts).reshape(shard, 4 * part)
    grad_query_shard, grad_key_shard, grad_value_shard = separated(mix_shard[:, : 3 * part])
    grad_out_shard = mix_shard[:, 3 * part :].T

    taps_part = jnp.concatenate([sums_own[:3, :KV] + sums_before[:3], sums_own[:3, KV:] + sums_halo[:3]], axis=1)
    taps_part = jnp.stack(separated(taps_part)).reshape(-1)
    small = jnp.concatenate([gain_two_part[0], gain_one_part[0], taps_part])
    small = sum_everywhere(small, "blk", groups)
    grad_gain_ffn, grad_gain_attn = small[:dim], small[dim : 2 * dim]
    grad_kernels = small[2 * dim :].reshape(3, 3, part)
    return (
        output,
        grad_tokens,
        grad_gain_attn,
        grad_query_shard,
        grad_key_shard,
        grad_value_shard,
        grad_kernels,
        grad_out_shard,
        grad_gain_ffn,
        grad_up_shard,
        grad_down_shard,
    )


def solution(mesh):
    return jax.shard_map(
        body,
        mesh=mesh,
        in_specs=(
            P("blk", None),
            P(),
            P(),
            P("blk", "head"),
            P("blk", "head"),
            P("blk", "head"),
            P(None, None, "head"),
            P("head", "blk"),
            P(),
            P("blk", "head"),
            P("head", "blk"),
            P("blk", None),
        ),
        out_specs=(
            P("blk", None),
            P("blk", None),
            P(),
            P("blk", "head"),
            P("blk", "head"),
            P("blk", "head"),
            P(None, None, "head"),
            P("head", "blk"),
            P(),
            P("blk", "head"),
            P("head", "blk"),
        ),
        check_vma=False,
    )
```

time: 389 us -> 301 us (0.77)
  Pallas kernels: 107 us -> 65.8 us
  starting transfers between devices: 95.2 us -> 73.7 us
  other arithmetic: 36.7 us -> 21.9 us
  waiting for transfers between devices: 113 us -> 98.4 us
  local copies, waits for them, and re-layouts: 35.6 us -> 39.6 us
    pallas_call x7 -> x8, Pallas kernels: 60 us -> 33.1 us  [the longest x1 12 us: own_back(): pl.pallas_call(own_back_kernel, out_shape=(jax.ShapeDtypeStruct((rows, wi...]
    ppermute x56 -> x59, starting transfers between devices: 85.9 us -> 64.4 us  [swap(): lax.ppermute(x, axis, [(i, i ^ mask) for i in range(lax.axis_size(axis))])]
    unnamed x80 -> x140, local copies, waits for them, and re-layouts: 6.32 us -> 16.8 us
    ppermute x4, waiting for transfers between devices: 32 us -> 24 us  [moved(): lax.ppermute(x, axis, [(i, i + distance) for i in range(size) if 0 <= i +...]
    ppermute x56 -> x59, waiting for transfers between devices: 80.6 us -> 74.4 us  [swap(): lax.ppermute(x, axis, [(i, i ^ mask) for i in range(lax.axis_size(axis))])]
    another operation x6 -> x7, other arithmetic: 1.94 us -> 6.54 us  [in_order(): both = jnp.stack(pieces)]
    reshape x4 -> x3, local copies, waits for them, and re-layouts: 0.66 us -> 4.98 us  [the longest x1 2.72 us: body(): cot = cotangent.reshape(2, 2, quarter, dim)]
  transfers between devices with their start and end apart: 60 -> 63, of which waited for: 21 -> 22; matrix products, arithmetic and copies ran while one was open for 15% -> 15% of each run, Pallas kernels for 25% -> 19%
where the time goes in v2:
time: 301 us; the launch traced here: 302 us
  waiting for transfers between devices  98.4 us (33%)
  starting transfers between devices  73.7 us (24%)
  Pallas kernels  65.8 us (22%)
  local copies, waits for them, and re-layouts  39.6 us (13%)
  other arithmetic  21.9 us (7%)
    ppermute x59, waiting for transfers between devices, swap(): lax.ppermute(x, axis, [(i, i ^ mask) for i in range(lax.axis_size(axis))])  74.4 us
    ppermute x59, starting transfers between devices, swap(): lax.ppermute(x, axis, [(i, i ^ mask) for i in range(lax.axis_size(axis))])  64.4 us
    ppermute x4, waiting for transfers between devices, moved(): lax.ppermute(x, axis, [(i, i + distance) for i in range(size) if 0 <= i +...  24 us
    unnamed x140, local copies, waits for them, and re-layouts  16.8 us
    pallas_call x1, Pallas kernels, earlier_back(): pl.pallas_call(earlier_back_kernel, out_shape=(jax.ShapeDtypeStruct((part...  12.7 us
    pallas_call x1, Pallas kernels, own_back(): pl.pallas_call(own_back_kernel, out_shape=(jax.ShapeDtypeStruct((rows, wi...  12 us
    ppermute x4, starting transfers between devices, moved(): lax.ppermute(x, axis, [(i, i + distance) for i in range(size) if 0 <= i +...  9.29 us
    pallas_call x1, Pallas kernels, project_earlier(): pl.pallas_call(project_earlier_kernel, out_shape=(jax.ShapeDtypeStruct((s...  7.24 us
  transfers between devices with their start and end apart: 63, of which 22 were waited for; matrix products, arithmetic and copies ran while one was open for 15% of the time, Pallas kernels for 19%

profile of v2, /device:TPU:0, one launch (start us, length us, event | category | flops | bytes accessed | tf_op | source)
XLA Modules:
  0.0 301.6 jit_solution(5498189309478157787)
XLA Ops:
  1.6 5.1 %collective-permute-start.3 = (bf16[1,96,576]{2,1,0:T(8,128)(2,1)S(1)}, bf16[1,96,576]{2,1,0:T(8,128)(2,1)S(1)}, u32[]{:S(2)}, u32[]{:S(2)}) collective-permute-start(bf16[1,96,576]{2,1,0:T(8,128)(2,1)S(1)} %get-tuple-element.296), channel_id=1, source_target_pairs={{0,24},{4,28},{8,16},{12,20},{16,8},{20,12},{24,0},{28,4},{1,25},{... | collective-permute-start | bytes 331784 | tf_op jit(solution)/shard_map/ppermute | solution.py:35
  8.7 3.6 %collective-permute-start = (bf16[16,768]{1,0:T(8,128)(2,1)}, bf16[16,768]{1,0:T(8,128)(2,1)S(1)}, u32[]{:S(2)}, u32[]{:S(2)}) collective-permute-start(bf16[16,768]{1,0:T(8,128)(2,1)} %slice.152), channel_id=1, source_target_pairs={{0,4},{4,8},{8,12},{12,16},{16,20},{20,24},{24,28},{1,5},{5,9},{9,... | collective-permute-start | bytes 73736 | tf_op jit(solution)/shard_map/ppermute | solution.py:40
  13.3 3.2 %collective-permute-start.5 = (bf16[256,768]{1,0:T(8,128)(2,1)S(1)}, bf16[256,768]{1,0:T(8,128)(2,1)S(1)}, u32[]{:S(2)}, u32[]{:S(2)}) collective-permute-start(bf16[256,768]{1,0:T(8,128)(2,1)S(1)} %constant_dynamic-slice_fusion.6.x_ref), channel_id=1, source_target_pairs={{0,8},{4,12},{8,16},{12,20},{16,24},{20,28},{1,9},{5,13},{9,17},{1... | collective-permute-start | bytes 1179656 | tf_op jit(solution)/shard_map/ppermute | solution.py:40
  20.8 1.4 collective-permute-start.4
  22.2 1.8 collective-permute-done.5.refs_0_
  24.0 1.5 collective-permute-start.6
  29.1 2.5 collective-permute-start.13
  31.5 2.6 collective-permute-start.14
  37.5 5.7 %collective-permute-done.7.refs_4_ = bf16[256,768]{1,0:T(8,128)(2,1)} collective-permute-done((bf16[256,768]{1,0:T(8,128)(2,1)S(1)}, bf16[256,768]{1,0:T(8,128)(2,1)}, u32[]{:S(2)}, u32[]{:S(2)}) %collective-permute-start.7) | collective-permute-done | bytes 393248 | tf_op jit(solution)/shard_map/ppermute | solution.py:35
  43.3 4.7 %project_own.1 = (bf16[768,576]{1,0:T(8,128)(2,1)S(1)}, bf16[16,192]{1,0:T(8,128)(2,1)S(1)}, bf16[1024,576]{1,0:T(8,128)(2,1)S(1)}, bf16[1024,768]{1,0:T(8,128)(...) custom-call(s32[21]{0:T(128)S(1)} %concatenate.24.meta_ref, ...), custom_call_target="tpu_custom_call" | custom-call | flops 1 | bytes 1 | tf_op jit(solution)/shard_map/project_own/pallas_call | solution.py:233
  50.8 2.7 collective-permute-start.24
  55.4 1.8 collective-permute-start.16
  57.2 2.7 copy.50
  59.9 1.8 collective-permute-done.8.refs_5_
  61.7 3.6 %attend_own.1 = (f32[192,1024]{1,0:T(8,128)S(1)}, f32[16,1024]{1,0:T(8,128)S(1)}) custom-call(bf16[1024,192]{1,0:T(8,128)(2,1)S(1)} %get-tuple-element.118.q_ref, bf16[1024,384]{1,0:T(8,128)(2,1)S(1)} %get-tuple-element.132.kv_ref.kv_own_ref, bf16[384,1024]{1,0:T(8,128)(2,1)S(1)} %copy-done.5, s32[1,1024]{1,0:T(1,128)S(1)} %bitcast.121), custom_call_target="tpu_custom_call" | custom-call | flops 1 | bytes 1 | tf_op jit(solution)/shard_map/attend_own/pallas_call | solution.py:475
  68.4 1.7 collective-permute-start.25
  70.4 1.5 pad_maximum_fusion
  74.5 1.8 copy.54
  77.5 1.6 collective-permute-start.17
  79.0 2.4 reverse_select_fusion.1
  81.5 7.2 %project_earlier.1 = (bf16[2048,384]{1,0:T(8,128)(2,1)S(1)}, bf16[2048,768]{1,0:T(8,128)(2,1)S(1)}, bf16[2048,384]{1,0:T(8,128)(2,1)S(1)}, bf16[384,2048]{1,0:T(8,128)(2,1)S(1)}) custom-call(s32[21]{0:T(128)S(1)} %concatenate.24.meta_ref, bf16[256,768]{1,0:T(8,128)(2,1)S(1)} %collective-permute-done.5.refs_0_, bf16[256,768]{1,0:T(8,128)(2,1)S(1)} %copy-done.57, ...), custom_call_target="tpu_custom_call" | custom-call | flops 1 | bytes 1 | tf_op jit(solution)/shard_map/project_earlier/pallas_call | solution.py:304
  88.7 1.7 copy-done.21
  92.5 1.6 copy-done.63
  94.2 1.4 pad_maximum_fusion.1
  95.7 1.4 attend_earlier.1
  99.5 6.3 %collective-permute-done.21 = bf16[2,192,256]{2,1,0:T(8,128)(2,1)S(1)} collective-permute-done((bf16[2,192,256]{2,1,0:T(8,128)(2,1)S(1)}, bf16[2,192,256]{2,1,0:T(8,128)(2,1)S(1)}, u32[]{:S(2)}, u32[]{:S(2)}) %collective-permute-start.21) | collective-permute-done | bytes 196640 | tf_op jit(solution)/shard_map/ppermute | solution.py:35
  107.2 9.9 %collective-permute-done.26.x2 = bf16[256,768]{1,0:T(8,128)(2,1)S(1)} collective-permute-done((bf16[256,768]{1,0:T(8,128)(2,1)S(1)}, bf16[256,768]{1,0:T(8,128)(2,1)S(1)}, u32[]{:S(2)}, u32[]{:S(2)}) %collective-permute-start.26) | collective-permute-done | bytes 393248 | tf_op jit(solution)/shard_map/ppermute | solution.py:35
  117.2 1.7 collective-permute-done.28.x3
  118.9 4.3 %feed.1 = (bf16[1024,768]{1,0:T(8,128)(2,1)S(1)}, bf16[1024,768]{1,0:T(8,128)(2,1)S(1)}, bf16[1024,768]{1,0:T(8,128)(2,1)S(1)}, bf16[512,768]{1,0:T(8,128)(2,1)S(1)}, bf16[512,768]{1,0:T(8,128)(2,1)S(1)}) custom-call(bf16[256,768]{1,0:T(8,128)(2,1)S(1)} %get-tuple-element.155.x0, bf16[256,768]{1,0:T(8,128)(2,1)S(1)} %collective-permute-done.26.x2, ...), custom_call_target="tpu_custom_call" | custom-call | flops 1 | bytes 1 | tf_op jit(solution)/shard_map/feed/pallas_call | solution.py:826
  124.5 2.1 collective-permute-done.29
  128.4 1.4 copy-done.29
  129.8 1.4 copy-done.31
  131.2 1.4 copy-done.33
  132.6 4.7 %feed_rest.1 = (bf16[2,768,768]{2,1,0:T(8,128)(2,1)S(1)}, bf16[512,768]{1,0:T(8,128)(2,1)S(1)}, bf16[512,768]{1,0:T(8,128)(2,1)S(1)}) custom-call(bf16[1024,768]{1,0:T(8,128)(2,1)S(1)} %copy-done.29, bf16[1024,768]{1,0:T(8,128)(2,1)S(1)} %copy-done.33, bf16[1024,768]{1,0:T(8,128)(2,1)S(1)} %bitcast.106, bf16[1024,768]{1,0:T(8,128)(2,1)S(1)} %copy-done.31, ...), custom_call_target="tpu_custom_call" | custom-call | flops 1 | bytes 1 | tf_op jit(solution)/shard_map/feed_rest/pallas_call | solution.py:858
  137.5 1.7 dynamic-slice_bitcast_fusion
  139.9 2.5 before_back.1
  142.5 1.6 collective-permute-start.31
  144.3 5.6 %collective-permute-done.31 = bf16[2,192,256]{2,1,0:T(8,128)(2,1)S(1)} collective-permute-done((bf16[2,192,256]{2,1,0:T(8,128)(2,1)S(1)}, bf16[2,192,256]{2,1,0:T(8,128)(2,1)S(1)}, u32[]{:S(2)}, u32[]{:S(2)}) %collective-permute-start.31) | collective-permute-done | bytes 196640 | tf_op jit(solution)/shard_map/ppermute | solution.py:35
  151.5 1.6 collective-permute-start.34
  153.7 7.1 %collective-permute-start.42 = (bf16[2,4,96,768]{3,2,1,0:T(8,128)(2,1)}, bf16[2,4,96,768]{3,2,1,0:T(8,128)(2,1)}, u32[]{:S(2)}, u32[]{:S(2)}) collective-permute-start(bf16[2,4,96,768]{3,2,1,0:T(8,128)(2,1)} %get-tuple-element.196), channel_id=1, source_target_pairs={{0,4},{4,0},{8,12},{12,8},{16,20},{20,16},{24,28},{28,24},{1,5},{5... | collective-permute-start | bytes 3538952 | tf_op jit(solution)/shard_map/ppermute | solution.py:35
  160.9 12.7 %earlier_back.1 = (f32[192,1024]{1,0:T(8,128)S(1)}, bf16[1024,384]{1,0:T(8,128)(2,1)}, bf16[1040,384]{1,0:T(8,128)(2,1)}, f32[256,384]{1,0:T(8,128)S(1)}, f32[8,384]{1,0:T(8,128)S(1)}, /*index=5*/f32[8,192]{1,0:T(8,128)S(1)}) custom-call(s32[21]{0:T(128)S(1)} %concatenate.24.meta_ref, bf16[1024,192]{1,0:T(8,128)(2,1)S(1)} %get-tuple-element.118.q_ref, ...), custom_call_target="tpu_custom_call" | custom-call | flops 1 | bytes 1 | tf_op jit(solution)/shard_map/earlier_back/pallas_call | solution.py:678
  174.9 12.0 %own_back.1 = (bf16[1024,576]{1,0:T(8,128)(2,1)S(1)}, f32[8,576]{1,0:T(8,128)S(1)}, bf16[768,768]{1,0:T(8,128)(2,1)S(1)}) custom-call(s32[21]{0:T(128)S(1)} %concatenate.24.meta_ref, bf16[1024,192]{1,0:T(8,128)(2,1)S(1)} %get-tuple-element.118.q_ref, bf16[4,192,256]{2,1,0:T(8,128)(2,1)S(1)} %pad_maximum_fusion.6.dt_ref, f32[192,1024]{1,0:T(8,128)S(1)} %copy-done.18, ...), custom_call_target="tpu_custom_call" | custom-call | flops 1 | bytes 1 | tf_op jit(solution)/shard_map/own_back/pallas_call | solution.py:753
  187.1 1.6 collective-permute-start.39
  192.0 5.6 %collective-permute-done.38 = f32[1,768]{1,0:T(1,128)S(1)} collective-permute-done((f32[1,768]{1,0:T(1,128)S(1)}, f32[1,768]{1,0:T(1,128)S(1)}, u32[]{:S(2)}, u32[]{:S(2)}) %collective-permute-start.38) | collective-permute-done | bytes 3104 | tf_op jit(solution)/shard_map/ppermute | solution.py:35
  198.2 2.3 dynamic-slice_bitcast_fusion.2
  200.6 4.6 %collective-permute-start.50 = (bf16[1,4,96,768]{3,2,1,0:T(8,128)(2,1)}, bf16[1,4,96,768]{3,2,1,0:T(8,128)(2,1)}, u32[]{:S(2)}, u32[]{:S(2)}) collective-permute-start(bf16[1,4,96,768]{3,2,1,0:T(8,128)(2,1)} %get-tuple-element.270), channel_id=1, source_target_pairs={{0,4},{4,0},{8,12},{12,8},{16,20},{20,16},{24,28},{28,24},{1,5},{5... | collective-permute-start | bytes 1769480 | tf_op jit(solution)/shard_map/ppermute | solution.py:35
  205.1 22.2 %collective-permute-done.44.two_ref = bf16[1024,384]{1,0:T(8,128)(2,1)} collective-permute-done((bf16[1024,384]{1,0:T(8,128)(2,1)}, bf16[1024,384]{1,0:T(8,128)(2,1)}, u32[]{:S(2)}, u32[]{:S(2)}) %collective-permute-start.44) | collective-permute-done | bytes 786464 | tf_op jit(solution)/shard_map/ppermute | solution.py:40
  228.7 4.5 %d_normed_parts.1 = (bf16[512,768]{1,0:T(8,128)(2,1)S(1)}, bf16[512,768]{1,0:T(8,128)(2,1)S(1)}, f32[1,768]{1,0:T(1,128)S(1)}) custom-call(s32[21]{0:T(128)S(1)} %concatenate.24.meta_ref, bf16[1024,576]{1,0:T(8,128)(2,1)S(1)} %copy-done.40, bf16[1040,384]{1,0:T(8,128)(2,1)} %collective-permute-done.43.one_ref.halo_ref, ...), custom_call_target="tpu_custom_call" | custom-call | flops 1 | bytes 1 | tf_op jit(solution)/shard_map/d_normed_parts/pallas_call | solution.py:955
  233.4 1.6 add_convert_fusion
  237.6 1.7 collective-permute-start.62
  240.3 1.6 collective-permute-start.60
  242.1 5.0 %collective-permute-done.46.r_ref = bf16[256,768]{1,0:T(8,128)(2,1)S(1)} collective-permute-done((bf16[256,768]{1,0:T(8,128)(2,1)S(1)}, bf16[256,768]{1,0:T(8,128)(2,1)S(1)}, u32[]{:S(2)}, u32[]{:S(2)}) %collective-permute-start.46) | collective-permute-done | bytes 393248 | tf_op jit(solution)/shard_map/ppermute | solution.py:35
  247.5 2.2 collective-permute-done.62
  249.7 16.9 %collective-permute-done.61 = bf16[2,1,96,768]{3,2,1,0:T(8,128)(2,1)} collective-permute-done((bf16[2,1,96,768]{3,2,1,0:T(8,128)(2,1)}, bf16[2,1,96,768]{3,2,1,0:T(8,128)(2,1)}, u32[]{:S(2)}, u32[]{:S(2)}) %collective-permute-start.61) | collective-permute-done | bytes 294944 | tf_op jit(solution)/shard_map/ppermute | solution.py:35
  270.2 1.5 collective-permute-done.49
  273.0 2.6 collective-permute-start.55
  275.6 1.9 collective-permute-start.53
  277.4 1.4 add_convert_fusion.4
  278.8 1.4 collective-permute-done.54
  281.0 1.5 collective-permute-start.59
  283.5 2.0 collective-permute-start.57
  285.4 3.4 %assemble.2 = bf16[1024,768]{1,0:T(8,128)(2,1)} custom-call(s32[21]{0:T(128)S(1)} %concatenate.24.meta_ref, bf16[256,768]{1,0:T(8,128)(2,1)S(1)} %add_convert_fusion.5.refs_0_, bf16[256,768]{1,0:T(8,128)(2,1)S(1)} %collective-permute-done.39.refs_1_, bf16[256,768]{1,0:T(8,128)(2,1)} %collective-permute-done.40.refs_2_, ...), custom_call_target="tpu_custom_call" | custom-call | flops 1 | bytes 1 | tf_op jit(solution)/shard_map/assemble/pallas_call | solution.py:1013
  290.1 4.0 %collective-permute-done.58 = bf16[1,1,96,768]{3,2,1,0:T(8,128)(2,1)S(1)} collective-permute-done((bf16[1,1,96,768]{3,2,1,0:T(8,128)(2,1)}, bf16[1,1,96,768]{3,2,1,0:T(8,128)(2,1)S(1)}, u32[]{:S(2)}, u32[]{:S(2)}) %collective-permute-start.58) | collective-permute-done | bytes 147488 | tf_op jit(solution)/shard_map/ppermute | solution.py:35
  298.6 2.7 assemble.3
  (315 shorter events, 62.3 us)
Async XLA Ops:
  1.6 18.1 %collective-permute-start.3 = (bf16[1,96,576]{2,1,0:T(8,128)(2,1)S(1)}, bf16[1,96,576]{2,1,0:T(8,128)(2,1)S(1)}, u32[]{:S(2)}, u32[]{:S(2)}) collective-permute-start(bf16[1,96,576]{2,1,0:T(8,128)(2,1)S(1)} %get-tuple-element.296), channel_id=1, source_target_pairs={{0,24},{4,28},{8,16},{12,20},{16,8},{20,12},{24,0},{28,4},{1,25},{... | collective-permute-start | bytes 331784 | tf_op jit(solution)/shard_map/ppermute | solution.py:35
  6.7 12.9 %collective-permute-start.2 = (bf16[1,96,576]{2,1,0:T(8,128)(2,1)S(1)}, bf16[1,96,576]{2,1,0:T(8,128)(2,1)S(1)}, u32[]{:S(2)}, u32[]{:S(2)}) collective-permute-start(bf16[1,96,576]{2,1,0:T(8,128)(2,1)S(1)} %get-tuple-element.296), channel_id=1, source_target_pairs={{0,16},{4,20},{8,24},{12,28},{16,0},{20,4},{24,8},{28,12},{1,17},{... | collective-permute-start | bytes 331784 | tf_op jit(solution)/shard_map/ppermute | solution.py:35
  6.7 12.9 %collective-permute-start.1 = (bf16[1,96,576]{2,1,0:T(8,128)(2,1)S(1)}, bf16[1,96,576]{2,1,0:T(8,128)(2,1)S(1)}, u32[]{:S(2)}, u32[]{:S(2)}) collective-permute-start(bf16[1,96,576]{2,1,0:T(8,128)(2,1)S(1)} %get-tuple-element.296), channel_id=1, source_target_pairs={{0,8},{4,12},{8,0},{12,4},{16,24},{20,28},{24,16},{28,20},{1,9},{5... | collective-permute-start | bytes 331784 | tf_op jit(solution)/shard_map/ppermute | solution.py:35
  8.7 34.6 %collective-permute-start = (bf16[16,768]{1,0:T(8,128)(2,1)}, bf16[16,768]{1,0:T(8,128)(2,1)S(1)}, u32[]{:S(2)}, u32[]{:S(2)}) collective-permute-start(bf16[16,768]{1,0:T(8,128)(2,1)} %slice.152), channel_id=1, source_target_pairs={{0,4},{4,8},{8,12},{12,16},{16,20},{20,24},{24,28},{1,5},{5,9},{9,... | collective-permute-start | bytes 73736 | tf_op jit(solution)/shard_map/ppermute | solution.py:40
  13.3 10.7 %collective-permute-start.5 = (bf16[256,768]{1,0:T(8,128)(2,1)S(1)}, bf16[256,768]{1,0:T(8,128)(2,1)S(1)}, u32[]{:S(2)}, u32[]{:S(2)}) collective-permute-start(bf16[256,768]{1,0:T(8,128)(2,1)S(1)} %constant_dynamic-slice_fusion.6.x_ref), channel_id=1, source_target_pairs={{0,8},{4,12},{8,16},{12,20},{16,24},{20,28},{1,9},{5,13},{9,17},{1... | collective-permute-start | bytes 1179656 | tf_op jit(solution)/shard_map/ppermute | solution.py:40
  20.8 13.5 %collective-permute-start.4 = (bf16[4,96,576]{2,1,0:T(8,128)(2,1)}, bf16[4,96,576]{2,1,0:T(8,128)(2,1)}, u32[]{:S(2)}, u32[]{:S(2)}) collective-permute-start(bf16[4,96,576]{2,1,0:T(8,128)(2,1)} %bitcast.13), channel_id=1, source_target_pairs={{0,4},{4,0},{8,12},{12,8},{16,20},{20,16},{24,28},{28,24},{1,5},{5... | collective-permute-start | bytes 1327112 | tf_op jit(solution)/shard_map/ppermute | solution.py:35
  24.0 12.9 %collective-permute-start.6 = (bf16[256,768]{1,0:T(8,128)(2,1)S(1)}, bf16[256,768]{1,0:T(8,128)(2,1)S(1)}, u32[]{:S(2)}, u32[]{:S(2)}) collective-permute-start(bf16[256,768]{1,0:T(8,128)(2,1)S(1)} %collective-permute-done.5.refs_0_), channel_id=1, source_target_pairs={{0,2},{1,3},{2,0},{3,1},{4,6},{5,7},{6,4},{7,5},{8,10},{9,11},{10,... | collective-permute-start | bytes 1179656 | tf_op jit(solution)/shard_map/ppermute | solution.py:35
  29.1 21.8 %collective-permute-start.13 = (bf16[1,120,768]{2,1,0:T(8,128)(2,1)S(1)}, bf16[1,120,768]{2,1,0:T(8,128)(2,1)S(1)}, u32[]{:S(2)}, u32[]{:S(2)}) collective-permute-start(bf16[1,120,768]{2,1,0:T(8,128)(2,1)S(1)} %bitcast.117), channel_id=1, source_target_pairs={{0,8},{4,12},{8,0},{12,4},{16,24},{20,28},{24,16},{28,20},{1,9},{5... | collective-permute-start | bytes 552968 | tf_op jit(solution)/shard_map/ppermute | solution.py:35
  31.5 22.0 %collective-permute-start.14 = (bf16[1,120,768]{2,1,0:T(8,128)(2,1)S(1)}, bf16[1,120,768]{2,1,0:T(8,128)(2,1)S(1)}, u32[]{:S(2)}, u32[]{:S(2)}) collective-permute-start(bf16[1,120,768]{2,1,0:T(8,128)(2,1)S(1)} %bitcast.118), channel_id=1, source_target_pairs={{0,16},{4,20},{8,24},{12,28},{16,0},{20,4},{24,8},{28,12},{1,17},{... | collective-permute-start | bytes 552968 | tf_op jit(solution)/shard_map/ppermute | solution.py:35
  34.3 9.0 %collective-permute-start.7 = (bf16[256,768]{1,0:T(8,128)(2,1)S(1)}, bf16[256,768]{1,0:T(8,128)(2,1)}, u32[]{:S(2)}, u32[]{:S(2)}) collective-permute-start(bf16[256,768]{1,0:T(8,128)(2,1)S(1)} %broadcast_select_fusion), channel_id=1, source_target_pairs={{0,4},{4,0},{8,12},{12,8},{16,20},{20,16},{24,28},{28,24},{1,5},{5... | collective-permute-start | bytes 1179656 | tf_op jit(solution)/shard_map/ppermute | solution.py:35
  36.9 16.7 %collective-permute-start.15 = (bf16[1,120,768]{2,1,0:T(8,128)(2,1)S(1)}, bf16[1,120,768]{2,1,0:T(8,128)(2,1)S(1)}, u32[]{:S(2)}, u32[]{:S(2)}) collective-permute-start(bf16[1,120,768]{2,1,0:T(8,128)(2,1)S(1)} %bitcast.119), channel_id=1, source_target_pairs={{0,24},{4,28},{8,16},{12,20},{16,8},{20,12},{24,0},{28,4},{1,25},{... | collective-permute-start | bytes 552968 | tf_op jit(solution)/shard_map/ppermute | solution.py:35
  49.1 16.3 %collective-permute-start.22 = (bf16[1,96,768]{2,1,0:T(8,128)(2,1)}, bf16[1,96,768]{2,1,0:T(8,128)(2,1)}, u32[]{:S(2)}, u32[]{:S(2)}) collective-permute-start(bf16[1,96,768]{2,1,0:T(8,128)(2,1)} %bitcast.45), channel_id=1, source_target_pairs={{0,8},{4,12},{8,0},{12,4},{16,24},{20,28},{24,16},{28,20},{1,9},{5... | collective-permute-start | bytes 442376 | tf_op jit(solution)/shard_map/ppermute | solution.py:35
  49.9 16.1 %collective-permute-start.23 = (bf16[1,96,768]{2,1,0:T(8,128)(2,1)}, bf16[1,96,768]{2,1,0:T(8,128)(2,1)}, u32[]{:S(2)}, u32[]{:S(2)}) collective-permute-start(bf16[1,96,768]{2,1,0:T(8,128)(2,1)} %bitcast.45), channel_id=1, source_target_pairs={{0,16},{4,20},{8,24},{12,28},{16,0},{20,4},{24,8},{28,12},{1,17},{... | collective-permute-start | bytes 442376 | tf_op jit(solution)/shard_map/ppermute | solution.py:35
  50.8 15.2 %collective-permute-start.24 = (bf16[1,96,768]{2,1,0:T(8,128)(2,1)}, bf16[1,96,768]{2,1,0:T(8,128)(2,1)}, u32[]{:S(2)}, u32[]{:S(2)}) collective-permute-start(bf16[1,96,768]{2,1,0:T(8,128)(2,1)} %bitcast.45), channel_id=1, source_target_pairs={{0,24},{4,28},{8,16},{12,20},{16,8},{20,12},{24,0},{28,4},{1,25},{... | collective-permute-start | bytes 442376 | tf_op jit(solution)/shard_map/ppermute | solution.py:35
  53.7 8.1 %collective-permute-start.8 = (bf16[256,768]{1,0:T(8,128)(2,1)}, bf16[256,768]{1,0:T(8,128)(2,1)S(1)}, u32[]{:S(2)}, u32[]{:S(2)}) collective-permute-start(bf16[256,768]{1,0:T(8,128)(2,1)} %collective-permute-done.7.refs_4_), channel_id=1, source_target_pairs={{0,2},{1,3},{2,0},{3,1},{4,6},{5,7},{6,4},{7,5},{8,10},{9,11},{10,... | collective-permute-start | bytes 1179656 | tf_op jit(solution)/shard_map/ppermute | solution.py:35
  55.4 15.0 %collective-permute-start.16 = (bf16[4,120,768]{2,1,0:T(8,128)(2,1)}, bf16[4,120,768]{2,1,0:T(8,128)(2,1)}, u32[]{:S(2)}, u32[]{:S(2)}) collective-permute-start(bf16[4,120,768]{2,1,0:T(8,128)(2,1)} %bitcast.29), channel_id=1, source_target_pairs={{0,4},{4,0},{8,12},{12,8},{16,20},{20,16},{24,28},{28,24},{1,5},{5... | collective-permute-start | bytes 2211848 | tf_op jit(solution)/shard_map/ppermute | solution.py:35
  61.7 15.7 %collective-permute-start.9 = (bf16[256,768]{1,0:T(8,128)(2,1)S(1)}, bf16[256,768]{1,0:T(8,128)(2,1)}, u32[]{:S(2)}, u32[]{:S(2)}) collective-permute-start(bf16[256,768]{1,0:T(8,128)(2,1)S(1)} %collective-permute-done.5.refs_0_), channel_id=1, source_target_pairs={{0,1},{1,0},{2,3},{3,2},{4,5},{5,4},{6,7},{7,6},{8,9},{9,8},{10,11... | collective-permute-start | bytes 1179656 | tf_op jit(solution)/shard_map/ppermute | solution.py:35
  65.4 16.0 %collective-permute-start.10 = (bf16[256,768]{1,0:T(8,128)(2,1)S(1)}, bf16[256,768]{1,0:T(8,128)(2,1)S(1)}, u32[]{:S(2)}, u32[]{:S(2)}) collective-permute-start(bf16[256,768]{1,0:T(8,128)(2,1)S(1)} %copy-done.57), channel_id=1, source_target_pairs={{0,1},{1,0},{2,3},{3,2},{4,5},{5,4},{6,7},{7,6},{8,9},{9,8},{10,11... | collective-permute-start | bytes 1179656 | tf_op jit(solution)/shard_map/ppermute | solution.py:35
  66.0 15.4 %collective-permute-start.11 = (bf16[256,768]{1,0:T(8,128)(2,1)}, bf16[256,768]{1,0:T(8,128)(2,1)S(1)}, u32[]{:S(2)}, u32[]{:S(2)}) collective-permute-start(bf16[256,768]{1,0:T(8,128)(2,1)} %collective-permute-done.7.refs_4_), channel_id=1, source_target_pairs={{0,1},{1,0},{2,3},{3,2},{4,5},{5,4},{6,7},{7,6},{8,9},{9,8},{10,11... | collective-permute-start | bytes 1179656 | tf_op jit(solution)/shard_map/ppermute | solution.py:35
  68.4 25.8 %collective-permute-start.25 = (bf16[4,96,768]{2,1,0:T(8,128)(2,1)}, bf16[4,96,768]{2,1,0:T(8,128)(2,1)}, u32[]{:S(2)}, u32[]{:S(2)}) collective-permute-start(bf16[4,96,768]{2,1,0:T(8,128)(2,1)} %bitcast.52), channel_id=1, source_target_pairs={{0,4},{4,0},{8,12},{12,8},{16,20},{20,16},{24,28},{28,24},{1,5},{5... | collective-permute-start | bytes 1769480 | tf_op jit(solution)/shard_map/ppermute | solution.py:35
  70.4 11.0 %collective-permute-start.12 = (bf16[256,768]{1,0:T(8,128)(2,1)S(1)}, bf16[256,768]{1,0:T(8,128)(2,1)S(1)}, u32[]{:S(2)}, u32[]{:S(2)}) collective-permute-start(bf16[256,768]{1,0:T(8,128)(2,1)S(1)} %collective-permute-done.8.refs_5_), channel_id=1, source_target_pairs={{0,1},{1,0},{2,3},{3,2},{4,5},{5,4},{6,7},{7,6},{8,9},{9,8},{10,11... | collective-permute-start | bytes 1179656 | tf_op jit(solution)/shard_map/ppermute | solution.py:35
  77.5 14.1 %collective-permute-start.17 = (bf16[192,768]{1,0:T(8,128)(2,1)S(1)}, bf16[192,768]{1,0:T(8,128)(2,1)S(1)}, u32[]{:S(2)}, u32[]{:S(2)}) collective-permute-start(bf16[192,768]{1,0:T(8,128)(2,1)S(1)} %bitcast.111), channel_id=1, source_target_pairs={{0,2},{1,3},{2,0},{3,1},{4,6},{5,7},{6,4},{7,5},{8,10},{9,11},{10,... | collective-permute-start | bytes 884744 | tf_op jit(solution)/shard_map/ppermute | solution.py:35
  91.6 4.0 %collective-permute-start.18 = (bf16[192,768]{1,0:T(8,128)(2,1)S(1)}, bf16[192,768]{1,0:T(8,128)(2,1)S(1)}, u32[]{:S(2)}, u32[]{:S(2)}) collective-permute-start(bf16[192,768]{1,0:T(8,128)(2,1)S(1)} %bitcast.112), channel_id=1, source_target_pairs={{0,1},{1,0},{2,3},{3,2},{4,5},{5,4},{6,7},{7,6},{8,9},{9,8},{10,11... | collective-permute-start | bytes 884744 | tf_op jit(solution)/shard_map/ppermute | solution.py:35
  91.9 3.7 %collective-permute-start.19 = (bf16[192,768]{1,0:T(8,128)(2,1)S(1)}, bf16[192,768]{1,0:T(8,128)(2,1)S(1)}, u32[]{:S(2)}, u32[]{:S(2)}) collective-permute-start(bf16[192,768]{1,0:T(8,128)(2,1)S(1)} %collective-permute-done.17.w1), channel_id=1, source_target_pairs={{0,1},{1,0},{2,3},{3,2},{4,5},{5,4},{6,7},{7,6},{8,9},{9,8},{10,11... | collective-permute-start | bytes 884744 | tf_op jit(solution)/shard_map/ppermute | solution.py:35
  97.2 1.5 collective-permute-start.20
  98.7 7.1 %collective-permute-start.21 = (bf16[2,192,256]{2,1,0:T(8,128)(2,1)S(1)}, bf16[2,192,256]{2,1,0:T(8,128)(2,1)S(1)}, u32[]{:S(2)}, u32[]{:S(2)}) collective-permute-start(bf16[2,192,256]{2,1,0:T(8,128)(2,1)S(1)} %pad_maximum_fusion.7), channel_id=1, source_target_pairs={{0,2},{1,3},{2,0},{3,1},{4,6},{5,7},{6,4},{7,5},{8,10},{9,11},{10,... | collective-permute-start | bytes 589832 | tf_op jit(solution)/shard_map/ppermute | solution.py:35
  106.7 10.5 %collective-permute-start.26 = (bf16[256,768]{1,0:T(8,128)(2,1)S(1)}, bf16[256,768]{1,0:T(8,128)(2,1)S(1)}, u32[]{:S(2)}, u32[]{:S(2)}) collective-permute-start(bf16[256,768]{1,0:T(8,128)(2,1)S(1)} %get-tuple-element.155.x0), channel_id=1, source_target_pairs={{0,2},{1,3},{2,0},{3,1},{4,6},{5,7},{6,4},{7,5},{8,10},{9,11},{10,... | collective-permute-start | bytes 1179656 | tf_op jit(solution)/shard_map/ppermute | solution.py:35
  107.2 9.9 %collective-permute-start.27 = (bf16[256,768]{1,0:T(8,128)(2,1)S(1)}, bf16[256,768]{1,0:T(8,128)(2,1)S(1)}, u32[]{:S(2)}, u32[]{:S(2)}) collective-permute-start(bf16[256,768]{1,0:T(8,128)(2,1)S(1)} %get-tuple-element.155.x0), channel_id=1, source_target_pairs={{0,1},{1,0},{2,3},{3,2},{4,5},{5,4},{6,7},{7,6},{8,9},{9,8},{10,11... | collective-permute-start | bytes 1179656 | tf_op jit(solution)/shard_map/ppermute | solution.py:35
  117.1 1.7 collective-permute-start.28
  124.4 2.3 collective-permute-start.29
  127.8 11.5 %collective-permute-start.30 = (bf16[256,768]{1,0:T(8,128)(2,1)}, bf16[256,768]{1,0:T(8,128)(2,1)}, u32[]{:S(2)}, u32[]{:S(2)}) collective-permute-start(bf16[256,768]{1,0:T(8,128)(2,1)} %get-tuple-element.274), channel_id=1, source_target_pairs={{0,2},{1,3},{2,0},{3,1},{4,6},{5,7},{6,4},{7,5},{8,10},{9,11},{10,... | collective-permute-start | bytes 1179656 | tf_op jit(solution)/shard_map/ppermute | solution.py:35
  137.3 12.6 %collective-permute-start.33 = (bf16[512,768]{1,0:T(8,128)(2,1)S(1)}, bf16[512,768]{1,0:T(8,128)(2,1)S(1)}, u32[]{:S(2)}, u32[]{:S(2)}) collective-permute-start(bf16[512,768]{1,0:T(8,128)(2,1)S(1)} %get-tuple-element.172), channel_id=1, source_target_pairs={{0,1},{1,0},{2,3},{3,2},{4,5},{5,4},{6,7},{7,6},{8,9},{9,8},{10,11... | collective-permute-start | bytes 2359304 | tf_op jit(solution)/shard_map/ppermute | solution.py:35
  142.5 7.4 %collective-permute-start.31 = (bf16[2,192,256]{2,1,0:T(8,128)(2,1)S(1)}, bf16[2,192,256]{2,1,0:T(8,128)(2,1)S(1)}, u32[]{:S(2)}, u32[]{:S(2)}) collective-permute-start(bf16[2,192,256]{2,1,0:T(8,128)(2,1)S(1)} %pad_maximum_fusion.8), channel_id=1, source_target_pairs={{0,2},{1,3},{2,0},{3,1},{4,6},{5,7},{6,4},{7,5},{8,10},{9,11},{10,... | collective-permute-start | bytes 589832 | tf_op jit(solution)/shard_map/ppermute | solution.py:35
  144.1 9.0 %collective-permute-start.35 = (bf16[2,192,768]{2,1,0:T(8,128)(2,1)S(1)}, bf16[2,192,768]{2,1,0:T(8,128)(2,1)S(1)}, u32[]{:S(2)}, u32[]{:S(2)}) collective-permute-start(bf16[2,192,768]{2,1,0:T(8,128)(2,1)S(1)} %get-tuple-element.180), channel_id=1, source_target_pairs={{0,1},{1,0},{2,3},{3,2},{4,5},{5,4},{6,7},{7,6},{8,9},{9,8},{10,11... | collective-permute-start | bytes 1769480 | tf_op jit(solution)/shard_map/ppermute | solution.py:35
  149.9 1.5 collective-permute-start.32
  151.5 23.4 %collective-permute-start.34 = (bf16[256,768]{1,0:T(8,128)(2,1)S(1)}, bf16[256,768]{1,0:T(8,128)(2,1)S(1)}, u32[]{:S(2)}, u32[]{:S(2)}) collective-permute-start(bf16[256,768]{1,0:T(8,128)(2,1)S(1)} %slice.171), channel_id=1, source_target_pairs={{0,2},{1,3},{2,0},{3,1},{4,6},{5,7},{6,4},{7,5},{8,10},{9,11},{10,... | collective-permute-start | bytes 1179656 | tf_op jit(solution)/shard_map/ppermute | solution.py:35
  153.1 21.8 %collective-permute-start.36 = (bf16[192,768]{1,0:T(8,128)(2,1)S(1)}, bf16[192,768]{1,0:T(8,128)(2,1)S(1)}, u32[]{:S(2)}, u32[]{:S(2)}) collective-permute-start(bf16[192,768]{1,0:T(8,128)(2,1)S(1)} %fusion), channel_id=1, source_target_pairs={{0,2},{1,3},{2,0},{3,1},{4,6},{5,7},{6,4},{7,5},{8,10},{9,11},{10,... | collective-permute-start | bytes 884744 | tf_op jit(solution)/shard_map/ppermute | solution.py:35
  153.7 46.8 %collective-permute-start.42 = (bf16[2,4,96,768]{3,2,1,0:T(8,128)(2,1)}, bf16[2,4,96,768]{3,2,1,0:T(8,128)(2,1)}, u32[]{:S(2)}, u32[]{:S(2)}) collective-permute-start(bf16[2,4,96,768]{3,2,1,0:T(8,128)(2,1)} %get-tuple-element.196), channel_id=1, source_target_pairs={{0,4},{4,0},{8,12},{12,8},{16,20},{20,16},{24,28},{28,24},{1,5},{5... | collective-permute-start | bytes 3538952 | tf_op jit(solution)/shard_map/ppermute | solution.py:35
  173.6 53.8 %collective-permute-start.43 = (bf16[1040,384]{1,0:T(8,128)(2,1)}, bf16[1040,384]{1,0:T(8,128)(2,1)}, u32[]{:S(2)}, u32[]{:S(2)}) collective-permute-start(bf16[1040,384]{1,0:T(8,128)(2,1)} %get-tuple-element.185.one_ref), channel_id=1, source_target_pairs={{4,0},{8,4},{12,8},{16,12},{20,16},{24,20},{28,24},{5,1},{9,5},{13... | collective-permute-start | bytes 2396168 | tf_op jit(solution)/shard_map/ppermute | solution.py:40
  187.0 40.4 %copy-start.13 = (bf16[768,576]{1,0:T(8,128)(2,1)S(1)}, bf16[768,576]{1,0:T(8,128)(2,1)}, u32[]{:S(2)}) copy-start(bf16[768,576]{1,0:T(8,128)(2,1)} %copy-done.11) | copy-start | bytes 2654212
  187.1 10.5 %collective-permute-start.39 = (bf16[256,768]{1,0:T(8,128)(2,1)S(1)}, bf16[256,768]{1,0:T(8,128)(2,1)S(1)}, u32[]{:S(2)}, u32[]{:S(2)}) collective-permute-start(bf16[256,768]{1,0:T(8,128)(2,1)S(1)} %add_convert_fusion.5.refs_0_), channel_id=1, source_target_pairs={{0,2},{1,3},{2,0},{3,1},{4,6},{5,7},{6,4},{7,5},{8,10},{9,11},{10,... | collective-permute-start | bytes 1179656 | tf_op jit(solution)/shard_map/ppermute | solution.py:35
  188.7 38.7 %collective-permute-start.44 = (bf16[1024,384]{1,0:T(8,128)(2,1)}, bf16[1024,384]{1,0:T(8,128)(2,1)}, u32[]{:S(2)}, u32[]{:S(2)}) collective-permute-start(bf16[1024,384]{1,0:T(8,128)(2,1)} %get-tuple-element.184.two_ref), channel_id=1, source_target_pairs={{8,0},{12,4},{16,8},{20,12},{24,16},{28,20},{9,1},{13,5},{17,9},{2... | collective-permute-start | bytes 2359304 | tf_op jit(solution)/shard_map/ppermute | solution.py:40
  190.0 1.2 collective-permute-start.37
  191.2 6.4 %collective-permute-start.38 = (f32[1,768]{1,0:T(1,128)S(1)}, f32[1,768]{1,0:T(1,128)S(1)}, u32[]{:S(2)}, u32[]{:S(2)}) collective-permute-start(f32[1,768]{1,0:T(1,128)S(1)} %add.154), channel_id=1, source_target_pairs={{0,2},{1,3},{2,0},{3,1},{4,6},{5,7},{6,4},{7,5},{8,10},{9,11},{10,... | collective-permute-start | bytes 9224 | tf_op jit(solution)/shard_map/ppermute | solution.py:35
  197.6 7.5 %collective-permute-start.40 = (bf16[256,768]{1,0:T(8,128)(2,1)S(1)}, bf16[256,768]{1,0:T(8,128)(2,1)}, u32[]{:S(2)}, u32[]{:S(2)}) collective-permute-start(bf16[256,768]{1,0:T(8,128)(2,1)S(1)} %add_convert_fusion.5.refs_0_), channel_id=1, source_target_pairs={{0,1},{1,0},{2,3},{3,2},{4,5},{5,4},{6,7},{7,6},{8,9},{9,8},{10,11... | collective-permute-start | bytes 1179656 | tf_op jit(solution)/shard_map/ppermute | solution.py:35
  197.6 7.5 %collective-permute-start.41 = (bf16[256,768]{1,0:T(8,128)(2,1)S(1)}, bf16[256,768]{1,0:T(8,128)(2,1)}, u32[]{:S(2)}, u32[]{:S(2)}) collective-permute-start(bf16[256,768]{1,0:T(8,128)(2,1)S(1)} %collective-permute-done.39.refs_1_), channel_id=1, source_target_pairs={{0,1},{1,0},{2,3},{3,2},{4,5},{5,4},{6,7},{7,6},{8,9},{9,8},{10,11... | collective-permute-start | bytes 1179656 | tf_op jit(solution)/shard_map/ppermute | solution.py:35
  200.6 72.4 %collective-permute-start.50 = (bf16[1,4,96,768]{3,2,1,0:T(8,128)(2,1)}, bf16[1,4,96,768]{3,2,1,0:T(8,128)(2,1)}, u32[]{:S(2)}, u32[]{:S(2)}) collective-permute-start(bf16[1,4,96,768]{3,2,1,0:T(8,128)(2,1)} %get-tuple-element.270), channel_id=1, source_target_pairs={{0,4},{4,0},{8,12},{12,8},{16,20},{20,16},{24,28},{28,24},{1,5},{5... | collective-permute-start | bytes 1769480 | tf_op jit(solution)/shard_map/ppermute | solution.py:35
  233.2 2.4 collective-permute-start.45
  235.9 11.2 %collective-permute-start.46 = (bf16[256,768]{1,0:T(8,128)(2,1)S(1)}, bf16[256,768]{1,0:T(8,128)(2,1)S(1)}, u32[]{:S(2)}, u32[]{:S(2)}) collective-permute-start(bf16[256,768]{1,0:T(8,128)(2,1)S(1)} %get-tuple-element.272), channel_id=1, source_target_pairs={{0,2},{1,3},{2,0},{3,1},{4,6},{5,7},{6,4},{7,5},{8,10},{9,11},{10,... | collective-permute-start | bytes 1179656 | tf_op jit(solution)/shard_map/ppermute | solution.py:35
  237.6 12.1 %collective-permute-start.62 = (bf16[2,1,96,768]{3,2,1,0:T(8,128)(2,1)}, bf16[2,1,96,768]{3,2,1,0:T(8,128)(2,1)}, u32[]{:S(2)}, u32[]{:S(2)}) collective-permute-start(bf16[2,1,96,768]{3,2,1,0:T(8,128)(2,1)} %get-tuple-element.268), channel_id=1, source_target_pairs={{0,24},{4,28},{8,16},{12,20},{16,8},{20,12},{24,0},{28,4},{1,25},{... | collective-permute-start | bytes 884744 | tf_op jit(solution)/shard_map/ppermute | solution.py:35
  239.3 27.3 %collective-permute-start.61 = (bf16[2,1,96,768]{3,2,1,0:T(8,128)(2,1)}, bf16[2,1,96,768]{3,2,1,0:T(8,128)(2,1)}, u32[]{:S(2)}, u32[]{:S(2)}) collective-permute-start(bf16[2,1,96,768]{3,2,1,0:T(8,128)(2,1)} %get-tuple-element.269), channel_id=1, source_target_pairs={{0,16},{4,20},{8,24},{12,28},{16,0},{20,4},{24,8},{28,12},{1,17},{... | collective-permute-start | bytes 884744 | tf_op jit(solution)/shard_map/ppermute | solution.py:35
  240.3 26.3 %collective-permute-start.60 = (bf16[2,1,96,768]{3,2,1,0:T(8,128)(2,1)}, bf16[2,1,96,768]{3,2,1,0:T(8,128)(2,1)}, u32[]{:S(2)}, u32[]{:S(2)}) collective-permute-start(bf16[2,1,96,768]{3,2,1,0:T(8,128)(2,1)} %get-tuple-element.267), channel_id=1, source_target_pairs={{0,8},{4,12},{8,0},{12,4},{16,24},{20,28},{24,16},{28,20},{1,9},{5... | collective-permute-start | bytes 884744 | tf_op jit(solution)/shard_map/ppermute | solution.py:35
  247.1 20.9 %collective-permute-start.48 = (f32[1,768]{1,0:T(1,128)S(1)}, f32[1,768]{1,0:T(1,128)S(1)}, u32[]{:S(2)}, u32[]{:S(2)}) collective-permute-start(f32[1,768]{1,0:T(1,128)S(1)} %get-tuple-element.202), channel_id=1, source_target_pairs={{0,1},{1,0},{2,3},{3,2},{4,5},{5,4},{6,7},{7,6},{8,9},{9,8},{10,11... | collective-permute-start | bytes 9224 | tf_op jit(solution)/shard_map/ppermute | solution.py:35
  249.7 23.2 %collective-permute-start.47 = (bf16[256,768]{1,0:T(8,128)(2,1)S(1)}, bf16[256,768]{1,0:T(8,128)(2,1)S(1)}, u32[]{:S(2)}, u32[]{:S(2)}) collective-permute-start(bf16[256,768]{1,0:T(8,128)(2,1)S(1)} %grad_tokens_own.1.refs_0_), channel_id=1, source_target_pairs={{0,1},{1,0},{2,3},{3,2},{4,5},{5,4},{6,7},{7,6},{8,9},{9,8},{10,11... | collective-permute-start | bytes 1179656 | tf_op jit(solution)/shard_map/ppermute | solution.py:35
  268.0 3.7 %collective-permute-start.49 = (f32[1,768]{1,0:T(1,128)S(1)}, f32[1,768]{1,0:T(1,128)S(1)}, u32[]{:S(2)}, u32[]{:S(2)}) collective-permute-start(f32[1,768]{1,0:T(1,128)S(1)} %add.159), channel_id=1, source_target_pairs={{0,2},{1,3},{2,0},{3,1},{4,6},{5,7},{6,4},{7,5},{8,10},{9,11},{10,... | collective-permute-start | bytes 9224 | tf_op jit(solution)/shard_map/ppermute | solution.py:35
  271.7 17.1 %collective-permute-start.51 = (bf16[256,768]{1,0:T(8,128)(2,1)S(1)}, bf16[256,768]{1,0:T(8,128)(2,1)S(1)}, u32[]{:S(2)}, u32[]{:S(2)}) collective-permute-start(bf16[256,768]{1,0:T(8,128)(2,1)S(1)} %grad_tokens_own.1.refs_0_), channel_id=1, source_target_pairs={{0,2},{1,3},{2,0},{3,1},{4,6},{5,7},{6,4},{7,5},{8,10},{9,11},{10,... | collective-permute-start | bytes 1179656 | tf_op jit(solution)/shard_map/ppermute | solution.py:35
  273.0 5.8 %collective-permute-start.55 = (f32[3264]{0:T(1024)S(1)}, f32[3264]{0:T(1024)S(1)}, u32[]{:S(2)}, u32[]{:S(2)}) collective-permute-start(f32[3264]{0:T(1024)S(1)} %pad_maximum_fusion.13), channel_id=1, source_target_pairs={{0,24},{4,28},{8,16},{12,20},{16,8},{20,12},{24,0},{28,4},{1,25},{... | collective-permute-start | bytes 39176 | tf_op jit(solution)/shard_map/ppermute | solution.py:35
  275.5 4.6 %collective-permute-start.54 = (f32[3264]{0:T(1024)S(1)}, f32[3264]{0:T(1024)S(1)}, u32[]{:S(2)}, u32[]{:S(2)}) collective-permute-start(f32[3264]{0:T(1024)S(1)} %pad_maximum_fusion.13), channel_id=1, source_target_pairs={{0,16},{4,20},{8,24},{12,28},{16,0},{20,4},{24,8},{28,12},{1,17},{... | collective-permute-start | bytes 39176 | tf_op jit(solution)/shard_map/ppermute | solution.py:35
  275.6 4.6 %collective-permute-start.53 = (f32[3264]{0:T(1024)S(1)}, f32[3264]{0:T(1024)S(1)}, u32[]{:S(2)}, u32[]{:S(2)}) collective-permute-start(f32[3264]{0:T(1024)S(1)} %pad_maximum_fusion.13), channel_id=1, source_target_pairs={{0,8},{4,12},{8,0},{12,4},{16,24},{20,28},{24,16},{28,20},{1,9},{5... | collective-permute-start | bytes 39176 | tf_op jit(solution)/shard_map/ppermute | solution.py:35
  280.2 8.6 %collective-permute-start.56 = (f32[3264]{0:T(1024)S(1)}, f32[3264]{0:T(1024)S(1)}, u32[]{:S(2)}, u32[]{:S(2)}) collective-permute-start(f32[3264]{0:T(1024)S(1)} %add_add_fusion), channel_id=1, source_target_pairs={{0,4},{4,0},{8,12},{12,8},{16,20},{20,16},{24,28},{28,24},{1,5},{5... | collective-permute-start | bytes 39176 | tf_op jit(solution)/shard_map/ppermute | solution.py:35
  281.0 9.1 %collective-permute-start.59 = (bf16[1,1,96,768]{3,2,1,0:T(8,128)(2,1)}, bf16[1,1,96,768]{3,2,1,0:T(8,128)(2,1)S(1)}, u32[]{:S(2)}, u32[]{:S(2)}) collective-permute-start(bf16[1,1,96,768]{3,2,1,0:T(8,128)(2,1)} %get-tuple-element.279), channel_id=1, source_target_pairs={{0,24},{4,28},{8,16},{12,20},{16,8},{20,12},{24,0},{28,4},{1,25},{... | collective-permute-start | bytes 442376 | tf_op jit(solution)/shard_map/ppermute | solution.py:35
  282.5 11.6 %collective-permute-start.58 = (bf16[1,1,96,768]{3,2,1,0:T(8,128)(2,1)}, bf16[1,1,96,768]{3,2,1,0:T(8,128)(2,1)S(1)}, u32[]{:S(2)}, u32[]{:S(2)}) collective-permute-start(bf16[1,1,96,768]{3,2,1,0:T(8,128)(2,1)} %get-tuple-element.280), channel_id=1, source_target_pairs={{0,16},{4,20},{8,24},{12,28},{16,0},{20,4},{24,8},{28,12},{1,17},{... | collective-permute-start | bytes 442376 | tf_op jit(solution)/shard_map/ppermute | solution.py:35
  283.5 11.3 %collective-permute-start.57 = (bf16[1,1,96,768]{3,2,1,0:T(8,128)(2,1)S(1)}, bf16[1,1,96,768]{3,2,1,0:T(8,128)(2,1)}, u32[]{:S(2)}, u32[]{:S(2)}) collective-permute-start(bf16[1,1,96,768]{3,2,1,0:T(8,128)(2,1)S(1)} %get-tuple-element.278), channel_id=1, source_target_pairs={{0,8},{4,12},{8,0},{12,4},{16,24},{20,28},{24,16},{28,20},{1,9},{5... | collective-permute-start | bytes 442376 | tf_op jit(solution)/shard_map/ppermute | solution.py:35
  288.8 9.8 %collective-permute-start.52 = (bf16[256,768]{1,0:T(8,128)(2,1)S(1)}, bf16[256,768]{1,0:T(8,128)(2,1)S(1)}, u32[]{:S(2)}, u32[]{:S(2)}) collective-permute-start(bf16[256,768]{1,0:T(8,128)(2,1)S(1)} %collective-permute-done.51.refs_1_), channel_id=1, source_target_pairs={{0,1},{1,0},{2,3},{3,2},{4,5},{5,4},{6,7},{7,6},{8,9},{9,8},{10,11... | collective-permute-start | bytes 1179656 | tf_op jit(solution)/shard_map/ppermute | solution.py:35
  (68 other events, 486.7 us)

commit v3 on v2

--- a/solution.py
+++ b/solution.py
@@ -53,16 +53,6 @@
     return ((lax.axis_index(axis) >> bit) & 1) == 1
 
 
-def in_order(pieces, axis, group):
-    both = jnp.stack(pieces)
-    if len(group) == 1:
-        return jnp.where(bit_of(axis, group[0]), both[::-1], both)
-    both = both.reshape(2, 2, *both.shape[1:])
-    both = jnp.where(bit_of(axis, group[0]), both[::-1], both)
-    both = jnp.where(bit_of(axis, group[1]), both[:, ::-1], both)
-    return both.reshape(4, *both.shape[2:])
-
-
 def masks_of(group):
     if len(group) == 1:
         return [0, 1 << group[0]]
@@ -70,14 +60,64 @@
     return [0, lo, hi, hi | lo]
 
 
-def gathered(out, axis, groups, size, after=None):
+def sent_round(shard, axis):
+    pieces = [shard[None]]
+    for group in bit_groups(axis)[:-1]:
+        out = jnp.concatenate(pieces)
+        pieces = [out] + [swap(out, axis, m) for m in masks_of(group)[1:]]
+    return pieces
+
+
+def gathered_masks(axis):
+    masks = [0]
+    *groups, last = bit_groups(axis)
     for group in groups:
-        pieces = [out] + [swap(out, axis, m) for m in masks_of(group)[1:]]
-        if after is not None:
-            *pieces, after = lax.optimization_barrier((*pieces, after))
-        out = jnp.moveaxis(in_order(pieces, axis, group), 0, 1)
-        out = out.reshape(-1, *size)
-    return out
+        masks = [m ^ old for m in masks_of(group) for old in masks]
+    return masks, [m ^ masks_of(last)[1] for m in masks]
+
+
+def joined_kernel(*refs):
+    *pieces, out_ref = refs
+    at = 0
+    for piece in pieces:
+        for n in range(piece.shape[0]):
+            out_ref[at] = piece[n]
+            at += 1
+
+
+def joined(pieces):
+    count = sum(piece.shape[0] for piece in pieces)
+    return pl.pallas_call(
+        joined_kernel,
+        out_shape=jax.ShapeDtypeStruct((count, *pieces[0].shape[1:]), pieces[0].dtype),
+        in_specs=[whole()] * len(pieces),
+        out_specs=whole(),
+        compiler_params=params(),
+        cost_estimate=COST,
+        name="joined",
+    )(*pieces)
+
+
+def pieces_of(own, axis, shard):
+    other = swap(own, axis, 1)
+    if shard % 16 == 0:
+        return own, other
+    size = lax.axis_size(axis)
+    masks = sum(gathered_masks(axis), [])
+    both = jnp.concatenate([own, other])
+    place = lax.axis_index(axis) ^ jnp.array(masks)
+    return (jnp.zeros_like(both).at[place].set(both),)
+
+
+def put_rows(to_ref, refs, blk, axis_masks, shard):
+    if len(refs) == 1:
+        for n in range(refs[0].shape[0]):
+            to_ref[n * shard : (n + 1) * shard, :] = refs[0][n, :shard, :].astype(to_ref.dtype)
+        return
+    for ref, masks in zip(refs, axis_masks):
+        for n, mask in enumerate(masks):
+            to = pl.ds(pl.multiple_of((blk ^ mask) * shard, 16), shard)
+            to_ref[to, :] = ref[n, :shard, :].astype(to_ref.dtype)
 
 
 def chosen(full, axis, group):
@@ -163,6 +203,41 @@
     )(w_up, w_out, w_down)
 
 
+def unpack_out_kernel(meta_ref, *refs, masks, shard):
+    *packed_refs, out_ref, out_t_ref = refs
+    few = packed_refs[0].shape[1] - shard
+    part = out_t_ref.shape[1]
+
+    def put(ref, n, place):
+        rows = ref[n].astype(F32)[shard:]
+        for k in range(shard // few):
+            to = pl.ds(place * shard + k * few, few)
+            out_t_ref[to, :] = rows[:, k * part : (k + 1) * part]
+
+    if len(packed_refs) == 1:
+        for n in range(packed_refs[0].shape[0]):
+            put(packed_refs[0], n, n)
+    else:
+        for ref, distances in zip(packed_refs, masks):
+            for n, mask in enumerate(distances):
+                put(ref, n, meta_ref[BLK] ^ mask)
+    out_ref[...] = out_t_ref[...].T.astype(BF16)
+
+
+def unpack_out(meta, packed, masks, shard, part):
+    dim = shard * sum(x.shape[0] for x in packed)
+    return pl.pallas_call(
+        functools.partial(unpack_out_kernel, masks=masks, shard=shard),
+        out_shape=jax.ShapeDtypeStruct((part, dim), BF16),
+        in_specs=[pl.BlockSpec(memory_space=pltpu.SMEM), *[whole()] * len(packed)],
+        out_specs=whole(),
+        scratch_shapes=[pltpu.VMEM((dim, part), F32)],
+        compiler_params=params(),
+        cost_estimate=COST,
+        name="unpack_out",
+    )(meta, *packed)
+
+
 def unit_times_gain(x, gain):
     return x * lax.rsqrt(jnp.mean(x * x, axis=-1, keepdims=True) + EPS) * gain
 
@@ -188,15 +263,16 @@
 
 
 def project_own_kernel(
-    meta_ref, x_ref, halo_ref, gain_ref, w_in_ref, taps_ref,
-    w_ref, raw_halo_ref, raw_ref, normed_ref, q_ref, kv_ref, kvt_ref, buf_ref, mix_ref, *, base,
+    meta_ref, x_ref, halo_ref, gain_ref, taps_ref, *refs, base, masks, shard,
 ):
+    *w_refs, w_ref, raw_halo_ref, raw_ref, normed_ref, q_ref, kv_ref, kvt_ref, buf_ref, mix_ref, w_in_ref = refs
     i = pl.program_id(0)
     rows = x_ref.shape[0]
     gain = gain_ref[...]
 
     @pl.when(i == 0)
     def _():
+        put_rows(w_in_ref, w_refs, meta_ref[BLK], masks, shard)
         w_in = w_in_ref[...]
         part = w_in.shape[1] // 3
         w_ref[...] = arranged(w_in[:, :part], w_in[:, part : 2 * part], w_in[:, 2 * part : 3 * part])
@@ -205,7 +281,8 @@
 
     @pl.when(i == 0)
     def _():
-        halo = jnp.where(meta_ref[HAS_ONE] == 1, halo_ref[...].astype(F32), 0.0)
+        halo = halo_ref[halo_ref.shape[0] - HALO :, :].astype(F32)
+        halo = jnp.where(meta_ref[HAS_ONE] == 1, halo, 0.0)
         normed = unit_times_gain(halo, gain).astype(BF16)
         raw_low = mm(normed, w).astype(BF16)
         raw_halo_ref[...] = raw_low[:, KV:]
@@ -225,13 +302,13 @@
     kvt_ref[...] = kv.T.astype(BF16)
 
 
-def project_own(meta, tokens, halo, gain, w, taps):
+def project_own(meta, tokens, halo, gain, taps, w, masks):
     rows, dim = tokens.shape
-    width = w.shape[1]
+    shard, width = w[0].shape[1:]
     step = 2 * TILE
     tile = lambda n: pl.BlockSpec((step, n), lambda i, *_: (i, 0))
     return pl.pallas_call(
-        functools.partial(project_own_kernel, base=REACH * rows),
+        functools.partial(project_own_kernel, base=REACH * rows, masks=masks, shard=shard),
         out_shape=(
             jax.ShapeDtypeStruct((dim, width), BF16),
             jax.ShapeDtypeStruct((HALO, width - KV), BF16),
@@ -244,7 +321,7 @@
         grid_spec=pltpu.PrefetchScalarGridSpec(
             num_scalar_prefetch=1,
             grid=(rows // step,),
-            in_specs=[tile(dim), whole(), whole(), whole(), whole()],
+            in_specs=[tile(dim), whole(), whole(), whole(), *[whole()] * len(w)],
             out_specs=(
                 whole(),
                 whole(),
@@ -254,12 +331,16 @@
                 tile(KV),
                 pl.BlockSpec((KV, step), lambda i, *_: (0, i)),
             ),
-            scratch_shapes=[pltpu.VMEM((8 + step, width), F32), pltpu.VMEM((step, width), F32)],
+            scratch_shapes=[
+                pltpu.VMEM((8 + step, width), F32),
+                pltpu.VMEM((step, width), F32),
+                pltpu.VMEM((dim, width), BF16),
+            ],
         ),
         compiler_params=params(),
         cost_estimate=COST,
         name="project_own",
-    )(meta, tokens, halo, gain, w, taps)
+    )(meta, tokens, halo, gain, taps, *w)
 
 
 def project_earlier_kernel(meta_ref, *refs):
@@ -267,7 +348,7 @@
     gain_ref, w_ref, taps_ref, raw_ref, normed_ref, kv_ref, kvt_ref, x_ref, buf_ref, mix_ref = refs[8:]
     i = pl.program_id(0)
     rows = x_ref.shape[0]
-    quarter = pieces[0].shape[0]
+    quarter = rows // 2
 
     @pl.when(i == 0)
     def _():
@@ -279,7 +360,7 @@
 
             @pl.when(i == place >> 1)
             def _(piece=pieces[4 * hop + slot], place=place):
-                x_ref[pl.ds(pl.multiple_of((place & 1) * quarter, quarter), quarter), :] = piece[...]
+                x_ref[pl.ds(pl.multiple_of((place & 1) * quarter, quarter), quarter), :] = piece[:quarter, :]
 
     exists = jnp.where(i < pl.num_programs(0) // REACH, meta_ref[HAS_TWO], meta_ref[HAS_ONE])
     x = jnp.where(exists == 1, x_ref[...].astype(F32), 0.0)
@@ -297,7 +378,8 @@
 
 
 def project_earlier(meta, pieces, gain, w, taps):
-    quarter, dim = pieces[0].shape
+    dim = pieces[0].shape[1]
+    quarter = pieces[0].shape[0] - HALO
     step = 2 * quarter
     span = len(pieces) * quarter
     tile = lambda n: pl.BlockSpec((step, n), lambda i, *_: (i, 0))
@@ -327,7 +409,7 @@
 
 
 LOW, FULL, STARTS = 1, 5, 9
-HAS_ONE, HAS_TWO, NEXT_ONE, NEXT_TWO = 17, 18, 19, 20
+HAS_ONE, HAS_TWO, NEXT_ONE, NEXT_TWO, BLK = 17, 18, 19, 20, 21
 
 
 STEP = 2 * TILE
@@ -797,7 +879,11 @@
     )(*attended, *w_out, x, gain)
 
 
-def feed_kernel(x0, x2, x1, x3, cot_ref, up_ref, down_ref, x_ref, act_ref, d_up_ref, keep_ref, send_ref):
+def feed_kernel(meta_ref, x0, x2, x1, x3, cot_ref, *refs, masks, shard):
+    count = (len(refs) - 7) // 2
+    packed_refs, down_refs = refs[:count], refs[count : 2 * count]
+    x_ref, act_ref, d_up_ref, keep_ref, send_ref, down_ref, up_ref = refs[2 * count :]
+
     def half(first, second, back_ref):
         x = jnp.concatenate([first[...], second[...]], axis=0)
         x_ref[...] = x
@@ -811,6 +897,8 @@
 
     @pl.when(pl.program_id(0) == 0)
     def _():
+        put_rows(up_ref, packed_refs, meta_ref[BLK], masks, shard)
+        put_rows(down_ref, down_refs, meta_ref[BLK], masks, shard)
         half(x0, x2, keep_ref)
 
     @pl.when(pl.program_id(0) == 1)
@@ -818,27 +906,32 @@
         half(x1, x3, send_ref)
 
 
-def feed(x, cot, w_up, w_down_t):
+def feed(meta, x, cot, packed, down, masks):
     rows, dim = cot.shape
-    units = w_up.shape[1]
+    shard, units = down[0].shape[1:]
     step = rows // 2
-    tile = lambda n: pl.BlockSpec((step, n), lambda i: (i, 0))
-    return pl.pallas_call(
-        feed_kernel,
+    tile = lambda n: pl.BlockSpec((step, n), lambda i, *_: (i, 0))
+    return pl.pallas_call(
+        functools.partial(feed_kernel, masks=masks, shard=shard),
         out_shape=(
             jax.ShapeDtypeStruct((rows, dim), BF16),
             jax.ShapeDtypeStruct((rows, units), BF16),
             jax.ShapeDtypeStruct((rows, units), BF16),
             jax.ShapeDtypeStruct((step, dim), BF16),
             jax.ShapeDtypeStruct((step, dim), BF16),
-        ),
-        grid=(2,),
-        in_specs=[whole()] * 4 + [tile(dim), whole(), whole()],
-        out_specs=(tile(dim), tile(units), tile(units), whole(), whole()),
+            jax.ShapeDtypeStruct((dim, units), BF16),
+        ),
+        grid_spec=pltpu.PrefetchScalarGridSpec(
+            num_scalar_prefetch=1,
+            grid=(2,),
+            in_specs=[whole()] * 4 + [tile(dim)] + [whole()] * (len(packed) + len(down)),
+            out_specs=(tile(dim), tile(units), tile(units), whole(), whole(), whole()),
+            scratch_shapes=[pltpu.VMEM((dim, units), BF16)],
+        ),
         compiler_params=params(),
         cost_estimate=COST,
         name="feed",
-    )(*x, cot, w_up, w_down_t)
+    )(meta, *x, cot, *packed, *down)
 
 
 def feed_rest_kernel(x_ref, d_up_ref, cot_ref, act_ref, down_ref, grads_ref, keep_ref, send_ref):
@@ -1049,18 +1142,21 @@
     blk = lax.axis_index("blk")
     head = lax.axis_index("head")
     groups = bit_groups("blk")
+    halves = [(bit,) for group in groups[:-1] for bit in group]
     together = lax.optimization_barrier
     own_quarter = lax.dynamic_slice_in_dim(tokens, head * quarter, quarter)
-    two = moved(own_quarter, "blk", 2)
+    sent = jnp.concatenate([own_quarter, tokens[rows - HALO :]])
+    two = moved(sent, "blk", 2)
     shard, units = w_up.shape
+    masks = gathered_masks("blk")
     w_mix = jnp.concatenate([w_query, w_key, w_value], axis=1)
+    w_some = sent_round(w_mix, "blk")
+    one = swap(jnp.where(bit_of("blk", 0), two, sent), "blk", 1)
+    pieces = [*quarters(two), *quarters(one)]
     packed, down_some = pack(w_up, w_out, w_down)
-    w_some = gathered(w_mix[None], "blk", groups[:-1], w_mix.shape)
-    one = swap(jnp.where(bit_of("blk", 0), two, own_quarter), "blk", 1)
-    pieces = [*quarters(two), *quarters(one)]
-    halo = moved(tokens[rows - HALO :], "blk", 1)
-    w_mix = gathered(w_some, "blk", groups[-1:], w_mix.shape).reshape(dim, 3 * part)
-    packed, _, _ = together((packed, w_some, two))
+    w_some, packed = together((joined(w_some), packed))
+    w_mix = pieces_of(w_some, "blk", shard)
+    packed_some = sent_round(packed, "blk")
     span = (REACH + 1) * rows
     padded_ids = jnp.pad(seg_ids, (REACH * rows, 0), constant_values=-1)
     window = lax.dynamic_slice_in_dim(padded_ids, blk * rows, span)
@@ -1071,41 +1167,39 @@
     full = (first_row[TILE - 1 :: TILE] + TILE - 1) // TILE
     last = lax.axis_size("blk") - 1
     exists = jnp.stack([blk >= 1, blk >= 2, blk + 1 <= last, blk + 2 <= last])
-    meta = jnp.concatenate([head[None], low, full, starts, exists]).astype(jnp.int32)
+    meta = jnp.concatenate([head[None], low, full, starts, exists, blk[None]]).astype(jnp.int32)
     first_row = first_row[None]
     taps = arranged(*conv_kernels)
     gain_one, gain_two = gain_attn[None], gain_ffn[None]
 
-    w_mix, *pieces[:2], pieces[4] = together((w_mix, *pieces[:2], pieces[4]))
-    w_mix, raw_halo, raw, normed, q, kv, kvt = project_own(meta, tokens, halo, gain_one, w_mix, taps)
-    packed_some = gathered(packed[None], "blk", groups[:-1], packed.shape, raw)
-    down_some, _ = together((down_some, raw))
-    q, pieces[5] = together((q, pieces[5]))
-    acc_own, stat_own = attend_own(q, kv, kvt, first_row)
-    wide = gathered(packed_some, "blk", groups[-1:], packed.shape, acc_own)
-    down_some = gathered(down_some[None], "blk", groups[:-1], (shard, dim), acc_own)
-    full_up = wide[:, :shard].reshape(dim, units)
-    out_full = wide[:, shard:].reshape(-1, packed.shape[0] - shard, units // part, part)
-    out_full = jnp.swapaxes(out_full, 1, 2).reshape(dim, part).T
-    out_far = swap(out_full, "head", 2)
-    down_t = gathered(down_some, "blk", groups[-1:], (shard, dim)).reshape(dim, units)
-    raw_e, normed_e, kv_e, kvt_e = project_earlier(meta, pieces, gain_one, w_mix, taps)
-    out_far, out_full, _ = together((out_far, out_full, raw_e))
-    out_pieces = [out_full, out_far, swap(out_full, "head", 1), swap(out_far, "head", 1)]
     hi, lo = bit_of("head", 1), bit_of("head", 0)
     cot = cotangent.reshape(2, 2, quarter, dim)
     cot = jnp.where(hi, cot[::-1], cot)
     cot = jnp.where(lo, cot[:, ::-1], cot)
     cot = jnp.swapaxes(cot, 0, 1).reshape(rows, dim)
-    kv_late, cot, full_up, *out_pieces = together((kv_e, cot, full_up, *out_pieces))
+    *w_mix, cot, pieces[0], pieces[1], pieces[4] = together((*w_mix, cot, pieces[0], pieces[1], pieces[4]))
+    w_mix, raw_halo, raw, normed, q, kv, kvt = project_own(meta, tokens, pieces[4], gain_one, taps, w_mix, masks)
+    q, pieces[5] = together((q, pieces[5]))
+    acc_own, stat_own = attend_own(q, kv, kvt, first_row)
+    acc_own, down_some, *packed_some = together((acc_own, down_some, *packed_some))
+    packed = pieces_of(joined(packed_some), "blk", shard)
+    down_some = sent_round(down_some, "blk")
+    raw_e, normed_e, kv_e, kvt_e = project_earlier(meta, pieces, gain_one, w_mix, taps)
+    raw_e, *more = together((raw_e, *packed, *down_some))
+    packed, down_some = more[: len(packed)], more[len(packed) :]
+    down = pieces_of(joined(down_some), "blk", shard)
+    out_full = unpack_out(meta, packed, masks, shard, part)
+    out_far = swap(out_full, "head", 2)
+    out_pieces = [out_full, out_far, swap(out_full, "head", 1), swap(out_far, "head", 1)]
+    kv_late, out_full = together((kv_e, out_full))
     att, out_t, lse = attend_earlier(meta, q, kv_late, kvt_e, first_row, acc_own, stat_own)
 
     near = swap(att[2:], "head", 1)
     across = swap(jnp.stack([att[1], near[1]]), "head", 2)
     attended = (att[0], across[0], near[0], across[1])
-    quarter_late, down_t = together((own_quarter, down_t))
+    quarter_late, *down = together((own_quarter, *down))
     hidden, normed_two = after_attend(attended, out_pieces, quarter_late, gain_two)
-    ffn_in, act, d_up, *back = feed(quarters(normed_two), cot, full_up, down_t)
+    ffn_in, act, d_up, *back, down_t = feed(meta, quarters(normed_two), cot, packed, down, masks)
     chip_back = sum_halves(*back)
     far_back = swap(chip_back[quarter:], "head", 2)
     feed_grads, *ffn = feed_rest(ffn_in, d_up, cot, act, down_t)
@@ -1129,44 +1223,49 @@
     )
     from_two = moved(d_two, "blk", -2)
     from_one = moved(d_one, "blk", -1)
-    dq_t, far_ffn, far_out = together((dq_t, far_ffn, far_out))
+    output = (hidden + total_of([chip_ffn[:quarter], far_ffn])).astype(BF16)
+    dq_t, output, far_out = together((dq_t, output, far_out))
+    output_far = swap(output, "head", 2)
     d_raw, sums_own, grad_mix = own_back(
         meta, q, d_out_t, out_t, lse, first_row, dq_t, kv, kvt, raw, taps, grad_next,
         normed_e, d_two, d_one, normed, keep_out, near_out, far_out,
     )
-    chip_ffn, far_ffn, _ = together((chip_ffn, far_ffn, d_raw))
-    output = list(quarters((hidden + total_of([chip_ffn[:quarter], far_ffn])).astype(BF16)))
-    gain_two_part, _ = together((gain_two_part, d_raw))
-    gain_two_part = sum_everywhere(gain_two_part, "head", [(0,), (1,)])
-    d_raw, gain_two_part, *more = together((d_raw, gain_two_part, *output, *near_parts))
-    output, near_parts = more[:4], more[4:]
     mix_parts = chosen(grad_mix.reshape(1, -1, shard, 4 * part), "blk", groups[-1])
     mix_parts = received(mix_parts, "blk", groups[-1])
+    output_far, output, d_raw = together((output_far, output, d_raw))
+    output = [output, output_far, swap(output, "head", 1), swap(output_far, "head", 1)]
+    d_raw, *more = together((d_raw, *output, *near_parts, *mix_parts))
+    output, near_parts, mix_parts = more[:4], more[4:6], more[6:]
     *back, gain_one_part = d_normed_parts(meta, d_raw, from_one, from_two, tokens, w_mix)
+    near_parts = total_of(near_parts).astype(BF16)
     chip_back = sum_halves(*back)
+    gains = jnp.concatenate([gain_two_part, gain_one_part])
+    gains = gains + swap(gains, "head", 1)
+    chip_back, gains, near_parts, *mix_parts = together((chip_back, gains, near_parts, *mix_parts))
     far_back = swap(chip_back[quarter:], "head", 2)
-    _, *near_parts = together((back[0], *near_parts))
-    feed_grads = sum_scatter(total_of(near_parts).astype(BF16), "blk", groups[:-1])
-    _, gain_one_part = together((chip_back, gain_one_part))
-    gain_one_part = sum_everywhere(gain_one_part, "head", [(0,), (1,)])
+    up_parts = sum_scatter(near_parts[:1], "blk", halves)
+    down_parts = sum_scatter(near_parts[1:], "blk", halves)
+    mix_parts = sum_scatter(total_of(mix_parts).astype(BF16), "blk", halves)
+    far_back, far_gains = together((far_back, swap(gains, "head", 2)))
     grad_tokens = grad_tokens_own(chip_back[:quarter], far_back, own_quarter, gain_one, d_hidden)
-    grad_tokens = list(quarters(grad_tokens))
-    grad_tokens[2], gain_one_part, output[0], *mix_parts = together(
-        (grad_tokens[2], gain_one_part, output[0], *mix_parts)
-    )
+    grad_tokens, far_gains = together((grad_tokens, far_gains))
+    gains = gains + far_gains
+    grad_far = swap(grad_tokens, "head", 2)
+    grad_far, output[0], *more = together((grad_far, output[0], *up_parts, *down_parts, *mix_parts))
+    up_parts, down_parts, mix_parts = more[:2], more[2:4], more[4:]
+    grad_tokens = [grad_tokens, grad_far, swap(grad_tokens, "head", 1), swap(grad_far, "head", 1)]
     grad_tokens = by_place(meta, grad_tokens, F32)
-    mix_parts = sum_scatter(total_of(mix_parts).astype(BF16), "blk", groups[:-1])
 
     output = by_place(meta, output, BF16)
-    feed_grads = total_of(feed_grads).reshape(2, shard, units)
-    grad_up_shard, grad_down_shard = feed_grads[0], feed_grads[1].T
+    grad_up_shard = total_of(up_parts).reshape(shard, units)
+    grad_down_shard = total_of(down_parts).reshape(shard, units).T
     mix_shard = total_of(mix_parts).reshape(shard, 4 * part)
     grad_query_shard, grad_key_shard, grad_value_shard = separated(mix_shard[:, : 3 * part])
     grad_out_shard = mix_shard[:, 3 * part :].T
 
     taps_part = jnp.concatenate([sums_own[:3, :KV] + sums_before[:3], sums_own[:3, KV:] + sums_halo[:3]], axis=1)
     taps_part = jnp.stack(separated(taps_part)).reshape(-1)
-    small = jnp.concatenate([gain_two_part[0], gain_one_part[0], taps_part])
+    small = jnp.concatenate([gains.reshape(-1), taps_part])
     small = sum_everywhere(small, "blk", groups)
     grad_gain_ffn, grad_gain_attn = small[:dim], small[dim : 2 * dim]
     grad_kernels = small[2 * dim :].reshape(3, 3, part)

time: 301 us -> 299 us (level); the launches traced: 302 us -> 293 us
  local copies, waits for them, and re-layouts: 39.6 us -> 35.2 us
  waiting for transfers between devices: 98.4 us -> 102 us
  starting transfers between devices: 73.7 us -> 70.3 us
    ppermute x59 -> x57, waiting for transfers between devices: 74.4 us -> 90.9 us  [swap(): lax.ppermute(x, axis, [(i, i ^ mask) for i in range(lax.axis_size(axis))])]
    ppermute x4 -> x3, waiting for transfers between devices: 24 us -> 10.8 us  [moved(): lax.ppermute(x, axis, [(i, i + distance) for i in range(size) if 0 <= i +...]
    another operation x7 -> x0, other arithmetic: 6.54 us -> none  [in_order(): both = jnp.stack(pieces)]
    unnamed x140 -> x163, local copies, waits for them, and re-layouts: 16.8 us -> 21.4 us
    select_n x10 -> x1, other arithmetic: 3.88 us -> 0.1 us  [body(): one = swap(jnp.where(bit_of('blk', 0), two, sent), 'blk', 1)]
    ppermute x4 -> x3, starting transfers between devices: 9.29 us -> 5.54 us  [moved(): lax.ppermute(x, axis, [(i, i + distance) for i in range(size) if 0 <= i +...]
    pallas_call x2 -> x6, Pallas kernels: 9 us -> 11.6 us  [the longest x1 5.61 us: project_own(): pl.pallas_call(functools.partial(project_own_kernel, base=REACH * rows, m...]
    ppermute x59 -> x57, starting transfers between devices: 64.4 us -> 64.8 us  [swap(): lax.ppermute(x, axis, [(i, i ^ mask) for i in range(lax.axis_size(axis))])]
  transfers between devices with their start and end apart: 63 -> 60, of which waited for: 22 -> 22; matrix products, arithmetic and copies ran while one was open for 15% -> 10% of each run, Pallas kernels for 19% -> 18%
where the time goes in v3:
time: 299 us; the launch traced here: 293 us
  waiting for transfers between devices  102 us (34%)
  starting transfers between devices  70.3 us (24%)
  Pallas kernels  64.8 us (22%)
  local copies, waits for them, and re-layouts  35.2 us (12%)
  other arithmetic  18.9 us (6%)
    ppermute x57, waiting for transfers between devices, swap(): lax.ppermute(x, axis, [(i, i ^ mask) for i in range(lax.axis_size(axis))])  90.9 us
    ppermute x57, starting transfers between devices, swap(): lax.ppermute(x, axis, [(i, i ^ mask) for i in range(lax.axis_size(axis))])  64.8 us
    unnamed x163, local copies, waits for them, and re-layouts  21.4 us
    pallas_call x1, Pallas kernels, earlier_back(): pl.pallas_call(earlier_back_kernel, out_shape=(jax.ShapeDtypeStruct((part...  11.8 us
    pallas_call x1, Pallas kernels, own_back(): pl.pallas_call(own_back_kernel, out_shape=(jax.ShapeDtypeStruct((rows, wi...  11.7 us
    ppermute x3, waiting for transfers between devices, moved(): lax.ppermute(x, axis, [(i, i + distance) for i in range(size) if 0 <= i +...  10.8 us
    pallas_call x1, Pallas kernels, project_earlier(): pl.pallas_call(project_earlier_kernel, out_shape=(jax.ShapeDtypeStruct((s...  7.24 us
  transfers between devices with their start and end apart: 60, of which 22 were waited for; matrix products, arithmetic and copies ran while one was open for 10% of the time, Pallas kernels for 18%

profile of v3, /device:TPU:0, one launch (start us, length us, event | category | flops | bytes accessed | tf_op | source)
XLA Modules:
  0.0 293.3 jit_solution(16944977127168339208)
XLA Ops:
  1.7 3.1 %collective-permute-start = (bf16[1,96,576]{2,1,0:T(8,128)(2,1)S(1)}, bf16[1,96,576]{2,1,0:T(8,128)(2,1)S(1)}, u32[]{:S(2)}, u32[]{:S(2)}) collective-permute-start(bf16[1,96,576]{2,1,0:T(8,128)(2,1)S(1)} %maximum_bitcast_fusion.refs_0_), channel_id=1, source_target_pairs={{0,8},{4,12},{8,0},{12,4},{16,24},{20,28},{24,16},{28,20},{1,9},{5... | collective-permute-start | bytes 331784 | tf_op jit(solution)/shard_map/ppermute | solution.py:35
  4.8 2.6 collective-permute-start.1
  9.2 2.8 collective-permute-start.4
  13.8 1.6 copy.34
  15.6 1.4 reverse_select_fusion.1
  17.0 4.6 %collective-permute-done.4.refs_0_ = bf16[272,768]{1,0:T(8,128)(2,1)S(1)} collective-permute-done((bf16[272,768]{1,0:T(8,128)(2,1)S(1)}, bf16[272,768]{1,0:T(8,128)(2,1)S(1)}, u32[]{:S(2)}, u32[]{:S(2)}) %collective-permute-start.4) | collective-permute-done | bytes 417824 | tf_op jit(solution)/shard_map/ppermute | solution.py:40
  21.7 1.6 collective-permute-start.6
  25.0 1.5 collective-permute-start.5
  26.5 8.0 %collective-permute-done.6.halo_ref.refs_4_ = bf16[272,768]{1,0:T(8,128)(2,1)} collective-permute-done((bf16[272,768]{1,0:T(8,128)(2,1)S(1)}, bf16[272,768]{1,0:T(8,128)(2,1)}, u32[]{:S(2)}, u32[]{:S(2)}) %collective-permute-start.6) | collective-permute-done | bytes 417824 | tf_op jit(solution)/shard_map/ppermute | solution.py:35
  34.5 1.5 collective-permute-start.7
  36.3 5.4 %collective-permute-start.12 = (bf16[1,120,768]{2,1,0:T(8,128)(2,1)S(1)}, bf16[1,120,768]{2,1,0:T(8,128)(2,1)S(1)}, u32[]{:S(2)}, u32[]{:S(2)}) collective-permute-start(bf16[1,120,768]{2,1,0:T(8,128)(2,1)S(1)} %bitcast.88), channel_id=1, source_target_pairs={{0,8},{4,12},{8,0},{12,4},{16,24},{20,28},{24,16},{28,20},{1,9},{5... | collective-permute-start | bytes 552968 | tf_op jit(solution)/shard_map/ppermute | solution.py:35
  41.7 2.0 collective-permute-start.13
  44.5 5.4 %collective-permute-start.14 = (bf16[1,120,768]{2,1,0:T(8,128)(2,1)S(1)}, bf16[1,120,768]{2,1,0:T(8,128)(2,1)S(1)}, u32[]{:S(2)}, u32[]{:S(2)}) collective-permute-start(bf16[1,120,768]{2,1,0:T(8,128)(2,1)S(1)} %bitcast.90), channel_id=1, source_target_pairs={{0,24},{4,28},{8,16},{12,20},{16,8},{20,12},{24,0},{28,4},{1,25},{... | collective-permute-start | bytes 552968 | tf_op jit(solution)/shard_map/ppermute | solution.py:35
  49.9 2.4 reverse_select_fusion
  53.0 5.6 %project_own.1 = (bf16[768,576]{1,0:T(8,128)(2,1)S(1)}, bf16[16,192]{1,0:T(8,128)(2,1)S(1)}, bf16[1024,576]{1,0:T(8,128)(2,1)S(1)}, bf16[1024,768]{1,0:T(8,128)(...) custom-call(s32[22]{0:T(128)S(1)} %concatenate.30.meta_ref, ...), custom_call_target="tpu_custom_call" | custom-call | flops 1 | bytes 1 | tf_op jit(solution)/shard_map/project_own/pallas_call | solution.py:310
  59.9 3.6 %attend_own.1 = (f32[192,1024]{1,0:T(8,128)S(1)}, f32[16,1024]{1,0:T(8,128)S(1)}) custom-call(bf16[1024,192]{1,0:T(8,128)(2,1)S(1)} %get-tuple-element.131.q_ref, bf16[1024,384]{1,0:T(8,128)(2,1)S(1)} %get-tuple-element.138.kv_ref.kv_own_ref, bf16[384,1024]{1,0:T(8,128)(2,1)S(1)} %get-tuple-element.139.kvt_ref.kvt_own_ref, s32[1,1024]{1,0:T(1,128)S(1)} %bitcast.96), custom_call_target="tpu_custom_call" | custom-call | flops 1 | bytes 1 | tf_op jit(solution)/shard_map/attend_own/pallas_call | solution.py:557
  63.6 1.6 collective-permute-start.15
  67.5 1.6 collective-permute-start.16
  69.1 2.8 collective-permute-start.18
  71.9 7.2 %project_earlier.1 = (bf16[2048,384]{1,0:T(8,128)(2,1)S(1)}, bf16[2048,768]{1,0:T(8,128)(2,1)S(1)}, bf16[2048,384]{1,0:T(8,128)(2,1)S(1)}, bf16[384,2048]{1,0:T(8,128)(2,1)S(1)}) custom-call(s32[22]{0:T(128)S(1)} %concatenate.30.meta_ref, bf16[272,768]{1,0:T(8,128)(2,1)S(1)} %copy-done.23, bf16[272,768]{1,0:T(8,128)(2,1)S(1)} %copy-done.56, ...), custom_call_target="tpu_custom_call" | custom-call | flops 1 | bytes 1 | tf_op jit(solution)/shard_map/project_earlier/pallas_call | solution.py:386
  80.4 2.4 collective-permute-done.17.refs_2_
  84.2 1.6 collective-permute-start.21
  89.4 1.9 collective-permute-done.21.w1
  91.3 4.5 %collective-permute-done.20 = bf16[2,192,256]{2,1,0:T(8,128)(2,1)S(1)} collective-permute-done((bf16[2,192,256]{2,1,0:T(8,128)(2,1)S(1)}, bf16[2,192,256]{2,1,0:T(8,128)(2,1)S(1)}, u32[]{:S(2)}, u32[]{:S(2)}) %collective-permute-start.20) | collective-permute-done | bytes 196640 | tf_op jit(solution)/shard_map/ppermute | solution.py:35
  98.2 1.5 collective-permute-start.25
  99.7 8.2 %collective-permute-done.25.x2 = bf16[256,768]{1,0:T(8,128)(2,1)S(1)} collective-permute-done((bf16[256,768]{1,0:T(8,128)(2,1)S(1)}, bf16[256,768]{1,0:T(8,128)(2,1)S(1)}, u32[]{:S(2)}, u32[]{:S(2)}) %collective-permute-start.25) | collective-permute-done | bytes 393248 | tf_op jit(solution)/shard_map/ppermute | solution.py:35
  107.9 1.7 collective-permute-done.27.x3
  109.6 5.0 %feed.1 = (bf16[1024,768]{1,0:T(8,128)(2,1)S(1)}, bf16[1024,768]{1,0:T(8,128)(2,1)S(1)}, bf16[1024,768]{1,0:T(8,128)(2,1)S(1)}, bf16[512,768]{1,0:T(8,128)(2,1)S...) custom-call(s32[22]{0:T(128)S(1)} %concatenate.30.meta_ref, bf16[256,768]{1,0:T(8,128)(2,1)S(1)} %get-tuple-element.160.x0, ...), custom_call_target="tpu_custom_call" | custom-call | flops 1 | bytes 1 | tf_op jit(solution)/shard_map/feed/pallas_call | solution.py:914
  116.9 2.1 collective-permute-done.28
  120.2 1.4 collective-permute-start.29
  123.0 1.4 copy-done.29
  124.5 1.4 copy-done.31
  127.1 4.7 %feed_rest.1 = (bf16[2,768,768]{2,1,0:T(8,128)(2,1)S(1)}, bf16[512,768]{1,0:T(8,128)(2,1)S(1)}, bf16[512,768]{1,0:T(8,128)(2,1)S(1)}) custom-call(bf16[1024,768]{1,0:T(8,128)(2,1)S(1)} %copy-done.27, bf16[1024,768]{1,0:T(8,128)(2,1)S(1)} %copy-done.31, bf16[1024,768]{1,0:T(8,128)(2,1)S(1)} %bitcast.85, bf16[1024,768]{1,0:T(8,128)(2,1)S(1)} %copy-done.29, ...), custom_call_target="tpu_custom_call" | custom-call | flops 1 | bytes 1 | tf_op jit(solution)/shard_map/feed_rest/pallas_call | solution.py:951
  132.0 1.6 dynamic-slice_bitcast_fusion
  134.5 2.4 before_back.1
  137.8 6.5 %collective-permute-done.30 = bf16[2,192,256]{2,1,0:T(8,128)(2,1)S(1)} collective-permute-done((bf16[2,192,256]{2,1,0:T(8,128)(2,1)S(1)}, bf16[2,192,256]{2,1,0:T(8,128)(2,1)S(1)}, u32[]{:S(2)}, u32[]{:S(2)}) %collective-permute-start.30) | collective-permute-done | bytes 196640 | tf_op jit(solution)/shard_map/ppermute | solution.py:35
  146.6 6.9 %collective-permute-start.39 = (bf16[2,4,96,768]{3,2,1,0:T(8,128)(2,1)}, bf16[2,4,96,768]{3,2,1,0:T(8,128)(2,1)}, u32[]{:S(2)}, u32[]{:S(2)}) collective-permute-start(bf16[2,4,96,768]{3,2,1,0:T(8,128)(2,1)} %get-tuple-element.203), channel_id=1, source_target_pairs={{0,4},{4,0},{8,12},{12,8},{16,20},{20,16},{24,28},{28,24},{1,5},{5... | collective-permute-start | bytes 3538952 | tf_op jit(solution)/shard_map/ppermute | solution.py:35
  155.7 1.4 copy-done.5
  157.1 1.4 copy-done.7
  161.1 11.8 %earlier_back.1 = (f32[192,1024]{1,0:T(8,128)S(1)}, bf16[1024,384]{1,0:T(8,128)(2,1)S(1)}, bf16[1040,384]{1,0:T(8,128)(2,1)S(1)}, f32[256,384]{1,0:T(8,128)S(1)}...) custom-call(s32[22]{0:T(128)S(1)} %concatenate.30.meta_ref, bf16[1024,192]{1,0:T(8,128)(2,1)S(1)} %get-tuple-element.131.q_ref, ...), custom_call_target="tpu_custom_call" | custom-call | flops 1 | bytes 1 | tf_op jit(solution)/shard_map/earlier_back/pallas_call | solution.py:760
  172.9 1.4 collective-permute-start.41
  177.0 11.7 %own_back.1 = (bf16[1024,576]{1,0:T(8,128)(2,1)S(1)}, f32[8,576]{1,0:T(8,128)S(1)}, bf16[768,768]{1,0:T(8,128)(2,1)S(1)}) custom-call(s32[22]{0:T(128)S(1)} %concatenate.30.meta_ref, bf16[1024,192]{1,0:T(8,128)(2,1)S(1)} %get-tuple-element.131.q_ref, bf16[4,192,256]{2,1,0:T(8,128)(2,1)S(1)} %pad_maximum_fusion.1.dt_ref, f32[192,1024]{1,0:T(8,128)S(1)} %copy-done.12, ...), custom_call_target="tpu_custom_call" | custom-call | flops 1 | bytes 1 | tf_op jit(solution)/shard_map/own_back/pallas_call | solution.py:835
  189.5 3.9 %collective-permute-start.40 = (bf16[1,4,96,768]{3,2,1,0:T(8,128)(2,1)S(1)}, bf16[1,4,96,768]{3,2,1,0:T(8,128)(2,1)S(1)}, u32[]{:S(2)}, u32[]{:S(2)}) collective-permute-start(bf16[1,4,96,768]{3,2,1,0:T(8,128)(2,1)S(1)} %get-tuple-element.276), channel_id=1, source_target_pairs={{0,4},{4,0},{8,12},{12,8},{16,20},{20,16},{24,28},{28,24},{1,5},{5... | collective-permute-start | bytes 1769480 | tf_op jit(solution)/shard_map/ppermute | solution.py:35
  193.5 1.5 collective-permute-start.36
  195.0 8.8 %collective-permute-done.36.refs_1_ = bf16[256,768]{1,0:T(8,128)(2,1)S(1)} collective-permute-done((bf16[256,768]{1,0:T(8,128)(2,1)S(1)}, bf16[256,768]{1,0:T(8,128)(2,1)S(1)}, u32[]{:S(2)}, u32[]{:S(2)}) %collective-permute-start.36) | collective-permute-done | bytes 393248 | tf_op jit(solution)/shard_map/ppermute | solution.py:35
  204.4 18.5 %collective-permute-done.40 = bf16[1,4,96,768]{3,2,1,0:T(8,128)(2,1)S(1)} collective-permute-done((bf16[1,4,96,768]{3,2,1,0:T(8,128)(2,1)S(1)}, bf16[1,4,96,768]{3,2,1,0:T(8,128)(2,1)S(1)}, u32[]{:S(2)}, u32[]{:S(2)}) %collective-permute-start.40) | collective-permute-done | bytes 589856 | tf_op jit(solution)/shard_map/ppermute | solution.py:35
  222.9 6.1 %collective-permute-done.42.two_ref = bf16[1024,384]{1,0:T(8,128)(2,1)S(1)} collective-permute-done((bf16[1024,384]{1,0:T(8,128)(2,1)S(1)}, bf16[1024,384]{1,0:T(8,128)(2,1)S(1)}, u32[]{:S(2)}, u32[]{:S(2)}) %collective-permute-start.42) | collective-permute-done | bytes 786464 | tf_op jit(solution)/shard_map/ppermute | solution.py:40
  229.1 4.0 %d_normed_parts.1 = (bf16[512,768]{1,0:T(8,128)(2,1)S(1)}, bf16[512,768]{1,0:T(8,128)(2,1)}, f32[1,768]{1,0:T(1,128)S(1)}) custom-call(s32[22]{0:T(128)S(1)} %concatenate.30.meta_ref, bf16[1024,576]{1,0:T(8,128)(2,1)S(1)} %get-tuple-element.205.own_ref, bf16[1040,384]{1,0:T(8,128)(2,1)S(1)} %collective-permute-done.41.one_ref.halo_ref, ...), custom_call_target="tpu_custom_call" | custom-call | flops 1 | bytes 1 | tf_op jit(solution)/shard_map/d_normed_parts/pallas_call | solution.py:1048
  233.8 1.9 add_convert_fusion
  237.6 2.1 collective-permute-start.50
  240.5 1.6 collective-permute-start.45
  242.6 4.7 %collective-permute-done.52 = bf16[1,2,96,768]{3,2,1,0:T(8,128)(2,1)S(1)} collective-permute-done((bf16[1,2,96,768]{3,2,1,0:T(8,128)(2,1)S(1)}, bf16[1,2,96,768]{3,2,1,0:T(8,128)(2,1)S(1)}, u32[]{:S(2)}, u32[]{:S(2)}) %collective-permute-start.52) | collective-permute-done | bytes 294944 | tf_op jit(solution)/shard_map/ppermute | solution.py:35
  248.1 2.2 collective-permute-start.53
  250.3 6.5 %collective-permute-done.50 = bf16[1,2,96,768]{3,2,1,0:T(8,128)(2,1)S(1)} collective-permute-done((bf16[1,2,96,768]{3,2,1,0:T(8,128)(2,1)S(1)}, bf16[1,2,96,768]{3,2,1,0:T(8,128)(2,1)S(1)}, u32[]{:S(2)}, u32[]{:S(2)}) %collective-permute-start.50) | collective-permute-done | bytes 294944 | tf_op jit(solution)/shard_map/ppermute | solution.py:35
  258.1 2.2 collective-permute-start.56
  261.2 2.4 collective-permute-done.48
  265.6 1.5 collective-permute-start.47
  267.2 3.2 %collective-permute-done.57 = f32[3264]{0:T(1024)S(1)} collective-permute-done((f32[3264]{0:T(1024)S(1)}, f32[3264]{0:T(1024)S(1)}, u32[]{:S(2)}, u32[]{:S(2)}) %collective-permute-start.57) | collective-permute-done | bytes 13088 | tf_op jit(solution)/shard_map/ppermute | solution.py:35
  271.9 2.3 collective-permute-done.59
  275.6 4.5 %collective-permute-done.49 = bf16[1,1,96,768]{3,2,1,0:T(8,128)(2,1)S(1)} collective-permute-done((bf16[1,1,96,768]{3,2,1,0:T(8,128)(2,1)}, bf16[1,1,96,768]{3,2,1,0:T(8,128)(2,1)S(1)}, u32[]{:S(2)}, u32[]{:S(2)}) %collective-permute-start.49) | collective-permute-done | bytes 147488 | tf_op jit(solution)/shard_map/ppermute | solution.py:35
  282.4 1.7 add_bitcast_fusion
  284.8 2.3 assemble.2
  288.5 1.7 add_bitcast_fusion.1
  290.2 2.7 assemble.3
  (324 shorter events, 55.3 us)
Async XLA Ops:
  1.7 21.6 %collective-permute-start = (bf16[1,96,576]{2,1,0:T(8,128)(2,1)S(1)}, bf16[1,96,576]{2,1,0:T(8,128)(2,1)S(1)}, u32[]{:S(2)}, u32[]{:S(2)}) collective-permute-start(bf16[1,96,576]{2,1,0:T(8,128)(2,1)S(1)} %maximum_bitcast_fusion.refs_0_), channel_id=1, source_target_pairs={{0,8},{4,12},{8,0},{12,4},{16,24},{20,28},{24,16},{28,20},{1,9},{5... | collective-permute-start | bytes 331784 | tf_op jit(solution)/shard_map/ppermute | solution.py:35
  4.8 18.5 %collective-permute-start.1 = (bf16[1,96,576]{2,1,0:T(8,128)(2,1)S(1)}, bf16[1,96,576]{2,1,0:T(8,128)(2,1)S(1)}, u32[]{:S(2)}, u32[]{:S(2)}) collective-permute-start(bf16[1,96,576]{2,1,0:T(8,128)(2,1)S(1)} %maximum_bitcast_fusion.refs_0_), channel_id=1, source_target_pairs={{0,16},{4,20},{8,24},{12,28},{16,0},{20,4},{24,8},{28,12},{1,17},{... | collective-permute-start | bytes 331784 | tf_op jit(solution)/shard_map/ppermute | solution.py:35
  7.4 16.0 %collective-permute-start.2 = (bf16[1,96,576]{2,1,0:T(8,128)(2,1)S(1)}, bf16[1,96,576]{2,1,0:T(8,128)(2,1)S(1)}, u32[]{:S(2)}, u32[]{:S(2)}) collective-permute-start(bf16[1,96,576]{2,1,0:T(8,128)(2,1)S(1)} %maximum_bitcast_fusion.refs_0_), channel_id=1, source_target_pairs={{0,24},{4,28},{8,16},{12,20},{16,8},{20,12},{24,0},{28,4},{1,25},{... | collective-permute-start | bytes 331784 | tf_op jit(solution)/shard_map/ppermute | solution.py:35
  9.2 12.4 %collective-permute-start.4 = (bf16[272,768]{1,0:T(8,128)(2,1)S(1)}, bf16[272,768]{1,0:T(8,128)(2,1)S(1)}, u32[]{:S(2)}, u32[]{:S(2)}) collective-permute-start(bf16[272,768]{1,0:T(8,128)(2,1)S(1)} %pad_maximum_fusion), channel_id=1, source_target_pairs={{0,8},{4,12},{8,16},{12,20},{16,24},{20,28},{1,9},{5,13},{9,17},{1... | collective-permute-start | bytes 1253384 | tf_op jit(solution)/shard_map/ppermute | solution.py:40
  21.6 30.6 %copy-start.22 = (bf16[272,768]{1,0:T(8,128)(2,1)}, bf16[272,768]{1,0:T(8,128)(2,1)S(1)}, u32[]{:S(2)}) copy-start(bf16[272,768]{1,0:T(8,128)(2,1)S(1)} %collective-permute-done.4.refs_0_) | copy-start | bytes 1253380
  21.7 12.8 %collective-permute-start.6 = (bf16[272,768]{1,0:T(8,128)(2,1)S(1)}, bf16[272,768]{1,0:T(8,128)(2,1)}, u32[]{:S(2)}, u32[]{:S(2)}) collective-permute-start(bf16[272,768]{1,0:T(8,128)(2,1)S(1)} %broadcast_select_fusion), channel_id=1, source_target_pairs={{0,4},{4,0},{8,12},{12,8},{16,20},{20,16},{24,28},{28,24},{1,5},{5... | collective-permute-start | bytes 1253384 | tf_op jit(solution)/shard_map/ppermute | solution.py:35
  23.4 20.3 %collective-permute-start.3 = (bf16[4,96,576]{2,1,0:T(8,128)(2,1)S(1)}, bf16[4,96,576]{2,1,0:T(8,128)(2,1)S(1)}, u32[]{:S(2)}, u32[]{:S(2)}) collective-permute-start(bf16[4,96,576]{2,1,0:T(8,128)(2,1)S(1)} %joined.3.refs_0_), channel_id=1, source_target_pairs={{0,4},{4,0},{8,12},{12,8},{16,20},{20,16},{24,28},{28,24},{1,5},{5... | collective-permute-start | bytes 1327112 | tf_op jit(solution)/shard_map/ppermute | solution.py:35
  25.0 27.3 %collective-permute-start.5 = (bf16[272,768]{1,0:T(8,128)(2,1)S(1)}, bf16[272,768]{1,0:T(8,128)(2,1)S(1)}, u32[]{:S(2)}, u32[]{:S(2)}) collective-permute-start(bf16[272,768]{1,0:T(8,128)(2,1)S(1)} %collective-permute-done.4.refs_0_), channel_id=1, source_target_pairs={{0,2},{1,3},{2,0},{3,1},{4,6},{5,7},{6,4},{7,5},{8,10},{9,11},{10,... | collective-permute-start | bytes 1253384 | tf_op jit(solution)/shard_map/ppermute | solution.py:35
  34.5 25.3 %collective-permute-start.7 = (bf16[272,768]{1,0:T(8,128)(2,1)}, bf16[272,768]{1,0:T(8,128)(2,1)}, u32[]{:S(2)}, u32[]{:S(2)}) collective-permute-start(bf16[272,768]{1,0:T(8,128)(2,1)} %collective-permute-done.6.halo_ref.refs_4_), channel_id=1, source_target_pairs={{0,2},{1,3},{2,0},{3,1},{4,6},{5,7},{6,4},{7,5},{8,10},{9,11},{10,... | collective-permute-start | bytes 1253384 | tf_op jit(solution)/shard_map/ppermute | solution.py:35
  36.3 27.2 %collective-permute-start.12 = (bf16[1,120,768]{2,1,0:T(8,128)(2,1)S(1)}, bf16[1,120,768]{2,1,0:T(8,128)(2,1)S(1)}, u32[]{:S(2)}, u32[]{:S(2)}) collective-permute-start(bf16[1,120,768]{2,1,0:T(8,128)(2,1)S(1)} %bitcast.88), channel_id=1, source_target_pairs={{0,8},{4,12},{8,0},{12,4},{16,24},{20,28},{24,16},{28,20},{1,9},{5... | collective-permute-start | bytes 552968 | tf_op jit(solution)/shard_map/ppermute | solution.py:35
  41.7 21.8 %collective-permute-start.13 = (bf16[1,120,768]{2,1,0:T(8,128)(2,1)S(1)}, bf16[1,120,768]{2,1,0:T(8,128)(2,1)S(1)}, u32[]{:S(2)}, u32[]{:S(2)}) collective-permute-start(bf16[1,120,768]{2,1,0:T(8,128)(2,1)S(1)} %bitcast.89), channel_id=1, source_target_pairs={{0,16},{4,20},{8,24},{12,28},{16,0},{20,4},{24,8},{28,12},{1,17},{... | collective-permute-start | bytes 552968 | tf_op jit(solution)/shard_map/ppermute | solution.py:35
  44.5 19.0 %collective-permute-start.14 = (bf16[1,120,768]{2,1,0:T(8,128)(2,1)S(1)}, bf16[1,120,768]{2,1,0:T(8,128)(2,1)S(1)}, u32[]{:S(2)}, u32[]{:S(2)}) collective-permute-start(bf16[1,120,768]{2,1,0:T(8,128)(2,1)S(1)} %bitcast.90), channel_id=1, source_target_pairs={{0,24},{4,28},{8,16},{12,20},{16,8},{20,12},{24,0},{28,4},{1,25},{... | collective-permute-start | bytes 552968 | tf_op jit(solution)/shard_map/ppermute | solution.py:35
  63.6 19.2 %collective-permute-start.15 = (bf16[4,120,768]{2,1,0:T(8,128)(2,1)S(1)}, bf16[4,120,768]{2,1,0:T(8,128)(2,1)S(1)}, u32[]{:S(2)}, u32[]{:S(2)}) collective-permute-start(bf16[4,120,768]{2,1,0:T(8,128)(2,1)S(1)} %joined.4.refs_0_), channel_id=1, source_target_pairs={{0,4},{4,0},{8,12},{12,8},{16,20},{20,16},{24,28},{28,24},{1,5},{5... | collective-permute-start | bytes 2211848 | tf_op jit(solution)/shard_map/ppermute | solution.py:35
  65.2 2.3 collective-permute-start.8
  65.2 3.9 %collective-permute-start.10 = (bf16[272,768]{1,0:T(8,128)(2,1)}, bf16[272,768]{1,0:T(8,128)(2,1)S(1)}, u32[]{:S(2)}, u32[]{:S(2)}) collective-permute-start(bf16[272,768]{1,0:T(8,128)(2,1)} %collective-permute-done.6.halo_ref.refs_4_), channel_id=1, source_target_pairs={{0,1},{1,0},{2,3},{3,2},{4,5},{5,4},{6,7},{7,6},{8,9},{9,8},{10,11... | collective-permute-start | bytes 1253384 | tf_op jit(solution)/shard_map/ppermute | solution.py:35
  65.7 3.4 %collective-permute-start.9 = (bf16[272,768]{1,0:T(8,128)(2,1)S(1)}, bf16[272,768]{1,0:T(8,128)(2,1)S(1)}, u32[]{:S(2)}, u32[]{:S(2)}) collective-permute-start(bf16[272,768]{1,0:T(8,128)(2,1)S(1)} %copy-done.56), channel_id=1, source_target_pairs={{0,1},{1,0},{2,3},{3,2},{4,5},{5,4},{6,7},{7,6},{8,9},{9,8},{10,11... | collective-permute-start | bytes 1253384 | tf_op jit(solution)/shard_map/ppermute | solution.py:35
  65.7 6.2 %collective-permute-start.11 = (bf16[272,768]{1,0:T(8,128)(2,1)}, bf16[272,768]{1,0:T(8,128)(2,1)S(1)}, u32[]{:S(2)}, u32[]{:S(2)}) collective-permute-start(bf16[272,768]{1,0:T(8,128)(2,1)} %collective-permute-done.7.refs_5_), channel_id=1, source_target_pairs={{0,1},{1,0},{2,3},{3,2},{4,5},{5,4},{6,7},{7,6},{8,9},{9,8},{10,11... | collective-permute-start | bytes 1253384 | tf_op jit(solution)/shard_map/ppermute | solution.py:35
  67.5 12.9 %collective-permute-start.16 = (bf16[1,96,768]{2,1,0:T(8,128)(2,1)S(1)}, bf16[1,96,768]{2,1,0:T(8,128)(2,1)S(1)}, u32[]{:S(2)}, u32[]{:S(2)}) collective-permute-start(bf16[1,96,768]{2,1,0:T(8,128)(2,1)S(1)} %bitcast.92), channel_id=1, source_target_pairs={{0,8},{4,12},{8,0},{12,4},{16,24},{20,28},{24,16},{28,20},{1,9},{5... | collective-permute-start | bytes 442376 | tf_op jit(solution)/shard_map/ppermute | solution.py:35
  69.1 13.7 %collective-permute-start.17 = (bf16[1,96,768]{2,1,0:T(8,128)(2,1)S(1)}, bf16[1,96,768]{2,1,0:T(8,128)(2,1)S(1)}, u32[]{:S(2)}, u32[]{:S(2)}) collective-permute-start(bf16[1,96,768]{2,1,0:T(8,128)(2,1)S(1)} %bitcast.93), channel_id=1, source_target_pairs={{0,16},{4,20},{8,24},{12,28},{16,0},{20,4},{24,8},{28,12},{1,17},{... | collective-permute-start | bytes 442376 | tf_op jit(solution)/shard_map/ppermute | solution.py:35
  69.1 13.7 %collective-permute-start.18 = (bf16[1,96,768]{2,1,0:T(8,128)(2,1)S(1)}, bf16[1,96,768]{2,1,0:T(8,128)(2,1)S(1)}, u32[]{:S(2)}, u32[]{:S(2)}) collective-permute-start(bf16[1,96,768]{2,1,0:T(8,128)(2,1)S(1)} %bitcast.94), channel_id=1, source_target_pairs={{0,24},{4,28},{8,16},{12,20},{16,8},{20,12},{24,0},{28,4},{1,25},{... | collective-permute-start | bytes 442376 | tf_op jit(solution)/shard_map/ppermute | solution.py:35
  82.8 13.7 %collective-permute-start.24 = (bf16[4,96,768]{2,1,0:T(8,128)(2,1)S(1)}, bf16[4,96,768]{2,1,0:T(8,128)(2,1)S(1)}, u32[]{:S(2)}, u32[]{:S(2)}) collective-permute-start(bf16[4,96,768]{2,1,0:T(8,128)(2,1)S(1)} %joined.5.refs_2_), channel_id=1, source_target_pairs={{0,4},{4,0},{8,12},{12,8},{16,20},{20,16},{24,28},{28,24},{1,5},{5... | collective-permute-start | bytes 1769480 | tf_op jit(solution)/shard_map/ppermute | solution.py:35
  84.2 7.1 %collective-permute-start.21 = (bf16[192,768]{1,0:T(8,128)(2,1)S(1)}, bf16[192,768]{1,0:T(8,128)(2,1)S(1)}, u32[]{:S(2)}, u32[]{:S(2)}) collective-permute-start(bf16[192,768]{1,0:T(8,128)(2,1)S(1)} %unpack_out.1.w0), channel_id=1, source_target_pairs={{0,2},{1,3},{2,0},{3,1},{4,6},{5,7},{6,4},{7,5},{8,10},{9,11},{10,... | collective-permute-start | bytes 884744 | tf_op jit(solution)/shard_map/ppermute | solution.py:35
  87.2 1.5 collective-permute-start.19
  88.8 7.0 %collective-permute-start.20 = (bf16[2,192,256]{2,1,0:T(8,128)(2,1)S(1)}, bf16[2,192,256]{2,1,0:T(8,128)(2,1)S(1)}, u32[]{:S(2)}, u32[]{:S(2)}) collective-permute-start(bf16[2,192,256]{2,1,0:T(8,128)(2,1)S(1)} %pad_maximum_fusion.2), channel_id=1, source_target_pairs={{0,2},{1,3},{2,0},{3,1},{4,6},{5,7},{6,4},{7,5},{8,10},{9,11},{10,... | collective-permute-start | bytes 589832 | tf_op jit(solution)/shard_map/ppermute | solution.py:35
  89.4 7.1 %collective-permute-start.22 = (bf16[192,768]{1,0:T(8,128)(2,1)S(1)}, bf16[192,768]{1,0:T(8,128)(2,1)S(1)}, u32[]{:S(2)}, u32[]{:S(2)}) collective-permute-start(bf16[192,768]{1,0:T(8,128)(2,1)S(1)} %unpack_out.1.w0), channel_id=1, source_target_pairs={{0,1},{1,0},{2,3},{3,2},{4,5},{5,4},{6,7},{7,6},{8,9},{9,8},{10,11... | collective-permute-start | bytes 884744 | tf_op jit(solution)/shard_map/ppermute | solution.py:35
  91.3 5.2 %collective-permute-start.23 = (bf16[192,768]{1,0:T(8,128)(2,1)S(1)}, bf16[192,768]{1,0:T(8,128)(2,1)S(1)}, u32[]{:S(2)}, u32[]{:S(2)}) collective-permute-start(bf16[192,768]{1,0:T(8,128)(2,1)S(1)} %collective-permute-done.21.w1), channel_id=1, source_target_pairs={{0,1},{1,0},{2,3},{3,2},{4,5},{5,4},{6,7},{7,6},{8,9},{9,8},{10,11... | collective-permute-start | bytes 884744 | tf_op jit(solution)/shard_map/ppermute | solution.py:35
  98.2 9.7 %collective-permute-start.25 = (bf16[256,768]{1,0:T(8,128)(2,1)S(1)}, bf16[256,768]{1,0:T(8,128)(2,1)S(1)}, u32[]{:S(2)}, u32[]{:S(2)}) collective-permute-start(bf16[256,768]{1,0:T(8,128)(2,1)S(1)} %get-tuple-element.160.x0), channel_id=1, source_target_pairs={{0,2},{1,3},{2,0},{3,1},{4,6},{5,7},{6,4},{7,5},{8,10},{9,11},{10,... | collective-permute-start | bytes 1179656 | tf_op jit(solution)/shard_map/ppermute | solution.py:35
  99.6 8.2 %collective-permute-start.26 = (bf16[256,768]{1,0:T(8,128)(2,1)S(1)}, bf16[256,768]{1,0:T(8,128)(2,1)S(1)}, u32[]{:S(2)}, u32[]{:S(2)}) collective-permute-start(bf16[256,768]{1,0:T(8,128)(2,1)S(1)} %get-tuple-element.160.x0), channel_id=1, source_target_pairs={{0,1},{1,0},{2,3},{3,2},{4,5},{5,4},{6,7},{7,6},{8,9},{9,8},{10,11... | collective-permute-start | bytes 1179656 | tf_op jit(solution)/shard_map/ppermute | solution.py:35
  107.9 1.7 collective-permute-start.27
  116.8 2.3 collective-permute-start.28
  120.2 13.5 %collective-permute-start.29 = (bf16[256,768]{1,0:T(8,128)(2,1)}, bf16[256,768]{1,0:T(8,128)(2,1)}, u32[]{:S(2)}, u32[]{:S(2)}) collective-permute-start(bf16[256,768]{1,0:T(8,128)(2,1)} %get-tuple-element.280), channel_id=1, source_target_pairs={{0,2},{1,3},{2,0},{3,1},{4,6},{5,7},{6,4},{7,5},{8,10},{9,11},{10,... | collective-permute-start | bytes 1179656 | tf_op jit(solution)/shard_map/ppermute | solution.py:35
  131.9 12.5 %collective-permute-start.32 = (bf16[512,768]{1,0:T(8,128)(2,1)S(1)}, bf16[512,768]{1,0:T(8,128)(2,1)S(1)}, u32[]{:S(2)}, u32[]{:S(2)}) collective-permute-start(bf16[512,768]{1,0:T(8,128)(2,1)S(1)} %get-tuple-element.178), channel_id=1, source_target_pairs={{0,1},{1,0},{2,3},{3,2},{4,5},{5,4},{6,7},{7,6},{8,9},{9,8},{10,11... | collective-permute-start | bytes 2359304 | tf_op jit(solution)/shard_map/ppermute | solution.py:35
  136.9 7.4 %collective-permute-start.30 = (bf16[2,192,256]{2,1,0:T(8,128)(2,1)S(1)}, bf16[2,192,256]{2,1,0:T(8,128)(2,1)S(1)}, u32[]{:S(2)}, u32[]{:S(2)}) collective-permute-start(bf16[2,192,256]{2,1,0:T(8,128)(2,1)S(1)} %pad_maximum_fusion.3), channel_id=1, source_target_pairs={{0,2},{1,3},{2,0},{3,1},{4,6},{5,7},{6,4},{7,5},{8,10},{9,11},{10,... | collective-permute-start | bytes 589832 | tf_op jit(solution)/shard_map/ppermute | solution.py:35
  137.6 15.9 %collective-permute-start.34 = (bf16[2,192,768]{2,1,0:T(8,128)(2,1)S(1)}, bf16[2,192,768]{2,1,0:T(8,128)(2,1)S(1)}, u32[]{:S(2)}, u32[]{:S(2)}) collective-permute-start(bf16[2,192,768]{2,1,0:T(8,128)(2,1)S(1)} %get-tuple-element.187), channel_id=1, source_target_pairs={{0,1},{1,0},{2,3},{3,2},{4,5},{5,4},{6,7},{7,6},{8,9},{9,8},{10,11... | collective-permute-start | bytes 1769480 | tf_op jit(solution)/shard_map/ppermute | solution.py:35
  144.3 1.5 collective-permute-start.31
  145.9 29.8 %collective-permute-start.33 = (bf16[256,768]{1,0:T(8,128)(2,1)S(1)}, bf16[256,768]{1,0:T(8,128)(2,1)}, u32[]{:S(2)}, u32[]{:S(2)}) collective-permute-start(bf16[256,768]{1,0:T(8,128)(2,1)S(1)} %slice.162), channel_id=1, source_target_pairs={{0,2},{1,3},{2,0},{3,1},{4,6},{5,7},{6,4},{7,5},{8,10},{9,11},{10,... | collective-permute-start | bytes 1179656 | tf_op jit(solution)/shard_map/ppermute | solution.py:35
  146.6 57.2 %collective-permute-start.39 = (bf16[2,4,96,768]{3,2,1,0:T(8,128)(2,1)}, bf16[2,4,96,768]{3,2,1,0:T(8,128)(2,1)}, u32[]{:S(2)}, u32[]{:S(2)}) collective-permute-start(bf16[2,4,96,768]{3,2,1,0:T(8,128)(2,1)} %get-tuple-element.203), channel_id=1, source_target_pairs={{0,4},{4,0},{8,12},{12,8},{16,20},{20,16},{24,28},{28,24},{1,5},{5... | collective-permute-start | bytes 3538952 | tf_op jit(solution)/shard_map/ppermute | solution.py:35
  155.1 21.7 %collective-permute-start.35 = (bf16[192,768]{1,0:T(8,128)(2,1)}, bf16[192,768]{1,0:T(8,128)(2,1)}, u32[]{:S(2)}, u32[]{:S(2)}) collective-permute-start(bf16[192,768]{1,0:T(8,128)(2,1)} %fusion.3), channel_id=1, source_target_pairs={{0,2},{1,3},{2,0},{3,1},{4,6},{5,7},{6,4},{7,5},{8,10},{9,11},{10,... | collective-permute-start | bytes 884744 | tf_op jit(solution)/shard_map/ppermute | solution.py:35
  172.9 56.1 %collective-permute-start.41 = (bf16[1040,384]{1,0:T(8,128)(2,1)S(1)}, bf16[1040,384]{1,0:T(8,128)(2,1)S(1)}, u32[]{:S(2)}, u32[]{:S(2)}) collective-permute-start(bf16[1040,384]{1,0:T(8,128)(2,1)S(1)} %get-tuple-element.194.one_ref), channel_id=1, source_target_pairs={{4,0},{8,4},{12,8},{16,12},{20,16},{24,20},{28,24},{5,1},{9,5},{13... | collective-permute-start | bytes 2396168 | tf_op jit(solution)/shard_map/ppermute | solution.py:40
  174.4 54.7 %collective-permute-start.42 = (bf16[1024,384]{1,0:T(8,128)(2,1)S(1)}, bf16[1024,384]{1,0:T(8,128)(2,1)S(1)}, u32[]{:S(2)}, u32[]{:S(2)}) collective-permute-start(bf16[1024,384]{1,0:T(8,128)(2,1)S(1)} %get-tuple-element.193.two_ref), channel_id=1, source_target_pairs={{8,0},{12,4},{16,8},{20,12},{24,16},{28,20},{9,1},{13,5},{17,9},{2... | collective-permute-start | bytes 2359304 | tf_op jit(solution)/shard_map/ppermute | solution.py:40
  176.9 52.1 %copy-start.9 = (bf16[768,576]{1,0:T(8,128)(2,1)S(1)}, bf16[768,576]{1,0:T(8,128)(2,1)}, u32[]{:S(2)}) copy-start(bf16[768,576]{1,0:T(8,128)(2,1)} %copy-done.8) | copy-start | bytes 2654212
  188.6 40.4 %copy-start.1 = (bf16[1024,768]{1,0:T(8,128)(2,1)S(1)}, bf16[1024,768]{1,0:T(8,128)(2,1)}, u32[]{:S(2)}) copy-start(bf16[1024,768]{1,0:T(8,128)(2,1)} %x_ref.3) | copy-start | bytes 4718596
  189.5 33.4 %collective-permute-start.40 = (bf16[1,4,96,768]{3,2,1,0:T(8,128)(2,1)S(1)}, bf16[1,4,96,768]{3,2,1,0:T(8,128)(2,1)S(1)}, u32[]{:S(2)}, u32[]{:S(2)}) collective-permute-start(bf16[1,4,96,768]{3,2,1,0:T(8,128)(2,1)S(1)} %get-tuple-element.276), channel_id=1, source_target_pairs={{0,4},{4,0},{8,12},{12,8},{16,20},{20,16},{24,28},{28,24},{1,5},{5... | collective-permute-start | bytes 1769480 | tf_op jit(solution)/shard_map/ppermute | solution.py:35
  193.5 10.3 %collective-permute-start.36 = (bf16[256,768]{1,0:T(8,128)(2,1)S(1)}, bf16[256,768]{1,0:T(8,128)(2,1)S(1)}, u32[]{:S(2)}, u32[]{:S(2)}) collective-permute-start(bf16[256,768]{1,0:T(8,128)(2,1)S(1)} %add_convert_fusion.5.refs_0_), channel_id=1, source_target_pairs={{0,2},{1,3},{2,0},{3,1},{4,6},{5,7},{6,4},{7,5},{8,10},{9,11},{10,... | collective-permute-start | bytes 1179656 | tf_op jit(solution)/shard_map/ppermute | solution.py:35
  203.8 19.1 %collective-permute-start.37 = (bf16[256,768]{1,0:T(8,128)(2,1)S(1)}, bf16[256,768]{1,0:T(8,128)(2,1)S(1)}, u32[]{:S(2)}, u32[]{:S(2)}) collective-permute-start(bf16[256,768]{1,0:T(8,128)(2,1)S(1)} %add_convert_fusion.5.refs_0_), channel_id=1, source_target_pairs={{0,1},{1,0},{2,3},{3,2},{4,5},{5,4},{6,7},{7,6},{8,9},{9,8},{10,11... | collective-permute-start | bytes 1179656 | tf_op jit(solution)/shard_map/ppermute | solution.py:35
  203.8 19.1 %collective-permute-start.38 = (bf16[256,768]{1,0:T(8,128)(2,1)S(1)}, bf16[256,768]{1,0:T(8,128)(2,1)S(1)}, u32[]{:S(2)}, u32[]{:S(2)}) collective-permute-start(bf16[256,768]{1,0:T(8,128)(2,1)S(1)} %collective-permute-done.36.refs_1_), channel_id=1, source_target_pairs={{0,1},{1,0},{2,3},{3,2},{4,5},{5,4},{6,7},{7,6},{8,9},{9,8},{10,11... | collective-permute-start | bytes 1179656 | tf_op jit(solution)/shard_map/ppermute | solution.py:35
  233.1 2.7 collective-permute-start.43
  233.2 2.5 collective-permute-start.44
  237.4 9.9 %collective-permute-start.52 = (bf16[1,2,96,768]{3,2,1,0:T(8,128)(2,1)S(1)}, bf16[1,2,96,768]{3,2,1,0:T(8,128)(2,1)S(1)}, u32[]{:S(2)}, u32[]{:S(2)}) collective-permute-start(bf16[1,2,96,768]{3,2,1,0:T(8,128)(2,1)S(1)} %dynamic-slice_bitcast_fusion.4), channel_id=1, source_target_pairs={{0,8},{4,12},{8,0},{12,4},{16,24},{20,28},{24,16},{28,20},{1,9},{5... | collective-permute-start | bytes 884744 | tf_op jit(solution)/shard_map/ppermute | solution.py:35
  237.6 19.2 %collective-permute-start.50 = (bf16[1,2,96,768]{3,2,1,0:T(8,128)(2,1)S(1)}, bf16[1,2,96,768]{3,2,1,0:T(8,128)(2,1)S(1)}, u32[]{:S(2)}, u32[]{:S(2)}) collective-permute-start(bf16[1,2,96,768]{3,2,1,0:T(8,128)(2,1)S(1)} %dynamic-slice_bitcast_fusion.5), channel_id=1, source_target_pairs={{0,8},{4,12},{8,0},{12,4},{16,24},{20,28},{24,16},{28,20},{1,9},{5... | collective-permute-start | bytes 884744 | tf_op jit(solution)/shard_map/ppermute | solution.py:35
  240.4 23.2 %collective-permute-start.48 = (bf16[1,2,96,768]{3,2,1,0:T(8,128)(2,1)}, bf16[1,2,96,768]{3,2,1,0:T(8,128)(2,1)}, u32[]{:S(2)}, u32[]{:S(2)}) collective-permute-start(bf16[1,2,96,768]{3,2,1,0:T(8,128)(2,1)} %dynamic-slice_bitcast_fusion.6), channel_id=1, source_target_pairs={{0,8},{4,12},{8,0},{12,4},{16,24},{20,28},{24,16},{28,20},{1,9},{5... | collective-permute-start | bytes 884744 | tf_op jit(solution)/shard_map/ppermute | solution.py:35
  240.5 17.1 %collective-permute-start.45 = (bf16[256,768]{1,0:T(8,128)(2,1)S(1)}, bf16[256,768]{1,0:T(8,128)(2,1)S(1)}, u32[]{:S(2)}, u32[]{:S(2)}) collective-permute-start(bf16[256,768]{1,0:T(8,128)(2,1)S(1)} %get-tuple-element.278), channel_id=1, source_target_pairs={{0,2},{1,3},{2,0},{3,1},{4,6},{5,7},{6,4},{7,5},{8,10},{9,11},{10,... | collective-permute-start | bytes 1179656 | tf_op jit(solution)/shard_map/ppermute | solution.py:35
  242.1 15.5 %collective-permute-start.46 = (f32[2,768]{1,0:T(2,128)S(1)}, f32[2,768]{1,0:T(2,128)S(1)}, u32[]{:S(2)}, u32[]{:S(2)}) collective-permute-start(f32[2,768]{1,0:T(2,128)S(1)} %fusion.4), channel_id=1, source_target_pairs={{0,2},{1,3},{2,0},{3,1},{4,6},{5,7},{6,4},{7,5},{8,10},{9,11},{10,... | collective-permute-start | bytes 18440 | tf_op jit(solution)/shard_map/ppermute | solution.py:35
  248.1 27.4 %collective-permute-start.53 = (bf16[1,1,96,768]{3,2,1,0:T(8,128)(2,1)}, bf16[1,1,96,768]{3,2,1,0:T(8,128)(2,1)}, u32[]{:S(2)}, u32[]{:S(2)}) collective-permute-start(bf16[1,1,96,768]{3,2,1,0:T(8,128)(2,1)} %get-tuple-element.290), channel_id=1, source_target_pairs={{0,16},{4,20},{8,24},{12,28},{16,0},{20,4},{24,8},{28,12},{1,17},{... | collective-permute-start | bytes 442376 | tf_op jit(solution)/shard_map/ppermute | solution.py:35
  257.6 17.9 %collective-permute-start.51 = (bf16[1,1,96,768]{3,2,1,0:T(8,128)(2,1)}, bf16[1,1,96,768]{3,2,1,0:T(8,128)(2,1)}, u32[]{:S(2)}, u32[]{:S(2)}) collective-permute-start(bf16[1,1,96,768]{3,2,1,0:T(8,128)(2,1)} %get-tuple-element.292), channel_id=1, source_target_pairs={{0,16},{4,20},{8,24},{12,28},{16,0},{20,4},{24,8},{28,12},{1,17},{... | collective-permute-start | bytes 442376 | tf_op jit(solution)/shard_map/ppermute | solution.py:35
  258.0 22.0 %copy-start.69 = (bf16[1,1,96,768]{3,2,1,0:T(8,128)(2,1)S(1)}, bf16[1,1,96,768]{3,2,1,0:T(8,128)(2,1)}, u32[]{:S(2)}) copy-start(bf16[1,1,96,768]{3,2,1,0:T(8,128)(2,1)} %get-tuple-element.233) | copy-start | bytes 442372
  258.1 7.5 %collective-permute-start.56 = (f32[3264]{0:T(1024)S(1)}, f32[3264]{0:T(1024)S(1)}, u32[]{:S(2)}, u32[]{:S(2)}) collective-permute-start(f32[3264]{0:T(1024)S(1)} %constant_dynamic-update-slice_fusion), channel_id=1, source_target_pairs={{0,8},{4,12},{8,0},{12,4},{16,24},{20,28},{24,16},{28,20},{1,9},{5... | collective-permute-start | bytes 39176 | tf_op jit(solution)/shard_map/ppermute | solution.py:35
  260.3 10.1 %collective-permute-start.57 = (f32[3264]{0:T(1024)S(1)}, f32[3264]{0:T(1024)S(1)}, u32[]{:S(2)}, u32[]{:S(2)}) collective-permute-start(f32[3264]{0:T(1024)S(1)} %constant_dynamic-update-slice_fusion), channel_id=1, source_target_pairs={{0,16},{4,20},{8,24},{12,28},{16,0},{20,4},{24,8},{28,12},{1,17},{... | collective-permute-start | bytes 39176 | tf_op jit(solution)/shard_map/ppermute | solution.py:35
  263.6 6.9 %collective-permute-start.58 = (f32[3264]{0:T(1024)S(1)}, f32[3264]{0:T(1024)S(1)}, u32[]{:S(2)}, u32[]{:S(2)}) collective-permute-start(f32[3264]{0:T(1024)S(1)} %constant_dynamic-update-slice_fusion), channel_id=1, source_target_pairs={{0,24},{4,28},{8,16},{12,20},{16,8},{20,12},{24,0},{28,4},{1,25},{... | collective-permute-start | bytes 39176 | tf_op jit(solution)/shard_map/ppermute | solution.py:35
  265.6 14.4 %collective-permute-start.47 = (bf16[256,768]{1,0:T(8,128)(2,1)S(1)}, bf16[256,768]{1,0:T(8,128)(2,1)S(1)}, u32[]{:S(2)}, u32[]{:S(2)}) collective-permute-start(bf16[256,768]{1,0:T(8,128)(2,1)S(1)} %grad_tokens_own.1.refs_0_), channel_id=1, source_target_pairs={{0,2},{1,3},{2,0},{3,1},{4,6},{5,7},{6,4},{7,5},{8,10},{9,11},{10,... | collective-permute-start | bytes 1179656 | tf_op jit(solution)/shard_map/ppermute | solution.py:35
  270.4 3.8 %collective-permute-start.59 = (f32[3264]{0:T(1024)S(1)}, f32[3264]{0:T(1024)S(1)}, u32[]{:S(2)}, u32[]{:S(2)}) collective-permute-start(f32[3264]{0:T(1024)S(1)} %add_add_fusion), channel_id=1, source_target_pairs={{0,4},{4,0},{8,12},{12,8},{16,20},{20,16},{24,28},{28,24},{1,5},{5... | collective-permute-start | bytes 39176 | tf_op jit(solution)/shard_map/ppermute | solution.py:35
  271.3 8.8 %collective-permute-start.49 = (bf16[1,1,96,768]{3,2,1,0:T(8,128)(2,1)}, bf16[1,1,96,768]{3,2,1,0:T(8,128)(2,1)S(1)}, u32[]{:S(2)}, u32[]{:S(2)}) collective-permute-start(bf16[1,1,96,768]{3,2,1,0:T(8,128)(2,1)} %get-tuple-element.294), channel_id=1, source_target_pairs={{0,16},{4,20},{8,24},{12,28},{16,0},{20,4},{24,8},{28,12},{1,17},{... | collective-permute-start | bytes 442376 | tf_op jit(solution)/shard_map/ppermute | solution.py:35
  274.2 15.9 %collective-permute-start.54 = (bf16[256,768]{1,0:T(8,128)(2,1)S(1)}, bf16[256,768]{1,0:T(8,128)(2,1)S(1)}, u32[]{:S(2)}, u32[]{:S(2)}) collective-permute-start(bf16[256,768]{1,0:T(8,128)(2,1)S(1)} %grad_tokens_own.1.refs_0_), channel_id=1, source_target_pairs={{0,1},{1,0},{2,3},{3,2},{4,5},{5,4},{6,7},{7,6},{8,9},{9,8},{10,11... | collective-permute-start | bytes 1179656 | tf_op jit(solution)/shard_map/ppermute | solution.py:35
  282.4 7.7 %collective-permute-start.55 = (bf16[256,768]{1,0:T(8,128)(2,1)S(1)}, bf16[256,768]{1,0:T(8,128)(2,1)S(1)}, u32[]{:S(2)}, u32[]{:S(2)}) collective-permute-start(bf16[256,768]{1,0:T(8,128)(2,1)S(1)} %collective-permute-done.47.refs_1_), channel_id=1, source_target_pairs={{0,1},{1,0},{2,3},{3,2},{4,5},{5,4},{6,7},{7,6},{8,9},{9,8},{10,11... | collective-permute-start | bytes 1179656 | tf_op jit(solution)/shard_map/ppermute | solution.py:35
  (76 other events, 512.2 us)

commit v4 on v3

--- a/solution.py
+++ b/solution.py
@@ -1177,7 +1177,7 @@
     cot = jnp.where(hi, cot[::-1], cot)
     cot = jnp.where(lo, cot[:, ::-1], cot)
     cot = jnp.swapaxes(cot, 0, 1).reshape(rows, dim)
-    *w_mix, cot, pieces[0], pieces[1], pieces[4] = together((*w_mix, cot, pieces[0], pieces[1], pieces[4]))
+    *w_mix, cot, pieces[4] = together((*w_mix, cot, pieces[4]))
     w_mix, raw_halo, raw, normed, q, kv, kvt = project_own(meta, tokens, pieces[4], gain_one, taps, w_mix, masks)
     q, pieces[5] = together((q, pieces[5]))
     acc_own, stat_own = attend_own(q, kv, kvt, first_row)

time: 299 us -> 293 us (0.980)
  waiting for transfers between devices: 102 us -> 87.5 us
  starting transfers between devices: 70.3 us -> 80.8 us
    ppermute x57, waiting for transfers between devices: 90.9 us -> 79.3 us  [swap(): lax.ppermute(x, axis, [(i, i ^ mask) for i in range(lax.axis_size(axis))])]
    ppermute x57, starting transfers between devices: 64.8 us -> 74.5 us  [swap(): lax.ppermute(x, axis, [(i, i ^ mask) for i in range(lax.axis_size(axis))])]
    unnamed x163 -> x147, local copies, waits for them, and re-layouts: 21.4 us -> 20.4 us
  transfers between devices with their start and end apart: 60 -> 60, of which waited for: 22 -> 24; matrix products, arithmetic and copies ran while one was open for 10% -> 10% of each run, Pallas kernels for 18% -> 18%
where the time goes in v4:
time: 293 us; the launch traced here: 289 us
  waiting for transfers between devices  87.5 us (30%)
  starting transfers between devices  80.8 us (28%)
  Pallas kernels  65.2 us (22%)
  local copies, waits for them, and re-layouts  34 us (12%)
  other arithmetic  19.5 us (7%)
    ppermute x57, waiting for transfers between devices, swap(): lax.ppermute(x, axis, [(i, i ^ mask) for i in range(lax.axis_size(axis))])  79.3 us
    ppermute x57, starting transfers between devices, swap(): lax.ppermute(x, axis, [(i, i ^ mask) for i in range(lax.axis_size(axis))])  74.5 us
    unnamed x147, local copies, waits for them, and re-layouts  20.4 us
    pallas_call x1, Pallas kernels, earlier_back(): pl.pallas_call(earlier_back_kernel, out_shape=(jax.ShapeDtypeStruct((part...  11.8 us
    pallas_call x1, Pallas kernels, own_back(): pl.pallas_call(own_back_kernel, out_shape=(jax.ShapeDtypeStruct((rows, wi...  11.8 us
    ppermute x3, waiting for transfers between devices, moved(): lax.ppermute(x, axis, [(i, i + distance) for i in range(size) if 0 <= i +...  8.16 us
    pallas_call x1, Pallas kernels, project_earlier(): pl.pallas_call(project_earlier_kernel, out_shape=(jax.ShapeDtypeStruct((s...  7.39 us
    ppermute x3, starting transfers between devices, moved(): lax.ppermute(x, axis, [(i, i + distance) for i in range(size) if 0 <= i +...  6.32 us
  transfers between devices with their start and end apart: 60, of which 24 were waited for; matrix products, arithmetic and copies ran while one was open for 10% of the time, Pallas kernels for 18%

profile of v4, /device:TPU:0, one launch (start us, length us, event | category | flops | bytes accessed | tf_op | source)
XLA Modules:
  0.0 289.3 jit_solution(2383752519534107655)
XLA Ops:
  1.7 3.1 %collective-permute-start = (bf16[1,96,576]{2,1,0:T(8,128)(2,1)S(1)}, bf16[1,96,576]{2,1,0:T(8,128)(2,1)S(1)}, u32[]{:S(2)}, u32[]{:S(2)}) collective-permute-start(bf16[1,96,576]{2,1,0:T(8,128)(2,1)S(1)} %maximum_bitcast_fusion.refs_0_), channel_id=1, source_target_pairs={{0,8},{4,12},{8,0},{12,4},{16,24},{20,28},{24,16},{28,20},{1,9},{5... | collective-permute-start | bytes 331784 | tf_op jit(solution)/shard_map/ppermute | solution.py:35
  4.8 2.6 collective-permute-start.1
  9.2 3.6 %collective-permute-start.4 = (bf16[272,768]{1,0:T(8,128)(2,1)S(1)}, bf16[272,768]{1,0:T(8,128)(2,1)}, u32[]{:S(2)}, u32[]{:S(2)}) collective-permute-start(bf16[272,768]{1,0:T(8,128)(2,1)S(1)} %pad_maximum_fusion), channel_id=1, source_target_pairs={{0,8},{4,12},{8,16},{12,20},{16,24},{20,28},{1,9},{5,13},{9,17},{1... | collective-permute-start | bytes 1253384 | tf_op jit(solution)/shard_map/ppermute | solution.py:40
  15.6 1.5 collective-permute-done.1.refs_2_
  17.2 1.6 collective-permute-start.3
  18.7 2.9 collective-permute-done.4.refs_0_
  22.5 2.5 collective-permute-start.5
  25.0 1.5 copy.34
  26.6 1.5 reverse_select_fusion.1
  28.0 8.9 %collective-permute-done.5.halo_ref.refs_4_ = bf16[272,768]{1,0:T(8,128)(2,1)} collective-permute-done((bf16[272,768]{1,0:T(8,128)(2,1)}, bf16[272,768]{1,0:T(8,128)(2,1)}, u32[]{:S(2)}, u32[]{:S(2)}) %collective-permute-start.5) | collective-permute-done | bytes 417824 | tf_op jit(solution)/shard_map/ppermute | solution.py:35
  36.9 1.5 collective-permute-start.6
  38.7 3.3 %collective-permute-start.12 = (bf16[1,120,768]{2,1,0:T(8,128)(2,1)S(1)}, bf16[1,120,768]{2,1,0:T(8,128)(2,1)S(1)}, u32[]{:S(2)}, u32[]{:S(2)}) collective-permute-start(bf16[1,120,768]{2,1,0:T(8,128)(2,1)S(1)} %bitcast.88), channel_id=1, source_target_pairs={{0,8},{4,12},{8,0},{12,4},{16,24},{20,28},{24,16},{28,20},{1,9},{5... | collective-permute-start | bytes 552968 | tf_op jit(solution)/shard_map/ppermute | solution.py:35
  46.0 2.4 reverse_select_fusion
  48.5 5.6 %project_own.1 = (bf16[768,576]{1,0:T(8,128)(2,1)S(1)}, bf16[16,192]{1,0:T(8,128)(2,1)S(1)}, bf16[1024,576]{1,0:T(8,128)(2,1)S(1)}, bf16[1024,768]{1,0:T(8,128)(...) custom-call(s32[22]{0:T(128)S(1)} %concatenate.30.meta_ref, ...), custom_call_target="tpu_custom_call" | custom-call | flops 1 | bytes 1 | tf_op jit(solution)/shard_map/project_own/pallas_call | solution.py:310
  55.2 3.7 %attend_own.1 = (f32[192,1024]{1,0:T(8,128)S(1)}, f32[16,1024]{1,0:T(8,128)S(1)}) custom-call(bf16[1024,192]{1,0:T(8,128)(2,1)S(1)} %get-tuple-element.129.q_ref, bf16[1024,384]{1,0:T(8,128)(2,1)S(1)} %get-tuple-element.134.kv_ref.kv_own_ref, bf16[384,1024]{1,0:T(8,128)(2,1)S(1)} %get-tuple-element.135.kvt_ref.kvt_own_ref, s32[1,1024]{1,0:T(1,128)S(1)} %bitcast.96), custom_call_target="tpu_custom_call" | custom-call | flops 1 | bytes 1 | tf_op jit(solution)/shard_map/attend_own/pallas_call | solution.py:557
  59.1 1.8 collective-permute-start.15
  64.0 2.0 collective-permute-start.17
  67.2 7.4 %project_earlier.1 = (bf16[2048,384]{1,0:T(8,128)(2,1)S(1)}, bf16[2048,768]{1,0:T(8,128)(2,1)S(1)}, bf16[2048,384]{1,0:T(8,128)(2,1)S(1)}, bf16[384,2048]{1,0:T(8,128)(2,1)S(1)}) custom-call(s32[22]{0:T(128)S(1)} %concatenate.30.meta_ref, bf16[272,768]{1,0:T(8,128)(2,1)} %collective-permute-done.4.refs_0_, ...), custom_call_target="tpu_custom_call" | custom-call | flops 1 | bytes 1 | tf_op jit(solution)/shard_map/project_earlier/pallas_call | solution.py:386
  75.8 2.2 collective-permute-done.17.refs_2_
  79.3 1.5 collective-permute-start.21
  82.3 1.4 collective-permute-done.19
  84.5 1.6 collective-permute-done.21.w1
  86.2 4.7 %collective-permute-done.20 = bf16[2,192,256]{2,1,0:T(8,128)(2,1)S(1)} collective-permute-done((bf16[2,192,256]{2,1,0:T(8,128)(2,1)S(1)}, bf16[2,192,256]{2,1,0:T(8,128)(2,1)S(1)}, u32[]{:S(2)}, u32[]{:S(2)}) %collective-permute-start.20) | collective-permute-done | bytes 196640 | tf_op jit(solution)/shard_map/ppermute | solution.py:35
  92.9 1.5 collective-permute-start.25
  94.4 8.5 %collective-permute-done.25.x2 = bf16[256,768]{1,0:T(8,128)(2,1)S(1)} collective-permute-done((bf16[256,768]{1,0:T(8,128)(2,1)S(1)}, bf16[256,768]{1,0:T(8,128)(2,1)S(1)}, u32[]{:S(2)}, u32[]{:S(2)}) %collective-permute-start.25) | collective-permute-done | bytes 393248 | tf_op jit(solution)/shard_map/ppermute | solution.py:35
  102.9 1.7 collective-permute-done.27.x3
  104.6 5.0 %feed.1 = (bf16[1024,768]{1,0:T(8,128)(2,1)S(1)}, bf16[1024,768]{1,0:T(8,128)(2,1)S(1)}, bf16[1024,768]{1,0:T(8,128)(2,1)S(1)}, bf16[512,768]{1,0:T(8,128)(2,1)S...) custom-call(s32[22]{0:T(128)S(1)} %concatenate.30.meta_ref, bf16[256,768]{1,0:T(8,128)(2,1)S(1)} %get-tuple-element.156.x0, ...), custom_call_target="tpu_custom_call" | custom-call | flops 1 | bytes 1 | tf_op jit(solution)/shard_map/feed/pallas_call | solution.py:914
  112.0 2.1 collective-permute-done.28
  118.0 1.4 copy-done.27
  119.4 1.4 copy-done.29
  122.1 4.8 %feed_rest.1 = (bf16[2,768,768]{2,1,0:T(8,128)(2,1)S(1)}, bf16[512,768]{1,0:T(8,128)(2,1)S(1)}, bf16[512,768]{1,0:T(8,128)(2,1)S(1)}) custom-call(bf16[1024,768]{1,0:T(8,128)(2,1)S(1)} %copy-done.25, bf16[1024,768]{1,0:T(8,128)(2,1)S(1)} %copy-done.29, bf16[1024,768]{1,0:T(8,128)(2,1)S(1)} %bitcast.85, bf16[1024,768]{1,0:T(8,128)(2,1)S(1)} %copy-done.27, ...), custom_call_target="tpu_custom_call" | custom-call | flops 1 | bytes 1 | tf_op jit(solution)/shard_map/feed_rest/pallas_call | solution.py:951
  127.0 1.6 dynamic-slice_bitcast_fusion
  129.4 2.4 before_back.1
  132.9 6.3 %collective-permute-done.30 = bf16[2,192,256]{2,1,0:T(8,128)(2,1)S(1)} collective-permute-done((bf16[2,192,256]{2,1,0:T(8,128)(2,1)S(1)}, bf16[2,192,256]{2,1,0:T(8,128)(2,1)S(1)}, u32[]{:S(2)}, u32[]{:S(2)}) %collective-permute-start.30) | collective-permute-done | bytes 196640 | tf_op jit(solution)/shard_map/ppermute | solution.py:35
  142.4 7.4 %collective-permute-start.39 = (bf16[2,4,96,768]{3,2,1,0:T(8,128)(2,1)}, bf16[2,4,96,768]{3,2,1,0:T(8,128)(2,1)}, u32[]{:S(2)}, u32[]{:S(2)}) collective-permute-start(bf16[2,4,96,768]{3,2,1,0:T(8,128)(2,1)} %get-tuple-element.199), channel_id=1, source_target_pairs={{0,4},{4,0},{8,12},{12,8},{16,20},{20,16},{24,28},{28,24},{1,5},{5... | collective-permute-start | bytes 3538952 | tf_op jit(solution)/shard_map/ppermute | solution.py:35
  152.0 1.4 copy-done.5
  153.4 1.4 copy-done.7
  155.9 1.4 copy-done.32
  157.3 11.8 %earlier_back.1 = (f32[192,1024]{1,0:T(8,128)S(1)}, bf16[1024,384]{1,0:T(8,128)(2,1)S(1)}, bf16[1040,384]{1,0:T(8,128)(2,1)S(1)}, f32[256,384]{1,0:T(8,128)S(1)}...) custom-call(s32[22]{0:T(128)S(1)} %concatenate.30.meta_ref, bf16[1024,192]{1,0:T(8,128)(2,1)S(1)} %get-tuple-element.129.q_ref, ...), custom_call_target="tpu_custom_call" | custom-call | flops 1 | bytes 1 | tf_op jit(solution)/shard_map/earlier_back/pallas_call | solution.py:760
  169.2 1.4 collective-permute-start.41
  173.2 11.8 %own_back.1 = (bf16[1024,576]{1,0:T(8,128)(2,1)S(1)}, f32[8,576]{1,0:T(8,128)S(1)}, bf16[768,768]{1,0:T(8,128)(2,1)S(1)}) custom-call(s32[22]{0:T(128)S(1)} %concatenate.30.meta_ref, bf16[1024,192]{1,0:T(8,128)(2,1)S(1)} %get-tuple-element.129.q_ref, bf16[4,192,256]{2,1,0:T(8,128)(2,1)S(1)} %pad_maximum_fusion.1.dt_ref, f32[192,1024]{1,0:T(8,128)S(1)} %copy-done.12, ...), custom_call_target="tpu_custom_call" | custom-call | flops 1 | bytes 1 | tf_op jit(solution)/shard_map/own_back/pallas_call | solution.py:835
  185.1 4.4 %collective-permute-start.40 = (bf16[1,4,96,768]{3,2,1,0:T(8,128)(2,1)S(1)}, bf16[1,4,96,768]{3,2,1,0:T(8,128)(2,1)S(1)}, u32[]{:S(2)}, u32[]{:S(2)}) collective-permute-start(bf16[1,4,96,768]{3,2,1,0:T(8,128)(2,1)S(1)} %get-tuple-element.272), channel_id=1, source_target_pairs={{0,4},{4,0},{8,12},{12,8},{16,20},{20,16},{24,28},{28,24},{1,5},{5... | collective-permute-start | bytes 1769480 | tf_op jit(solution)/shard_map/ppermute | solution.py:35
  189.5 1.5 collective-permute-start.36
  191.0 8.8 %collective-permute-done.36.refs_1_ = bf16[256,768]{1,0:T(8,128)(2,1)S(1)} collective-permute-done((bf16[256,768]{1,0:T(8,128)(2,1)S(1)}, bf16[256,768]{1,0:T(8,128)(2,1)S(1)}, u32[]{:S(2)}, u32[]{:S(2)}) %collective-permute-start.36) | collective-permute-done | bytes 393248 | tf_op jit(solution)/shard_map/ppermute | solution.py:35
  200.4 6.1 %collective-permute-done.40 = bf16[1,4,96,768]{3,2,1,0:T(8,128)(2,1)S(1)} collective-permute-done((bf16[1,4,96,768]{3,2,1,0:T(8,128)(2,1)S(1)}, bf16[1,4,96,768]{3,2,1,0:T(8,128)(2,1)S(1)}, u32[]{:S(2)}, u32[]{:S(2)}) %collective-permute-start.40) | collective-permute-done | bytes 589856 | tf_op jit(solution)/shard_map/ppermute | solution.py:35
  206.5 5.3 %collective-permute-done.42.two_ref = bf16[1024,384]{1,0:T(8,128)(2,1)S(1)} collective-permute-done((bf16[1024,384]{1,0:T(8,128)(2,1)S(1)}, bf16[1024,384]{1,0:T(8,128)(2,1)S(1)}, u32[]{:S(2)}, u32[]{:S(2)}) %collective-permute-start.42) | collective-permute-done | bytes 786464 | tf_op jit(solution)/shard_map/ppermute | solution.py:40
  211.8 4.0 %d_normed_parts.1 = (bf16[512,768]{1,0:T(8,128)(2,1)S(1)}, bf16[512,768]{1,0:T(8,128)(2,1)}, f32[1,768]{1,0:T(1,128)S(1)}) custom-call(s32[22]{0:T(128)S(1)} %concatenate.30.meta_ref, bf16[1024,576]{1,0:T(8,128)(2,1)S(1)} %get-tuple-element.201.own_ref, bf16[1040,384]{1,0:T(8,128)(2,1)S(1)} %collective-permute-done.41.one_ref.halo_ref, ...), custom_call_target="tpu_custom_call" | custom-call | flops 1 | bytes 1 | tf_op jit(solution)/shard_map/d_normed_parts/pallas_call | solution.py:1048
  216.5 1.9 add_convert_fusion
  220.0 14.7 %collective-permute-start.52 = (bf16[1,2,96,768]{3,2,1,0:T(8,128)(2,1)S(1)}, bf16[1,2,96,768]{3,2,1,0:T(8,128)(2,1)S(1)}, u32[]{:S(2)}, u32[]{:S(2)}) collective-permute-start(bf16[1,2,96,768]{3,2,1,0:T(8,128)(2,1)S(1)} %dynamic-slice_bitcast_fusion.4), channel_id=1, source_target_pairs={{0,8},{4,12},{8,0},{12,4},{16,24},{20,28},{24,16},{28,20},{1,9},{5... | collective-permute-start | bytes 884744 | tf_op jit(solution)/shard_map/ppermute | solution.py:35
  235.7 2.0 collective-permute-start.48
  237.8 1.6 collective-permute-start.45
  239.8 2.7 collective-permute-done.52
  244.4 7.7 %collective-permute-done.50 = bf16[1,2,96,768]{3,2,1,0:T(8,128)(2,1)S(1)} collective-permute-done((bf16[1,2,96,768]{3,2,1,0:T(8,128)(2,1)S(1)}, bf16[1,2,96,768]{3,2,1,0:T(8,128)(2,1)S(1)}, u32[]{:S(2)}, u32[]{:S(2)}) %collective-permute-start.50) | collective-permute-done | bytes 294944 | tf_op jit(solution)/shard_map/ppermute | solution.py:35
  254.4 2.0 collective-permute-start.57
  256.4 1.8 collective-permute-done.48
  258.2 2.5 collective-permute-start.58
  261.8 1.6 collective-permute-start.47
  263.4 2.1 collective-permute-done.57
  266.8 2.5 collective-permute-done.59
  270.6 5.6 %collective-permute-done.49 = bf16[1,1,96,768]{3,2,1,0:T(8,128)(2,1)S(1)} collective-permute-done((bf16[1,1,96,768]{3,2,1,0:T(8,128)(2,1)}, bf16[1,1,96,768]{3,2,1,0:T(8,128)(2,1)S(1)}, u32[]{:S(2)}, u32[]{:S(2)}) %collective-permute-start.49) | collective-permute-done | bytes 147488 | tf_op jit(solution)/shard_map/ppermute | solution.py:35
  278.5 1.7 add_bitcast_fusion
  280.8 2.3 assemble.2
  284.5 1.7 add_bitcast_fusion.1
  286.2 2.7 assemble.3
  (308 shorter events, 57.9 us)
Async XLA Ops:
  1.7 13.9 %collective-permute-start = (bf16[1,96,576]{2,1,0:T(8,128)(2,1)S(1)}, bf16[1,96,576]{2,1,0:T(8,128)(2,1)S(1)}, u32[]{:S(2)}, u32[]{:S(2)}) collective-permute-start(bf16[1,96,576]{2,1,0:T(8,128)(2,1)S(1)} %maximum_bitcast_fusion.refs_0_), channel_id=1, source_target_pairs={{0,8},{4,12},{8,0},{12,4},{16,24},{20,28},{24,16},{28,20},{1,9},{5... | collective-permute-start | bytes 331784 | tf_op jit(solution)/shard_map/ppermute | solution.py:35
  4.8 12.3 %collective-permute-start.1 = (bf16[1,96,576]{2,1,0:T(8,128)(2,1)S(1)}, bf16[1,96,576]{2,1,0:T(8,128)(2,1)S(1)}, u32[]{:S(2)}, u32[]{:S(2)}) collective-permute-start(bf16[1,96,576]{2,1,0:T(8,128)(2,1)S(1)} %maximum_bitcast_fusion.refs_0_), channel_id=1, source_target_pairs={{0,16},{4,20},{8,24},{12,28},{16,0},{20,4},{24,8},{28,12},{1,17},{... | collective-permute-start | bytes 331784 | tf_op jit(solution)/shard_map/ppermute | solution.py:35
  7.4 9.7 %collective-permute-start.2 = (bf16[1,96,576]{2,1,0:T(8,128)(2,1)S(1)}, bf16[1,96,576]{2,1,0:T(8,128)(2,1)S(1)}, u32[]{:S(2)}, u32[]{:S(2)}) collective-permute-start(bf16[1,96,576]{2,1,0:T(8,128)(2,1)S(1)} %maximum_bitcast_fusion.refs_0_), channel_id=1, source_target_pairs={{0,24},{4,28},{8,16},{12,20},{16,8},{20,12},{24,0},{28,4},{1,25},{... | collective-permute-start | bytes 331784 | tf_op jit(solution)/shard_map/ppermute | solution.py:35
  9.2 12.4 %collective-permute-start.4 = (bf16[272,768]{1,0:T(8,128)(2,1)S(1)}, bf16[272,768]{1,0:T(8,128)(2,1)}, u32[]{:S(2)}, u32[]{:S(2)}) collective-permute-start(bf16[272,768]{1,0:T(8,128)(2,1)S(1)} %pad_maximum_fusion), channel_id=1, source_target_pairs={{0,8},{4,12},{8,16},{12,20},{16,24},{20,28},{1,9},{5,13},{9,17},{1... | collective-permute-start | bytes 1253384 | tf_op jit(solution)/shard_map/ppermute | solution.py:40
  17.2 27.5 %collective-permute-start.3 = (bf16[4,96,576]{2,1,0:T(8,128)(2,1)S(1)}, bf16[4,96,576]{2,1,0:T(8,128)(2,1)S(1)}, u32[]{:S(2)}, u32[]{:S(2)}) collective-permute-start(bf16[4,96,576]{2,1,0:T(8,128)(2,1)S(1)} %joined.3.refs_0_), channel_id=1, source_target_pairs={{0,4},{4,0},{8,12},{12,8},{16,20},{20,16},{24,28},{28,24},{1,5},{5... | collective-permute-start | bytes 1327112 | tf_op jit(solution)/shard_map/ppermute | solution.py:35
  22.5 14.4 %collective-permute-start.5 = (bf16[272,768]{1,0:T(8,128)(2,1)}, bf16[272,768]{1,0:T(8,128)(2,1)}, u32[]{:S(2)}, u32[]{:S(2)}) collective-permute-start(bf16[272,768]{1,0:T(8,128)(2,1)} %broadcast_select_fusion), channel_id=1, source_target_pairs={{0,4},{4,0},{8,12},{12,8},{16,20},{20,16},{24,28},{28,24},{1,5},{5... | collective-permute-start | bytes 1253384 | tf_op jit(solution)/shard_map/ppermute | solution.py:35
  36.9 18.3 %collective-permute-start.6 = (bf16[272,768]{1,0:T(8,128)(2,1)}, bf16[272,768]{1,0:T(8,128)(2,1)}, u32[]{:S(2)}, u32[]{:S(2)}) collective-permute-start(bf16[272,768]{1,0:T(8,128)(2,1)} %collective-permute-done.5.halo_ref.refs_4_), channel_id=1, source_target_pairs={{0,2},{1,3},{2,0},{3,1},{4,6},{5,7},{6,4},{7,5},{8,10},{9,11},{10,... | collective-permute-start | bytes 1253384 | tf_op jit(solution)/shard_map/ppermute | solution.py:35
  38.7 20.3 %collective-permute-start.12 = (bf16[1,120,768]{2,1,0:T(8,128)(2,1)S(1)}, bf16[1,120,768]{2,1,0:T(8,128)(2,1)S(1)}, u32[]{:S(2)}, u32[]{:S(2)}) collective-permute-start(bf16[1,120,768]{2,1,0:T(8,128)(2,1)S(1)} %bitcast.88), channel_id=1, source_target_pairs={{0,8},{4,12},{8,0},{12,4},{16,24},{20,28},{24,16},{28,20},{1,9},{5... | collective-permute-start | bytes 552968 | tf_op jit(solution)/shard_map/ppermute | solution.py:35
  41.9 17.0 %collective-permute-start.13 = (bf16[1,120,768]{2,1,0:T(8,128)(2,1)S(1)}, bf16[1,120,768]{2,1,0:T(8,128)(2,1)S(1)}, u32[]{:S(2)}, u32[]{:S(2)}) collective-permute-start(bf16[1,120,768]{2,1,0:T(8,128)(2,1)S(1)} %bitcast.89), channel_id=1, source_target_pairs={{0,16},{4,20},{8,24},{12,28},{16,0},{20,4},{24,8},{28,12},{1,17},{... | collective-permute-start | bytes 552968 | tf_op jit(solution)/shard_map/ppermute | solution.py:35
  43.3 15.7 %collective-permute-start.14 = (bf16[1,120,768]{2,1,0:T(8,128)(2,1)S(1)}, bf16[1,120,768]{2,1,0:T(8,128)(2,1)S(1)}, u32[]{:S(2)}, u32[]{:S(2)}) collective-permute-start(bf16[1,120,768]{2,1,0:T(8,128)(2,1)S(1)} %bitcast.90), channel_id=1, source_target_pairs={{0,24},{4,28},{8,16},{12,20},{16,8},{20,12},{24,0},{28,4},{1,25},{... | collective-permute-start | bytes 552968 | tf_op jit(solution)/shard_map/ppermute | solution.py:35
  45.5 15.9 %collective-permute-start.7 = (bf16[272,768]{1,0:T(8,128)(2,1)}, bf16[272,768]{1,0:T(8,128)(2,1)S(1)}, u32[]{:S(2)}, u32[]{:S(2)}) collective-permute-start(bf16[272,768]{1,0:T(8,128)(2,1)} %collective-permute-done.4.refs_0_), channel_id=1, source_target_pairs={{0,2},{1,3},{2,0},{3,1},{4,6},{5,7},{6,4},{7,5},{8,10},{9,11},{10,... | collective-permute-start | bytes 1253384 | tf_op jit(solution)/shard_map/ppermute | solution.py:35
  59.1 18.9 %collective-permute-start.15 = (bf16[4,120,768]{2,1,0:T(8,128)(2,1)S(1)}, bf16[4,120,768]{2,1,0:T(8,128)(2,1)S(1)}, u32[]{:S(2)}, u32[]{:S(2)}) collective-permute-start(bf16[4,120,768]{2,1,0:T(8,128)(2,1)S(1)} %joined.4.refs_0_), channel_id=1, source_target_pairs={{0,4},{4,0},{8,12},{12,8},{16,20},{20,16},{24,28},{28,24},{1,5},{5... | collective-permute-start | bytes 2211848 | tf_op jit(solution)/shard_map/ppermute | solution.py:35
  60.9 2.0 collective-permute-start.8
  60.9 3.2 %collective-permute-start.10 = (bf16[272,768]{1,0:T(8,128)(2,1)}, bf16[272,768]{1,0:T(8,128)(2,1)S(1)}, u32[]{:S(2)}, u32[]{:S(2)}) collective-permute-start(bf16[272,768]{1,0:T(8,128)(2,1)} %collective-permute-done.5.halo_ref.refs_4_), channel_id=1, source_target_pairs={{0,1},{1,0},{2,3},{3,2},{4,5},{5,4},{6,7},{7,6},{8,9},{9,8},{10,11... | collective-permute-start | bytes 1253384 | tf_op jit(solution)/shard_map/ppermute | solution.py:35
  61.4 4.7 %collective-permute-start.9 = (bf16[272,768]{1,0:T(8,128)(2,1)S(1)}, bf16[272,768]{1,0:T(8,128)(2,1)S(1)}, u32[]{:S(2)}, u32[]{:S(2)}) collective-permute-start(bf16[272,768]{1,0:T(8,128)(2,1)S(1)} %collective-permute-done.7.refs_1_), channel_id=1, source_target_pairs={{0,1},{1,0},{2,3},{3,2},{4,5},{5,4},{6,7},{7,6},{8,9},{9,8},{10,11... | collective-permute-start | bytes 1253384 | tf_op jit(solution)/shard_map/ppermute | solution.py:35
  61.4 5.9 %collective-permute-start.11 = (bf16[272,768]{1,0:T(8,128)(2,1)}, bf16[272,768]{1,0:T(8,128)(2,1)S(1)}, u32[]{:S(2)}, u32[]{:S(2)}) collective-permute-start(bf16[272,768]{1,0:T(8,128)(2,1)} %collective-permute-done.6.refs_5_), channel_id=1, source_target_pairs={{0,1},{1,0},{2,3},{3,2},{4,5},{5,4},{6,7},{7,6},{8,9},{9,8},{10,11... | collective-permute-start | bytes 1253384 | tf_op jit(solution)/shard_map/ppermute | solution.py:35
  62.8 13.0 %collective-permute-start.16 = (bf16[1,96,768]{2,1,0:T(8,128)(2,1)S(1)}, bf16[1,96,768]{2,1,0:T(8,128)(2,1)S(1)}, u32[]{:S(2)}, u32[]{:S(2)}) collective-permute-start(bf16[1,96,768]{2,1,0:T(8,128)(2,1)S(1)} %bitcast.92), channel_id=1, source_target_pairs={{0,8},{4,12},{8,0},{12,4},{16,24},{20,28},{24,16},{28,20},{1,9},{5... | collective-permute-start | bytes 442376 | tf_op jit(solution)/shard_map/ppermute | solution.py:35
  64.0 14.0 %collective-permute-start.17 = (bf16[1,96,768]{2,1,0:T(8,128)(2,1)S(1)}, bf16[1,96,768]{2,1,0:T(8,128)(2,1)S(1)}, u32[]{:S(2)}, u32[]{:S(2)}) collective-permute-start(bf16[1,96,768]{2,1,0:T(8,128)(2,1)S(1)} %bitcast.93), channel_id=1, source_target_pairs={{0,16},{4,20},{8,24},{12,28},{16,0},{20,4},{24,8},{28,12},{1,17},{... | collective-permute-start | bytes 442376 | tf_op jit(solution)/shard_map/ppermute | solution.py:35
  66.1 11.9 %collective-permute-start.18 = (bf16[1,96,768]{2,1,0:T(8,128)(2,1)S(1)}, bf16[1,96,768]{2,1,0:T(8,128)(2,1)S(1)}, u32[]{:S(2)}, u32[]{:S(2)}) collective-permute-start(bf16[1,96,768]{2,1,0:T(8,128)(2,1)S(1)} %bitcast.94), channel_id=1, source_target_pairs={{0,24},{4,28},{8,16},{12,20},{16,8},{20,12},{24,0},{28,4},{1,25},{... | collective-permute-start | bytes 442376 | tf_op jit(solution)/shard_map/ppermute | solution.py:35
  78.0 13.2 %collective-permute-start.24 = (bf16[4,96,768]{2,1,0:T(8,128)(2,1)S(1)}, bf16[4,96,768]{2,1,0:T(8,128)(2,1)S(1)}, u32[]{:S(2)}, u32[]{:S(2)}) collective-permute-start(bf16[4,96,768]{2,1,0:T(8,128)(2,1)S(1)} %joined.5.refs_2_), channel_id=1, source_target_pairs={{0,4},{4,0},{8,12},{12,8},{16,20},{20,16},{24,28},{28,24},{1,5},{5... | collective-permute-start | bytes 1769480 | tf_op jit(solution)/shard_map/ppermute | solution.py:35
  79.3 6.8 %collective-permute-start.21 = (bf16[192,768]{1,0:T(8,128)(2,1)S(1)}, bf16[192,768]{1,0:T(8,128)(2,1)S(1)}, u32[]{:S(2)}, u32[]{:S(2)}) collective-permute-start(bf16[192,768]{1,0:T(8,128)(2,1)S(1)} %unpack_out.1.w0), channel_id=1, source_target_pairs={{0,2},{1,3},{2,0},{3,1},{4,6},{5,7},{6,4},{7,5},{8,10},{9,11},{10,... | collective-permute-start | bytes 884744 | tf_op jit(solution)/shard_map/ppermute | solution.py:35
  82.2 1.5 collective-permute-start.19
  83.8 7.0 %collective-permute-start.20 = (bf16[2,192,256]{2,1,0:T(8,128)(2,1)S(1)}, bf16[2,192,256]{2,1,0:T(8,128)(2,1)S(1)}, u32[]{:S(2)}, u32[]{:S(2)}) collective-permute-start(bf16[2,192,256]{2,1,0:T(8,128)(2,1)S(1)} %pad_maximum_fusion.2), channel_id=1, source_target_pairs={{0,2},{1,3},{2,0},{3,1},{4,6},{5,7},{6,4},{7,5},{8,10},{9,11},{10,... | collective-permute-start | bytes 589832 | tf_op jit(solution)/shard_map/ppermute | solution.py:35
  84.5 6.7 %collective-permute-start.22 = (bf16[192,768]{1,0:T(8,128)(2,1)S(1)}, bf16[192,768]{1,0:T(8,128)(2,1)S(1)}, u32[]{:S(2)}, u32[]{:S(2)}) collective-permute-start(bf16[192,768]{1,0:T(8,128)(2,1)S(1)} %unpack_out.1.w0), channel_id=1, source_target_pairs={{0,1},{1,0},{2,3},{3,2},{4,5},{5,4},{6,7},{7,6},{8,9},{9,8},{10,11... | collective-permute-start | bytes 884744 | tf_op jit(solution)/shard_map/ppermute | solution.py:35
  86.1 5.1 %collective-permute-start.23 = (bf16[192,768]{1,0:T(8,128)(2,1)S(1)}, bf16[192,768]{1,0:T(8,128)(2,1)S(1)}, u32[]{:S(2)}, u32[]{:S(2)}) collective-permute-start(bf16[192,768]{1,0:T(8,128)(2,1)S(1)} %collective-permute-done.21.w1), channel_id=1, source_target_pairs={{0,1},{1,0},{2,3},{3,2},{4,5},{5,4},{6,7},{7,6},{8,9},{9,8},{10,11... | collective-permute-start | bytes 884744 | tf_op jit(solution)/shard_map/ppermute | solution.py:35
  90.8 18.8 %copy-start.45 = (bf16[192,256]{1,0:T(8,128)(2,1)}, bf16[192,256]{1,0:T(8,128)(2,1)S(1)}, u32[]{:S(2)}) copy-start(bf16[192,256]{1,0:T(8,128)(2,1)S(1)} %get-tuple-element.294.a3) | copy-start | bytes 294916
  91.2 18.4 %copy-start.41 = (bf16[192,768]{1,0:T(8,128)(2,1)}, bf16[192,768]{1,0:T(8,128)(2,1)S(1)}, u32[]{:S(2)}) copy-start(bf16[192,768]{1,0:T(8,128)(2,1)S(1)} %collective-permute-done.23.w3) | copy-start | bytes 884740
  92.9 10.0 %collective-permute-start.25 = (bf16[256,768]{1,0:T(8,128)(2,1)S(1)}, bf16[256,768]{1,0:T(8,128)(2,1)S(1)}, u32[]{:S(2)}, u32[]{:S(2)}) collective-permute-start(bf16[256,768]{1,0:T(8,128)(2,1)S(1)} %get-tuple-element.156.x0), channel_id=1, source_target_pairs={{0,2},{1,3},{2,0},{3,1},{4,6},{5,7},{6,4},{7,5},{8,10},{9,11},{10,... | collective-permute-start | bytes 1179656 | tf_op jit(solution)/shard_map/ppermute | solution.py:35
  94.4 8.5 %collective-permute-start.26 = (bf16[256,768]{1,0:T(8,128)(2,1)S(1)}, bf16[256,768]{1,0:T(8,128)(2,1)S(1)}, u32[]{:S(2)}, u32[]{:S(2)}) collective-permute-start(bf16[256,768]{1,0:T(8,128)(2,1)S(1)} %get-tuple-element.156.x0), channel_id=1, source_target_pairs={{0,1},{1,0},{2,3},{3,2},{4,5},{5,4},{6,7},{7,6},{8,9},{9,8},{10,11... | collective-permute-start | bytes 1179656 | tf_op jit(solution)/shard_map/ppermute | solution.py:35
  102.9 1.7 collective-permute-start.27
  111.8 2.3 collective-permute-start.28
  115.3 13.4 %collective-permute-start.29 = (bf16[256,768]{1,0:T(8,128)(2,1)}, bf16[256,768]{1,0:T(8,128)(2,1)}, u32[]{:S(2)}, u32[]{:S(2)}) collective-permute-start(bf16[256,768]{1,0:T(8,128)(2,1)} %get-tuple-element.276), channel_id=1, source_target_pairs={{0,2},{1,3},{2,0},{3,1},{4,6},{5,7},{6,4},{7,5},{8,10},{9,11},{10,... | collective-permute-start | bytes 1179656 | tf_op jit(solution)/shard_map/ppermute | solution.py:35
  126.9 12.5 %collective-permute-start.32 = (bf16[512,768]{1,0:T(8,128)(2,1)S(1)}, bf16[512,768]{1,0:T(8,128)(2,1)S(1)}, u32[]{:S(2)}, u32[]{:S(2)}) collective-permute-start(bf16[512,768]{1,0:T(8,128)(2,1)S(1)} %get-tuple-element.174), channel_id=1, source_target_pairs={{0,1},{1,0},{2,3},{3,2},{4,5},{5,4},{6,7},{7,6},{8,9},{9,8},{10,11... | collective-permute-start | bytes 2359304 | tf_op jit(solution)/shard_map/ppermute | solution.py:35
  131.9 7.4 %collective-permute-start.30 = (bf16[2,192,256]{2,1,0:T(8,128)(2,1)S(1)}, bf16[2,192,256]{2,1,0:T(8,128)(2,1)S(1)}, u32[]{:S(2)}, u32[]{:S(2)}) collective-permute-start(bf16[2,192,256]{2,1,0:T(8,128)(2,1)S(1)} %pad_maximum_fusion.3), channel_id=1, source_target_pairs={{0,2},{1,3},{2,0},{3,1},{4,6},{5,7},{6,4},{7,5},{8,10},{9,11},{10,... | collective-permute-start | bytes 589832 | tf_op jit(solution)/shard_map/ppermute | solution.py:35
  132.7 17.1 %collective-permute-start.34 = (bf16[2,192,768]{2,1,0:T(8,128)(2,1)S(1)}, bf16[2,192,768]{2,1,0:T(8,128)(2,1)S(1)}, u32[]{:S(2)}, u32[]{:S(2)}) collective-permute-start(bf16[2,192,768]{2,1,0:T(8,128)(2,1)S(1)} %get-tuple-element.183), channel_id=1, source_target_pairs={{0,1},{1,0},{2,3},{3,2},{4,5},{5,4},{6,7},{7,6},{8,9},{9,8},{10,11... | collective-permute-start | bytes 1769480 | tf_op jit(solution)/shard_map/ppermute | solution.py:35
  139.3 1.5 collective-permute-start.31
  141.6 30.3 %collective-permute-start.33 = (bf16[256,768]{1,0:T(8,128)(2,1)}, bf16[256,768]{1,0:T(8,128)(2,1)}, u32[]{:S(2)}, u32[]{:S(2)}) collective-permute-start(bf16[256,768]{1,0:T(8,128)(2,1)} %slice.162), channel_id=1, source_target_pairs={{0,2},{1,3},{2,0},{3,1},{4,6},{5,7},{6,4},{7,5},{8,10},{9,11},{10,... | collective-permute-start | bytes 1179656 | tf_op jit(solution)/shard_map/ppermute | solution.py:35
  142.4 57.4 %collective-permute-start.39 = (bf16[2,4,96,768]{3,2,1,0:T(8,128)(2,1)}, bf16[2,4,96,768]{3,2,1,0:T(8,128)(2,1)}, u32[]{:S(2)}, u32[]{:S(2)}) collective-permute-start(bf16[2,4,96,768]{3,2,1,0:T(8,128)(2,1)} %get-tuple-element.199), channel_id=1, source_target_pairs={{0,4},{4,0},{8,12},{12,8},{16,20},{20,16},{24,28},{28,24},{1,5},{5... | collective-permute-start | bytes 3538952 | tf_op jit(solution)/shard_map/ppermute | solution.py:35
  151.4 21.7 %collective-permute-start.35 = (bf16[192,768]{1,0:T(8,128)(2,1)}, bf16[192,768]{1,0:T(8,128)(2,1)}, u32[]{:S(2)}, u32[]{:S(2)}) collective-permute-start(bf16[192,768]{1,0:T(8,128)(2,1)} %fusion.3), channel_id=1, source_target_pairs={{0,2},{1,3},{2,0},{3,1},{4,6},{5,7},{6,4},{7,5},{8,10},{9,11},{10,... | collective-permute-start | bytes 884744 | tf_op jit(solution)/shard_map/ppermute | solution.py:35
  169.2 42.5 %collective-permute-start.41 = (bf16[1040,384]{1,0:T(8,128)(2,1)S(1)}, bf16[1040,384]{1,0:T(8,128)(2,1)S(1)}, u32[]{:S(2)}, u32[]{:S(2)}) collective-permute-start(bf16[1040,384]{1,0:T(8,128)(2,1)S(1)} %get-tuple-element.190.one_ref), channel_id=1, source_target_pairs={{4,0},{8,4},{12,8},{16,12},{20,16},{24,20},{28,24},{5,1},{9,5},{13... | collective-permute-start | bytes 2396168 | tf_op jit(solution)/shard_map/ppermute | solution.py:40
  170.6 41.1 %collective-permute-start.42 = (bf16[1024,384]{1,0:T(8,128)(2,1)S(1)}, bf16[1024,384]{1,0:T(8,128)(2,1)S(1)}, u32[]{:S(2)}, u32[]{:S(2)}) collective-permute-start(bf16[1024,384]{1,0:T(8,128)(2,1)S(1)} %get-tuple-element.189.two_ref), channel_id=1, source_target_pairs={{8,0},{12,4},{16,8},{20,12},{24,16},{28,20},{9,1},{13,5},{17,9},{2... | collective-permute-start | bytes 2359304 | tf_op jit(solution)/shard_map/ppermute | solution.py:40
  173.2 38.6 %copy-start.9 = (bf16[768,576]{1,0:T(8,128)(2,1)S(1)}, bf16[768,576]{1,0:T(8,128)(2,1)}, u32[]{:S(2)}) copy-start(bf16[768,576]{1,0:T(8,128)(2,1)} %copy-done.8) | copy-start | bytes 2654212
  185.0 26.8 %copy-start.1 = (bf16[1024,768]{1,0:T(8,128)(2,1)S(1)}, bf16[1024,768]{1,0:T(8,128)(2,1)}, u32[]{:S(2)}) copy-start(bf16[1024,768]{1,0:T(8,128)(2,1)} %x_ref.3) | copy-start | bytes 4718596
  185.1 21.4 %collective-permute-start.40 = (bf16[1,4,96,768]{3,2,1,0:T(8,128)(2,1)S(1)}, bf16[1,4,96,768]{3,2,1,0:T(8,128)(2,1)S(1)}, u32[]{:S(2)}, u32[]{:S(2)}) collective-permute-start(bf16[1,4,96,768]{3,2,1,0:T(8,128)(2,1)S(1)} %get-tuple-element.272), channel_id=1, source_target_pairs={{0,4},{4,0},{8,12},{12,8},{16,20},{20,16},{24,28},{28,24},{1,5},{5... | collective-permute-start | bytes 1769480 | tf_op jit(solution)/shard_map/ppermute | solution.py:35
  189.5 10.3 %collective-permute-start.36 = (bf16[256,768]{1,0:T(8,128)(2,1)S(1)}, bf16[256,768]{1,0:T(8,128)(2,1)S(1)}, u32[]{:S(2)}, u32[]{:S(2)}) collective-permute-start(bf16[256,768]{1,0:T(8,128)(2,1)S(1)} %add_convert_fusion.5.refs_0_), channel_id=1, source_target_pairs={{0,2},{1,3},{2,0},{3,1},{4,6},{5,7},{6,4},{7,5},{8,10},{9,11},{10,... | collective-permute-start | bytes 1179656 | tf_op jit(solution)/shard_map/ppermute | solution.py:35
  199.8 6.7 %collective-permute-start.37 = (bf16[256,768]{1,0:T(8,128)(2,1)S(1)}, bf16[256,768]{1,0:T(8,128)(2,1)S(1)}, u32[]{:S(2)}, u32[]{:S(2)}) collective-permute-start(bf16[256,768]{1,0:T(8,128)(2,1)S(1)} %add_convert_fusion.5.refs_0_), channel_id=1, source_target_pairs={{0,1},{1,0},{2,3},{3,2},{4,5},{5,4},{6,7},{7,6},{8,9},{9,8},{10,11... | collective-permute-start | bytes 1179656 | tf_op jit(solution)/shard_map/ppermute | solution.py:35
  199.8 6.7 %collective-permute-start.38 = (bf16[256,768]{1,0:T(8,128)(2,1)S(1)}, bf16[256,768]{1,0:T(8,128)(2,1)S(1)}, u32[]{:S(2)}, u32[]{:S(2)}) collective-permute-start(bf16[256,768]{1,0:T(8,128)(2,1)S(1)} %collective-permute-done.36.refs_1_), channel_id=1, source_target_pairs={{0,1},{1,0},{2,3},{3,2},{4,5},{5,4},{6,7},{7,6},{8,9},{9,8},{10,11... | collective-permute-start | bytes 1179656 | tf_op jit(solution)/shard_map/ppermute | solution.py:35
  215.8 2.6 collective-permute-start.43
  215.9 2.5 collective-permute-start.44
  220.0 22.5 %collective-permute-start.52 = (bf16[1,2,96,768]{3,2,1,0:T(8,128)(2,1)S(1)}, bf16[1,2,96,768]{3,2,1,0:T(8,128)(2,1)S(1)}, u32[]{:S(2)}, u32[]{:S(2)}) collective-permute-start(bf16[1,2,96,768]{3,2,1,0:T(8,128)(2,1)S(1)} %dynamic-slice_bitcast_fusion.4), channel_id=1, source_target_pairs={{0,8},{4,12},{8,0},{12,4},{16,24},{20,28},{24,16},{28,20},{1,9},{5... | collective-permute-start | bytes 884744 | tf_op jit(solution)/shard_map/ppermute | solution.py:35
  234.9 17.2 %collective-permute-start.50 = (bf16[1,2,96,768]{3,2,1,0:T(8,128)(2,1)S(1)}, bf16[1,2,96,768]{3,2,1,0:T(8,128)(2,1)S(1)}, u32[]{:S(2)}, u32[]{:S(2)}) collective-permute-start(bf16[1,2,96,768]{3,2,1,0:T(8,128)(2,1)S(1)} %dynamic-slice_bitcast_fusion.5), channel_id=1, source_target_pairs={{0,8},{4,12},{8,0},{12,4},{16,24},{20,28},{24,16},{28,20},{1,9},{5... | collective-permute-start | bytes 884744 | tf_op jit(solution)/shard_map/ppermute | solution.py:35
  235.7 22.6 %collective-permute-start.48 = (bf16[1,2,96,768]{3,2,1,0:T(8,128)(2,1)}, bf16[1,2,96,768]{3,2,1,0:T(8,128)(2,1)}, u32[]{:S(2)}, u32[]{:S(2)}) collective-permute-start(bf16[1,2,96,768]{3,2,1,0:T(8,128)(2,1)} %dynamic-slice_bitcast_fusion.6), channel_id=1, source_target_pairs={{0,8},{4,12},{8,0},{12,4},{16,24},{20,28},{24,16},{28,20},{1,9},{5... | collective-permute-start | bytes 884744 | tf_op jit(solution)/shard_map/ppermute | solution.py:35
  237.8 15.1 %collective-permute-start.45 = (bf16[256,768]{1,0:T(8,128)(2,1)S(1)}, bf16[256,768]{1,0:T(8,128)(2,1)S(1)}, u32[]{:S(2)}, u32[]{:S(2)}) collective-permute-start(bf16[256,768]{1,0:T(8,128)(2,1)S(1)} %get-tuple-element.274), channel_id=1, source_target_pairs={{0,2},{1,3},{2,0},{3,1},{4,6},{5,7},{6,4},{7,5},{8,10},{9,11},{10,... | collective-permute-start | bytes 1179656 | tf_op jit(solution)/shard_map/ppermute | solution.py:35
  239.3 13.5 %collective-permute-start.46 = (f32[2,768]{1,0:T(2,128)S(1)}, f32[2,768]{1,0:T(2,128)S(1)}, u32[]{:S(2)}, u32[]{:S(2)}) collective-permute-start(f32[2,768]{1,0:T(2,128)S(1)} %fusion.4), channel_id=1, source_target_pairs={{0,2},{1,3},{2,0},{3,1},{4,6},{5,7},{6,4},{7,5},{8,10},{9,11},{10,... | collective-permute-start | bytes 18440 | tf_op jit(solution)/shard_map/ppermute | solution.py:35
  243.3 27.2 %collective-permute-start.53 = (bf16[1,1,96,768]{3,2,1,0:T(8,128)(2,1)}, bf16[1,1,96,768]{3,2,1,0:T(8,128)(2,1)}, u32[]{:S(2)}, u32[]{:S(2)}) collective-permute-start(bf16[1,1,96,768]{3,2,1,0:T(8,128)(2,1)} %get-tuple-element.286), channel_id=1, source_target_pairs={{0,16},{4,20},{8,24},{12,28},{16,0},{20,4},{24,8},{28,12},{1,17},{... | collective-permute-start | bytes 442376 | tf_op jit(solution)/shard_map/ppermute | solution.py:35
  252.8 17.7 %collective-permute-start.51 = (bf16[1,1,96,768]{3,2,1,0:T(8,128)(2,1)}, bf16[1,1,96,768]{3,2,1,0:T(8,128)(2,1)}, u32[]{:S(2)}, u32[]{:S(2)}) collective-permute-start(bf16[1,1,96,768]{3,2,1,0:T(8,128)(2,1)} %get-tuple-element.288), channel_id=1, source_target_pairs={{0,16},{4,20},{8,24},{12,28},{16,0},{20,4},{24,8},{28,12},{1,17},{... | collective-permute-start | bytes 442376 | tf_op jit(solution)/shard_map/ppermute | solution.py:35
  253.3 8.5 %collective-permute-start.56 = (f32[3264]{0:T(1024)S(1)}, f32[3264]{0:T(1024)S(1)}, u32[]{:S(2)}, u32[]{:S(2)}) collective-permute-start(f32[3264]{0:T(1024)S(1)} %constant_dynamic-update-slice_fusion), channel_id=1, source_target_pairs={{0,8},{4,12},{8,0},{12,4},{16,24},{20,28},{24,16},{28,20},{1,9},{5... | collective-permute-start | bytes 39176 | tf_op jit(solution)/shard_map/ppermute | solution.py:35
  254.4 11.0 %collective-permute-start.57 = (f32[3264]{0:T(1024)S(1)}, f32[3264]{0:T(1024)S(1)}, u32[]{:S(2)}, u32[]{:S(2)}) collective-permute-start(f32[3264]{0:T(1024)S(1)} %constant_dynamic-update-slice_fusion), channel_id=1, source_target_pairs={{0,16},{4,20},{8,24},{12,28},{16,0},{20,4},{24,8},{28,12},{1,17},{... | collective-permute-start | bytes 39176 | tf_op jit(solution)/shard_map/ppermute | solution.py:35
  258.2 7.2 %collective-permute-start.58 = (f32[3264]{0:T(1024)S(1)}, f32[3264]{0:T(1024)S(1)}, u32[]{:S(2)}, u32[]{:S(2)}) collective-permute-start(f32[3264]{0:T(1024)S(1)} %constant_dynamic-update-slice_fusion), channel_id=1, source_target_pairs={{0,24},{4,28},{8,16},{12,20},{16,8},{20,12},{24,0},{28,4},{1,25},{... | collective-permute-start | bytes 39176 | tf_op jit(solution)/shard_map/ppermute | solution.py:35
  261.8 14.3 %collective-permute-start.47 = (bf16[256,768]{1,0:T(8,128)(2,1)S(1)}, bf16[256,768]{1,0:T(8,128)(2,1)S(1)}, u32[]{:S(2)}, u32[]{:S(2)}) collective-permute-start(bf16[256,768]{1,0:T(8,128)(2,1)S(1)} %grad_tokens_own.1.refs_0_), channel_id=1, source_target_pairs={{0,2},{1,3},{2,0},{3,1},{4,6},{5,7},{6,4},{7,5},{8,10},{9,11},{10,... | collective-permute-start | bytes 1179656 | tf_op jit(solution)/shard_map/ppermute | solution.py:35
  265.5 3.8 %collective-permute-start.59 = (f32[3264]{0:T(1024)S(1)}, f32[3264]{0:T(1024)S(1)}, u32[]{:S(2)}, u32[]{:S(2)}) collective-permute-start(f32[3264]{0:T(1024)S(1)} %add_add_fusion), channel_id=1, source_target_pairs={{0,4},{4,0},{8,12},{12,8},{16,20},{20,16},{24,28},{28,24},{1,5},{5... | collective-permute-start | bytes 39176 | tf_op jit(solution)/shard_map/ppermute | solution.py:35
  266.2 9.9 %collective-permute-start.49 = (bf16[1,1,96,768]{3,2,1,0:T(8,128)(2,1)}, bf16[1,1,96,768]{3,2,1,0:T(8,128)(2,1)S(1)}, u32[]{:S(2)}, u32[]{:S(2)}) collective-permute-start(bf16[1,1,96,768]{3,2,1,0:T(8,128)(2,1)} %get-tuple-element.290), channel_id=1, source_target_pairs={{0,16},{4,20},{8,24},{12,28},{16,0},{20,4},{24,8},{28,12},{1,17},{... | collective-permute-start | bytes 442376 | tf_op jit(solution)/shard_map/ppermute | solution.py:35
  269.3 16.9 %collective-permute-start.54 = (bf16[256,768]{1,0:T(8,128)(2,1)S(1)}, bf16[256,768]{1,0:T(8,128)(2,1)S(1)}, u32[]{:S(2)}, u32[]{:S(2)}) collective-permute-start(bf16[256,768]{1,0:T(8,128)(2,1)S(1)} %grad_tokens_own.1.refs_0_), channel_id=1, source_target_pairs={{0,1},{1,0},{2,3},{3,2},{4,5},{5,4},{6,7},{7,6},{8,9},{9,8},{10,11... | collective-permute-start | bytes 1179656 | tf_op jit(solution)/shard_map/ppermute | solution.py:35
  278.5 7.7 %collective-permute-start.55 = (bf16[256,768]{1,0:T(8,128)(2,1)S(1)}, bf16[256,768]{1,0:T(8,128)(2,1)S(1)}, u32[]{:S(2)}, u32[]{:S(2)}) collective-permute-start(bf16[256,768]{1,0:T(8,128)(2,1)S(1)} %collective-permute-done.47.refs_1_), channel_id=1, source_target_pairs={{0,1},{1,0},{2,3},{3,2},{4,5},{5,4},{6,7},{7,6},{8,9},{9,8},{10,11... | collective-permute-start | bytes 1179656 | tf_op jit(solution)/shard_map/ppermute | solution.py:35
  (68 other events, 423.0 us)
